TPU v7x, 32 devices: a whole 2x2x4 slice. The times are simulated.
32 devices in a mesh: sky: 8 (over z, x), band: 4 (over y, core).
Axes of the slice: x: 2, y: 2, z: 4, core: 2. Of those that a mesh axis runs over, the one named last changes fastest.
Arguments:
- raw_blocks: bfloat16 [168, 172032], P(None, ('sky', 'band')), may hold values from -6 to 6
- patch_of_block: int32 [1024, 1], P(('sky', 'band')), may hold values from 0 to 7; in each aligned block of 32 rows (0 to 31, 32 to 63, ...) at most 8 rows name the same one
- cell_of_block: int32 [1024], P(('sky', 'band')), may hold values from 0 to 15
- band_of_block: int32 [1024], P(('sky', 'band')), may hold values from 0 to 5
- block_weight: bfloat16 [1024], P(('sky', 'band')), may hold values from 0.25 to 4
- basis_coef: bfloat16 [1024, 3], P(('sky', 'band')), may hold values from 0.25 to 1
- row_basis: float32 [3, 41], replicated, may hold values from -1 to 1
- col_basis: float32 [3, 41], replicated, may hold values from -1 to 1
- band_gain: float32 [6], replicated, may hold values from 0.5 to 2
- filter_taps: float32 [41], replicated, may hold values from -1 to 1
Outputs:
- detection: float32 [8, 512, 512], P('sky', 'band')
Inputs may be any that keep to these rules, and one draw needn't show every extreme that they name: `patch_of_block`: of the 32 blocks of one device at most 8 intersect one patch, and on some device exactly 8 do.
All inputs are finite; a program needn't handle non-finite values.
Results may differ from a plain program's by a relative error of at most 0.015.
Values may be sent and summed in bfloat16 or wider, within the bound.
No kernel may reach another device: no remote copies, remote signals or barrier semaphores. Data moves between devices by JAX's collectives and lax.ppermute only.
A program may use at most 128 MiB of HBM per device.

v0:
```python
import functools

import jax
import jax.numpy as jnp
from jax import lax
from jax.experimental import pallas as pl
from jax.experimental.pallas import tpu as pltpu
from jax.sharding import PartitionSpec as P

BANDS = 6
CR = 4
CC = 4
CELLS = 16
VMEM = pltpu.VMEM
SMEM = pltpu.SMEM


def up(value, unit):
    return -(-value // unit) * unit


def banded(row, rows, width):
    tile = pltpu.roll(jnp.broadcast_to(row, (8, width)), 0, 1, stride=1, stride_axis=0)
    return jnp.concatenate([tile if i == 0 else pltpu.roll(tile, 8 * i, 1) for i in range(rows // 8)], axis=0)


def lanes_at(row, start, width):
    parts = [row, jnp.zeros((1, width - start - row.shape[1]), row.dtype)]
    if start:
        parts.insert(0, jnp.zeros((1, start), row.dtype))
    return jnp.concatenate(parts, axis=1)


def match_kernel(small_ref, raw_ref, *rest):
    outs, (rowk_ref, colk_ref) = rest[:-2], rest[-2:]
    margin_side = raw_ref.shape[0]
    basis_count = small_ref.shape[0] // 3
    count, unused, block_side = outs[0].shape
    tap_count = margin_side - block_side + 1
    width = colk_ref.shape[0] // basis_count
    for k in range(basis_count):
        rows = banded(lanes_at(small_ref[k : k + 1, :tap_count], 0, width), block_side, width)
        rowk_ref[k * block_side : (k + 1) * block_side, :] = rows[:, :margin_side].astype(jnp.bfloat16)
        place = basis_count + k
        cols = banded(lanes_at(small_ref[place : place + 1, :tap_count], 0, width), block_side, width)
        colk_ref[k * width : (k + 1) * width, :] = cols.T.astype(jnp.bfloat16)
    for n in range(count):
        block = raw_ref[:, n * margin_side : (n + 1) * margin_side]
        sectioned = jnp.dot(rowk_ref[...], block, preferred_element_type=jnp.float32)
        total = None
        for k in range(basis_count):
            place = 2 * basis_count + k
            part = sectioned[k * block_side : (k + 1) * block_side] * small_ref[place : place + 1, n : n + 1]
            term = jnp.dot(
                part.astype(jnp.bfloat16),
                colk_ref[k * width : k * width + margin_side, :],
                preferred_element_type=jnp.float32,
            )
            total = term if total is None else total + term
        total = total.astype(jnp.bfloat16)
        start = 0
        for out_ref in outs:
            out_ref[n] = total[start : start + out_ref.shape[1]]
            start += out_ref.shape[1]


def match_blocks(small, raw, rows, block_side):
    margin_side = raw.shape[0]
    count = raw.shape[1] // margin_side
    basis_count = small.shape[0] // 3
    width = up(margin_side, 128)
    flops = 2 * count * basis_count * block_side * margin_side * (margin_side + block_side)
    return pl.pallas_call(
        match_kernel,
        out_shape=[jax.ShapeDtypeStruct((count, height, block_side), jnp.bfloat16) for height in rows],
        in_specs=[pl.BlockSpec(memory_space=VMEM)] * 2,
        out_specs=[pl.BlockSpec(memory_space=VMEM)] * len(rows),
        scratch_shapes=[
            VMEM((basis_count * block_side, margin_side), jnp.bfloat16),
            VMEM((basis_count * width, block_side), jnp.bfloat16),
        ],
        compiler_params=pltpu.CompilerParams(vmem_limit_bytes=12 << 20),
        cost_estimate=pl.CostEstimate(flops=4 * flops, bytes_accessed=4 << 20, transcendentals=0),
        name="match_blocks",
    )(small, raw)


def bin_kernel(bins_ref, scale_ref, *rest):
    groups = len(rest) // 4
    owns, others, outs, accs = (rest[i * groups : (i + 1) * groups] for i in range(4))
    step = outs[0].shape[0]
    low = pl.program_id(0) * step
    for group in range(groups):
        acc_ref = accs[group]
        acc_ref[...] = jnp.zeros_like(acc_ref)
        for source, blocks_ref in enumerate((owns[group], others[group])):
            for n in range(blocks_ref.shape[0]):
                slot = bins_ref[2 * group + source, n] - low

                @pl.when((slot >= 0) & (slot < step))
                def _(acc_ref=acc_ref, blocks_ref=blocks_ref, n=n, slot=slot, row=source * (group + 1)):
                    acc_ref[slot] += scale_ref[row, n] * blocks_ref[n].astype(jnp.float32)

        outs[group][...] = acc_ref[...].astype(outs[group].dtype)


def bin_blocks(bins, scale, own, other, size, name):
    step = min(size, 32)
    blocks = list(own) + list(other)
    rows = [part.shape[1:] for part in own]
    moved = 2 * sum(part.size for part in blocks) + 2 * size * sum(height * width for height, width in rows)
    return pl.pallas_call(
        bin_kernel,
        grid=(size // step,),
        out_shape=[jax.ShapeDtypeStruct((size,) + shape, jnp.bfloat16) for shape in rows],
        in_specs=[pl.BlockSpec(memory_space=SMEM), pl.BlockSpec(memory_space=SMEM)]
        + [pl.BlockSpec(part.shape, lambda g: (0, 0, 0)) for part in blocks],
        out_specs=[pl.BlockSpec((step,) + shape, lambda g: (g, 0, 0)) for shape in rows],
        scratch_shapes=[VMEM((step,) + shape, jnp.float32) for shape in rows],
        compiler_params=pltpu.CompilerParams(vmem_limit_bytes=20 << 20),
        cost_estimate=pl.CostEstimate(flops=2 * moved, bytes_accessed=moved, transcendentals=0),
        name=name,
    )(bins, scale, *blocks)


def filter_kernel(taps_ref, mid_ref, low_ref, high_ref, out_ref):
    cells, side, unused = mid_ref.shape
    edge = low_ref.shape[1]
    tap_count = taps_ref.shape[1]
    radius = (tap_count - 1) // 2
    taps = taps_ref[...]
    rows_in = side + 2 * edge
    row_filter = banded(lanes_at(taps, edge - radius, up(rows_in + 1, 128)), side, up(rows_in + 1, 128))
    row_filter = row_filter[:, :rows_in].astype(jnp.bfloat16)
    col_filter = banded(lanes_at(taps, side - radius, 3 * side), side, 3 * side).astype(jnp.bfloat16).T
    zero = jnp.zeros((side, side), jnp.bfloat16)
    smoothed = [zero]
    for c in range(cells):
        column = jnp.concatenate([low_ref[c], mid_ref[c], high_ref[c]], axis=0)
        smoothed.append(jnp.dot(row_filter, column, preferred_element_type=jnp.float32).astype(jnp.bfloat16))
    smoothed.append(zero)
    for c in range(cells):
        window = jnp.concatenate(smoothed[c : c + 3], axis=1)
        out_ref[:, c * side : (c + 1) * side] = jnp.dot(window, col_filter, preferred_element_type=jnp.float32)


def detect(taps, mid, low, high):
    cells, side, unused = mid.shape
    return pl.pallas_call(
        filter_kernel,
        out_shape=jax.ShapeDtypeStruct((side, cells * side), jnp.float32),
        in_specs=[pl.BlockSpec(memory_space=VMEM)] * 4,
        out_specs=pl.BlockSpec(memory_space=VMEM),
        compiler_params=pltpu.CompilerParams(vmem_limit_bytes=12 << 20),
        name="detect",
    )(taps, mid, low, high)


def halves(parts, send):
    total = None
    for part in parts:
        half = part.shape[0] // 2
        piece = (part[half:] if send else part[:half]).astype(jnp.float32)
        total = piece if total is None else total + piece
    return total


def first_halves(parts):
    return [part[: part.shape[0] // 2] for part in parts]


def local(
    raw_blocks,
    patch_of_block,
    cell_of_block,
    band_of_block,
    block_weight,
    basis_coef,
    row_basis,
    col_basis,
    band_gain,
    filter_taps,
):
    sky_count = lax.axis_size("sky")
    band_count = lax.axis_size("band")
    sky_bits = sky_count.bit_length() - 1
    band_bits = band_count.bit_length() - 1
    margin_side = raw_blocks.shape[0]
    block_count = raw_blocks.shape[1] // margin_side
    radius = (filter_taps.shape[0] - 1) // 2
    block_side = margin_side - 2 * radius
    sky_here = lax.axis_index("sky")
    band_here = lax.axis_index("band")

    def swap(array, bit):
        axis, count, bit = ("band", band_count, bit) if bit < band_bits else ("sky", sky_count, bit - band_bits)
        return lax.ppermute(array, axis, [(i, i ^ (1 << bit)) for i in range(count)])

    turn = [1, band_bits, band_bits + 1]
    later = list(range(2, band_bits)) + list(range(band_bits + 2, band_bits + sky_bits))
    orders = [turn[group:] + turn[:group] for group in range(len(turn))]
    heights = [up(block_side // 3, 16)] * 2
    heights.append(block_side - sum(heights))

    key = (patch_of_block[:, 0] * BANDS + band_of_block) * CELLS + cell_of_block
    facts = jnp.stack([key.astype(jnp.float32), block_weight.astype(jnp.float32)])[None]
    small = [row_basis, col_basis, basis_coef.T.astype(jnp.float32)]
    lanes = max(part.shape[1] for part in small)
    small = jnp.concatenate([jnp.pad(part, ((0, 0), (0, lanes - part.shape[1]))) for part in small])
    matched = match_blocks(small, raw_blocks, heights, block_side)
    others = [swap(part, order[0]) for part, order in zip(matched, orders)]
    for bit in range(band_bits + sky_bits):
        facts = jnp.concatenate([facts, swap(facts, bit)])

    near = jnp.stack([facts[0]] + [facts[1 << order[0]] for order in orders])
    near_key, near_weight = near[:, 0], near[:, 1]
    same = near_key[:, :, None, None] == facts[None, None, :, 0]
    weight_sum = jnp.sum(jnp.where(same, facts[None, None, :, 1], 0.0), axis=(2, 3))
    near_key = near_key.astype(jnp.int32)
    cell = near_key % CELLS
    band = near_key // CELLS % BANDS
    gain = jnp.sum(jnp.where(band[..., None] == jnp.arange(BANDS), band_gain, 0.0), axis=2)
    scale = gain * near_weight / jnp.maximum(weight_sum, 1.0)

    owner_off = (near_key // (CELLS * BANDS) ^ sky_here) << band_bits | (cell // CC ^ band_here)
    size = (1 << (len(turn) + len(later) - 1)) * CC
    sent_bins, kept_bins = [], []
    for group, order in enumerate(orders):
        for row in (0, group + 1):
            off = owner_off[row]
            place = jnp.zeros_like(off)
            for bit in [0] + order[1:] + later:
                place = place * 2 + (off >> bit & 1)
            place = place * CC + cell[row] % CC
            mine = off >> order[0] & 1 == 0
            sent_bins.append(jnp.where(mine, place - size, -1))
            kept_bins.append(jnp.where(mine & (place < size), place, -1))
    outgoing = bin_blocks(jnp.stack(sent_bins), scale, matched, others, size, "bins_sent")
    got = [swap(part, 0) for part in outgoing]
    kept = bin_blocks(jnp.stack(kept_bins), scale, matched, others, size, "bins_kept")
    groups = [list(pair) for pair in zip(kept, got)]
    for phase in range(1, len(turn)):
        got = [swap(halves(parts, True).astype(jnp.bfloat16), order[phase]) for parts, order in zip(groups, orders)]
        groups = [first_halves(parts) + [part] for parts, part in zip(groups, got)]
    joined = []
    for bit in later:
        outgoing = jnp.concatenate([halves(parts, True) for parts in groups], axis=1)
        for part in joined:
            outgoing = outgoing + part[part.shape[0] // 2 :].astype(jnp.float32)
        got = swap(outgoing.astype(jnp.bfloat16), bit)
        groups = [first_halves(parts) for parts in groups]
        joined = first_halves(joined) + [got]

    def full(parts):
        return functools.reduce(jnp.add, [part.astype(jnp.float32) for part in parts])

    combined = jnp.concatenate([full(parts) for parts in groups], axis=1)
    if joined:
        combined = combined + full(joined)
    combined = combined.astype(jnp.bfloat16)

    edge = up(radius, 16)
    forward = [(i, i + 1) for i in range(band_count - 1)]
    backward = [(i + 1, i) for i in range(band_count - 1)]
    low = lax.ppermute(combined[:, block_side - edge :], "band", forward)
    high = lax.ppermute(combined[:, :edge], "band", backward)
    taps = filter_taps.astype(jnp.bfloat16).astype(jnp.float32)[None]
    return detect(taps, combined, low, high)[None]


def solution(mesh):
    return jax.shard_map(
        local,
        mesh=mesh,
        in_specs=(
            P(None, ("sky", "band")),
            P(("sky", "band"), None),
            P(("sky", "band")),
            P(("sky", "band")),
            P(("sky", "band")),
            P(("sky", "band"), None),
            P(),
            P(),
            P(),
            P(),
        ),
        out_specs=P("sky", "band", None),
        check_vma=False,
    )
```

profile of v0, /device:TPU:1, one launch (start us, length us, event | category | flops | bytes accessed | tf_op | source)
XLA Modules:
  0.0 81.2 jit_solution(6944138523066544268)
XLA Ops:
  0.0 0.7 bitcast_convert_fusion
  0.7 0.7 convert_bitcast_fusion
  1.4 0.1 collective-permute-start
  1.5 0.7 pad_convert_fusion
  2.2 0.7 pad_maximum_fusion.2.small_ref
  2.9 0.0 copy-start
  2.9 1.5 %copy-done = bf16[168,5376]{1,0:T(8,128)(2,1)S(1)} copy-done((bf16[168,5376]{1,0:T(8,128)(2,1)S(1)}, bf16[168,5376]{1,0:T(8,128)(2,1)}, u32[]{:S(2)}) %copy-start) | copy-done | bytes 1806360
  4.4 4.2 %match_blocks.1 = (bf16[32,48,128]{2,1,0:T(8,128)(2,1)S(1)}, bf16[32,48,128]{2,1,0:T(8,128)(2,1)S(1)}, bf16[32,32,128]{2,1,0:T(8,128)(2,1)S(1)}) custom-call(f32[9,41]{1,0:T(8,128)S(1)} %pad_maximum_fusion.2.small_ref, bf16[168,5376]{1,0:T(8,128)(2,1)S(1)} %copy-done), custom_call_target="tpu_custom_call" | custom-call | flops 4888461312 | bytes 4194304 | tf_op jit(solution)/shard_map/match_blocks/pallas_call | solution.py:73
  8.6 2.8 %collective-permute-start.5 = (bf16[32,48,128]{2,1,0:T(8,128)(2,1)S(1)}, bf16[32,48,128]{2,1,0:T(8,128)(2,1)S(1)}, u32[]{:S(2)}, u32[]{:S(2)}) collective-permute-start(bf16[32,48,128]{2,1,0:T(8,128)(2,1)S(1)} %get-tuple-element.14.rest_0_), channel_id=1, source_target_pairs={{0,2},{1,3},{2,0},{3,1},{4,6},{5,7},{6,4},{7,5},{8,10},{9,11},{10,... | collective-permute-start | bytes 1179656 | tf_op jit(solution)/shard_map/ppermute | solution.py:197
  11.3 1.2 %collective-permute-start.6 = (bf16[32,48,128]{2,1,0:T(8,128)(2,1)S(1)}, bf16[32,48,128]{2,1,0:T(8,128)(2,1)S(1)}, u32[]{:S(2)}, u32[]{:S(2)}) collective-permute-start(bf16[32,48,128]{2,1,0:T(8,128)(2,1)S(1)} %get-tuple-element.15.rest_1_), channel_id=1, source_target_pairs={{0,4},{4,0},{8,12},{12,8},{16,20},{20,16},{24,28},{28,24},{1,5},{5... | collective-permute-start | bytes 1179656 | tf_op jit(solution)/shard_map/ppermute | solution.py:197
  12.5 1.3 %collective-permute-start.7 = (bf16[32,32,128]{2,1,0:T(8,128)(2,1)S(1)}, bf16[32,32,128]{2,1,0:T(8,128)(2,1)S(1)}, u32[]{:S(2)}, u32[]{:S(2)}) collective-permute-start(bf16[32,32,128]{2,1,0:T(8,128)(2,1)S(1)} %get-tuple-element.16.rest_2_), channel_id=1, source_target_pairs={{0,8},{4,12},{8,0},{12,4},{16,24},{20,28},{24,16},{28,20},{1,9},{5... | collective-permute-start | bytes 786440 | tf_op jit(solution)/shard_map/ppermute | solution.py:197
  13.8 0.0 collective-permute-done
  13.9 0.3 collective-permute-start.1
  14.2 6.7 %collective-permute-done.1 = f32[2,2,32]{2,1,0:T(2,128)S(1)} collective-permute-done((f32[2,2,32]{2,1,0:T(2,128)S(1)}, f32[2,2,32]{2,1,0:T(2,128)S(1)}, u32[]{:S(2)}, u32[]{:S(2)}) %collective-permute-start.1) | collective-permute-done | bytes 544 | tf_op jit(solution)/shard_map/ppermute | solution.py:197
  20.9 1.2 %collective-permute-start.2 = (f32[4,2,32]{2,1,0:T(2,128)S(1)}, f32[4,2,32]{2,1,0:T(2,128)S(1)}, u32[]{:S(2)}, u32[]{:S(2)}) collective-permute-start(f32[4,2,32]{2,1,0:T(2,128)S(1)} %fusion.3), channel_id=1, source_target_pairs={{0,4},{4,0},{8,12},{12,8},{16,20},{20,16},{24,28},{28,24},{1,5},{5... | collective-permute-start | bytes 3080 | tf_op jit(solution)/shard_map/ppermute | solution.py:197
  22.1 1.2 %collective-permute-done.2 = f32[4,2,32]{2,1,0:T(2,128)S(1)} collective-permute-done((f32[4,2,32]{2,1,0:T(2,128)S(1)}, f32[4,2,32]{2,1,0:T(2,128)S(1)}, u32[]{:S(2)}, u32[]{:S(2)}) %collective-permute-start.2) | collective-permute-done | bytes 1056 | tf_op jit(solution)/shard_map/ppermute | solution.py:197
  23.3 1.4 %collective-permute-start.3 = (f32[8,2,32]{2,1,0:T(2,128)S(1)}, f32[8,2,32]{2,1,0:T(2,128)S(1)}, u32[]{:S(2)}, u32[]{:S(2)}) collective-permute-start(f32[8,2,32]{2,1,0:T(2,128)S(1)} %pad_maximum_fusion.1), channel_id=1, source_target_pairs={{0,8},{4,12},{8,0},{12,4},{16,24},{20,28},{24,16},{28,20},{1,9},{5... | collective-permute-start | bytes 6152 | tf_op jit(solution)/shard_map/ppermute | solution.py:197
  24.7 1.2 %collective-permute-done.3 = f32[8,2,32]{2,1,0:T(2,128)S(1)} collective-permute-done((f32[8,2,32]{2,1,0:T(2,128)S(1)}, f32[8,2,32]{2,1,0:T(2,128)S(1)}, u32[]{:S(2)}, u32[]{:S(2)}) %collective-permute-start.3) | collective-permute-done | bytes 2080 | tf_op jit(solution)/shard_map/ppermute | solution.py:197
  25.9 0.6 and_select_fusion
  26.5 0.6 and_select_fusion.5
  27.1 2.4 %collective-permute-start.4 = (f32[16,2,32]{2,1,0:T(2,128)S(1)}, f32[16,2,32]{2,1,0:T(2,128)S(1)}, u32[]{:S(2)}, u32[]{:S(2)}) collective-permute-start(f32[16,2,32]{2,1,0:T(2,128)S(1)} %get-tuple-element.46), channel_id=1, source_target_pairs={{0,16},{4,20},{8,24},{12,28},{16,0},{20,4},{24,8},{28,12},{1,17},{... | collective-permute-start | bytes 12296 | tf_op jit(solution)/shard_map/ppermute | solution.py:197
  29.5 0.0 copy-done.1
  29.5 0.1 select_reduce_fusion.1
  29.6 1.0 %collective-permute-done.4 = f32[16,2,32]{2,1,0:T(2,128)S(1)} collective-permute-done((f32[16,2,32]{2,1,0:T(2,128)S(1)}, f32[16,2,32]{2,1,0:T(2,128)S(1)}, u32[]{:S(2)}, u32[]{:S(2)}) %collective-permute-start.4) | collective-permute-done | bytes 4128 | tf_op jit(solution)/shard_map/ppermute | solution.py:197
  30.7 0.9 %select_reduce_fusion = f32[4,32]{1,0:T(4,128)S(1)} fusion(f32[32,32]{1,0:T(8,128)S(1)} %bitcast.29, f32[32,32]{1,0:T(8,128)S(1)} %bitcast.28, f32[4,32]{1,0:T(4,128)S(1)} %bitcast.31), kind=kLoop, calls=%fused_computation | loop fusion | flops 393088 | bytes 9216 | tf_op jit(solution)/shard_map/reduce_sum | solution.py:218
  31.6 0.0 collective-permute-done.7.rest_5_
  31.6 0.0 collective-permute-done.5.rest_3_
  31.6 0.0 collective-permute-done.6.rest_4_
  31.7 2.6 %bins_sent.1 = (bf16[32,48,128]{2,1,0:T(8,128)(2,1)S(1)}, bf16[32,48,128]{2,1,0:T(8,128)(2,1)S(1)}, bf16[32,32,128]{2,1,0:T(8,128)(2,1)S(1)}) custom-call(s32[6,32]{1,0:T(8,128)S(1)} %stack.39.bins_ref, f32[4,32]{1,0:T(4,128)S(1)} %maximum_divide_fusion.scale_ref, bf16[32,48,128]{2,1,0:T(8,128)(2,1)S(1)} %get-tuple-element.14.rest_0_, ...), custom_call_target="tpu_custom_call" | custom-call | flops 6291456 | bytes 3145728 | tf_op jit(solution)/shard_map/bins_sent/pallas_call | solution.py:112
  34.3 4.2 %collective-permute-start.14 = (bf16[32,32,128]{2,1,0:T(8,128)(2,1)S(1)}, bf16[32,32,128]{2,1,0:T(8,128)(2,1)}, u32[]{:S(2)}, u32[]{:S(2)}) collective-permute-start(bf16[32,32,128]{2,1,0:T(8,128)(2,1)S(1)} %get-tuple-element.22), channel_id=1, source_target_pairs={{0,1},{1,0},{2,3},{3,2},{4,5},{5,4},{6,7},{7,6},{8,9},{9,8},{10,11... | collective-permute-start | bytes 786440 | tf_op jit(solution)/shard_map/ppermute | solution.py:197
  38.5 0.1 collective-permute-start.8
  38.5 0.7 stack.38.bins_ref
  39.2 0.5 collective-permute-start.11
  39.7 2.7 %bins_kept.1 = (bf16[32,48,128]{2,1,0:T(8,128)(2,1)S(1)}, bf16[32,48,128]{2,1,0:T(8,128)(2,1)S(1)}, bf16[32,32,128]{2,1,0:T(8,128)(2,1)S(1)}) custom-call(s32[6,32]{1,0:T(8,128)S(1)} %stack.38.bins_ref, f32[4,32]{1,0:T(4,128)S(1)} %maximum_divide_fusion.scale_ref, bf16[32,48,128]{2,1,0:T(8,128)(2,1)S(1)} %get-tuple-element.14.rest_0_, ...), custom_call_target="tpu_custom_call" | custom-call | flops 6291456 | bytes 3145728 | tf_op jit(solution)/shard_map/bins_kept/pallas_call | solution.py:112
  42.4 0.0 collective-permute-done.14
  42.4 0.9 %add_convert_fusion.2 = bf16[16,32,128]{2,1,0:T(8,128)(2,1)S(1)} fusion(bf16[32,32,128]{2,1,0:T(8,128)(2,1)} %collective-permute-done.14, bf16[32,32,128]{2,1,0:T(8,128)(2,1)S(1)} %get-tuple-element.21), kind=kLoop, calls=%fused_computation.5 | loop fusion | flops 262144 | bytes 393216 | tf_op jit(solution)/shard_map/convert_element_type | solution.py:243
  43.3 1.5 %collective-permute-start.15 = (bf16[16,32,128]{2,1,0:T(8,128)(2,1)S(1)}, bf16[16,32,128]{2,1,0:T(8,128)(2,1)S(1)}, u32[]{:S(2)}, u32[]{:S(2)}) collective-permute-start(bf16[16,32,128]{2,1,0:T(8,128)(2,1)S(1)} %add_convert_fusion.2), channel_id=1, source_target_pairs={{0,2},{1,3},{2,0},{3,1},{4,6},{5,7},{6,4},{7,5},{8,10},{9,11},{10,... | collective-permute-start | bytes 393224 | tf_op jit(solution)/shard_map/ppermute | solution.py:197
  44.9 0.0 collective-permute-done.8
  44.9 0.1 add_convert_fusion.1
  44.9 1.3 %collective-permute-start.9 = (bf16[16,48,128]{2,1,0:T(8,128)(2,1)S(1)}, bf16[16,48,128]{2,1,0:T(8,128)(2,1)S(1)}, u32[]{:S(2)}, u32[]{:S(2)}) collective-permute-start(bf16[16,48,128]{2,1,0:T(8,128)(2,1)S(1)} %add_convert_fusion.1), channel_id=1, source_target_pairs={{0,4},{4,0},{8,12},{12,8},{16,20},{20,16},{24,28},{28,24},{1,5},{5... | collective-permute-start | bytes 589832 | tf_op jit(solution)/shard_map/ppermute | solution.py:197
  46.2 2.3 %collective-permute-done.15 = bf16[16,32,128]{2,1,0:T(8,128)(2,1)S(1)} collective-permute-done((bf16[16,32,128]{2,1,0:T(8,128)(2,1)S(1)}, bf16[16,32,128]{2,1,0:T(8,128)(2,1)S(1)}, u32[]{:S(2)}, u32[]{:S(2)}) %collective-permute-start.15) | collective-permute-done | bytes 131104 | tf_op jit(solution)/shard_map/ppermute | solution.py:197
  48.5 0.9 %add_convert_fusion.5 = bf16[8,32,128]{2,1,0:T(8,128)(2,1)S(1)} fusion(bf16[16,32,128]{2,1,0:T(8,128)(2,1)S(1)} %collective-permute-done.15, bf16[32,32,128]{2,1,0:T(8,128)(2,1)} %collective-permute-done.14, bf16[32,32,128]{2,1,0:T(8,128)(2,1)S(1)} %get-tuple-element.21), kind=kLoop, calls=%fused_computation.9 | loop fusion | flops 196608 | bytes 262144 | tf_op jit(solution)/shard_map/convert_element_type | solution.py:243
  49.3 1.5 %collective-permute-start.16 = (bf16[8,32,128]{2,1,0:T(8,128)(2,1)S(1)}, bf16[8,32,128]{2,1,0:T(8,128)(2,1)S(1)}, u32[]{:S(2)}, u32[]{:S(2)}) collective-permute-start(bf16[8,32,128]{2,1,0:T(8,128)(2,1)S(1)} %add_convert_fusion.5), channel_id=1, source_target_pairs={{0,4},{4,0},{8,12},{12,8},{16,20},{20,16},{24,28},{28,24},{1,5},{5... | collective-permute-start | bytes 196616 | tf_op jit(solution)/shard_map/ppermute | solution.py:197
  50.8 0.0 collective-permute-done.11
  50.9 0.1 add_convert_fusion
  50.9 1.4 %collective-permute-start.12 = (bf16[16,48,128]{2,1,0:T(8,128)(2,1)S(1)}, bf16[16,48,128]{2,1,0:T(8,128)(2,1)S(1)}, u32[]{:S(2)}, u32[]{:S(2)}) collective-permute-start(bf16[16,48,128]{2,1,0:T(8,128)(2,1)S(1)} %add_convert_fusion), channel_id=1, source_target_pairs={{0,8},{4,12},{8,0},{12,4},{16,24},{20,28},{24,16},{28,20},{1,9},{5... | collective-permute-start | bytes 589832 | tf_op jit(solution)/shard_map/ppermute | solution.py:197
  52.3 0.2 collective-permute-done.16
  52.5 0.8 %add_convert_fusion.8 = (bf16[4,32,128]{2,1,0:T(8,128)(2,1)S(1)}, f32[4,32,128]{2,1,0:T(8,128)S(1)}) fusion(bf16[8,32,128]{2,1,0:T(8,128)(2,1)S(1)} %collective-permute-done.16, bf16[16,32,128]{2,1,0:T(8,128)(2,1)S(1)} %collective-permute-done.15, bf16[32,32,128]{2,1,0:T(8,128)(2,1)} %collective-permute-done.14, bf16[32,32,128]{2,1,0:T(8,128)(2,1)S(1)} %get-tuple-element.21), kind=kLoop, calls=%fused_computation.14 | loop fusion | flops 245760 | bytes 360448 | tf_op jit(solution)/shard_map/convert.7
  53.3 0.0 collective-permute-done.9
  53.4 1.6 %collective-permute-start.10 = (bf16[8,48,128]{2,1,0:T(8,128)(2,1)S(1)}, bf16[8,48,128]{2,1,0:T(8,128)(2,1)S(1)}, u32[]{:S(2)}, u32[]{:S(2)}) collective-permute-start(bf16[8,48,128]{2,1,0:T(8,128)(2,1)S(1)} %add_convert_fusion.4), channel_id=1, source_target_pairs={{0,8},{4,12},{8,0},{12,4},{16,24},{20,28},{24,16},{28,20},{1,9},{5... | collective-permute-start | bytes 294920 | tf_op jit(solution)/shard_map/ppermute | solution.py:197
  55.0 1.2 %collective-permute-done.12 = bf16[16,48,128]{2,1,0:T(8,128)(2,1)S(1)} collective-permute-done((bf16[16,48,128]{2,1,0:T(8,128)(2,1)S(1)}, bf16[16,48,128]{2,1,0:T(8,128)(2,1)S(1)}, u32[]{:S(2)}, u32[]{:S(2)}) %collective-permute-start.12) | collective-permute-done | bytes 196640 | tf_op jit(solution)/shard_map/ppermute | solution.py:197
  56.3 1.3 %collective-permute-start.13 = (bf16[8,48,128]{2,1,0:T(8,128)(2,1)S(1)}, bf16[8,48,128]{2,1,0:T(8,128)(2,1)S(1)}, u32[]{:S(2)}, u32[]{:S(2)}) collective-permute-start(bf16[8,48,128]{2,1,0:T(8,128)(2,1)S(1)} %add_convert_fusion.3), channel_id=1, source_target_pairs={{0,2},{1,3},{2,0},{3,1},{4,6},{5,7},{6,4},{7,5},{8,10},{9,11},{10,... | collective-permute-start | bytes 294920 | tf_op jit(solution)/shard_map/ppermute | solution.py:197
  57.6 0.8 collective-permute-done.10
  58.4 0.1 add_convert_fusion.7
  58.4 1.6 %collective-permute-done.13 = bf16[8,48,128]{2,1,0:T(8,128)(2,1)S(1)} collective-permute-done((bf16[8,48,128]{2,1,0:T(8,128)(2,1)S(1)}, bf16[8,48,128]{2,1,0:T(8,128)(2,1)S(1)}, u32[]{:S(2)}, u32[]{:S(2)}) %collective-permute-start.13) | collective-permute-done | bytes 98336 | tf_op jit(solution)/shard_map/ppermute | solution.py:197
  60.0 0.1 add_convert_fusion.6
  60.1 2.3 %collective-permute-start.17 = (bf16[4,128,128]{2,1,0:T(8,128)(2,1)S(1)}, bf16[4,128,128]{2,1,0:T(8,128)(2,1)S(1)}, u32[]{:S(2)}, u32[]{:S(2)}) collective-permute-start(bf16[4,128,128]{2,1,0:T(8,128)(2,1)S(1)} %pad_maximum_fusion), channel_id=1, source_target_pairs={{0,16},{4,20},{8,24},{12,28},{16,0},{20,4},{24,8},{28,12},{1,17},{... | collective-permute-start | bytes 393224 | tf_op jit(solution)/shard_map/ppermute | solution.py:197
  62.4 3.8 %collective-permute-done.17 = bf16[4,128,128]{2,1,0:T(8,128)(2,1)S(1)} collective-permute-done((bf16[4,128,128]{2,1,0:T(8,128)(2,1)S(1)}, bf16[4,128,128]{2,1,0:T(8,128)(2,1)S(1)}, u32[]{:S(2)}, u32[]{:S(2)}) %collective-permute-start.17) | collective-permute-done | bytes 131104 | tf_op jit(solution)/shard_map/ppermute | solution.py:197
  66.3 8.3 %collective-permute-start.18 = (bf16[4,32,128]{2,1,0:T(8,128)(2,1)S(1)}, bf16[4,32,128]{2,1,0:T(8,128)(2,1)S(1)}, u32[]{:S(2)}, u32[]{:S(2)}) collective-permute-start(bf16[4,32,128]{2,1,0:T(8,128)(2,1)S(1)} %get-tuple-element.43), channel_id=1, source_target_pairs={{0,1},{1,2},{2,3},{4,5},{5,6},{6,7},{8,9},{9,10},{10,11},{12,13},{... | collective-permute-start | bytes 98312 | tf_op jit(solution)/shard_map/ppermute | solution.py:265
  74.6 1.9 %collective-permute-start.19 = (bf16[4,32,128]{2,1,0:T(8,128)(2,1)S(1)}, bf16[4,32,128]{2,1,0:T(8,128)(2,1)S(1)}, u32[]{:S(2)}, u32[]{:S(2)}) collective-permute-start(bf16[4,32,128]{2,1,0:T(8,128)(2,1)S(1)} %get-tuple-element.42), channel_id=1, source_target_pairs={{1,0},{2,1},{3,2},{5,4},{6,5},{7,6},{9,8},{10,9},{11,10},{13,12},{... | collective-permute-start | bytes 98312 | tf_op jit(solution)/shard_map/ppermute | solution.py:266
  76.5 0.0 copy-done.2
  76.5 0.0 collective-permute-done.18.low_ref
  76.5 3.3 %collective-permute-done.19.high_ref = bf16[4,32,128]{2,1,0:T(8,128)(2,1)S(1)} collective-permute-done((bf16[4,32,128]{2,1,0:T(8,128)(2,1)S(1)}, bf16[4,32,128]{2,1,0:T(8,128)(2,1)S(1)}, u32[]{:S(2)}, u32[]{:S(2)}) %collective-permute-start.19) | collective-permute-done | bytes 32800 | tf_op jit(solution)/shard_map/ppermute | solution.py:266
  79.8 1.4 %detect.1 = f32[128,512]{1,0:T(8,128)} custom-call(f32[1,41]{1,0:T(1,128)S(1)} %bitcast_convert_fusion.1.taps_ref, bf16[4,128,128]{2,1,0:T(8,128)(2,1)S(1)} %fusion.mid_ref, bf16[4,32,128]{2,1,0:T(8,128)(2,1)S(1)} %collective-permute-done.18.low_ref, bf16[4,32,128]{2,1,0:T(8,128)(2,1)S(1)} %collective-permute-done.19.high_ref), custom_call_target="tpu_custom_call" | custom-call | tf_op jit(solution)/shard_map/detect/pallas_call | solution.py:149
  (28 shorter events, 0.3 us)
Async XLA Ops:
  1.4 12.5 %collective-permute-start = (f32[1,2,32]{2,1,0:T(2,128)S(1)}, f32[1,2,32]{2,1,0:T(2,128)S(1)}, u32[]{:S(2)}, u32[]{:S(2)}) collective-permute-start(f32[1,2,32]{2,1,0:T(2,128)S(1)} %maximum_bitcast_fusion), channel_id=1, source_target_pairs={{0,1},{1,0},{2,3},{3,2},{4,5},{5,4},{6,7},{7,6},{8,9},{9,8},{10,11... | collective-permute-start | bytes 776 | tf_op jit(solution)/shard_map/ppermute | solution.py:197
  2.9 1.5 %copy-start = (bf16[168,5376]{1,0:T(8,128)(2,1)S(1)}, bf16[168,5376]{1,0:T(8,128)(2,1)}, u32[]{:S(2)}) copy-start(bf16[168,5376]{1,0:T(8,128)(2,1)} %raw_ref.1) | copy-start | bytes 5419012
  4.4 25.1 %copy-start.1 = (f32[6]{0:T(128)S(1)}, f32[6]{0:T(128)}, u32[]{:S(2)}) copy-start(f32[6]{0:T(128)} %param.18) | copy-start | bytes 76
  8.6 23.1 %collective-permute-start.5 = (bf16[32,48,128]{2,1,0:T(8,128)(2,1)S(1)}, bf16[32,48,128]{2,1,0:T(8,128)(2,1)S(1)}, u32[]{:S(2)}, u32[]{:S(2)}) collective-permute-start(bf16[32,48,128]{2,1,0:T(8,128)(2,1)S(1)} %get-tuple-element.14.rest_0_), channel_id=1, source_target_pairs={{0,2},{1,3},{2,0},{3,1},{4,6},{5,7},{6,4},{7,5},{8,10},{9,11},{10,... | collective-permute-start | bytes 1179656 | tf_op jit(solution)/shard_map/ppermute | solution.py:197
  11.3 20.3 %collective-permute-start.6 = (bf16[32,48,128]{2,1,0:T(8,128)(2,1)S(1)}, bf16[32,48,128]{2,1,0:T(8,128)(2,1)S(1)}, u32[]{:S(2)}, u32[]{:S(2)}) collective-permute-start(bf16[32,48,128]{2,1,0:T(8,128)(2,1)S(1)} %get-tuple-element.15.rest_1_), channel_id=1, source_target_pairs={{0,4},{4,0},{8,12},{12,8},{16,20},{20,16},{24,28},{28,24},{1,5},{5... | collective-permute-start | bytes 1179656 | tf_op jit(solution)/shard_map/ppermute | solution.py:197
  12.5 19.1 %collective-permute-start.7 = (bf16[32,32,128]{2,1,0:T(8,128)(2,1)S(1)}, bf16[32,32,128]{2,1,0:T(8,128)(2,1)S(1)}, u32[]{:S(2)}, u32[]{:S(2)}) collective-permute-start(bf16[32,32,128]{2,1,0:T(8,128)(2,1)S(1)} %get-tuple-element.16.rest_2_), channel_id=1, source_target_pairs={{0,8},{4,12},{8,0},{12,4},{16,24},{20,28},{24,16},{28,20},{1,9},{5... | collective-permute-start | bytes 786440 | tf_op jit(solution)/shard_map/ppermute | solution.py:197
  13.9 7.0 %collective-permute-start.1 = (f32[2,2,32]{2,1,0:T(2,128)S(1)}, f32[2,2,32]{2,1,0:T(2,128)S(1)}, u32[]{:S(2)}, u32[]{:S(2)}) collective-permute-start(f32[2,2,32]{2,1,0:T(2,128)S(1)} %pad_maximum_fusion.5), channel_id=1, source_target_pairs={{0,2},{1,3},{2,0},{3,1},{4,6},{5,7},{6,4},{7,5},{8,10},{9,11},{10,... | collective-permute-start | bytes 1544 | tf_op jit(solution)/shard_map/ppermute | solution.py:197
  20.9 2.5 %collective-permute-start.2 = (f32[4,2,32]{2,1,0:T(2,128)S(1)}, f32[4,2,32]{2,1,0:T(2,128)S(1)}, u32[]{:S(2)}, u32[]{:S(2)}) collective-permute-start(f32[4,2,32]{2,1,0:T(2,128)S(1)} %fusion.3), channel_id=1, source_target_pairs={{0,4},{4,0},{8,12},{12,8},{16,20},{20,16},{24,28},{28,24},{1,5},{5... | collective-permute-start | bytes 3080 | tf_op jit(solution)/shard_map/ppermute | solution.py:197
  23.3 2.6 %collective-permute-start.3 = (f32[8,2,32]{2,1,0:T(2,128)S(1)}, f32[8,2,32]{2,1,0:T(2,128)S(1)}, u32[]{:S(2)}, u32[]{:S(2)}) collective-permute-start(f32[8,2,32]{2,1,0:T(2,128)S(1)} %pad_maximum_fusion.1), channel_id=1, source_target_pairs={{0,8},{4,12},{8,0},{12,4},{16,24},{20,28},{24,16},{28,20},{1,9},{5... | collective-permute-start | bytes 6152 | tf_op jit(solution)/shard_map/ppermute | solution.py:197
  27.1 3.6 %collective-permute-start.4 = (f32[16,2,32]{2,1,0:T(2,128)S(1)}, f32[16,2,32]{2,1,0:T(2,128)S(1)}, u32[]{:S(2)}, u32[]{:S(2)}) collective-permute-start(f32[16,2,32]{2,1,0:T(2,128)S(1)} %get-tuple-element.46), channel_id=1, source_target_pairs={{0,16},{4,20},{8,24},{12,28},{16,0},{20,4},{24,8},{28,12},{1,17},{... | collective-permute-start | bytes 12296 | tf_op jit(solution)/shard_map/ppermute | solution.py:197
  34.3 8.1 %collective-permute-start.14 = (bf16[32,32,128]{2,1,0:T(8,128)(2,1)S(1)}, bf16[32,32,128]{2,1,0:T(8,128)(2,1)}, u32[]{:S(2)}, u32[]{:S(2)}) collective-permute-start(bf16[32,32,128]{2,1,0:T(8,128)(2,1)S(1)} %get-tuple-element.22), channel_id=1, source_target_pairs={{0,1},{1,0},{2,3},{3,2},{4,5},{5,4},{6,7},{7,6},{8,9},{9,8},{10,11... | collective-permute-start | bytes 786440 | tf_op jit(solution)/shard_map/ppermute | solution.py:197
  38.5 6.4 %collective-permute-start.8 = (bf16[32,48,128]{2,1,0:T(8,128)(2,1)S(1)}, bf16[32,48,128]{2,1,0:T(8,128)(2,1)S(1)}, u32[]{:S(2)}, u32[]{:S(2)}) collective-permute-start(bf16[32,48,128]{2,1,0:T(8,128)(2,1)S(1)} %get-tuple-element.18), channel_id=1, source_target_pairs={{0,1},{1,0},{2,3},{3,2},{4,5},{5,4},{6,7},{7,6},{8,9},{9,8},{10,11... | collective-permute-start | bytes 1179656 | tf_op jit(solution)/shard_map/ppermute | solution.py:197
  39.2 11.6 %collective-permute-start.11 = (bf16[32,48,128]{2,1,0:T(8,128)(2,1)S(1)}, bf16[32,48,128]{2,1,0:T(8,128)(2,1)S(1)}, u32[]{:S(2)}, u32[]{:S(2)}) collective-permute-start(bf16[32,48,128]{2,1,0:T(8,128)(2,1)S(1)} %get-tuple-element.20), channel_id=1, source_target_pairs={{0,1},{1,0},{2,3},{3,2},{4,5},{5,4},{6,7},{7,6},{8,9},{9,8},{10,11... | collective-permute-start | bytes 1179656 | tf_op jit(solution)/shard_map/ppermute | solution.py:197
  43.3 5.1 %collective-permute-start.15 = (bf16[16,32,128]{2,1,0:T(8,128)(2,1)S(1)}, bf16[16,32,128]{2,1,0:T(8,128)(2,1)S(1)}, u32[]{:S(2)}, u32[]{:S(2)}) collective-permute-start(bf16[16,32,128]{2,1,0:T(8,128)(2,1)S(1)} %add_convert_fusion.2), channel_id=1, source_target_pairs={{0,2},{1,3},{2,0},{3,1},{4,6},{5,7},{6,4},{7,5},{8,10},{9,11},{10,... | collective-permute-start | bytes 393224 | tf_op jit(solution)/shard_map/ppermute | solution.py:197
  44.9 8.4 %collective-permute-start.9 = (bf16[16,48,128]{2,1,0:T(8,128)(2,1)S(1)}, bf16[16,48,128]{2,1,0:T(8,128)(2,1)S(1)}, u32[]{:S(2)}, u32[]{:S(2)}) collective-permute-start(bf16[16,48,128]{2,1,0:T(8,128)(2,1)S(1)} %add_convert_fusion.1), channel_id=1, source_target_pairs={{0,4},{4,0},{8,12},{12,8},{16,20},{20,16},{24,28},{28,24},{1,5},{5... | collective-permute-start | bytes 589832 | tf_op jit(solution)/shard_map/ppermute | solution.py:197
  49.3 3.2 %collective-permute-start.16 = (bf16[8,32,128]{2,1,0:T(8,128)(2,1)S(1)}, bf16[8,32,128]{2,1,0:T(8,128)(2,1)S(1)}, u32[]{:S(2)}, u32[]{:S(2)}) collective-permute-start(bf16[8,32,128]{2,1,0:T(8,128)(2,1)S(1)} %add_convert_fusion.5), channel_id=1, source_target_pairs={{0,4},{4,0},{8,12},{12,8},{16,20},{20,16},{24,28},{28,24},{1,5},{5... | collective-permute-start | bytes 196616 | tf_op jit(solution)/shard_map/ppermute | solution.py:197
  50.9 25.7 %copy-start.2 = (f32[41]{0:T(128)S(1)}, f32[41]{0:T(128)}, u32[]{:S(2)}) copy-start(f32[41]{0:T(128)} %param.19) | copy-start | bytes 496
  50.9 5.3 %collective-permute-start.12 = (bf16[16,48,128]{2,1,0:T(8,128)(2,1)S(1)}, bf16[16,48,128]{2,1,0:T(8,128)(2,1)S(1)}, u32[]{:S(2)}, u32[]{:S(2)}) collective-permute-start(bf16[16,48,128]{2,1,0:T(8,128)(2,1)S(1)} %add_convert_fusion), channel_id=1, source_target_pairs={{0,8},{4,12},{8,0},{12,4},{16,24},{20,28},{24,16},{28,20},{1,9},{5... | collective-permute-start | bytes 589832 | tf_op jit(solution)/shard_map/ppermute | solution.py:197
  53.4 5.0 %collective-permute-start.10 = (bf16[8,48,128]{2,1,0:T(8,128)(2,1)S(1)}, bf16[8,48,128]{2,1,0:T(8,128)(2,1)S(1)}, u32[]{:S(2)}, u32[]{:S(2)}) collective-permute-start(bf16[8,48,128]{2,1,0:T(8,128)(2,1)S(1)} %add_convert_fusion.4), channel_id=1, source_target_pairs={{0,8},{4,12},{8,0},{12,4},{16,24},{20,28},{24,16},{28,20},{1,9},{5... | collective-permute-start | bytes 294920 | tf_op jit(solution)/shard_map/ppermute | solution.py:197
  56.3 3.7 %collective-permute-start.13 = (bf16[8,48,128]{2,1,0:T(8,128)(2,1)S(1)}, bf16[8,48,128]{2,1,0:T(8,128)(2,1)S(1)}, u32[]{:S(2)}, u32[]{:S(2)}) collective-permute-start(bf16[8,48,128]{2,1,0:T(8,128)(2,1)S(1)} %add_convert_fusion.3), channel_id=1, source_target_pairs={{0,2},{1,3},{2,0},{3,1},{4,6},{5,7},{6,4},{7,5},{8,10},{9,11},{10,... | collective-permute-start | bytes 294920 | tf_op jit(solution)/shard_map/ppermute | solution.py:197
  60.1 6.2 %collective-permute-start.17 = (bf16[4,128,128]{2,1,0:T(8,128)(2,1)S(1)}, bf16[4,128,128]{2,1,0:T(8,128)(2,1)S(1)}, u32[]{:S(2)}, u32[]{:S(2)}) collective-permute-start(bf16[4,128,128]{2,1,0:T(8,128)(2,1)S(1)} %pad_maximum_fusion), channel_id=1, source_target_pairs={{0,16},{4,20},{8,24},{12,28},{16,0},{20,4},{24,8},{28,12},{1,17},{... | collective-permute-start | bytes 393224 | tf_op jit(solution)/shard_map/ppermute | solution.py:197
  66.3 10.2 %collective-permute-start.18 = (bf16[4,32,128]{2,1,0:T(8,128)(2,1)S(1)}, bf16[4,32,128]{2,1,0:T(8,128)(2,1)S(1)}, u32[]{:S(2)}, u32[]{:S(2)}) collective-permute-start(bf16[4,32,128]{2,1,0:T(8,128)(2,1)S(1)} %get-tuple-element.43), channel_id=1, source_target_pairs={{0,1},{1,2},{2,3},{4,5},{5,6},{6,7},{8,9},{9,10},{10,11},{12,13},{... | collective-permute-start | bytes 98312 | tf_op jit(solution)/shard_map/ppermute | solution.py:265
  74.6 5.2 %collective-permute-start.19 = (bf16[4,32,128]{2,1,0:T(8,128)(2,1)S(1)}, bf16[4,32,128]{2,1,0:T(8,128)(2,1)S(1)}, u32[]{:S(2)}, u32[]{:S(2)}) collective-permute-start(bf16[4,32,128]{2,1,0:T(8,128)(2,1)S(1)} %get-tuple-element.42), channel_id=1, source_target_pairs={{1,0},{2,1},{3,2},{5,4},{6,5},{7,6},{9,8},{10,9},{11,10},{13,12},{... | collective-permute-start | bytes 98312 | tf_op jit(solution)/shard_map/ppermute | solution.py:266
where the time goes:
time: 81.6 us; the launch traced here: 81.2 us
  starting transfers between devices  36.5 us (45%)
  waiting for transfers between devices  23.3 us (29%)
  Pallas kernels  10.9 us (13%)
  other arithmetic  7.94 us (10%)
  local copies, waits for them, and re-layouts  2.29 us (3%)
    ppermute x18, starting transfers between devices, swap(): return lax.ppermute(array, axis, [(i, i ^ 1 << bit) for i in range(count)])  26.3 us
    ppermute x18, waiting for transfers between devices, swap(): return lax.ppermute(array, axis, [(i, i ^ 1 << bit) for i in range(count)])  20.1 us
    ppermute x1, starting transfers between devices, local(): low = lax.ppermute(combined[:, block_side - edge:], 'band', forward)  8.25 us
    pallas_call x2, Pallas kernels, bin_blocks(): pl.pallas_call(bin_kernel, grid=(size // step,), out_shape=[jax.ShapeDtyp...  5.29 us
    pallas_call x1, Pallas kernels, match_blocks(): pl.pallas_call(match_kernel, out_shape=[jax.ShapeDtypeStruct((count, heig...  4.21 us
    ppermute x1, waiting for transfers between devices, local(): high = lax.ppermute(combined[:, :edge], 'band', backward)  3.27 us
    convert_element_type x6, other arithmetic, local(): halves(parts, True).astype(jnp.bfloat16)  2.01 us
    ppermute x1, starting transfers between devices, local(): high = lax.ppermute(combined[:, :edge], 'band', backward)  1.92 us
  transfers between devices with their start and end apart: 20, of which 11 were waited for; matrix products, arithmetic and copies ran while one was open for 9% of the time, Pallas kernels for 8%

commit v1 on v0

--- a/solution.py
+++ b/solution.py
@@ -31,26 +31,19 @@
     return jnp.concatenate(parts, axis=1)
 
 
-def match_kernel(small_ref, raw_ref, *rest):
-    outs, (rowk_ref, colk_ref) = rest[:-2], rest[-2:]
+def match_part(first, small_ref, raw_ref, rowk_ref, colk_ref, outs):
     margin_side = raw_ref.shape[0]
     basis_count = small_ref.shape[0] // 3
     count, unused, block_side = outs[0].shape
-    tap_count = margin_side - block_side + 1
     width = colk_ref.shape[0] // basis_count
-    for k in range(basis_count):
-        rows = banded(lanes_at(small_ref[k : k + 1, :tap_count], 0, width), block_side, width)
-        rowk_ref[k * block_side : (k + 1) * block_side, :] = rows[:, :margin_side].astype(jnp.bfloat16)
-        place = basis_count + k
-        cols = banded(lanes_at(small_ref[place : place + 1, :tap_count], 0, width), block_side, width)
-        colk_ref[k * width : (k + 1) * width, :] = cols.T.astype(jnp.bfloat16)
     for n in range(count):
-        block = raw_ref[:, n * margin_side : (n + 1) * margin_side]
+        here = first + n
+        block = raw_ref[:, here * margin_side : (here + 1) * margin_side]
         sectioned = jnp.dot(rowk_ref[...], block, preferred_element_type=jnp.float32)
         total = None
         for k in range(basis_count):
             place = 2 * basis_count + k
-            part = sectioned[k * block_side : (k + 1) * block_side] * small_ref[place : place + 1, n : n + 1]
+            part = sectioned[k * block_side : (k + 1) * block_side] * small_ref[place : place + 1, here : here + 1]
             term = jnp.dot(
                 part.astype(jnp.bfloat16),
                 colk_ref[k * width : k * width + margin_side, :],
@@ -64,59 +57,81 @@
             start += out_ref.shape[1]
 
 
-def match_blocks(small, raw, rows, block_side):
+def match_first(after_ref, small_ref, raw_ref, *rest):
+    outs, (rowk_ref, colk_ref) = rest[:-2], rest[-2:]
+    margin_side = raw_ref.shape[0]
+    basis_count = small_ref.shape[0] // 3
+    block_side = outs[0].shape[2]
+    tap_count = margin_side - block_side + 1
+    width = colk_ref.shape[0] // basis_count
+    for k in range(basis_count):
+        rows = banded(lanes_at(small_ref[k : k + 1, :tap_count], 0, width), block_side, width)
+        rowk_ref[k * block_side : (k + 1) * block_side, :] = rows[:, :margin_side].astype(jnp.bfloat16)
+        place = basis_count + k
+        cols = banded(lanes_at(small_ref[place : place + 1, :tap_count], 0, width), block_side, width)
+        colk_ref[k * width : (k + 1) * width, :] = cols.T.astype(jnp.bfloat16)
+    match_part(0, small_ref, raw_ref, rowk_ref, colk_ref, outs)
+
+
+def match_next(first, after_ref, small_ref, raw_ref, rowk_ref, colk_ref, *outs):
+    match_part(first, small_ref, raw_ref, rowk_ref, colk_ref, outs)
+
+
+def match_blocks(first, count, small, raw, kernels, rows, block_side, after):
     margin_side = raw.shape[0]
-    count = raw.shape[1] // margin_side
     basis_count = small.shape[0] // 3
     width = up(margin_side, 128)
     flops = 2 * count * basis_count * block_side * margin_side * (margin_side + block_side)
+    out_shape = [jax.ShapeDtypeStruct((count, height, block_side), jnp.bfloat16) for height in rows]
+    if first == 0:
+        out_shape += [
+            jax.ShapeDtypeStruct((basis_count * block_side, margin_side), jnp.bfloat16),
+            jax.ShapeDtypeStruct((basis_count * width, block_side), jnp.bfloat16),
+        ]
+    found = pl.pallas_call(
+        match_first if first == 0 else functools.partial(match_next, first),
+        out_shape=out_shape,
+        in_specs=[pl.BlockSpec(memory_space=pl.ANY)] + [pl.BlockSpec(memory_space=VMEM)] * (2 + len(kernels)),
+        out_specs=[pl.BlockSpec(memory_space=VMEM)] * len(out_shape),
+        compiler_params=pltpu.CompilerParams(vmem_limit_bytes=12 << 20),
+        cost_estimate=pl.CostEstimate(flops=4 * flops, bytes_accessed=2 << 20, transcendentals=0),
+        name="match_first" if first == 0 else "match_next",
+    )(after, small, raw, *kernels)
+    return found[: len(rows)], kernels or tuple(found[len(rows) :])
+
+
+def bin_kernel(groups, bins_ref, scale_ref, *rest):
+    blocks_refs, (out_ref, acc_ref) = rest[:-2], rest[-2:]
+    parts = len(blocks_refs) // (2 * groups)
+    step = acc_ref.shape[0]
+    low = pl.program_id(0) * step
+    acc_ref[...] = jnp.zeros_like(acc_ref)
+    for index, blocks_ref in enumerate(blocks_refs):
+        line, part = index // parts, index % parts
+        group, source = line // 2, line % 2
+        count = blocks_ref.shape[0]
+        for n in range(count):
+            slot = bins_ref[line, part * count + n] - low
+
+            @pl.when((slot >= 0) & (slot < step))
+            def _(blocks_ref=blocks_ref, n=n, slot=slot, row=source * (group + 1), place=part * count + n):
+                acc_ref[slot] += scale_ref[row, place] * blocks_ref[n].astype(jnp.float32)
+
+    out_ref[...] = acc_ref[...].astype(out_ref.dtype)
+
+
+def bin_blocks(bins, scale, blocks, groups, size, name):
+    shape = blocks[0].shape[1:]
+    step = min(groups * size, 64)
+    moved = 2 * sum(part.size for part in blocks) + 2 * groups * size * shape[0] * shape[1]
     return pl.pallas_call(
-        match_kernel,
-        out_shape=[jax.ShapeDtypeStruct((count, height, block_side), jnp.bfloat16) for height in rows],
-        in_specs=[pl.BlockSpec(memory_space=VMEM)] * 2,
-        out_specs=[pl.BlockSpec(memory_space=VMEM)] * len(rows),
-        scratch_shapes=[
-            VMEM((basis_count * block_side, margin_side), jnp.bfloat16),
-            VMEM((basis_count * width, block_side), jnp.bfloat16),
-        ],
-        compiler_params=pltpu.CompilerParams(vmem_limit_bytes=12 << 20),
-        cost_estimate=pl.CostEstimate(flops=4 * flops, bytes_accessed=4 << 20, transcendentals=0),
-        name="match_blocks",
-    )(small, raw)
-
-
-def bin_kernel(bins_ref, scale_ref, *rest):
-    groups = len(rest) // 4
-    owns, others, outs, accs = (rest[i * groups : (i + 1) * groups] for i in range(4))
-    step = outs[0].shape[0]
-    low = pl.program_id(0) * step
-    for group in range(groups):
-        acc_ref = accs[group]
-        acc_ref[...] = jnp.zeros_like(acc_ref)
-        for source, blocks_ref in enumerate((owns[group], others[group])):
-            for n in range(blocks_ref.shape[0]):
-                slot = bins_ref[2 * group + source, n] - low
-
-                @pl.when((slot >= 0) & (slot < step))
-                def _(acc_ref=acc_ref, blocks_ref=blocks_ref, n=n, slot=slot, row=source * (group + 1)):
-                    acc_ref[slot] += scale_ref[row, n] * blocks_ref[n].astype(jnp.float32)
-
-        outs[group][...] = acc_ref[...].astype(outs[group].dtype)
-
-
-def bin_blocks(bins, scale, own, other, size, name):
-    step = min(size, 32)
-    blocks = list(own) + list(other)
-    rows = [part.shape[1:] for part in own]
-    moved = 2 * sum(part.size for part in blocks) + 2 * size * sum(height * width for height, width in rows)
-    return pl.pallas_call(
-        bin_kernel,
-        grid=(size // step,),
-        out_shape=[jax.ShapeDtypeStruct((size,) + shape, jnp.bfloat16) for shape in rows],
+        functools.partial(bin_kernel, groups),
+        grid=(groups * size // step,),
+        out_shape=jax.ShapeDtypeStruct((groups * size,) + shape, jnp.bfloat16),
         in_specs=[pl.BlockSpec(memory_space=SMEM), pl.BlockSpec(memory_space=SMEM)]
         + [pl.BlockSpec(part.shape, lambda g: (0, 0, 0)) for part in blocks],
-        out_specs=[pl.BlockSpec((step,) + shape, lambda g: (g, 0, 0)) for shape in rows],
-        scratch_shapes=[VMEM((step,) + shape, jnp.float32) for shape in rows],
+        out_specs=pl.BlockSpec((step,) + shape, lambda g: (g, 0, 0)),
+        scratch_shapes=[VMEM((step,) + shape, jnp.float32)],
         compiler_params=pltpu.CompilerParams(vmem_limit_bytes=20 << 20),
         cost_estimate=pl.CostEstimate(flops=2 * moved, bytes_accessed=moved, transcendentals=0),
         name=name,
@@ -196,21 +211,34 @@
         axis, count, bit = ("band", band_count, bit) if bit < band_bits else ("sky", sky_count, bit - band_bits)
         return lax.ppermute(array, axis, [(i, i ^ (1 << bit)) for i in range(count)])
 
-    turn = [1, band_bits, band_bits + 1]
-    later = list(range(2, band_bits)) + list(range(band_bits + 2, band_bits + sky_bits))
+    turn = [1, band_bits]
+    later = list(range(2, band_bits)) + list(range(band_bits + 1, band_bits + sky_bits))
     orders = [turn[group:] + turn[:group] for group in range(len(turn))]
-    heights = [up(block_side // 3, 16)] * 2
-    heights.append(block_side - sum(heights))
+    heights = [block_side // len(orders)] * len(orders)
 
     key = (patch_of_block[:, 0] * BANDS + band_of_block) * CELLS + cell_of_block
     facts = jnp.stack([key.astype(jnp.float32), block_weight.astype(jnp.float32)])[None]
+    facts = jnp.concatenate(
+        [facts]
+        + [lax.ppermute(facts, "band", [(i, i ^ off) for i in range(band_count)]) for off in range(1, band_count)]
+    )
     small = [row_basis, col_basis, basis_coef.T.astype(jnp.float32)]
     lanes = max(part.shape[1] for part in small)
     small = jnp.concatenate([jnp.pad(part, ((0, 0), (0, lanes - part.shape[1]))) for part in small])
-    matched = match_blocks(small, raw_blocks, heights, block_side)
-    others = [swap(part, order[0]) for part, order in zip(matched, orders)]
-    for bit in range(band_bits + sky_bits):
-        facts = jnp.concatenate([facts, swap(facts, bit)])
+    part_count = 2 if block_count % 2 == 0 else 1
+    part_blocks = block_count // part_count
+    kernels, own, others = (), [[], []], [[], []]
+    for part in range(max(part_count, sky_bits)):
+        got = swap(facts, band_bits + part) if part < sky_bits else None
+        if part < part_count:
+            found, kernels = match_blocks(
+                part * part_blocks, part_blocks, small, raw_blocks, kernels, heights, block_side, facts
+            )
+            for group, order in enumerate(orders):
+                own[group].append(found[group])
+                others[group].append(swap(found[group], order[0]))
+        if got is not None:
+            facts = jnp.concatenate([facts, got])
 
     near = jnp.stack([facts[0]] + [facts[1 << order[0]] for order in orders])
     near_key, near_weight = near[:, 0], near[:, 1]
@@ -224,8 +252,9 @@
 
     owner_off = (near_key // (CELLS * BANDS) ^ sky_here) << band_bits | (cell // CC ^ band_here)
     size = (1 << (len(turn) + len(later) - 1)) * CC
-    sent_bins, kept_bins = [], []
+    sent_bins, kept_bins, blocks = [], [], []
     for group, order in enumerate(orders):
+        blocks += own[group] + others[group]
         for row in (0, group + 1):
             off = owner_off[row]
             place = jnp.zeros_like(off)
@@ -233,12 +262,12 @@
                 place = place * 2 + (off >> bit & 1)
             place = place * CC + cell[row] % CC
             mine = off >> order[0] & 1 == 0
-            sent_bins.append(jnp.where(mine, place - size, -1))
-            kept_bins.append(jnp.where(mine & (place < size), place, -1))
-    outgoing = bin_blocks(jnp.stack(sent_bins), scale, matched, others, size, "bins_sent")
-    got = [swap(part, 0) for part in outgoing]
-    kept = bin_blocks(jnp.stack(kept_bins), scale, matched, others, size, "bins_kept")
-    groups = [list(pair) for pair in zip(kept, got)]
+            sent_bins.append(jnp.where(mine & (place >= size), place - size + group * size, -1))
+            kept_bins.append(jnp.where(mine & (place < size), place + group * size, -1))
+    outgoing = bin_blocks(jnp.stack(sent_bins), scale, blocks, len(orders), size, "bins_sent")
+    got = swap(outgoing, 0)
+    kept = bin_blocks(jnp.stack(kept_bins), scale, blocks, len(orders), size, "bins_kept")
+    groups = [[part[group * size : (group + 1) * size] for part in (kept, got)] for group in range(len(orders))]
     for phase in range(1, len(turn)):
         got = [swap(halves(parts, True).astype(jnp.bfloat16), order[phase]) for parts, order in zip(groups, orders)]
         groups = [first_halves(parts) + [part] for parts, part in zip(groups, got)]

time: 81.6 us -> 65.4 us (0.80)
  starting transfers between devices: 36.5 us -> 25.6 us
  other arithmetic: 7.94 us -> 4.38 us
    ppermute x18 -> x12, starting transfers between devices: 26.3 us -> 14.6 us  [swap(): return lax.ppermute(array, axis, [(i, i ^ 1 << bit) for i in range(count)])]
    ppermute x0 -> x3, starting transfers between devices: none -> 2.86 us  [local(): lax.ppermute(facts, 'band', [(i, i ^ off) for i in range(band_count)])]
    ppermute x1, starting transfers between devices: 8.25 us -> 6.17 us  [local(): low = lax.ppermute(combined[:, block_side - edge:], 'band', forward)]
    convert_element_type x6 -> x1, other arithmetic: 2.01 us -> 0.18 us  [local(): halves(parts, True).astype(jnp.bfloat16)]
    ppermute x18 -> x12, waiting for transfers between devices: 20.1 us -> 18.5 us  [swap(): return lax.ppermute(array, axis, [(i, i ^ 1 << bit) for i in range(count)])]
    ppermute x0 -> x3, waiting for transfers between devices: none -> 1.54 us  [local(): lax.ppermute(facts, 'band', [(i, i ^ off) for i in range(band_count)])]
    select_n x3, other arithmetic: 1.15 us -> 0.05 us  [the longest x2 0.04 us: local(): kept_bins.append(jnp.where(mine & (place < size), place + group * size, -1))]
    pallas_call x3 -> x4, Pallas kernels: 9.5 us -> 8.69 us  [the longest x2 4.55 us: match_blocks(): pl.pallas_call(match_first if first == 0 else functools.partial(match_nex...]
  transfers between devices with their start and end apart: 20 -> 17, of which waited for: 11 -> 9; matrix products, arithmetic and copies ran while one was open for 9% -> 4% of each run, Pallas kernels for 8% -> 10%
where the time goes in v1:
time: 65.4 us; the launch traced here: 65.2 us
  starting transfers between devices  25.6 us (39%)
  waiting for transfers between devices  23.3 us (36%)
  Pallas kernels  10.1 us (15%)
  other arithmetic  4.38 us (7%)
  local copies, waits for them, and re-layouts  1.6 us (2%)
    ppermute x12, waiting for transfers between devices, swap(): return lax.ppermute(array, axis, [(i, i ^ 1 << bit) for i in range(count)])  18.5 us
    ppermute x12, starting transfers between devices, swap(): return lax.ppermute(array, axis, [(i, i ^ 1 << bit) for i in range(count)])  14.6 us
    ppermute x1, starting transfers between devices, local(): low = lax.ppermute(combined[:, block_side - edge:], 'band', forward)  6.17 us
    pallas_call x2, Pallas kernels, match_blocks(): pl.pallas_call(match_first if first == 0 else functools.partial(match_nex...  4.55 us
    pallas_call x2, Pallas kernels, bin_blocks(): pl.pallas_call(functools.partial(bin_kernel, groups), grid=(groups * size...  4.14 us
    ppermute x1, waiting for transfers between devices, local(): high = lax.ppermute(combined[:, :edge], 'band', backward)  3.27 us
    ppermute x3, starting transfers between devices, local(): lax.ppermute(facts, 'band', [(i, i ^ off) for i in range(band_count)])  2.86 us
    ppermute x1, starting transfers between devices, local(): high = lax.ppermute(combined[:, :edge], 'band', backward)  1.92 us
  transfers between devices with their start and end apart: 17, of which 9 were waited for; matrix products, arithmetic and copies ran while one was open for 4% of the time, Pallas kernels for 10%

profile of v1, /device:TPU:1, one launch (start us, length us, event | category | flops | bytes accessed | tf_op | source)
XLA Modules:
  0.0 65.2 jit_solution(890407956883253868)
XLA Ops:
  0.0 0.7 %bitcast_convert_fusion = f32[1,32]{1,0:T(1,128)S(1)} fusion(bf16[32]{0:T(256)(128)(2,1)} %param.14), kind=kLoop, calls=%fused_computation.88 | loop fusion | flops 32 | bytes 192 | tf_op jit(solution)/shard_map/stack | solution.py:220
  0.7 0.7 %convert_bitcast_fusion = f32[1,32]{1,0:T(1,128)S(1)} fusion(s32[32]{0:T(128)} %param.12, s32[32]{0:T(128)} %param.13, s32[32,1]{0,1:T(1,128)} %param.11), kind=kLoop, calls=%fused_computation.102 | loop fusion | flops 160 | bytes 512 | tf_op jit(solution)/shard_map/stack | solution.py:220
  1.4 0.1 collective-permute-start.1
  1.5 2.7 %collective-permute-start = (f32[1,2,32]{2,1,0:T(2,128)S(1)}, f32[1,2,32]{2,1,0:T(2,128)S(1)}, u32[]{:S(2)}, u32[]{:S(2)}) collective-permute-start(f32[1,2,32]{2,1,0:T(2,128)S(1)} %maximum_bitcast_fusion), channel_id=1, source_target_pairs={{0,2},{1,3},{2,0},{3,1},{4,6},{5,7},{6,4},{7,5},{8,10},{9,11},{10,... | collective-permute-start | bytes 776 | tf_op jit(solution)/shard_map/ppermute | solution.py:223
  4.2 0.0 collective-permute-start.2
  4.2 0.7 %pad_convert_fusion = f32[3,41]{1,0:T(4,128)S(1)} fusion(bf16[3,32]{1,0:T(4,128)(2,1)} %bitcast.46), kind=kLoop, calls=%fused_computation.81 | loop fusion | flops 123 | bytes 684 | tf_op jit(solution)/shard_map/jit(_pad)/pad | solution.py:227
  4.9 0.7 %pad_maximum_fusion.1.small_ref = f32[9,41]{1,0:T(8,128)S(1)} fusion(f32[3,41]{1,0:T(4,128)S(1)} %pad_convert_fusion, f32[3,41]{1,0:T(4,128)} %param.17, f32[3,41]{1,0:T(4,128)} %param.16), kind=kLoop, calls=%fused_computation.34 | loop fusion | flops 738 | bytes 2952 | tf_op jit(solution)/shard_map/concatenate | solution.py:227
  5.6 0.0 collective-permute-done.1
  5.6 0.0 collective-permute-done
  5.6 1.5 %collective-permute-done.2 = f32[1,2,32]{2,1,0:T(2,128)S(1)} collective-permute-done((f32[1,2,32]{2,1,0:T(2,128)S(1)}, f32[1,2,32]{2,1,0:T(2,128)S(1)}, u32[]{:S(2)}, u32[]{:S(2)}) %collective-permute-start.2) | collective-permute-done | bytes 288 | tf_op jit(solution)/shard_map/ppermute | solution.py:223
  7.2 1.2 %collective-permute-start.3 = (f32[4,2,32]{2,1,0:T(2,128)S(1)}, f32[4,2,32]{2,1,0:T(2,128)S(1)}, u32[]{:S(2)}, u32[]{:S(2)}) collective-permute-start(f32[4,2,32]{2,1,0:T(2,128)S(1)} %pad_maximum_fusion.2.after_ref), channel_id=1, source_target_pairs={{0,4},{4,0},{8,12},{12,8},{16,20},{20,16},{24,28},{28,24},{1,5},{5... | collective-permute-start | bytes 3080 | tf_op jit(solution)/shard_map/ppermute | solution.py:212
  8.4 0.0 copy-start
  8.4 1.5 %copy-done = bf16[168,5376]{1,0:T(8,128)(2,1)S(1)} copy-done((bf16[168,5376]{1,0:T(8,128)(2,1)S(1)}, bf16[168,5376]{1,0:T(8,128)(2,1)}, u32[]{:S(2)}) %copy-start) | copy-done | bytes 1806360
  9.9 2.4 %match_first.1 = (bf16[16,64,128]{2,1,0:T(8,128)(2,1)S(1)}, bf16[16,64,128]{2,1,0:T(8,128)(2,1)S(1)}, bf16[384,168]{1,0:T(8,128)(2,1)S(1)}, bf16[768,128]{1,0:T(8,128)(2,1)S(1)}) custom-call(f32[4,2,32]{2,1,0:T(2,128)S(1)} %pad_maximum_fusion.2.after_ref, f32[9,41]{1,0:T(8,128)S(1)} %pad_maximum_fusion.1.small_ref, bf16[168,5376]{1,0:T(8,128)(2,1)S(1)} %copy-done), custom_call_target="tpu_custom_call" | custom-call | flops 2444230656 | bytes 2097152 | tf_op jit(solution)/shard_map/match_first/pallas_call | solution.py:91
  12.3 0.3 collective-permute-start.6
  12.6 0.3 collective-permute-start.8
  12.9 0.0 collective-permute-done.3
  12.9 1.4 %collective-permute-start.4 = (f32[8,2,32]{2,1,0:T(2,128)S(1)}, f32[8,2,32]{2,1,0:T(2,128)S(1)}, u32[]{:S(2)}, u32[]{:S(2)}) collective-permute-start(f32[8,2,32]{2,1,0:T(2,128)S(1)} %get-tuple-element.44.after_ref), channel_id=1, source_target_pairs={{0,8},{4,12},{8,0},{12,4},{16,24},{20,28},{24,16},{28,20},{1,9},{5... | collective-permute-start | bytes 6152 | tf_op jit(solution)/shard_map/ppermute | solution.py:212
  14.2 0.0 copy-start.1
  14.2 2.2 %match_next.1 = (bf16[16,64,128]{2,1,0:T(8,128)(2,1)S(1)}, bf16[16,64,128]{2,1,0:T(8,128)(2,1)S(1)}) custom-call(f32[8,2,32]{2,1,0:T(2,128)S(1)} %get-tuple-element.44.after_ref, f32[9,41]{1,0:T(8,128)S(1)} %pad_maximum_fusion.1.small_ref, bf16[168,5376]{1,0:T(8,128)(2,1)S(1)} %copy-done, bf16[384,168]{1,0:T(8,128)(2,1)S(1)} %get-tuple-element.12.rowk_ref, ...), custom_call_target="tpu_custom_call" | custom-call | flops 2444230656 | bytes 2097152 | tf_op jit(solution)/shard_map/match_next/pallas_call | solution.py:91
  16.4 1.3 %collective-permute-start.7 = (bf16[16,64,128]{2,1,0:T(8,128)(2,1)S(1)}, bf16[16,64,128]{2,1,0:T(8,128)(2,1)S(1)}, u32[]{:S(2)}, u32[]{:S(2)}) collective-permute-start(bf16[16,64,128]{2,1,0:T(8,128)(2,1)S(1)} %get-tuple-element.14.rest_1_), channel_id=1, source_target_pairs={{0,2},{1,3},{2,0},{3,1},{4,6},{5,7},{6,4},{7,5},{8,10},{9,11},{10,... | collective-permute-start | bytes 786440 | tf_op jit(solution)/shard_map/ppermute | solution.py:212
  17.7 1.2 %collective-permute-start.9 = (bf16[16,64,128]{2,1,0:T(8,128)(2,1)S(1)}, bf16[16,64,128]{2,1,0:T(8,128)(2,1)S(1)}, u32[]{:S(2)}, u32[]{:S(2)}) collective-permute-start(bf16[16,64,128]{2,1,0:T(8,128)(2,1)S(1)} %get-tuple-element.16.rest_5_), channel_id=1, source_target_pairs={{0,4},{4,0},{8,12},{12,8},{16,20},{20,16},{24,28},{28,24},{1,5},{5... | collective-permute-start | bytes 786440 | tf_op jit(solution)/shard_map/ppermute | solution.py:212
  19.0 0.0 copy-done.1
  19.1 0.1 select_reduce_fusion.1
  19.1 0.0 collective-permute-done.4
  19.2 2.4 %collective-permute-start.5 = (f32[16,2,32]{2,1,0:T(2,128)S(1)}, f32[16,2,32]{2,1,0:T(2,128)S(1)}, u32[]{:S(2)}, u32[]{:S(2)}) collective-permute-start(f32[16,2,32]{2,1,0:T(2,128)S(1)} %get-tuple-element.40), channel_id=1, source_target_pairs={{0,16},{4,20},{8,24},{12,28},{16,0},{20,4},{24,8},{28,12},{1,17},{... | collective-permute-start | bytes 12296 | tf_op jit(solution)/shard_map/ppermute | solution.py:212
  21.6 1.2 %collective-permute-done.5 = f32[16,2,32]{2,1,0:T(2,128)S(1)} collective-permute-done((f32[16,2,32]{2,1,0:T(2,128)S(1)}, f32[16,2,32]{2,1,0:T(2,128)S(1)}, u32[]{:S(2)}, u32[]{:S(2)}) %collective-permute-start.5) | collective-permute-done | bytes 4128 | tf_op jit(solution)/shard_map/ppermute | solution.py:212
  22.8 0.9 %select_reduce_fusion = f32[3,32]{1,0:T(4,128)S(1)} fusion(f32[32,32]{1,0:T(8,128)S(1)} %bitcast.44, f32[32,32]{1,0:T(8,128)S(1)} %bitcast.43, f32[3,32]{1,0:T(4,128)S(1)} %bitcast.45), kind=kLoop, calls=%fused_computation | loop fusion | flops 294816 | bytes 8960 | tf_op jit(solution)/shard_map/reduce_sum | solution.py:246
  23.8 0.0 collective-permute-done.6.rest_2_
  23.8 0.0 collective-permute-done.8.rest_6_
  23.8 1.4 %collective-permute-done.7.rest_3_ = bf16[16,64,128]{2,1,0:T(8,128)(2,1)S(1)} collective-permute-done((bf16[16,64,128]{2,1,0:T(8,128)(2,1)S(1)}, bf16[16,64,128]{2,1,0:T(8,128)(2,1)S(1)}, u32[]{:S(2)}, u32[]{:S(2)}) %collective-permute-start.7) | collective-permute-done | bytes 262176 | tf_op jit(solution)/shard_map/ppermute | solution.py:212
  25.2 0.0 collective-permute-done.9.rest_7_
  25.2 2.1 %bins_sent.1 = bf16[64,64,128]{2,1,0:T(8,128)(2,1)S(1)} custom-call(s32[4,32]{1,0:T(4,128)S(1)} %pad_add_fusion.1.bins_ref, f32[3,32]{1,0:T(4,128)S(1)} %fusion.6.scale_ref, bf16[16,64,128]{2,1,0:T(8,128)(2,1)S(1)} %get-tuple-element.11.rest_0_, bf16[16,64,128]{2,1,0:T(8,128)(2,1)S(1)} %get-tuple-element.14.rest_1_, ...), custom_call_target="tpu_custom_call" | custom-call | flops 6291456 | bytes 3145728 | tf_op jit(solution)/shard_map/bins_sent/pallas_call | solution.py:127
  27.3 1.9 %collective-permute-start.10 = (bf16[64,64,128]{2,1,0:T(8,128)(2,1)S(1)}, bf16[64,64,128]{2,1,0:T(8,128)(2,1)S(1)}, u32[]{:S(2)}, u32[]{:S(2)}) collective-permute-start(bf16[64,64,128]{2,1,0:T(8,128)(2,1)S(1)} %bins_sent.1), channel_id=1, source_target_pairs={{0,1},{1,0},{2,3},{3,2},{4,5},{5,4},{6,7},{7,6},{8,9},{9,8},{10,11... | collective-permute-start | bytes 3145736 | tf_op jit(solution)/shard_map/ppermute | solution.py:212
  29.1 2.1 %bins_kept.1 = bf16[64,64,128]{2,1,0:T(8,128)(2,1)S(1)} custom-call(s32[4,32]{1,0:T(4,128)S(1)} %pad_add_fusion.bins_ref, f32[3,32]{1,0:T(4,128)S(1)} %fusion.6.scale_ref, bf16[16,64,128]{2,1,0:T(8,128)(2,1)S(1)} %get-tuple-element.11.rest_0_, bf16[16,64,128]{2,1,0:T(8,128)(2,1)S(1)} %get-tuple-element.14.rest_1_, ...), custom_call_target="tpu_custom_call" | custom-call | flops 6291456 | bytes 3145728 | tf_op jit(solution)/shard_map/bins_kept/pallas_call | solution.py:127
  31.2 0.2 collective-permute-done.10
  31.4 0.2 add_convert_fusion.1
  31.6 0.8 %collective-permute-start.11 = (bf16[16,64,128]{2,1,0:T(8,128)(2,1)S(1)}, bf16[16,64,128]{2,1,0:T(8,128)(2,1)S(1)}, u32[]{:S(2)}, u32[]{:S(2)}) collective-permute-start(bf16[16,64,128]{2,1,0:T(8,128)(2,1)S(1)} %get-tuple-element.34), channel_id=1, source_target_pairs={{0,4},{4,0},{8,12},{12,8},{16,20},{20,16},{24,28},{28,24},{1,5},{5... | collective-permute-start | bytes 786440 | tf_op jit(solution)/shard_map/ppermute | solution.py:212
  32.4 0.8 %collective-permute-start.12 = (bf16[16,64,128]{2,1,0:T(8,128)(2,1)S(1)}, bf16[16,64,128]{2,1,0:T(8,128)(2,1)S(1)}, u32[]{:S(2)}, u32[]{:S(2)}) collective-permute-start(bf16[16,64,128]{2,1,0:T(8,128)(2,1)S(1)} %get-tuple-element.35), channel_id=1, source_target_pairs={{0,2},{1,3},{2,0},{3,1},{4,6},{5,7},{6,4},{7,5},{8,10},{9,11},{10,... | collective-permute-start | bytes 786440 | tf_op jit(solution)/shard_map/ppermute | solution.py:212
  33.1 6.1 %collective-permute-done.11 = bf16[16,64,128]{2,1,0:T(8,128)(2,1)S(1)} collective-permute-done((bf16[16,64,128]{2,1,0:T(8,128)(2,1)S(1)}, bf16[16,64,128]{2,1,0:T(8,128)(2,1)S(1)}, u32[]{:S(2)}, u32[]{:S(2)}) %collective-permute-start.11) | collective-permute-done | bytes 262176 | tf_op jit(solution)/shard_map/ppermute | solution.py:212
  39.2 0.4 collective-permute-done.12
  39.6 0.1 add_convert_fusion.3
  39.7 0.0 copy-start.2
  39.7 0.9 %collective-permute-start.13 = (bf16[8,128,128]{2,1,0:T(8,128)(2,1)S(1)}, bf16[8,128,128]{2,1,0:T(8,128)(2,1)S(1)}, u32[]{:S(2)}, u32[]{:S(2)}) collective-permute-start(bf16[8,128,128]{2,1,0:T(8,128)(2,1)S(1)} %pad_maximum_fusion), channel_id=1, source_target_pairs={{0,8},{4,12},{8,0},{12,4},{16,24},{20,28},{24,16},{28,20},{1,9},{5... | collective-permute-start | bytes 786440 | tf_op jit(solution)/shard_map/ppermute | solution.py:212
  40.6 0.1 convert_add_fusion.1
  40.7 5.3 %collective-permute-done.13 = bf16[8,128,128]{2,1,0:T(8,128)(2,1)S(1)} collective-permute-done((bf16[8,128,128]{2,1,0:T(8,128)(2,1)S(1)}, bf16[8,128,128]{2,1,0:T(8,128)(2,1)S(1)}, u32[]{:S(2)}, u32[]{:S(2)}) %collective-permute-start.13) | collective-permute-done | bytes 262176 | tf_op jit(solution)/shard_map/ppermute | solution.py:212
  46.1 2.4 %collective-permute-start.14 = (bf16[4,128,128]{2,1,0:T(8,128)(2,1)S(1)}, bf16[4,128,128]{2,1,0:T(8,128)(2,1)S(1)}, u32[]{:S(2)}, u32[]{:S(2)}) collective-permute-start(bf16[4,128,128]{2,1,0:T(8,128)(2,1)S(1)} %fusion.1), channel_id=1, source_target_pairs={{0,16},{4,20},{8,24},{12,28},{16,0},{20,4},{24,8},{28,12},{1,17},{... | collective-permute-start | bytes 393224 | tf_op jit(solution)/shard_map/ppermute | solution.py:212
  48.5 3.8 %collective-permute-done.14 = bf16[4,128,128]{2,1,0:T(8,128)(2,1)S(1)} collective-permute-done((bf16[4,128,128]{2,1,0:T(8,128)(2,1)S(1)}, bf16[4,128,128]{2,1,0:T(8,128)(2,1)S(1)}, u32[]{:S(2)}, u32[]{:S(2)}) %collective-permute-start.14) | collective-permute-done | bytes 131104 | tf_op jit(solution)/shard_map/ppermute | solution.py:212
  52.4 6.2 %collective-permute-start.15 = (bf16[4,32,128]{2,1,0:T(8,128)(2,1)S(1)}, bf16[4,32,128]{2,1,0:T(8,128)(2,1)S(1)}, u32[]{:S(2)}, u32[]{:S(2)}) collective-permute-start(bf16[4,32,128]{2,1,0:T(8,128)(2,1)S(1)} %get-tuple-element.37), channel_id=1, source_target_pairs={{0,1},{1,2},{2,3},{4,5},{5,6},{6,7},{8,9},{9,10},{10,11},{12,13},{... | collective-permute-start | bytes 98312 | tf_op jit(solution)/shard_map/ppermute | solution.py:294
  58.5 1.9 %collective-permute-start.16 = (bf16[4,32,128]{2,1,0:T(8,128)(2,1)S(1)}, bf16[4,32,128]{2,1,0:T(8,128)(2,1)S(1)}, u32[]{:S(2)}, u32[]{:S(2)}) collective-permute-start(bf16[4,32,128]{2,1,0:T(8,128)(2,1)S(1)} %get-tuple-element.36), channel_id=1, source_target_pairs={{1,0},{2,1},{3,2},{5,4},{6,5},{7,6},{9,8},{10,9},{11,10},{13,12},{... | collective-permute-start | bytes 98312 | tf_op jit(solution)/shard_map/ppermute | solution.py:295
  60.5 0.0 copy-done.2
  60.5 0.0 collective-permute-done.15.low_ref
  60.5 3.3 %collective-permute-done.16.high_ref = bf16[4,32,128]{2,1,0:T(8,128)(2,1)S(1)} collective-permute-done((bf16[4,32,128]{2,1,0:T(8,128)(2,1)S(1)}, bf16[4,32,128]{2,1,0:T(8,128)(2,1)S(1)}, u32[]{:S(2)}, u32[]{:S(2)}) %collective-permute-start.16) | collective-permute-done | bytes 32800 | tf_op jit(solution)/shard_map/ppermute | solution.py:295
  63.8 1.4 %detect.1 = f32[128,512]{1,0:T(8,128)} custom-call(f32[1,41]{1,0:T(1,128)S(1)} %bitcast_convert_fusion.1.taps_ref, bf16[4,128,128]{2,1,0:T(8,128)(2,1)S(1)} %fusion.mid_ref, bf16[4,32,128]{2,1,0:T(8,128)(2,1)S(1)} %collective-permute-done.15.low_ref, bf16[4,32,128]{2,1,0:T(8,128)(2,1)S(1)} %collective-permute-done.16.high_ref), custom_call_target="tpu_custom_call" | custom-call | tf_op jit(solution)/shard_map/detect/pallas_call | solution.py:164
  (26 shorter events, 0.3 us)
Async XLA Ops:
  1.4 4.3 %collective-permute-start.1 = (f32[1,2,32]{2,1,0:T(2,128)S(1)}, f32[1,2,32]{2,1,0:T(2,128)S(1)}, u32[]{:S(2)}, u32[]{:S(2)}) collective-permute-start(f32[1,2,32]{2,1,0:T(2,128)S(1)} %maximum_bitcast_fusion), channel_id=1, source_target_pairs={{0,1},{1,0},{2,3},{3,2},{4,5},{5,4},{6,7},{7,6},{8,9},{9,8},{10,11... | collective-permute-start | bytes 776 | tf_op jit(solution)/shard_map/ppermute | solution.py:223
  1.5 4.2 %collective-permute-start = (f32[1,2,32]{2,1,0:T(2,128)S(1)}, f32[1,2,32]{2,1,0:T(2,128)S(1)}, u32[]{:S(2)}, u32[]{:S(2)}) collective-permute-start(f32[1,2,32]{2,1,0:T(2,128)S(1)} %maximum_bitcast_fusion), channel_id=1, source_target_pairs={{0,2},{1,3},{2,0},{3,1},{4,6},{5,7},{6,4},{7,5},{8,10},{9,11},{10,... | collective-permute-start | bytes 776 | tf_op jit(solution)/shard_map/ppermute | solution.py:223
  4.2 3.0 %collective-permute-start.2 = (f32[1,2,32]{2,1,0:T(2,128)S(1)}, f32[1,2,32]{2,1,0:T(2,128)S(1)}, u32[]{:S(2)}, u32[]{:S(2)}) collective-permute-start(f32[1,2,32]{2,1,0:T(2,128)S(1)} %maximum_bitcast_fusion), channel_id=1, source_target_pairs={{0,3},{1,2},{2,1},{3,0},{4,7},{5,6},{6,5},{7,4},{8,11},{9,10},{10,... | collective-permute-start | bytes 776 | tf_op jit(solution)/shard_map/ppermute | solution.py:223
  7.2 5.7 %collective-permute-start.3 = (f32[4,2,32]{2,1,0:T(2,128)S(1)}, f32[4,2,32]{2,1,0:T(2,128)S(1)}, u32[]{:S(2)}, u32[]{:S(2)}) collective-permute-start(f32[4,2,32]{2,1,0:T(2,128)S(1)} %pad_maximum_fusion.2.after_ref), channel_id=1, source_target_pairs={{0,4},{4,0},{8,12},{12,8},{16,20},{20,16},{24,28},{28,24},{1,5},{5... | collective-permute-start | bytes 3080 | tf_op jit(solution)/shard_map/ppermute | solution.py:212
  8.4 1.5 %copy-start = (bf16[168,5376]{1,0:T(8,128)(2,1)S(1)}, bf16[168,5376]{1,0:T(8,128)(2,1)}, u32[]{:S(2)}) copy-start(bf16[168,5376]{1,0:T(8,128)(2,1)} %raw_ref.3) | copy-start | bytes 5419012
  12.3 11.5 %collective-permute-start.6 = (bf16[16,64,128]{2,1,0:T(8,128)(2,1)S(1)}, bf16[16,64,128]{2,1,0:T(8,128)(2,1)S(1)}, u32[]{:S(2)}, u32[]{:S(2)}) collective-permute-start(bf16[16,64,128]{2,1,0:T(8,128)(2,1)S(1)} %get-tuple-element.11.rest_0_), channel_id=1, source_target_pairs={{0,2},{1,3},{2,0},{3,1},{4,6},{5,7},{6,4},{7,5},{8,10},{9,11},{10,... | collective-permute-start | bytes 786440 | tf_op jit(solution)/shard_map/ppermute | solution.py:212
  12.6 11.2 %collective-permute-start.8 = (bf16[16,64,128]{2,1,0:T(8,128)(2,1)S(1)}, bf16[16,64,128]{2,1,0:T(8,128)(2,1)S(1)}, u32[]{:S(2)}, u32[]{:S(2)}) collective-permute-start(bf16[16,64,128]{2,1,0:T(8,128)(2,1)S(1)} %get-tuple-element.15.rest_4_), channel_id=1, source_target_pairs={{0,4},{4,0},{8,12},{12,8},{16,20},{20,16},{24,28},{28,24},{1,5},{5... | collective-permute-start | bytes 786440 | tf_op jit(solution)/shard_map/ppermute | solution.py:212
  12.9 6.3 %collective-permute-start.4 = (f32[8,2,32]{2,1,0:T(2,128)S(1)}, f32[8,2,32]{2,1,0:T(2,128)S(1)}, u32[]{:S(2)}, u32[]{:S(2)}) collective-permute-start(f32[8,2,32]{2,1,0:T(2,128)S(1)} %get-tuple-element.44.after_ref), channel_id=1, source_target_pairs={{0,8},{4,12},{8,0},{12,4},{16,24},{20,28},{24,16},{28,20},{1,9},{5... | collective-permute-start | bytes 6152 | tf_op jit(solution)/shard_map/ppermute | solution.py:212
  14.2 4.8 %copy-start.1 = (f32[6]{0:T(128)S(1)}, f32[6]{0:T(128)}, u32[]{:S(2)}) copy-start(f32[6]{0:T(128)} %param.18) | copy-start | bytes 76
  16.4 8.7 %collective-permute-start.7 = (bf16[16,64,128]{2,1,0:T(8,128)(2,1)S(1)}, bf16[16,64,128]{2,1,0:T(8,128)(2,1)S(1)}, u32[]{:S(2)}, u32[]{:S(2)}) collective-permute-start(bf16[16,64,128]{2,1,0:T(8,128)(2,1)S(1)} %get-tuple-element.14.rest_1_), channel_id=1, source_target_pairs={{0,2},{1,3},{2,0},{3,1},{4,6},{5,7},{6,4},{7,5},{8,10},{9,11},{10,... | collective-permute-start | bytes 786440 | tf_op jit(solution)/shard_map/ppermute | solution.py:212
  17.7 7.5 %collective-permute-start.9 = (bf16[16,64,128]{2,1,0:T(8,128)(2,1)S(1)}, bf16[16,64,128]{2,1,0:T(8,128)(2,1)S(1)}, u32[]{:S(2)}, u32[]{:S(2)}) collective-permute-start(bf16[16,64,128]{2,1,0:T(8,128)(2,1)S(1)} %get-tuple-element.16.rest_5_), channel_id=1, source_target_pairs={{0,4},{4,0},{8,12},{12,8},{16,20},{20,16},{24,28},{28,24},{1,5},{5... | collective-permute-start | bytes 786440 | tf_op jit(solution)/shard_map/ppermute | solution.py:212
  19.2 3.6 %collective-permute-start.5 = (f32[16,2,32]{2,1,0:T(2,128)S(1)}, f32[16,2,32]{2,1,0:T(2,128)S(1)}, u32[]{:S(2)}, u32[]{:S(2)}) collective-permute-start(f32[16,2,32]{2,1,0:T(2,128)S(1)} %get-tuple-element.40), channel_id=1, source_target_pairs={{0,16},{4,20},{8,24},{12,28},{16,0},{20,4},{24,8},{28,12},{1,17},{... | collective-permute-start | bytes 12296 | tf_op jit(solution)/shard_map/ppermute | solution.py:212
  27.3 4.2 %collective-permute-start.10 = (bf16[64,64,128]{2,1,0:T(8,128)(2,1)S(1)}, bf16[64,64,128]{2,1,0:T(8,128)(2,1)S(1)}, u32[]{:S(2)}, u32[]{:S(2)}) collective-permute-start(bf16[64,64,128]{2,1,0:T(8,128)(2,1)S(1)} %bins_sent.1), channel_id=1, source_target_pairs={{0,1},{1,0},{2,3},{3,2},{4,5},{5,4},{6,7},{7,6},{8,9},{9,8},{10,11... | collective-permute-start | bytes 3145736 | tf_op jit(solution)/shard_map/ppermute | solution.py:212
  31.6 7.6 %collective-permute-start.11 = (bf16[16,64,128]{2,1,0:T(8,128)(2,1)S(1)}, bf16[16,64,128]{2,1,0:T(8,128)(2,1)S(1)}, u32[]{:S(2)}, u32[]{:S(2)}) collective-permute-start(bf16[16,64,128]{2,1,0:T(8,128)(2,1)S(1)} %get-tuple-element.34), channel_id=1, source_target_pairs={{0,4},{4,0},{8,12},{12,8},{16,20},{20,16},{24,28},{28,24},{1,5},{5... | collective-permute-start | bytes 786440 | tf_op jit(solution)/shard_map/ppermute | solution.py:212
  32.4 7.2 %collective-permute-start.12 = (bf16[16,64,128]{2,1,0:T(8,128)(2,1)S(1)}, bf16[16,64,128]{2,1,0:T(8,128)(2,1)S(1)}, u32[]{:S(2)}, u32[]{:S(2)}) collective-permute-start(bf16[16,64,128]{2,1,0:T(8,128)(2,1)S(1)} %get-tuple-element.35), channel_id=1, source_target_pairs={{0,2},{1,3},{2,0},{3,1},{4,6},{5,7},{6,4},{7,5},{8,10},{9,11},{10,... | collective-permute-start | bytes 786440 | tf_op jit(solution)/shard_map/ppermute | solution.py:212
  39.7 20.8 %copy-start.2 = (f32[41]{0:T(128)S(1)}, f32[41]{0:T(128)}, u32[]{:S(2)}) copy-start(f32[41]{0:T(128)} %param.19) | copy-start | bytes 496
  39.7 6.3 %collective-permute-start.13 = (bf16[8,128,128]{2,1,0:T(8,128)(2,1)S(1)}, bf16[8,128,128]{2,1,0:T(8,128)(2,1)S(1)}, u32[]{:S(2)}, u32[]{:S(2)}) collective-permute-start(bf16[8,128,128]{2,1,0:T(8,128)(2,1)S(1)} %pad_maximum_fusion), channel_id=1, source_target_pairs={{0,8},{4,12},{8,0},{12,4},{16,24},{20,28},{24,16},{28,20},{1,9},{5... | collective-permute-start | bytes 786440 | tf_op jit(solution)/shard_map/ppermute | solution.py:212
  46.1 6.2 %collective-permute-start.14 = (bf16[4,128,128]{2,1,0:T(8,128)(2,1)S(1)}, bf16[4,128,128]{2,1,0:T(8,128)(2,1)S(1)}, u32[]{:S(2)}, u32[]{:S(2)}) collective-permute-start(bf16[4,128,128]{2,1,0:T(8,128)(2,1)S(1)} %fusion.1), channel_id=1, source_target_pairs={{0,16},{4,20},{8,24},{12,28},{16,0},{20,4},{24,8},{28,12},{1,17},{... | collective-permute-start | bytes 393224 | tf_op jit(solution)/shard_map/ppermute | solution.py:212
  52.4 8.1 %collective-permute-start.15 = (bf16[4,32,128]{2,1,0:T(8,128)(2,1)S(1)}, bf16[4,32,128]{2,1,0:T(8,128)(2,1)S(1)}, u32[]{:S(2)}, u32[]{:S(2)}) collective-permute-start(bf16[4,32,128]{2,1,0:T(8,128)(2,1)S(1)} %get-tuple-element.37), channel_id=1, source_target_pairs={{0,1},{1,2},{2,3},{4,5},{5,6},{6,7},{8,9},{9,10},{10,11},{12,13},{... | collective-permute-start | bytes 98312 | tf_op jit(solution)/shard_map/ppermute | solution.py:294
  58.5 5.2 %collective-permute-start.16 = (bf16[4,32,128]{2,1,0:T(8,128)(2,1)S(1)}, bf16[4,32,128]{2,1,0:T(8,128)(2,1)S(1)}, u32[]{:S(2)}, u32[]{:S(2)}) collective-permute-start(bf16[4,32,128]{2,1,0:T(8,128)(2,1)S(1)} %get-tuple-element.36), channel_id=1, source_target_pairs={{1,0},{2,1},{3,2},{5,4},{6,5},{7,6},{9,8},{10,9},{11,10},{13,12},{... | collective-permute-start | bytes 98312 | tf_op jit(solution)/shard_map/ppermute | solution.py:295

commit v2 on v1

--- a/solution.py
+++ b/solution.py
@@ -138,37 +138,56 @@
     )(bins, scale, *blocks)
 
 
-def filter_kernel(taps_ref, mid_ref, low_ref, high_ref, out_ref):
+def filters_kernel(edge, taps_ref, rows_ref, cols_ref):
+    side, rows_in = rows_ref.shape
+    radius = (taps_ref.shape[1] - 1) // 2
+    taps = taps_ref[...]
+    width = up(rows_in + 1, 128)
+    rows_ref[...] = banded(lanes_at(taps, edge - radius, width), side, width)[:, :rows_in].astype(jnp.bfloat16)
+    cols_ref[...] = banded(lanes_at(taps, side - radius, 3 * side), side, 3 * side).T.astype(jnp.bfloat16)
+
+
+def filters(taps, side, edge):
+    return pl.pallas_call(
+        functools.partial(filters_kernel, edge),
+        out_shape=[
+            jax.ShapeDtypeStruct((side, side + 2 * edge), jnp.bfloat16),
+            jax.ShapeDtypeStruct((3 * side, side), jnp.bfloat16),
+        ],
+        in_specs=[pl.BlockSpec(memory_space=VMEM)],
+        out_specs=[pl.BlockSpec(memory_space=VMEM)] * 2,
+        compiler_params=pltpu.CompilerParams(vmem_limit_bytes=12 << 20),
+        cost_estimate=pl.CostEstimate(flops=1 << 20, bytes_accessed=1 << 20, transcendentals=0),
+        name="filters",
+    )(taps)
+
+
+def filter_kernel(row_filter_ref, col_filter_ref, mid_ref, low_ref, high_ref, out_ref):
     cells, side, unused = mid_ref.shape
-    edge = low_ref.shape[1]
-    tap_count = taps_ref.shape[1]
-    radius = (tap_count - 1) // 2
-    taps = taps_ref[...]
-    rows_in = side + 2 * edge
-    row_filter = banded(lanes_at(taps, edge - radius, up(rows_in + 1, 128)), side, up(rows_in + 1, 128))
-    row_filter = row_filter[:, :rows_in].astype(jnp.bfloat16)
-    col_filter = banded(lanes_at(taps, side - radius, 3 * side), side, 3 * side).astype(jnp.bfloat16).T
     zero = jnp.zeros((side, side), jnp.bfloat16)
     smoothed = [zero]
     for c in range(cells):
         column = jnp.concatenate([low_ref[c], mid_ref[c], high_ref[c]], axis=0)
-        smoothed.append(jnp.dot(row_filter, column, preferred_element_type=jnp.float32).astype(jnp.bfloat16))
+        rows = jnp.dot(row_filter_ref[...], column, preferred_element_type=jnp.float32)
+        smoothed.append(rows.astype(jnp.bfloat16))
     smoothed.append(zero)
     for c in range(cells):
         window = jnp.concatenate(smoothed[c : c + 3], axis=1)
-        out_ref[:, c * side : (c + 1) * side] = jnp.dot(window, col_filter, preferred_element_type=jnp.float32)
-
-
-def detect(taps, mid, low, high):
+        out_ref[:, c * side : (c + 1) * side] = jnp.dot(
+            window, col_filter_ref[...], preferred_element_type=jnp.float32
+        )
+
+
+def detect(row_filter, col_filter, mid, low, high):
     cells, side, unused = mid.shape
     return pl.pallas_call(
         filter_kernel,
         out_shape=jax.ShapeDtypeStruct((side, cells * side), jnp.float32),
-        in_specs=[pl.BlockSpec(memory_space=VMEM)] * 4,
+        in_specs=[pl.BlockSpec(memory_space=VMEM)] * 5,
         out_specs=pl.BlockSpec(memory_space=VMEM),
         compiler_params=pltpu.CompilerParams(vmem_limit_bytes=12 << 20),
         name="detect",
-    )(taps, mid, low, high)
+    )(row_filter, col_filter, mid, low, high)
 
 
 def halves(parts, send):
@@ -211,9 +230,9 @@
         axis, count, bit = ("band", band_count, bit) if bit < band_bits else ("sky", sky_count, bit - band_bits)
         return lax.ppermute(array, axis, [(i, i ^ (1 << bit)) for i in range(count)])
 
-    turn = [1, band_bits]
-    later = list(range(2, band_bits)) + list(range(band_bits + 1, band_bits + sky_bits))
-    orders = [turn[group:] + turn[:group] for group in range(len(turn))]
+    band_bit, sky_bit, next_bit = 1, band_bits, band_bits + 1
+    orders = [[band_bit, next_bit, sky_bit], [sky_bit, band_bit, next_bit]]
+    later = list(range(2, band_bits)) + list(range(band_bits + 2, band_bits + sky_bits))
     heights = [block_side // len(orders)] * len(orders)
 
     key = (patch_of_block[:, 0] * BANDS + band_of_block) * CELLS + cell_of_block
@@ -251,7 +270,7 @@
     scale = gain * near_weight / jnp.maximum(weight_sum, 1.0)
 
     owner_off = (near_key // (CELLS * BANDS) ^ sky_here) << band_bits | (cell // CC ^ band_here)
-    size = (1 << (len(turn) + len(later) - 1)) * CC
+    size = (1 << (len(orders[0]) + len(later) - 1)) * CC
     sent_bins, kept_bins, blocks = [], [], []
     for group, order in enumerate(orders):
         blocks += own[group] + others[group]
@@ -268,7 +287,7 @@
     got = swap(outgoing, 0)
     kept = bin_blocks(jnp.stack(kept_bins), scale, blocks, len(orders), size, "bins_kept")
     groups = [[part[group * size : (group + 1) * size] for part in (kept, got)] for group in range(len(orders))]
-    for phase in range(1, len(turn)):
+    for phase in range(1, len(orders[0])):
         got = [swap(halves(parts, True).astype(jnp.bfloat16), order[phase]) for parts, order in zip(groups, orders)]
         groups = [first_halves(parts) + [part] for parts, part in zip(groups, got)]
     joined = []
@@ -289,12 +308,16 @@
     combined = combined.astype(jnp.bfloat16)
 
     edge = up(radius, 16)
-    forward = [(i, i + 1) for i in range(band_count - 1)]
-    backward = [(i + 1, i) for i in range(band_count - 1)]
-    low = lax.ppermute(combined[:, block_side - edge :], "band", forward)
-    high = lax.ppermute(combined[:, :edge], "band", backward)
+    top, bottom = combined[:, :edge], combined[:, block_side - edge :]
+    even = band_here & 1 == 0
+    inner = [(i, i + 1) for i in range(1, band_count - 1, 2)]
+    beyond = lax.ppermute(jnp.where(even, top, bottom), "band", inner + [(i, j) for j, i in inner])
+    paired = swap(jnp.where(even, bottom, top), 0)
     taps = filter_taps.astype(jnp.bfloat16).astype(jnp.float32)[None]
-    return detect(taps, combined, low, high)[None]
+    row_filter, col_filter = filters(taps, block_side, edge)
+    return detect(
+        row_filter, col_filter, combined, jnp.where(even, beyond, paired), jnp.where(even, paired, beyond)
+    )[None]
 
 
 def solution(mesh):

time: 65.4 us -> 60.7 us (0.928)
  waiting for transfers between devices: 23.3 us -> 18.6 us
    ppermute x12 -> x14, waiting for transfers between devices: 18.5 us -> 15.9 us  [swap(): return lax.ppermute(array, axis, [(i, i ^ 1 << bit) for i in range(count)])]
    ppermute x2 -> x1, waiting for transfers between devices: 3.28 us -> 1.17 us  [local(): lax.ppermute(jnp.where(even, top, bottom), 'band', inner + [(i, j) for j,...]
    ppermute x12 -> x14, starting transfers between devices: 14.6 us -> 15.7 us  [swap(): return lax.ppermute(array, axis, [(i, i ^ 1 << bit) for i in range(count)])]
    ppermute x2 -> x1, starting transfers between devices: 8.09 us -> 7 us  [local(): lax.ppermute(jnp.where(even, top, bottom), 'band', inner + [(i, j) for j,...]
  transfers between devices with their start and end apart: 17 -> 18, of which waited for: 9 -> 10; matrix products, arithmetic and copies ran while one was open for 4% -> 4% of each run, Pallas kernels for 10% -> 11%
where the time goes in v2:
time: 60.7 us; the launch traced here: 60.5 us
  starting transfers between devices  25.6 us (42%)
  waiting for transfers between devices  18.6 us (31%)
  Pallas kernels  10.1 us (17%)
  other arithmetic  4.42 us (7%)
  local copies, waits for them, and re-layouts  1.59 us (3%)
    ppermute x14, waiting for transfers between devices, swap(): return lax.ppermute(array, axis, [(i, i ^ 1 << bit) for i in range(count)])  15.9 us
    ppermute x14, starting transfers between devices, swap(): return lax.ppermute(array, axis, [(i, i ^ 1 << bit) for i in range(count)])  15.7 us
    ppermute x1, starting transfers between devices, local(): lax.ppermute(jnp.where(even, top, bottom), 'band', inner + [(i, j) for j,...  7 us
    pallas_call x2, Pallas kernels, match_blocks(): pl.pallas_call(match_first if first == 0 else functools.partial(match_nex...  4.55 us
    pallas_call x2, Pallas kernels, bin_blocks(): pl.pallas_call(functools.partial(bin_kernel, groups), grid=(groups * size...  4.15 us
    ppermute x3, starting transfers between devices, local(): lax.ppermute(facts, 'band', [(i, i ^ off) for i in range(band_count)])  2.86 us
    ppermute x3, waiting for transfers between devices, local(): lax.ppermute(facts, 'band', [(i, i ^ off) for i in range(band_count)])  1.54 us
    unnamed x11, local copies, waits for them, and re-layouts  1.54 us
  transfers between devices with their start and end apart: 18, of which 10 were waited for; matrix products, arithmetic and copies ran while one was open for 4% of the time, Pallas kernels for 11%

profile of v2, /device:TPU:1, one launch (start us, length us, event | category | flops | bytes accessed | tf_op | source)
XLA Modules:
  0.0 60.5 jit_solution(3958681476318874306)
XLA Ops:
  0.0 0.7 %bitcast_convert_fusion = f32[1,32]{1,0:T(1,128)S(1)} fusion(bf16[32]{0:T(256)(128)(2,1)} %param.14), kind=kLoop, calls=%fused_computation.90 | loop fusion | flops 32 | bytes 192 | tf_op jit(solution)/shard_map/stack | solution.py:239
  0.7 0.7 %convert_bitcast_fusion = f32[1,32]{1,0:T(1,128)S(1)} fusion(s32[32]{0:T(128)} %param.12, s32[32]{0:T(128)} %param.13, s32[32,1]{0,1:T(1,128)} %param.11), kind=kLoop, calls=%fused_computation.104 | loop fusion | flops 160 | bytes 512 | tf_op jit(solution)/shard_map/stack | solution.py:239
  1.4 0.1 collective-permute-start.1
  1.5 2.7 %collective-permute-start = (f32[1,2,32]{2,1,0:T(2,128)S(1)}, f32[1,2,32]{2,1,0:T(2,128)S(1)}, u32[]{:S(2)}, u32[]{:S(2)}) collective-permute-start(f32[1,2,32]{2,1,0:T(2,128)S(1)} %maximum_bitcast_fusion), channel_id=1, source_target_pairs={{0,2},{1,3},{2,0},{3,1},{4,6},{5,7},{6,4},{7,5},{8,10},{9,11},{10,... | collective-permute-start | bytes 776 | tf_op jit(solution)/shard_map/ppermute | solution.py:242
  4.2 0.0 collective-permute-start.2
  4.2 0.7 %pad_convert_fusion = f32[3,41]{1,0:T(4,128)S(1)} fusion(bf16[3,32]{1,0:T(4,128)(2,1)} %bitcast.46), kind=kLoop, calls=%fused_computation.83 | loop fusion | flops 123 | bytes 684 | tf_op jit(solution)/shard_map/jit(_pad)/pad | solution.py:246
  4.9 0.7 %pad_maximum_fusion.1.small_ref = f32[9,41]{1,0:T(8,128)S(1)} fusion(f32[3,41]{1,0:T(4,128)S(1)} %pad_convert_fusion, f32[3,41]{1,0:T(4,128)} %param.17, f32[3,41]{1,0:T(4,128)} %param.16), kind=kLoop, calls=%fused_computation.36 | loop fusion | flops 738 | bytes 2952 | tf_op jit(solution)/shard_map/concatenate | solution.py:246
  5.6 0.0 collective-permute-done.1
  5.6 0.0 collective-permute-done
  5.6 1.5 %collective-permute-done.2 = f32[1,2,32]{2,1,0:T(2,128)S(1)} collective-permute-done((f32[1,2,32]{2,1,0:T(2,128)S(1)}, f32[1,2,32]{2,1,0:T(2,128)S(1)}, u32[]{:S(2)}, u32[]{:S(2)}) %collective-permute-start.2) | collective-permute-done | bytes 288 | tf_op jit(solution)/shard_map/ppermute | solution.py:242
  7.2 1.2 %collective-permute-start.3 = (f32[4,2,32]{2,1,0:T(2,128)S(1)}, f32[4,2,32]{2,1,0:T(2,128)S(1)}, u32[]{:S(2)}, u32[]{:S(2)}) collective-permute-start(f32[4,2,32]{2,1,0:T(2,128)S(1)} %pad_maximum_fusion.2.after_ref), channel_id=1, source_target_pairs={{0,4},{4,0},{8,12},{12,8},{16,20},{20,16},{24,28},{28,24},{1,5},{5... | collective-permute-start | bytes 3080 | tf_op jit(solution)/shard_map/ppermute | solution.py:231
  8.4 0.0 copy-start
  8.4 1.5 %copy-done = bf16[168,5376]{1,0:T(8,128)(2,1)S(1)} copy-done((bf16[168,5376]{1,0:T(8,128)(2,1)S(1)}, bf16[168,5376]{1,0:T(8,128)(2,1)}, u32[]{:S(2)}) %copy-start) | copy-done | bytes 1806360
  9.9 2.4 %match_first.1 = (bf16[16,64,128]{2,1,0:T(8,128)(2,1)S(1)}, bf16[16,64,128]{2,1,0:T(8,128)(2,1)S(1)}, bf16[384,168]{1,0:T(8,128)(2,1)S(1)}, bf16[768,128]{1,0:T(8,128)(2,1)S(1)}) custom-call(f32[4,2,32]{2,1,0:T(2,128)S(1)} %pad_maximum_fusion.2.after_ref, f32[9,41]{1,0:T(8,128)S(1)} %pad_maximum_fusion.1.small_ref, bf16[168,5376]{1,0:T(8,128)(2,1)S(1)} %copy-done), custom_call_target="tpu_custom_call" | custom-call | flops 2444230656 | bytes 2097152 | tf_op jit(solution)/shard_map/match_first/pallas_call | solution.py:91
  12.3 0.3 collective-permute-start.6
  12.6 0.3 collective-permute-start.8
  12.9 0.0 collective-permute-done.3
  12.9 1.4 %collective-permute-start.4 = (f32[8,2,32]{2,1,0:T(2,128)S(1)}, f32[8,2,32]{2,1,0:T(2,128)S(1)}, u32[]{:S(2)}, u32[]{:S(2)}) collective-permute-start(f32[8,2,32]{2,1,0:T(2,128)S(1)} %get-tuple-element.50.after_ref), channel_id=1, source_target_pairs={{0,8},{4,12},{8,0},{12,4},{16,24},{20,28},{24,16},{28,20},{1,9},{5... | collective-permute-start | bytes 6152 | tf_op jit(solution)/shard_map/ppermute | solution.py:231
  14.2 0.0 copy-start.1
  14.2 2.2 %match_next.1 = (bf16[16,64,128]{2,1,0:T(8,128)(2,1)S(1)}, bf16[16,64,128]{2,1,0:T(8,128)(2,1)S(1)}) custom-call(f32[8,2,32]{2,1,0:T(2,128)S(1)} %get-tuple-element.50.after_ref, f32[9,41]{1,0:T(8,128)S(1)} %pad_maximum_fusion.1.small_ref, bf16[168,5376]{1,0:T(8,128)(2,1)S(1)} %copy-done, bf16[384,168]{1,0:T(8,128)(2,1)S(1)} %get-tuple-element.16.rowk_ref, ...), custom_call_target="tpu_custom_call" | custom-call | flops 2444230656 | bytes 2097152 | tf_op jit(solution)/shard_map/match_next/pallas_call | solution.py:91
  16.4 1.3 %collective-permute-start.7 = (bf16[16,64,128]{2,1,0:T(8,128)(2,1)S(1)}, bf16[16,64,128]{2,1,0:T(8,128)(2,1)S(1)}, u32[]{:S(2)}, u32[]{:S(2)}) collective-permute-start(bf16[16,64,128]{2,1,0:T(8,128)(2,1)S(1)} %get-tuple-element.18.rest_1_), channel_id=1, source_target_pairs={{0,2},{1,3},{2,0},{3,1},{4,6},{5,7},{6,4},{7,5},{8,10},{9,11},{10,... | collective-permute-start | bytes 786440 | tf_op jit(solution)/shard_map/ppermute | solution.py:231
  17.7 1.2 %collective-permute-start.9 = (bf16[16,64,128]{2,1,0:T(8,128)(2,1)S(1)}, bf16[16,64,128]{2,1,0:T(8,128)(2,1)S(1)}, u32[]{:S(2)}, u32[]{:S(2)}) collective-permute-start(bf16[16,64,128]{2,1,0:T(8,128)(2,1)S(1)} %get-tuple-element.20.rest_5_), channel_id=1, source_target_pairs={{0,4},{4,0},{8,12},{12,8},{16,20},{20,16},{24,28},{28,24},{1,5},{5... | collective-permute-start | bytes 786440 | tf_op jit(solution)/shard_map/ppermute | solution.py:231
  19.0 0.0 copy-done.1
  19.1 0.1 select_reduce_fusion.1
  19.1 0.0 collective-permute-done.4
  19.2 2.4 %collective-permute-start.5 = (f32[16,2,32]{2,1,0:T(2,128)S(1)}, f32[16,2,32]{2,1,0:T(2,128)S(1)}, u32[]{:S(2)}, u32[]{:S(2)}) collective-permute-start(f32[16,2,32]{2,1,0:T(2,128)S(1)} %get-tuple-element.46), channel_id=1, source_target_pairs={{0,16},{4,20},{8,24},{12,28},{16,0},{20,4},{24,8},{28,12},{1,17},{... | collective-permute-start | bytes 12296 | tf_op jit(solution)/shard_map/ppermute | solution.py:231
  21.6 1.2 %collective-permute-done.5 = f32[16,2,32]{2,1,0:T(2,128)S(1)} collective-permute-done((f32[16,2,32]{2,1,0:T(2,128)S(1)}, f32[16,2,32]{2,1,0:T(2,128)S(1)}, u32[]{:S(2)}, u32[]{:S(2)}) %collective-permute-start.5) | collective-permute-done | bytes 4128 | tf_op jit(solution)/shard_map/ppermute | solution.py:231
  22.8 0.9 %select_reduce_fusion = f32[3,32]{1,0:T(4,128)S(1)} fusion(f32[32,32]{1,0:T(8,128)S(1)} %bitcast.44, f32[32,32]{1,0:T(8,128)S(1)} %bitcast.43, f32[3,32]{1,0:T(4,128)S(1)} %bitcast.45), kind=kLoop, calls=%fused_computation | loop fusion | flops 294816 | bytes 8960 | tf_op jit(solution)/shard_map/reduce_sum | solution.py:265
  23.8 0.0 collective-permute-done.6.rest_2_
  23.8 0.0 collective-permute-done.8.rest_6_
  23.8 1.4 %collective-permute-done.7.rest_3_ = bf16[16,64,128]{2,1,0:T(8,128)(2,1)S(1)} collective-permute-done((bf16[16,64,128]{2,1,0:T(8,128)(2,1)S(1)}, bf16[16,64,128]{2,1,0:T(8,128)(2,1)S(1)}, u32[]{:S(2)}, u32[]{:S(2)}) %collective-permute-start.7) | collective-permute-done | bytes 262176 | tf_op jit(solution)/shard_map/ppermute | solution.py:231
  25.2 0.0 collective-permute-done.9.rest_7_
  25.2 2.1 %bins_sent.1 = bf16[64,64,128]{2,1,0:T(8,128)(2,1)S(1)} custom-call(s32[4,32]{1,0:T(4,128)S(1)} %pad_add_fusion.1.bins_ref, f32[3,32]{1,0:T(4,128)S(1)} %fusion.5.scale_ref, bf16[16,64,128]{2,1,0:T(8,128)(2,1)S(1)} %get-tuple-element.15.rest_0_, bf16[16,64,128]{2,1,0:T(8,128)(2,1)S(1)} %get-tuple-element.18.rest_1_, ...), custom_call_target="tpu_custom_call" | custom-call | flops 6291456 | bytes 3145728 | tf_op jit(solution)/shard_map/bins_sent/pallas_call | solution.py:127
  27.3 1.8 %collective-permute-start.10 = (bf16[64,64,128]{2,1,0:T(8,128)(2,1)S(1)}, bf16[64,64,128]{2,1,0:T(8,128)(2,1)S(1)}, u32[]{:S(2)}, u32[]{:S(2)}) collective-permute-start(bf16[64,64,128]{2,1,0:T(8,128)(2,1)S(1)} %bins_sent.1), channel_id=1, source_target_pairs={{0,1},{1,0},{2,3},{3,2},{4,5},{5,4},{6,7},{7,6},{8,9},{9,8},{10,11... | collective-permute-start | bytes 3145736 | tf_op jit(solution)/shard_map/ppermute | solution.py:231
  29.1 2.0 %bins_kept.1 = bf16[64,64,128]{2,1,0:T(8,128)(2,1)S(1)} custom-call(s32[4,32]{1,0:T(4,128)S(1)} %pad_add_fusion.bins_ref, f32[3,32]{1,0:T(4,128)S(1)} %fusion.5.scale_ref, bf16[16,64,128]{2,1,0:T(8,128)(2,1)S(1)} %get-tuple-element.15.rest_0_, bf16[16,64,128]{2,1,0:T(8,128)(2,1)S(1)} %get-tuple-element.18.rest_1_, ...), custom_call_target="tpu_custom_call" | custom-call | flops 6291456 | bytes 3145728 | tf_op jit(solution)/shard_map/bins_kept/pallas_call | solution.py:127
  31.2 0.2 collective-permute-done.10
  31.4 0.2 add_convert_fusion.1
  31.6 1.3 %collective-permute-start.11 = (bf16[16,64,128]{2,1,0:T(8,128)(2,1)S(1)}, bf16[16,64,128]{2,1,0:T(8,128)(2,1)S(1)}, u32[]{:S(2)}, u32[]{:S(2)}) collective-permute-start(bf16[16,64,128]{2,1,0:T(8,128)(2,1)S(1)} %get-tuple-element.38), channel_id=1, source_target_pairs={{0,8},{4,12},{8,0},{12,4},{16,24},{20,28},{24,16},{28,20},{1,9},{5... | collective-permute-start | bytes 786440 | tf_op jit(solution)/shard_map/ppermute | solution.py:231
  32.9 0.0 copy-start.2
  32.9 1.2 %collective-permute-start.13 = (bf16[16,64,128]{2,1,0:T(8,128)(2,1)S(1)}, bf16[16,64,128]{2,1,0:T(8,128)(2,1)S(1)}, u32[]{:S(2)}, u32[]{:S(2)}) collective-permute-start(bf16[16,64,128]{2,1,0:T(8,128)(2,1)S(1)} %get-tuple-element.39), channel_id=1, source_target_pairs={{0,2},{1,3},{2,0},{3,1},{4,6},{5,7},{6,4},{7,5},{8,10},{9,11},{10,... | collective-permute-start | bytes 786440 | tf_op jit(solution)/shard_map/ppermute | solution.py:231
  34.1 5.1 %collective-permute-done.11 = bf16[16,64,128]{2,1,0:T(8,128)(2,1)S(1)} collective-permute-done((bf16[16,64,128]{2,1,0:T(8,128)(2,1)S(1)}, bf16[16,64,128]{2,1,0:T(8,128)(2,1)S(1)}, u32[]{:S(2)}, u32[]{:S(2)}) %collective-permute-start.11) | collective-permute-done | bytes 262176 | tf_op jit(solution)/shard_map/ppermute | solution.py:231
  39.2 1.0 %collective-permute-done.13 = bf16[16,64,128]{2,1,0:T(8,128)(2,1)S(1)} collective-permute-done((bf16[16,64,128]{2,1,0:T(8,128)(2,1)S(1)}, bf16[16,64,128]{2,1,0:T(8,128)(2,1)S(1)}, u32[]{:S(2)}, u32[]{:S(2)}) %collective-permute-start.13) | collective-permute-done | bytes 262176 | tf_op jit(solution)/shard_map/ppermute | solution.py:231
  40.1 0.1 add_convert_fusion.3
  40.3 0.3 collective-permute-start.12
  40.6 0.7 %collective-permute-start.14 = (bf16[8,64,128]{2,1,0:T(8,128)(2,1)S(1)}, bf16[8,64,128]{2,1,0:T(8,128)(2,1)S(1)}, u32[]{:S(2)}, u32[]{:S(2)}) collective-permute-start(bf16[8,64,128]{2,1,0:T(8,128)(2,1)S(1)} %get-tuple-element.37), channel_id=1, source_target_pairs={{0,8},{4,12},{8,0},{12,4},{16,24},{20,28},{24,16},{28,20},{1,9},{5... | collective-permute-start | bytes 393224 | tf_op jit(solution)/shard_map/ppermute | solution.py:231
  41.2 2.9 %collective-permute-done.12 = bf16[8,64,128]{2,1,0:T(8,128)(2,1)S(1)} collective-permute-done((bf16[8,64,128]{2,1,0:T(8,128)(2,1)S(1)}, bf16[8,64,128]{2,1,0:T(8,128)(2,1)S(1)}, u32[]{:S(2)}, u32[]{:S(2)}) %collective-permute-start.12) | collective-permute-done | bytes 131104 | tf_op jit(solution)/shard_map/ppermute | solution.py:231
  44.1 0.2 collective-permute-done.14
  44.4 0.2 add_convert_fusion.5
  44.6 2.4 %collective-permute-start.15 = (bf16[4,128,128]{2,1,0:T(8,128)(2,1)S(1)}, bf16[4,128,128]{2,1,0:T(8,128)(2,1)S(1)}, u32[]{:S(2)}, u32[]{:S(2)}) collective-permute-start(bf16[4,128,128]{2,1,0:T(8,128)(2,1)S(1)} %pad_maximum_fusion), channel_id=1, source_target_pairs={{0,16},{4,20},{8,24},{12,28},{16,0},{20,4},{24,8},{28,12},{1,17},{... | collective-permute-start | bytes 393224 | tf_op jit(solution)/shard_map/ppermute | solution.py:231
  47.0 3.8 %collective-permute-done.15 = bf16[4,128,128]{2,1,0:T(8,128)(2,1)S(1)} collective-permute-done((bf16[4,128,128]{2,1,0:T(8,128)(2,1)S(1)}, bf16[4,128,128]{2,1,0:T(8,128)(2,1)S(1)}, u32[]{:S(2)}, u32[]{:S(2)}) %collective-permute-start.15) | collective-permute-done | bytes 131104 | tf_op jit(solution)/shard_map/ppermute | solution.py:231
  50.8 7.0 %collective-permute-start.16 = (bf16[4,32,128]{2,1,0:T(8,128)(2,1)S(1)}, bf16[4,32,128]{2,1,0:T(8,128)(2,1)S(1)}, u32[]{:S(2)}, u32[]{:S(2)}) collective-permute-start(bf16[4,32,128]{2,1,0:T(8,128)(2,1)S(1)} %get-tuple-element.41), channel_id=1, source_target_pairs={{1,2},{2,1},{5,6},{6,5},{9,10},{10,9},{13,14},{14,13},{17,18},{18,... | collective-permute-start | bytes 98312 | tf_op jit(solution)/shard_map/ppermute | solution.py:314
  57.8 0.1 collective-permute-start.17
  57.9 0.0 copy-done.2
  57.9 0.3 filters.1
  58.2 1.2 %collective-permute-done.16 = bf16[4,32,128]{2,1,0:T(8,128)(2,1)S(1)} collective-permute-done((bf16[4,32,128]{2,1,0:T(8,128)(2,1)S(1)}, bf16[4,32,128]{2,1,0:T(8,128)(2,1)S(1)}, u32[]{:S(2)}, u32[]{:S(2)}) %collective-permute-start.16) | collective-permute-done | bytes 32800 | tf_op jit(solution)/shard_map/ppermute | solution.py:314
  59.4 0.0 collective-permute-done.17
  59.4 1.1 %detect.1 = f32[128,512]{1,0:T(8,128)} custom-call(bf16[128,192]{1,0:T(8,128)(2,1)S(1)} %get-tuple-element.13.row_filter_ref, bf16[384,128]{1,0:T(8,128)(2,1)S(1)} %get-tuple-element.14.col_filter_ref, bf16[4,128,128]{2,1,0:T(8,128)(2,1)S(1)} %fusion.mid_ref, bf16[4,32,128]{2,1,0:T(8,128)(2,1)S(1)} %get-tuple-element.43.low_ref, ...), custom_call_target="tpu_custom_call" | custom-call | tf_op jit(solution)/shard_map/detect/pallas_call | solution.py:183
  (26 shorter events, 0.3 us)
Async XLA Ops:
  1.4 4.3 %collective-permute-start.1 = (f32[1,2,32]{2,1,0:T(2,128)S(1)}, f32[1,2,32]{2,1,0:T(2,128)S(1)}, u32[]{:S(2)}, u32[]{:S(2)}) collective-permute-start(f32[1,2,32]{2,1,0:T(2,128)S(1)} %maximum_bitcast_fusion), channel_id=1, source_target_pairs={{0,1},{1,0},{2,3},{3,2},{4,5},{5,4},{6,7},{7,6},{8,9},{9,8},{10,11... | collective-permute-start | bytes 776 | tf_op jit(solution)/shard_map/ppermute | solution.py:242
  1.5 4.2 %collective-permute-start = (f32[1,2,32]{2,1,0:T(2,128)S(1)}, f32[1,2,32]{2,1,0:T(2,128)S(1)}, u32[]{:S(2)}, u32[]{:S(2)}) collective-permute-start(f32[1,2,32]{2,1,0:T(2,128)S(1)} %maximum_bitcast_fusion), channel_id=1, source_target_pairs={{0,2},{1,3},{2,0},{3,1},{4,6},{5,7},{6,4},{7,5},{8,10},{9,11},{10,... | collective-permute-start | bytes 776 | tf_op jit(solution)/shard_map/ppermute | solution.py:242
  4.2 3.0 %collective-permute-start.2 = (f32[1,2,32]{2,1,0:T(2,128)S(1)}, f32[1,2,32]{2,1,0:T(2,128)S(1)}, u32[]{:S(2)}, u32[]{:S(2)}) collective-permute-start(f32[1,2,32]{2,1,0:T(2,128)S(1)} %maximum_bitcast_fusion), channel_id=1, source_target_pairs={{0,3},{1,2},{2,1},{3,0},{4,7},{5,6},{6,5},{7,4},{8,11},{9,10},{10,... | collective-permute-start | bytes 776 | tf_op jit(solution)/shard_map/ppermute | solution.py:242
  7.2 5.7 %collective-permute-start.3 = (f32[4,2,32]{2,1,0:T(2,128)S(1)}, f32[4,2,32]{2,1,0:T(2,128)S(1)}, u32[]{:S(2)}, u32[]{:S(2)}) collective-permute-start(f32[4,2,32]{2,1,0:T(2,128)S(1)} %pad_maximum_fusion.2.after_ref), channel_id=1, source_target_pairs={{0,4},{4,0},{8,12},{12,8},{16,20},{20,16},{24,28},{28,24},{1,5},{5... | collective-permute-start | bytes 3080 | tf_op jit(solution)/shard_map/ppermute | solution.py:231
  8.4 1.5 %copy-start = (bf16[168,5376]{1,0:T(8,128)(2,1)S(1)}, bf16[168,5376]{1,0:T(8,128)(2,1)}, u32[]{:S(2)}) copy-start(bf16[168,5376]{1,0:T(8,128)(2,1)} %raw_ref.3) | copy-start | bytes 5419012
  12.3 11.5 %collective-permute-start.6 = (bf16[16,64,128]{2,1,0:T(8,128)(2,1)S(1)}, bf16[16,64,128]{2,1,0:T(8,128)(2,1)S(1)}, u32[]{:S(2)}, u32[]{:S(2)}) collective-permute-start(bf16[16,64,128]{2,1,0:T(8,128)(2,1)S(1)} %get-tuple-element.15.rest_0_), channel_id=1, source_target_pairs={{0,2},{1,3},{2,0},{3,1},{4,6},{5,7},{6,4},{7,5},{8,10},{9,11},{10,... | collective-permute-start | bytes 786440 | tf_op jit(solution)/shard_map/ppermute | solution.py:231
  12.6 11.2 %collective-permute-start.8 = (bf16[16,64,128]{2,1,0:T(8,128)(2,1)S(1)}, bf16[16,64,128]{2,1,0:T(8,128)(2,1)S(1)}, u32[]{:S(2)}, u32[]{:S(2)}) collective-permute-start(bf16[16,64,128]{2,1,0:T(8,128)(2,1)S(1)} %get-tuple-element.19.rest_4_), channel_id=1, source_target_pairs={{0,4},{4,0},{8,12},{12,8},{16,20},{20,16},{24,28},{28,24},{1,5},{5... | collective-permute-start | bytes 786440 | tf_op jit(solution)/shard_map/ppermute | solution.py:231
  12.9 6.3 %collective-permute-start.4 = (f32[8,2,32]{2,1,0:T(2,128)S(1)}, f32[8,2,32]{2,1,0:T(2,128)S(1)}, u32[]{:S(2)}, u32[]{:S(2)}) collective-permute-start(f32[8,2,32]{2,1,0:T(2,128)S(1)} %get-tuple-element.50.after_ref), channel_id=1, source_target_pairs={{0,8},{4,12},{8,0},{12,4},{16,24},{20,28},{24,16},{28,20},{1,9},{5... | collective-permute-start | bytes 6152 | tf_op jit(solution)/shard_map/ppermute | solution.py:231
  14.2 4.8 %copy-start.1 = (f32[6]{0:T(128)S(1)}, f32[6]{0:T(128)}, u32[]{:S(2)}) copy-start(f32[6]{0:T(128)} %param.18) | copy-start | bytes 76
  16.4 8.7 %collective-permute-start.7 = (bf16[16,64,128]{2,1,0:T(8,128)(2,1)S(1)}, bf16[16,64,128]{2,1,0:T(8,128)(2,1)S(1)}, u32[]{:S(2)}, u32[]{:S(2)}) collective-permute-start(bf16[16,64,128]{2,1,0:T(8,128)(2,1)S(1)} %get-tuple-element.18.rest_1_), channel_id=1, source_target_pairs={{0,2},{1,3},{2,0},{3,1},{4,6},{5,7},{6,4},{7,5},{8,10},{9,11},{10,... | collective-permute-start | bytes 786440 | tf_op jit(solution)/shard_map/ppermute | solution.py:231
  17.7 7.5 %collective-permute-start.9 = (bf16[16,64,128]{2,1,0:T(8,128)(2,1)S(1)}, bf16[16,64,128]{2,1,0:T(8,128)(2,1)S(1)}, u32[]{:S(2)}, u32[]{:S(2)}) collective-permute-start(bf16[16,64,128]{2,1,0:T(8,128)(2,1)S(1)} %get-tuple-element.20.rest_5_), channel_id=1, source_target_pairs={{0,4},{4,0},{8,12},{12,8},{16,20},{20,16},{24,28},{28,24},{1,5},{5... | collective-permute-start | bytes 786440 | tf_op jit(solution)/shard_map/ppermute | solution.py:231
  19.2 3.6 %collective-permute-start.5 = (f32[16,2,32]{2,1,0:T(2,128)S(1)}, f32[16,2,32]{2,1,0:T(2,128)S(1)}, u32[]{:S(2)}, u32[]{:S(2)}) collective-permute-start(f32[16,2,32]{2,1,0:T(2,128)S(1)} %get-tuple-element.46), channel_id=1, source_target_pairs={{0,16},{4,20},{8,24},{12,28},{16,0},{20,4},{24,8},{28,12},{1,17},{... | collective-permute-start | bytes 12296 | tf_op jit(solution)/shard_map/ppermute | solution.py:231
  27.3 4.1 %collective-permute-start.10 = (bf16[64,64,128]{2,1,0:T(8,128)(2,1)S(1)}, bf16[64,64,128]{2,1,0:T(8,128)(2,1)S(1)}, u32[]{:S(2)}, u32[]{:S(2)}) collective-permute-start(bf16[64,64,128]{2,1,0:T(8,128)(2,1)S(1)} %bins_sent.1), channel_id=1, source_target_pairs={{0,1},{1,0},{2,3},{3,2},{4,5},{5,4},{6,7},{7,6},{8,9},{9,8},{10,11... | collective-permute-start | bytes 3145736 | tf_op jit(solution)/shard_map/ppermute | solution.py:231
  31.6 7.6 %collective-permute-start.11 = (bf16[16,64,128]{2,1,0:T(8,128)(2,1)S(1)}, bf16[16,64,128]{2,1,0:T(8,128)(2,1)S(1)}, u32[]{:S(2)}, u32[]{:S(2)}) collective-permute-start(bf16[16,64,128]{2,1,0:T(8,128)(2,1)S(1)} %get-tuple-element.38), channel_id=1, source_target_pairs={{0,8},{4,12},{8,0},{12,4},{16,24},{20,28},{24,16},{28,20},{1,9},{5... | collective-permute-start | bytes 786440 | tf_op jit(solution)/shard_map/ppermute | solution.py:231
  32.9 25.0 %copy-start.2 = (f32[41]{0:T(128)S(1)}, f32[41]{0:T(128)}, u32[]{:S(2)}) copy-start(f32[41]{0:T(128)} %param.19) | copy-start | bytes 496
  32.9 7.2 %collective-permute-start.13 = (bf16[16,64,128]{2,1,0:T(8,128)(2,1)S(1)}, bf16[16,64,128]{2,1,0:T(8,128)(2,1)S(1)}, u32[]{:S(2)}, u32[]{:S(2)}) collective-permute-start(bf16[16,64,128]{2,1,0:T(8,128)(2,1)S(1)} %get-tuple-element.39), channel_id=1, source_target_pairs={{0,2},{1,3},{2,0},{3,1},{4,6},{5,7},{6,4},{7,5},{8,10},{9,11},{10,... | collective-permute-start | bytes 786440 | tf_op jit(solution)/shard_map/ppermute | solution.py:231
  40.3 3.9 %collective-permute-start.12 = (bf16[8,64,128]{2,1,0:T(8,128)(2,1)S(1)}, bf16[8,64,128]{2,1,0:T(8,128)(2,1)S(1)}, u32[]{:S(2)}, u32[]{:S(2)}) collective-permute-start(bf16[8,64,128]{2,1,0:T(8,128)(2,1)S(1)} %get-tuple-element.36), channel_id=1, source_target_pairs={{0,4},{4,0},{8,12},{12,8},{16,20},{20,16},{24,28},{28,24},{1,5},{5... | collective-permute-start | bytes 393224 | tf_op jit(solution)/shard_map/ppermute | solution.py:231
  40.6 3.8 %collective-permute-start.14 = (bf16[8,64,128]{2,1,0:T(8,128)(2,1)S(1)}, bf16[8,64,128]{2,1,0:T(8,128)(2,1)S(1)}, u32[]{:S(2)}, u32[]{:S(2)}) collective-permute-start(bf16[8,64,128]{2,1,0:T(8,128)(2,1)S(1)} %get-tuple-element.37), channel_id=1, source_target_pairs={{0,8},{4,12},{8,0},{12,4},{16,24},{20,28},{24,16},{28,20},{1,9},{5... | collective-permute-start | bytes 393224 | tf_op jit(solution)/shard_map/ppermute | solution.py:231
  44.6 6.2 %collective-permute-start.15 = (bf16[4,128,128]{2,1,0:T(8,128)(2,1)S(1)}, bf16[4,128,128]{2,1,0:T(8,128)(2,1)S(1)}, u32[]{:S(2)}, u32[]{:S(2)}) collective-permute-start(bf16[4,128,128]{2,1,0:T(8,128)(2,1)S(1)} %pad_maximum_fusion), channel_id=1, source_target_pairs={{0,16},{4,20},{8,24},{12,28},{16,0},{20,4},{24,8},{28,12},{1,17},{... | collective-permute-start | bytes 393224 | tf_op jit(solution)/shard_map/ppermute | solution.py:231
  50.8 8.6 %collective-permute-start.16 = (bf16[4,32,128]{2,1,0:T(8,128)(2,1)S(1)}, bf16[4,32,128]{2,1,0:T(8,128)(2,1)S(1)}, u32[]{:S(2)}, u32[]{:S(2)}) collective-permute-start(bf16[4,32,128]{2,1,0:T(8,128)(2,1)S(1)} %get-tuple-element.41), channel_id=1, source_target_pairs={{1,2},{2,1},{5,6},{6,5},{9,10},{10,9},{13,14},{14,13},{17,18},{18,... | collective-permute-start | bytes 98312 | tf_op jit(solution)/shard_map/ppermute | solution.py:314
  57.8 1.6 %collective-permute-start.17 = (bf16[4,32,128]{2,1,0:T(8,128)(2,1)S(1)}, bf16[4,32,128]{2,1,0:T(8,128)(2,1)S(1)}, u32[]{:S(2)}, u32[]{:S(2)}) collective-permute-start(bf16[4,32,128]{2,1,0:T(8,128)(2,1)S(1)} %get-tuple-element.40), channel_id=1, source_target_pairs={{0,1},{1,0},{2,3},{3,2},{4,5},{5,4},{6,7},{7,6},{8,9},{9,8},{10,11... | collective-permute-start | bytes 98312 | tf_op jit(solution)/shard_map/ppermute | solution.py:231

commit v3 on v2

--- a/solution.py
+++ b/solution.py
@@ -31,10 +31,63 @@
     return jnp.concatenate(parts, axis=1)
 
 
-def match_part(first, small_ref, raw_ref, rowk_ref, colk_ref, outs):
+def load_kernel(*refs):
+    sources, (facts_ref, coef_ref, rowk_ref, colk_ref, raw_ref) = refs[:8], refs[8:13]
+    patch_ref, cell_ref, band_ref, weight_ref, row_ref, col_ref, coef_in = targets = refs[13:20]
+    sems = refs[20]
+    copies = [
+        pltpu.make_async_copy(source, target, sems.at[i])
+        for i, (source, target) in enumerate(zip(sources, targets + (raw_ref,)))
+    ]
+    for copy in copies:
+        copy.start()
+    for copy in copies[:-1]:
+        copy.wait()
+    key = (patch_ref[...] * BANDS + band_ref[...]) * CELLS + cell_ref[...]
+    facts_ref[0, 0:1, :] = key.astype(jnp.float32)
+    facts_ref[0, 1:2, :] = weight_ref[...].astype(jnp.float32).reshape(1, -1)
+    coef_ref[...] = coef_in[...].astype(jnp.float32)
+    basis_count, margin_side = row_ref.shape[0], raw_ref.shape[0]
+    block_side = rowk_ref.shape[0] // basis_count
+    width = colk_ref.shape[0] // basis_count
+    for k in range(basis_count):
+        rows = banded(lanes_at(row_ref[k : k + 1, :], 0, width), block_side, width)
+        rowk_ref[k * block_side : (k + 1) * block_side, :] = rows[:, :margin_side].astype(jnp.bfloat16)
+        cols = banded(lanes_at(col_ref[k : k + 1, :], 0, width), block_side, width)
+        colk_ref[k * width : (k + 1) * width, :] = cols.T.astype(jnp.bfloat16)
+    copies[-1].wait()
+
+
+def load(patch, cell, band, weight, row_basis, col_basis, coef, raw, block_side):
+    basis_count = row_basis.shape[0]
+    margin_side = raw.shape[0]
+    width = up(margin_side, 128)
+    operands = (patch, cell, band, weight, row_basis, col_basis, coef, raw)
+    out_shape = [
+        jax.ShapeDtypeStruct((1, 2, patch.shape[1]), jnp.float32),
+        jax.ShapeDtypeStruct(coef.shape, jnp.float32),
+        jax.ShapeDtypeStruct((basis_count * block_side, margin_side), jnp.bfloat16),
+        jax.ShapeDtypeStruct((basis_count * width, block_side), jnp.bfloat16),
+        jax.ShapeDtypeStruct(raw.shape, raw.dtype),
+    ]
+    return pl.pallas_call(
+        load_kernel,
+        out_shape=out_shape,
+        in_specs=[pl.BlockSpec(memory_space=pltpu.HBM)] * len(operands),
+        out_specs=[pl.BlockSpec(memory_space=VMEM)] * len(out_shape),
+        scratch_shapes=[VMEM(value.shape, value.dtype) for value in operands[:-1]]
+        + [pltpu.SemaphoreType.DMA((len(operands),))],
+        compiler_params=pltpu.CompilerParams(vmem_limit_bytes=12 << 20),
+        cost_estimate=pl.CostEstimate(flops=1 << 20, bytes_accessed=4 << 20, transcendentals=0),
+        name="load",
+    )(*(pltpu.with_memory_space_constraint(value, pltpu.HBM) for value in operands))
+
+
+def match_kernel(first, count, skip, fresh, after_ref, coef_ref, rowk_ref, colk_ref, raw_ref, *outs):
     margin_side = raw_ref.shape[0]
-    basis_count = small_ref.shape[0] // 3
-    count, unused, block_side = outs[0].shape
+    basis_count = coef_ref.shape[0]
+    outs = outs if fresh else outs[len(outs) // 2 :]
+    block_side = outs[0].shape[2]
     width = colk_ref.shape[0] // basis_count
     for n in range(count):
         here = first + n
@@ -42,8 +95,7 @@
         sectioned = jnp.dot(rowk_ref[...], block, preferred_element_type=jnp.float32)
         total = None
         for k in range(basis_count):
-            place = 2 * basis_count + k
-            part = sectioned[k * block_side : (k + 1) * block_side] * small_ref[place : place + 1, here : here + 1]
+            part = sectioned[k * block_side : (k + 1) * block_side] * coef_ref[k : k + 1, here : here + 1]
             term = jnp.dot(
                 part.astype(jnp.bfloat16),
                 colk_ref[k * width : k * width + margin_side, :],
@@ -53,54 +105,28 @@
         total = total.astype(jnp.bfloat16)
         start = 0
         for out_ref in outs:
-            out_ref[n] = total[start : start + out_ref.shape[1]]
+            out_ref[skip + n] = total[start : start + out_ref.shape[1]]
             start += out_ref.shape[1]
 
 
-def match_first(after_ref, small_ref, raw_ref, *rest):
-    outs, (rowk_ref, colk_ref) = rest[:-2], rest[-2:]
-    margin_side = raw_ref.shape[0]
-    basis_count = small_ref.shape[0] // 3
-    block_side = outs[0].shape[2]
-    tap_count = margin_side - block_side + 1
-    width = colk_ref.shape[0] // basis_count
-    for k in range(basis_count):
-        rows = banded(lanes_at(small_ref[k : k + 1, :tap_count], 0, width), block_side, width)
-        rowk_ref[k * block_side : (k + 1) * block_side, :] = rows[:, :margin_side].astype(jnp.bfloat16)
-        place = basis_count + k
-        cols = banded(lanes_at(small_ref[place : place + 1, :tap_count], 0, width), block_side, width)
-        colk_ref[k * width : (k + 1) * width, :] = cols.T.astype(jnp.bfloat16)
-    match_part(0, small_ref, raw_ref, rowk_ref, colk_ref, outs)
-
-
-def match_next(first, after_ref, small_ref, raw_ref, rowk_ref, colk_ref, *outs):
-    match_part(first, small_ref, raw_ref, rowk_ref, colk_ref, outs)
-
-
-def match_blocks(first, count, small, raw, kernels, rows, block_side, after):
-    margin_side = raw.shape[0]
-    basis_count = small.shape[0] // 3
-    width = up(margin_side, 128)
-    flops = 2 * count * basis_count * block_side * margin_side * (margin_side + block_side)
-    out_shape = [jax.ShapeDtypeStruct((count, height, block_side), jnp.bfloat16) for height in rows]
-    if first == 0:
-        out_shape += [
-            jax.ShapeDtypeStruct((basis_count * block_side, margin_side), jnp.bfloat16),
-            jax.ShapeDtypeStruct((basis_count * width, block_side), jnp.bfloat16),
-        ]
-    found = pl.pallas_call(
-        match_first if first == 0 else functools.partial(match_next, first),
-        out_shape=out_shape,
-        in_specs=[pl.BlockSpec(memory_space=pl.ANY)] + [pl.BlockSpec(memory_space=VMEM)] * (2 + len(kernels)),
-        out_specs=[pl.BlockSpec(memory_space=VMEM)] * len(out_shape),
-        compiler_params=pltpu.CompilerParams(vmem_limit_bytes=12 << 20),
+def match_blocks(first, count, size, loaded, rows, block_side, after, into=()):
+    raw = loaded[-1]
+    basis_count = loaded[0].shape[0]
+    skip = size - count if into else 0
+    flops = 2 * count * basis_count * block_side * raw.shape[0] * (raw.shape[0] + block_side)
+    return pl.pallas_call(
+        functools.partial(match_kernel, first, count, skip, not into),
+        out_shape=[jax.ShapeDtypeStruct((size, height, block_side), jnp.bfloat16) for height in rows],
+        in_specs=[pl.BlockSpec(memory_space=pl.ANY)] + [pl.BlockSpec(memory_space=VMEM)] * (len(loaded) + len(into)),
+        out_specs=[pl.BlockSpec(memory_space=VMEM)] * len(rows),
+        input_output_aliases={1 + len(loaded) + i: i for i in range(len(into))},
+        compiler_params=pltpu.CompilerParams(vmem_limit_bytes=8 << 20),
         cost_estimate=pl.CostEstimate(flops=4 * flops, bytes_accessed=2 << 20, transcendentals=0),
-        name="match_first" if first == 0 else "match_next",
-    )(after, small, raw, *kernels)
-    return found[: len(rows)], kernels or tuple(found[len(rows) :])
-
-
-def bin_kernel(groups, bins_ref, scale_ref, *rest):
+        name="match_blocks",
+    )(after, *loaded, *into)
+
+
+def bin_kernel(groups, bins_ref, scale_ref, after_ref, *rest):
     blocks_refs, (out_ref, acc_ref) = rest[:-2], rest[-2:]
     parts = len(blocks_refs) // (2 * groups)
     step = acc_ref.shape[0]
@@ -109,18 +135,18 @@
     for index, blocks_ref in enumerate(blocks_refs):
         line, part = index // parts, index % parts
         group, source = line // 2, line % 2
-        count = blocks_ref.shape[0]
-        for n in range(count):
-            slot = bins_ref[line, part * count + n] - low
+        start = sum(ref.shape[0] for ref in blocks_refs[:part])
+        for n in range(blocks_ref.shape[0]):
+            slot = bins_ref[line, start + n] - low
 
             @pl.when((slot >= 0) & (slot < step))
-            def _(blocks_ref=blocks_ref, n=n, slot=slot, row=source * (group + 1), place=part * count + n):
+            def _(blocks_ref=blocks_ref, n=n, slot=slot, row=source * (group + 1), place=start + n):
                 acc_ref[slot] += scale_ref[row, place] * blocks_ref[n].astype(jnp.float32)
 
     out_ref[...] = acc_ref[...].astype(out_ref.dtype)
 
 
-def bin_blocks(bins, scale, blocks, groups, size, name):
+def bin_blocks(bins, scale, blocks, groups, size, name, after):
     shape = blocks[0].shape[1:]
     step = min(groups * size, 64)
     moved = 2 * sum(part.size for part in blocks) + 2 * groups * size * shape[0] * shape[1]
@@ -128,14 +154,14 @@
         functools.partial(bin_kernel, groups),
         grid=(groups * size // step,),
         out_shape=jax.ShapeDtypeStruct((groups * size,) + shape, jnp.bfloat16),
-        in_specs=[pl.BlockSpec(memory_space=SMEM), pl.BlockSpec(memory_space=SMEM)]
+        in_specs=[pl.BlockSpec(memory_space=SMEM), pl.BlockSpec(memory_space=SMEM), pl.BlockSpec(memory_space=pl.ANY)]
         + [pl.BlockSpec(part.shape, lambda g: (0, 0, 0)) for part in blocks],
         out_specs=pl.BlockSpec((step,) + shape, lambda g: (g, 0, 0)),
         scratch_shapes=[VMEM((step,) + shape, jnp.float32)],
         compiler_params=pltpu.CompilerParams(vmem_limit_bytes=20 << 20),
         cost_estimate=pl.CostEstimate(flops=2 * moved, bytes_accessed=moved, transcendentals=0),
         name=name,
-    )(bins, scale, *blocks)
+    )(bins, scale, after, *blocks)
 
 
 def filters_kernel(edge, taps_ref, rows_ref, cols_ref):
@@ -235,24 +261,31 @@
     later = list(range(2, band_bits)) + list(range(band_bits + 2, band_bits + sky_bits))
     heights = [block_side // len(orders)] * len(orders)
 
-    key = (patch_of_block[:, 0] * BANDS + band_of_block) * CELLS + cell_of_block
-    facts = jnp.stack([key.astype(jnp.float32), block_weight.astype(jnp.float32)])[None]
+    own_facts, *loaded = load(
+        patch_of_block.reshape(1, -1),
+        cell_of_block.reshape(1, -1),
+        band_of_block.reshape(1, -1),
+        block_weight,
+        row_basis,
+        col_basis,
+        basis_coef.T,
+        raw_blocks,
+        block_side,
+    )
     facts = jnp.concatenate(
-        [facts]
-        + [lax.ppermute(facts, "band", [(i, i ^ off) for i in range(band_count)]) for off in range(1, band_count)]
+        [own_facts]
+        + [lax.ppermute(own_facts, "band", [(i, i ^ off) for i in range(band_count)]) for off in range(1, band_count)]
     )
-    small = [row_basis, col_basis, basis_coef.T.astype(jnp.float32)]
-    lanes = max(part.shape[1] for part in small)
-    small = jnp.concatenate([jnp.pad(part, ((0, 0), (0, lanes - part.shape[1]))) for part in small])
-    part_count = 2 if block_count % 2 == 0 else 1
-    part_blocks = block_count // part_count
-    kernels, own, others = (), [[], []], [[], []]
-    for part in range(max(part_count, sky_bits)):
+    cut, early = block_count * 5 // 8, block_count * 3 // 8
+    own, others = [[], []], [[], []]
+    begun = match_blocks(0, early, cut, loaded, heights, block_side, own_facts)
+    for part in range(max(2, sky_bits)):
         got = swap(facts, band_bits + part) if part < sky_bits else None
-        if part < part_count:
-            found, kernels = match_blocks(
-                part * part_blocks, part_blocks, small, raw_blocks, kernels, heights, block_side, facts
-            )
+        if part == 0:
+            found = match_blocks(early, cut - early, cut, loaded, heights, block_side, facts, begun)
+        elif part == 1:
+            found = match_blocks(cut, block_count - cut, block_count - cut, loaded, heights, block_side, facts)
+        if part < 2:
             for group, order in enumerate(orders):
                 own[group].append(found[group])
                 others[group].append(swap(found[group], order[0]))
@@ -271,7 +304,8 @@
 
     owner_off = (near_key // (CELLS * BANDS) ^ sky_here) << band_bits | (cell // CC ^ band_here)
     size = (1 << (len(orders[0]) + len(later) - 1)) * CC
-    sent_bins, kept_bins, blocks = [], [], []
+    half = size // 2
+    bins, blocks = ([], [], []), []
     for group, order in enumerate(orders):
         blocks += own[group] + others[group]
         for row in (0, group + 1):
@@ -280,16 +314,24 @@
             for bit in [0] + order[1:] + later:
                 place = place * 2 + (off >> bit & 1)
             place = place * CC + cell[row] % CC
-            mine = off >> order[0] & 1 == 0
-            sent_bins.append(jnp.where(mine & (place >= size), place - size + group * size, -1))
-            kept_bins.append(jnp.where(mine & (place < size), place + group * size, -1))
-    outgoing = bin_blocks(jnp.stack(sent_bins), scale, blocks, len(orders), size, "bins_sent")
-    got = swap(outgoing, 0)
-    kept = bin_blocks(jnp.stack(kept_bins), scale, blocks, len(orders), size, "bins_kept")
-    groups = [[part[group * size : (group + 1) * size] for part in (kept, got)] for group in range(len(orders))]
-    for phase in range(1, len(orders[0])):
-        got = [swap(halves(parts, True).astype(jnp.bfloat16), order[phase]) for parts, order in zip(groups, orders)]
-        groups = [first_halves(parts) + [part] for parts, part in zip(groups, got)]
+            place = jnp.where(off >> order[0] & 1 == 0, place, -1)
+            for lines, low, count in zip(bins, (size, half, 0), (size, half, half)):
+                lines.append(jnp.where((place >= low) & (place < low + count), place - low + group * count, -1))
+    for_pair, for_next, for_rest = (jnp.stack(lines) for lines in bins)
+    got = swap(bin_blocks(for_pair, scale, blocks, len(orders), size, "bins_for_pair", scale), 0)
+    sent = bin_blocks(for_next, scale, blocks, len(orders), half, "bins_for_next", scale)
+    edge = up(radius, 16)
+    taps = filter_taps.astype(jnp.bfloat16).astype(jnp.float32)[None]
+    row_filter, col_filter = filters(taps, block_side, edge)
+    kept = bin_blocks(for_rest, scale, blocks, len(orders), half, "bins_kept", row_filter)
+    groups = []
+    for group, order in enumerate(orders):
+        mine = got[group * size : (group + 1) * size]
+        outgoing = sent[group * half : (group + 1) * half].astype(jnp.float32) + mine[half:].astype(jnp.float32)
+        back = swap(outgoing.astype(jnp.bfloat16), order[1])
+        groups.append([kept[group * half : (group + 1) * half], mine[:half], back])
+    got = [swap(halves(parts, True).astype(jnp.bfloat16), order[2]) for parts, order in zip(groups, orders)]
+    groups = [first_halves(parts) + [part] for parts, part in zip(groups, got)]
     joined = []
     for bit in later:
         outgoing = jnp.concatenate([halves(parts, True) for parts in groups], axis=1)
@@ -307,14 +349,11 @@
         combined = combined + full(joined)
     combined = combined.astype(jnp.bfloat16)
 
-    edge = up(radius, 16)
     top, bottom = combined[:, :edge], combined[:, block_side - edge :]
     even = band_here & 1 == 0
     inner = [(i, i + 1) for i in range(1, band_count - 1, 2)]
     beyond = lax.ppermute(jnp.where(even, top, bottom), "band", inner + [(i, j) for j, i in inner])
     paired = swap(jnp.where(even, bottom, top), 0)
-    taps = filter_taps.astype(jnp.bfloat16).astype(jnp.float32)[None]
-    row_filter, col_filter = filters(taps, block_side, edge)
     return detect(
         row_filter, col_filter, combined, jnp.where(even, beyond, paired), jnp.where(even, paired, beyond)
     )[None]

time: 60.7 us -> 58.4 us (0.962)
  Pallas kernels: 10.1 us -> 13.7 us
  other arithmetic: 4.42 us -> 1.66 us
  local copies, waits for them, and re-layouts: 1.59 us -> 0.11 us
  starting transfers between devices: 25.6 us -> 24.6 us
  waiting for transfers between devices: 18.6 us -> 17.9 us
    pallas_call x2 -> x4, Pallas kernels: 4.55 us -> 6.41 us  [the longest x3 4.74 us: match_blocks(): pl.pallas_call(functools.partial(match_kernel, first, count, skip, not in...]
    pallas_call x2 -> x3, Pallas kernels: 4.15 us -> 5.9 us  [bin_blocks(): pl.pallas_call(functools.partial(bin_kernel, groups), grid=(groups * size...]
    unnamed x11 -> x10, local copies, waits for them, and re-layouts: 1.54 us -> 0.06 us
    another operation x5 -> x4, other arithmetic: 1.54 us -> 0.2 us  [the longest x2 1.35 us: local(): jnp.stack([key.astype(jnp.float32), block_weight.astype(jnp.float32)])[None]]
    concatenate x2 -> x0, other arithmetic: 0.71 us -> none  [the longest x1 0.71 us: local(): jnp.concatenate([jnp.pad(part, ((0, 0), (0, lanes - part.shape[1]))) for...]
    pad x1 -> x0, other arithmetic: 0.68 us -> none  [local(): jnp.pad(part, ((0, 0), (0, lanes - part.shape[1])))]
    ppermute x14, starting transfers between devices: 15.7 us -> 15.1 us  [swap(): return lax.ppermute(array, axis, [(i, i ^ 1 << bit) for i in range(count)])]
    ppermute x14, waiting for transfers between devices: 15.9 us -> 15.2 us  [swap(): return lax.ppermute(array, axis, [(i, i ^ 1 << bit) for i in range(count)])]
  transfers between devices with their start and end apart: 18 -> 18, of which waited for: 10 -> 11; matrix products, arithmetic and copies ran while one was open for 4% -> 2% of each run, Pallas kernels for 11% -> 15%
where the time goes in v3:
time: 58.4 us; the launch traced here: 58.3 us
  starting transfers between devices  24.6 us (42%)
  waiting for transfers between devices  17.9 us (31%)
  Pallas kernels  13.7 us (23%)
  other arithmetic  1.66 us (3%)
    ppermute x14, waiting for transfers between devices, swap(): return lax.ppermute(array, axis, [(i, i ^ 1 << bit) for i in range(count)])  15.2 us
    ppermute x14, starting transfers between devices, swap(): return lax.ppermute(array, axis, [(i, i ^ 1 << bit) for i in range(count)])  15.1 us
    ppermute x1, starting transfers between devices, local(): lax.ppermute(jnp.where(even, top, bottom), 'band', inner + [(i, j) for j,...  6.65 us
    pallas_call x3, Pallas kernels, bin_blocks(): pl.pallas_call(functools.partial(bin_kernel, groups), grid=(groups * size...  5.9 us
    pallas_call x3, Pallas kernels, match_blocks(): pl.pallas_call(functools.partial(match_kernel, first, count, skip, not in...  4.74 us
    ppermute x3, starting transfers between devices, local(): lax.ppermute(own_facts, 'band', [(i, i ^ off) for i in range(band_count)])  2.87 us
    pallas_call x1, Pallas kernels, load(): pl.pallas_call(load_kernel, out_shape=out_shape, in_specs=[pl.BlockSpec(m...  1.67 us
    ppermute x1, waiting for transfers between devices, local(): lax.ppermute(jnp.where(even, top, bottom), 'band', inner + [(i, j) for j,...  1.5 us
  transfers between devices with their start and end apart: 18, of which 11 were waited for; matrix products, arithmetic and copies ran while one was open for 2% of the time, Pallas kernels for 15%

profile of v3, /device:TPU:1, one launch (start us, length us, event | category | flops | bytes accessed | tf_op | source)
XLA Modules:
  0.0 58.3 jit_solution(15547472510737777389)
XLA Ops:
  0.0 1.7 %load.1 = (f32[1,2,32]{2,1,0:T(2,128)S(1)}, f32[3,32]{1,0:T(4,128)S(1)}, bf16[384,168]{1,0:T(8,128)(2,1)S(1)}, bf16[768,128]{1,0:T(8,128)(2,1)S(1)}, bf16[168,5376]{1,0:T(8,128)(2,1)S(1)}) custom-call(s32[1,32]{1,0:T(1,128)} %bitcast.29, s32[1,32]{1,0:T(1,128)} %bitcast.30, s32[1,32]{1,0:T(1,128)} %bitcast.31, bf16[32]{0:T(256)(128)(2,1)} %refs_3_.1, ...), custom_call_target="tpu_custom_call" | custom-call | flops 1048576 | bytes 4194304 | tf_op jit(solution)/shard_map/load/pallas_call | solution.py:73
  1.7 0.1 collective-permute-start.1
  1.8 2.7 %collective-permute-start = (f32[1,2,32]{2,1,0:T(2,128)S(1)}, f32[1,2,32]{2,1,0:T(2,128)S(1)}, u32[]{:S(2)}, u32[]{:S(2)}) collective-permute-start(f32[1,2,32]{2,1,0:T(2,128)S(1)} %get-tuple-element.20.after_ref), channel_id=1, source_target_pairs={{0,2},{1,3},{2,0},{3,1},{4,6},{5,7},{6,4},{7,5},{8,10},{9,11},{10,... | collective-permute-start | bytes 776 | tf_op jit(solution)/shard_map/ppermute | solution.py:277
  4.5 0.0 collective-permute-start.2
  4.5 1.7 %match_blocks.3 = (bf16[20,64,128]{2,1,0:T(8,128)(2,1)S(1)}, bf16[20,64,128]{2,1,0:T(8,128)(2,1)S(1)}) custom-call(f32[1,2,32]{2,1,0:T(2,128)S(1)} %get-tuple-element.20.after_ref, f32[3,32]{1,0:T(4,128)S(1)} %get-tuple-element.21.coef_ref, bf16[384,168]{1,0:T(8,128)(2,1)S(1)} %get-tuple-element.22.rowk_ref, ...), custom_call_target="tpu_custom_call" | custom-call | flops 1833172992 | bytes 2097152 | tf_op jit(solution)/shard_map/match_blocks/pallas_call | solution.py:117
  6.3 0.0 collective-permute-done.1
  6.3 0.0 collective-permute-done
  6.3 1.2 %collective-permute-done.2 = f32[1,2,32]{2,1,0:T(2,128)S(1)} collective-permute-done((f32[1,2,32]{2,1,0:T(2,128)S(1)}, f32[1,2,32]{2,1,0:T(2,128)S(1)}, u32[]{:S(2)}, u32[]{:S(2)}) %collective-permute-start.2) | collective-permute-done | bytes 288 | tf_op jit(solution)/shard_map/ppermute | solution.py:277
  7.5 1.2 %collective-permute-start.3 = (f32[4,2,32]{2,1,0:T(2,128)S(1)}, f32[4,2,32]{2,1,0:T(2,128)S(1)}, u32[]{:S(2)}, u32[]{:S(2)}) collective-permute-start(f32[4,2,32]{2,1,0:T(2,128)S(1)} %get-tuple-element.74.after_ref), channel_id=1, source_target_pairs={{0,4},{4,0},{8,12},{12,8},{16,20},{20,16},{24,28},{28,24},{1,5},{5... | collective-permute-start | bytes 3080 | tf_op jit(solution)/shard_map/ppermute | solution.py:257
  8.7 1.3 %match_blocks.4 = (bf16[20,64,128]{2,1,0:T(8,128)(2,1)S(1)}, bf16[20,64,128]{2,1,0:T(8,128)(2,1)S(1)}) custom-call(f32[4,2,32]{2,1,0:T(2,128)S(1)} %get-tuple-element.74.after_ref, f32[3,32]{1,0:T(4,128)S(1)} %get-tuple-element.21.coef_ref, bf16[384,168]{1,0:T(8,128)(2,1)S(1)} %get-tuple-element.22.rowk_ref, ...), custom_call_target="tpu_custom_call", output_to_operand_aliasing={{0}: (5, {}), {1}: (6, {})} | custom-call | flops 1222115328 | bytes 2097152 | tf_op jit(solution)/shard_map/match_blocks/pallas_call | solution.py:117
  10.0 0.6 %collective-permute-start.6 = (bf16[20,64,128]{2,1,0:T(8,128)(2,1)S(1)}, bf16[20,64,128]{2,1,0:T(8,128)(2,1)S(1)}, u32[]{:S(2)}, u32[]{:S(2)}) collective-permute-start(bf16[20,64,128]{2,1,0:T(8,128)(2,1)S(1)} %get-tuple-element.27.rest_0_), channel_id=1, source_target_pairs={{0,2},{1,3},{2,0},{3,1},{4,6},{5,7},{6,4},{7,5},{8,10},{9,11},{10,... | collective-permute-start | bytes 983048 | tf_op jit(solution)/shard_map/ppermute | solution.py:257
  10.6 0.3 collective-permute-start.8
  10.9 0.0 collective-permute-done.3
  10.9 0.0 copy-start
  10.9 1.8 %match_blocks.5 = (bf16[12,64,128]{2,1,0:T(8,128)(2,1)S(1)}, bf16[12,64,128]{2,1,0:T(8,128)(2,1)S(1)}) custom-call(f32[8,2,32]{2,1,0:T(2,128)S(1)} %get-tuple-element.60.after_ref, f32[3,32]{1,0:T(4,128)S(1)} %get-tuple-element.21.coef_ref, bf16[384,168]{1,0:T(8,128)(2,1)S(1)} %get-tuple-element.22.rowk_ref, ...), custom_call_target="tpu_custom_call" | custom-call | flops 1833172992 | bytes 2097152 | tf_op jit(solution)/shard_map/match_blocks/pallas_call | solution.py:117
  12.7 1.4 %collective-permute-start.4 = (f32[8,2,32]{2,1,0:T(2,128)S(1)}, f32[8,2,32]{2,1,0:T(2,128)S(1)}, u32[]{:S(2)}, u32[]{:S(2)}) collective-permute-start(f32[8,2,32]{2,1,0:T(2,128)S(1)} %get-tuple-element.60.after_ref), channel_id=1, source_target_pairs={{0,8},{4,12},{8,0},{12,4},{16,24},{20,28},{24,16},{28,20},{1,9},{5... | collective-permute-start | bytes 6152 | tf_op jit(solution)/shard_map/ppermute | solution.py:257
  14.0 1.0 %collective-permute-start.7 = (bf16[12,64,128]{2,1,0:T(8,128)(2,1)S(1)}, bf16[12,64,128]{2,1,0:T(8,128)(2,1)S(1)}, u32[]{:S(2)}, u32[]{:S(2)}) collective-permute-start(bf16[12,64,128]{2,1,0:T(8,128)(2,1)S(1)} %get-tuple-element.28.rest_1_), channel_id=1, source_target_pairs={{0,2},{1,3},{2,0},{3,1},{4,6},{5,7},{6,4},{7,5},{8,10},{9,11},{10,... | collective-permute-start | bytes 589832 | tf_op jit(solution)/shard_map/ppermute | solution.py:257
  15.0 1.2 %collective-permute-start.9 = (bf16[12,64,128]{2,1,0:T(8,128)(2,1)S(1)}, bf16[12,64,128]{2,1,0:T(8,128)(2,1)S(1)}, u32[]{:S(2)}, u32[]{:S(2)}) collective-permute-start(bf16[12,64,128]{2,1,0:T(8,128)(2,1)S(1)} %get-tuple-element.30.rest_5_), channel_id=1, source_target_pairs={{0,4},{4,0},{8,12},{12,8},{16,20},{20,16},{24,28},{28,24},{1,5},{5... | collective-permute-start | bytes 589832 | tf_op jit(solution)/shard_map/ppermute | solution.py:257
  16.3 0.0 copy-done
  16.4 0.1 select_reduce_fusion.1
  16.4 0.0 collective-permute-done.4
  16.5 2.4 %collective-permute-start.5 = (f32[16,2,32]{2,1,0:T(2,128)S(1)}, f32[16,2,32]{2,1,0:T(2,128)S(1)}, u32[]{:S(2)}, u32[]{:S(2)}) collective-permute-start(f32[16,2,32]{2,1,0:T(2,128)S(1)} %get-tuple-element.56), channel_id=1, source_target_pairs={{0,16},{4,20},{8,24},{12,28},{16,0},{20,4},{24,8},{28,12},{1,17},{... | collective-permute-start | bytes 12296 | tf_op jit(solution)/shard_map/ppermute | solution.py:257
  18.9 1.2 %collective-permute-done.5 = f32[16,2,32]{2,1,0:T(2,128)S(1)} collective-permute-done((f32[16,2,32]{2,1,0:T(2,128)S(1)}, f32[16,2,32]{2,1,0:T(2,128)S(1)}, u32[]{:S(2)}, u32[]{:S(2)}) %collective-permute-start.5) | collective-permute-done | bytes 4128 | tf_op jit(solution)/shard_map/ppermute | solution.py:257
  20.1 0.9 %select_reduce_fusion = f32[3,32]{1,0:T(4,128)S(1)} fusion(f32[32,32]{1,0:T(8,128)S(1)} %bitcast.26, f32[32,32]{1,0:T(8,128)S(1)} %bitcast.25, f32[3,32]{1,0:T(4,128)S(1)} %bitcast.27), kind=kLoop, calls=%fused_computation | loop fusion | flops 294816 | bytes 8960 | tf_op jit(solution)/shard_map/reduce_sum | solution.py:298
  21.0 1.9 %collective-permute-done.7.rest_3_ = bf16[12,64,128]{2,1,0:T(8,128)(2,1)S(1)} collective-permute-done((bf16[12,64,128]{2,1,0:T(8,128)(2,1)S(1)}, bf16[12,64,128]{2,1,0:T(8,128)(2,1)S(1)}, u32[]{:S(2)}, u32[]{:S(2)}) %collective-permute-start.7) | collective-permute-done | bytes 196640 | tf_op jit(solution)/shard_map/ppermute | solution.py:257
  22.9 0.4 collective-permute-done.9.rest_7_
  23.3 0.0 collective-permute-done.6.rest_2_
  23.3 0.0 collective-permute-done.8.rest_6_
  23.3 2.1 %bins_for_pair.1 = bf16[64,64,128]{2,1,0:T(8,128)(2,1)S(1)} custom-call(s32[4,32]{1,0:T(4,128)S(1)} %pad_add_fusion.1.bins_ref, f32[3,32]{1,0:T(4,128)S(1)} %fusion.5.scale_ref.after_ref, f32[3,32]{1,0:T(4,128)S(1)} %fusion.5.scale_ref.after_ref, bf16[20,64,128]{2,1,0:T(8,128)(2,1)S(1)} %get-tuple-element.27.rest_0_, ...), custom_call_target="tpu_custom_call" | custom-call | flops 6291456 | bytes 3145728 | tf_op jit(solution)/shard_map/bins_for_pair/pallas_call | solution.py:153
  25.5 1.6 %collective-permute-start.10 = (bf16[64,64,128]{2,1,0:T(8,128)(2,1)S(1)}, bf16[64,64,128]{2,1,0:T(8,128)(2,1)S(1)}, u32[]{:S(2)}, u32[]{:S(2)}) collective-permute-start(bf16[64,64,128]{2,1,0:T(8,128)(2,1)S(1)} %bins_for_pair.1), channel_id=1, source_target_pairs={{0,1},{1,0},{2,3},{3,2},{4,5},{5,4},{6,7},{7,6},{8,9},{9,8},{10,11... | collective-permute-start | bytes 3145736 | tf_op jit(solution)/shard_map/ppermute | solution.py:257
  27.1 0.0 copy-start.1
  27.1 1.9 %bins_for_next.1 = bf16[32,64,128]{2,1,0:T(8,128)(2,1)S(1)} custom-call(s32[4,32]{1,0:T(4,128)S(1)} %pad_add_fusion.2.bins_ref, f32[3,32]{1,0:T(4,128)S(1)} %fusion.5.scale_ref.after_ref, f32[3,32]{1,0:T(4,128)S(1)} %fusion.5.scale_ref.after_ref, bf16[20,64,128]{2,1,0:T(8,128)(2,1)S(1)} %get-tuple-element.27.rest_0_, ...), custom_call_target="tpu_custom_call" | custom-call | flops 5242880 | bytes 2621440 | tf_op jit(solution)/shard_map/bins_for_next/pallas_call | solution.py:153
  29.0 0.4 collective-permute-done.10
  29.4 0.2 add_convert_fusion.1
  29.6 1.4 %collective-permute-start.11 = (bf16[16,64,128]{2,1,0:T(8,128)(2,1)S(1)}, bf16[16,64,128]{2,1,0:T(8,128)(2,1)S(1)}, u32[]{:S(2)}, u32[]{:S(2)}) collective-permute-start(bf16[16,64,128]{2,1,0:T(8,128)(2,1)S(1)} %get-tuple-element.48), channel_id=1, source_target_pairs={{0,8},{4,12},{8,0},{12,4},{16,24},{20,28},{24,16},{28,20},{1,9},{5... | collective-permute-start | bytes 786440 | tf_op jit(solution)/shard_map/ppermute | solution.py:257
  31.0 0.9 %collective-permute-start.13 = (bf16[16,64,128]{2,1,0:T(8,128)(2,1)S(1)}, bf16[16,64,128]{2,1,0:T(8,128)(2,1)S(1)}, u32[]{:S(2)}, u32[]{:S(2)}) collective-permute-start(bf16[16,64,128]{2,1,0:T(8,128)(2,1)S(1)} %get-tuple-element.49), channel_id=1, source_target_pairs={{0,2},{1,3},{2,0},{3,1},{4,6},{5,7},{6,4},{7,5},{8,10},{9,11},{10,... | collective-permute-start | bytes 786440 | tf_op jit(solution)/shard_map/ppermute | solution.py:257
  31.9 0.0 copy-done.1
  31.9 0.3 filters.1
  32.2 1.9 %bins_kept.1 = bf16[32,64,128]{2,1,0:T(8,128)(2,1)S(1)} custom-call(s32[4,32]{1,0:T(4,128)S(1)} %pad_add_fusion.bins_ref, f32[3,32]{1,0:T(4,128)S(1)} %fusion.5.scale_ref.after_ref, bf16[128,192]{1,0:T(8,128)(2,1)S(1)} %get-tuple-element.18.after_ref.row_filter_ref, bf16[20,64,128]{2,1,0:T(8,128)(2,1)S(1)} %get-tuple-element.27.rest_0_, ...), custom_call_target="tpu_custom_call" | custom-call | flops 5242880 | bytes 2621440 | tf_op jit(solution)/shard_map/bins_kept/pallas_call | solution.py:153
  34.1 3.0 %collective-permute-done.11 = bf16[16,64,128]{2,1,0:T(8,128)(2,1)S(1)} collective-permute-done((bf16[16,64,128]{2,1,0:T(8,128)(2,1)S(1)}, bf16[16,64,128]{2,1,0:T(8,128)(2,1)S(1)}, u32[]{:S(2)}, u32[]{:S(2)}) %collective-permute-start.11) | collective-permute-done | bytes 262176 | tf_op jit(solution)/shard_map/ppermute | solution.py:257
  37.2 1.0 %collective-permute-done.13 = bf16[16,64,128]{2,1,0:T(8,128)(2,1)S(1)} collective-permute-done((bf16[16,64,128]{2,1,0:T(8,128)(2,1)S(1)}, bf16[16,64,128]{2,1,0:T(8,128)(2,1)S(1)}, u32[]{:S(2)}, u32[]{:S(2)}) %collective-permute-start.13) | collective-permute-done | bytes 262176 | tf_op jit(solution)/shard_map/ppermute | solution.py:257
  38.2 0.1 add_convert_fusion.3
  38.3 0.3 collective-permute-start.12
  38.6 0.3 collective-permute-start.14
  39.0 3.2 %collective-permute-done.12 = bf16[8,64,128]{2,1,0:T(8,128)(2,1)S(1)} collective-permute-done((bf16[8,64,128]{2,1,0:T(8,128)(2,1)S(1)}, bf16[8,64,128]{2,1,0:T(8,128)(2,1)S(1)}, u32[]{:S(2)}, u32[]{:S(2)}) %collective-permute-start.12) | collective-permute-done | bytes 131104 | tf_op jit(solution)/shard_map/ppermute | solution.py:257
  42.2 0.3 collective-permute-done.14
  42.5 0.2 add_convert_fusion.5
  42.7 2.4 %collective-permute-start.15 = (bf16[4,128,128]{2,1,0:T(8,128)(2,1)S(1)}, bf16[4,128,128]{2,1,0:T(8,128)(2,1)S(1)}, u32[]{:S(2)}, u32[]{:S(2)}) collective-permute-start(bf16[4,128,128]{2,1,0:T(8,128)(2,1)S(1)} %pad_maximum_fusion), channel_id=1, source_target_pairs={{0,16},{4,20},{8,24},{12,28},{16,0},{20,4},{24,8},{28,12},{1,17},{... | collective-permute-start | bytes 393224 | tf_op jit(solution)/shard_map/ppermute | solution.py:257
  45.0 3.8 %collective-permute-done.15 = bf16[4,128,128]{2,1,0:T(8,128)(2,1)S(1)} collective-permute-done((bf16[4,128,128]{2,1,0:T(8,128)(2,1)S(1)}, bf16[4,128,128]{2,1,0:T(8,128)(2,1)S(1)}, u32[]{:S(2)}, u32[]{:S(2)}) %collective-permute-start.15) | collective-permute-done | bytes 131104 | tf_op jit(solution)/shard_map/ppermute | solution.py:257
  48.9 6.7 %collective-permute-start.16 = (bf16[4,32,128]{2,1,0:T(8,128)(2,1)S(1)}, bf16[4,32,128]{2,1,0:T(8,128)(2,1)S(1)}, u32[]{:S(2)}, u32[]{:S(2)}) collective-permute-start(bf16[4,32,128]{2,1,0:T(8,128)(2,1)S(1)} %get-tuple-element.51), channel_id=1, source_target_pairs={{1,2},{2,1},{5,6},{6,5},{9,10},{10,9},{13,14},{14,13},{17,18},{18,... | collective-permute-start | bytes 98312 | tf_op jit(solution)/shard_map/ppermute | solution.py:355
  55.6 0.1 collective-permute-start.17
  55.6 1.5 %collective-permute-done.16 = bf16[4,32,128]{2,1,0:T(8,128)(2,1)S(1)} collective-permute-done((bf16[4,32,128]{2,1,0:T(8,128)(2,1)S(1)}, bf16[4,32,128]{2,1,0:T(8,128)(2,1)S(1)}, u32[]{:S(2)}, u32[]{:S(2)}) %collective-permute-start.16) | collective-permute-done | bytes 32800 | tf_op jit(solution)/shard_map/ppermute | solution.py:355
  57.1 0.0 collective-permute-done.17
  57.2 1.1 %detect.1 = f32[128,512]{1,0:T(8,128)} custom-call(bf16[128,192]{1,0:T(8,128)(2,1)S(1)} %get-tuple-element.18.after_ref.row_filter_ref, bf16[384,128]{1,0:T(8,128)(2,1)S(1)} %get-tuple-element.19.col_filter_ref, bf16[4,128,128]{2,1,0:T(8,128)(2,1)S(1)} %fusion.mid_ref, bf16[4,32,128]{2,1,0:T(8,128)(2,1)S(1)} %get-tuple-element.53.low_ref, ...), custom_call_target="tpu_custom_call" | custom-call | tf_op jit(solution)/shard_map/detect/pallas_call | solution.py:209
  (26 shorter events, 0.3 us)
Async XLA Ops:
  1.7 4.6 %collective-permute-start.1 = (f32[1,2,32]{2,1,0:T(2,128)S(1)}, f32[1,2,32]{2,1,0:T(2,128)S(1)}, u32[]{:S(2)}, u32[]{:S(2)}) collective-permute-start(f32[1,2,32]{2,1,0:T(2,128)S(1)} %get-tuple-element.20.after_ref), channel_id=1, source_target_pairs={{0,1},{1,0},{2,3},{3,2},{4,5},{5,4},{6,7},{7,6},{8,9},{9,8},{10,11... | collective-permute-start | bytes 776 | tf_op jit(solution)/shard_map/ppermute | solution.py:277
  1.8 4.5 %collective-permute-start = (f32[1,2,32]{2,1,0:T(2,128)S(1)}, f32[1,2,32]{2,1,0:T(2,128)S(1)}, u32[]{:S(2)}, u32[]{:S(2)}) collective-permute-start(f32[1,2,32]{2,1,0:T(2,128)S(1)} %get-tuple-element.20.after_ref), channel_id=1, source_target_pairs={{0,2},{1,3},{2,0},{3,1},{4,6},{5,7},{6,4},{7,5},{8,10},{9,11},{10,... | collective-permute-start | bytes 776 | tf_op jit(solution)/shard_map/ppermute | solution.py:277
  4.5 3.0 %collective-permute-start.2 = (f32[1,2,32]{2,1,0:T(2,128)S(1)}, f32[1,2,32]{2,1,0:T(2,128)S(1)}, u32[]{:S(2)}, u32[]{:S(2)}) collective-permute-start(f32[1,2,32]{2,1,0:T(2,128)S(1)} %get-tuple-element.20.after_ref), channel_id=1, source_target_pairs={{0,3},{1,2},{2,1},{3,0},{4,7},{5,6},{6,5},{7,4},{8,11},{9,10},{10,... | collective-permute-start | bytes 776 | tf_op jit(solution)/shard_map/ppermute | solution.py:277
  7.5 3.4 %collective-permute-start.3 = (f32[4,2,32]{2,1,0:T(2,128)S(1)}, f32[4,2,32]{2,1,0:T(2,128)S(1)}, u32[]{:S(2)}, u32[]{:S(2)}) collective-permute-start(f32[4,2,32]{2,1,0:T(2,128)S(1)} %get-tuple-element.74.after_ref), channel_id=1, source_target_pairs={{0,4},{4,0},{8,12},{12,8},{16,20},{20,16},{24,28},{28,24},{1,5},{5... | collective-permute-start | bytes 3080 | tf_op jit(solution)/shard_map/ppermute | solution.py:257
  10.0 13.3 %collective-permute-start.6 = (bf16[20,64,128]{2,1,0:T(8,128)(2,1)S(1)}, bf16[20,64,128]{2,1,0:T(8,128)(2,1)S(1)}, u32[]{:S(2)}, u32[]{:S(2)}) collective-permute-start(bf16[20,64,128]{2,1,0:T(8,128)(2,1)S(1)} %get-tuple-element.27.rest_0_), channel_id=1, source_target_pairs={{0,2},{1,3},{2,0},{3,1},{4,6},{5,7},{6,4},{7,5},{8,10},{9,11},{10,... | collective-permute-start | bytes 983048 | tf_op jit(solution)/shard_map/ppermute | solution.py:257
  10.6 12.7 %collective-permute-start.8 = (bf16[20,64,128]{2,1,0:T(8,128)(2,1)S(1)}, bf16[20,64,128]{2,1,0:T(8,128)(2,1)S(1)}, u32[]{:S(2)}, u32[]{:S(2)}) collective-permute-start(bf16[20,64,128]{2,1,0:T(8,128)(2,1)S(1)} %get-tuple-element.29.rest_4_), channel_id=1, source_target_pairs={{0,4},{4,0},{8,12},{12,8},{16,20},{20,16},{24,28},{28,24},{1,5},{5... | collective-permute-start | bytes 983048 | tf_op jit(solution)/shard_map/ppermute | solution.py:257
  10.9 5.5 %copy-start = (f32[6]{0:T(128)S(1)}, f32[6]{0:T(128)}, u32[]{:S(2)}) copy-start(f32[6]{0:T(128)} %param.18) | copy-start | bytes 76
  12.7 3.8 %collective-permute-start.4 = (f32[8,2,32]{2,1,0:T(2,128)S(1)}, f32[8,2,32]{2,1,0:T(2,128)S(1)}, u32[]{:S(2)}, u32[]{:S(2)}) collective-permute-start(f32[8,2,32]{2,1,0:T(2,128)S(1)} %get-tuple-element.60.after_ref), channel_id=1, source_target_pairs={{0,8},{4,12},{8,0},{12,4},{16,24},{20,28},{24,16},{28,20},{1,9},{5... | collective-permute-start | bytes 6152 | tf_op jit(solution)/shard_map/ppermute | solution.py:257
  14.0 8.9 %collective-permute-start.7 = (bf16[12,64,128]{2,1,0:T(8,128)(2,1)S(1)}, bf16[12,64,128]{2,1,0:T(8,128)(2,1)S(1)}, u32[]{:S(2)}, u32[]{:S(2)}) collective-permute-start(bf16[12,64,128]{2,1,0:T(8,128)(2,1)S(1)} %get-tuple-element.28.rest_1_), channel_id=1, source_target_pairs={{0,2},{1,3},{2,0},{3,1},{4,6},{5,7},{6,4},{7,5},{8,10},{9,11},{10,... | collective-permute-start | bytes 589832 | tf_op jit(solution)/shard_map/ppermute | solution.py:257
  15.0 8.3 %collective-permute-start.9 = (bf16[12,64,128]{2,1,0:T(8,128)(2,1)S(1)}, bf16[12,64,128]{2,1,0:T(8,128)(2,1)S(1)}, u32[]{:S(2)}, u32[]{:S(2)}) collective-permute-start(bf16[12,64,128]{2,1,0:T(8,128)(2,1)S(1)} %get-tuple-element.30.rest_5_), channel_id=1, source_target_pairs={{0,4},{4,0},{8,12},{12,8},{16,20},{20,16},{24,28},{28,24},{1,5},{5... | collective-permute-start | bytes 589832 | tf_op jit(solution)/shard_map/ppermute | solution.py:257
  16.5 3.6 %collective-permute-start.5 = (f32[16,2,32]{2,1,0:T(2,128)S(1)}, f32[16,2,32]{2,1,0:T(2,128)S(1)}, u32[]{:S(2)}, u32[]{:S(2)}) collective-permute-start(f32[16,2,32]{2,1,0:T(2,128)S(1)} %get-tuple-element.56), channel_id=1, source_target_pairs={{0,16},{4,20},{8,24},{12,28},{16,0},{20,4},{24,8},{28,12},{1,17},{... | collective-permute-start | bytes 12296 | tf_op jit(solution)/shard_map/ppermute | solution.py:257
  25.5 3.9 %collective-permute-start.10 = (bf16[64,64,128]{2,1,0:T(8,128)(2,1)S(1)}, bf16[64,64,128]{2,1,0:T(8,128)(2,1)S(1)}, u32[]{:S(2)}, u32[]{:S(2)}) collective-permute-start(bf16[64,64,128]{2,1,0:T(8,128)(2,1)S(1)} %bins_for_pair.1), channel_id=1, source_target_pairs={{0,1},{1,0},{2,3},{3,2},{4,5},{5,4},{6,7},{7,6},{8,9},{9,8},{10,11... | collective-permute-start | bytes 3145736 | tf_op jit(solution)/shard_map/ppermute | solution.py:257
  27.1 4.8 %copy-start.1 = (f32[41]{0:T(128)S(1)}, f32[41]{0:T(128)}, u32[]{:S(2)}) copy-start(f32[41]{0:T(128)} %param.19) | copy-start | bytes 496
  29.6 7.6 %collective-permute-start.11 = (bf16[16,64,128]{2,1,0:T(8,128)(2,1)S(1)}, bf16[16,64,128]{2,1,0:T(8,128)(2,1)S(1)}, u32[]{:S(2)}, u32[]{:S(2)}) collective-permute-start(bf16[16,64,128]{2,1,0:T(8,128)(2,1)S(1)} %get-tuple-element.48), channel_id=1, source_target_pairs={{0,8},{4,12},{8,0},{12,4},{16,24},{20,28},{24,16},{28,20},{1,9},{5... | collective-permute-start | bytes 786440 | tf_op jit(solution)/shard_map/ppermute | solution.py:257
  31.0 7.2 %collective-permute-start.13 = (bf16[16,64,128]{2,1,0:T(8,128)(2,1)S(1)}, bf16[16,64,128]{2,1,0:T(8,128)(2,1)S(1)}, u32[]{:S(2)}, u32[]{:S(2)}) collective-permute-start(bf16[16,64,128]{2,1,0:T(8,128)(2,1)S(1)} %get-tuple-element.49), channel_id=1, source_target_pairs={{0,2},{1,3},{2,0},{3,1},{4,6},{5,7},{6,4},{7,5},{8,10},{9,11},{10,... | collective-permute-start | bytes 786440 | tf_op jit(solution)/shard_map/ppermute | solution.py:257
  38.3 3.9 %collective-permute-start.12 = (bf16[8,64,128]{2,1,0:T(8,128)(2,1)S(1)}, bf16[8,64,128]{2,1,0:T(8,128)(2,1)S(1)}, u32[]{:S(2)}, u32[]{:S(2)}) collective-permute-start(bf16[8,64,128]{2,1,0:T(8,128)(2,1)S(1)} %get-tuple-element.46), channel_id=1, source_target_pairs={{0,4},{4,0},{8,12},{12,8},{16,20},{20,16},{24,28},{28,24},{1,5},{5... | collective-permute-start | bytes 393224 | tf_op jit(solution)/shard_map/ppermute | solution.py:257
  38.6 3.8 %collective-permute-start.14 = (bf16[8,64,128]{2,1,0:T(8,128)(2,1)S(1)}, bf16[8,64,128]{2,1,0:T(8,128)(2,1)S(1)}, u32[]{:S(2)}, u32[]{:S(2)}) collective-permute-start(bf16[8,64,128]{2,1,0:T(8,128)(2,1)S(1)} %get-tuple-element.47), channel_id=1, source_target_pairs={{0,8},{4,12},{8,0},{12,4},{16,24},{20,28},{24,16},{28,20},{1,9},{5... | collective-permute-start | bytes 393224 | tf_op jit(solution)/shard_map/ppermute | solution.py:257
  42.7 6.2 %collective-permute-start.15 = (bf16[4,128,128]{2,1,0:T(8,128)(2,1)S(1)}, bf16[4,128,128]{2,1,0:T(8,128)(2,1)S(1)}, u32[]{:S(2)}, u32[]{:S(2)}) collective-permute-start(bf16[4,128,128]{2,1,0:T(8,128)(2,1)S(1)} %pad_maximum_fusion), channel_id=1, source_target_pairs={{0,16},{4,20},{8,24},{12,28},{16,0},{20,4},{24,8},{28,12},{1,17},{... | collective-permute-start | bytes 393224 | tf_op jit(solution)/shard_map/ppermute | solution.py:257
  48.9 8.2 %collective-permute-start.16 = (bf16[4,32,128]{2,1,0:T(8,128)(2,1)S(1)}, bf16[4,32,128]{2,1,0:T(8,128)(2,1)S(1)}, u32[]{:S(2)}, u32[]{:S(2)}) collective-permute-start(bf16[4,32,128]{2,1,0:T(8,128)(2,1)S(1)} %get-tuple-element.51), channel_id=1, source_target_pairs={{1,2},{2,1},{5,6},{6,5},{9,10},{10,9},{13,14},{14,13},{17,18},{18,... | collective-permute-start | bytes 98312 | tf_op jit(solution)/shard_map/ppermute | solution.py:355
  55.6 1.6 %collective-permute-start.17 = (bf16[4,32,128]{2,1,0:T(8,128)(2,1)S(1)}, bf16[4,32,128]{2,1,0:T(8,128)(2,1)S(1)}, u32[]{:S(2)}, u32[]{:S(2)}) collective-permute-start(bf16[4,32,128]{2,1,0:T(8,128)(2,1)S(1)} %get-tuple-element.50), channel_id=1, source_target_pairs={{0,1},{1,0},{2,3},{3,2},{4,5},{5,4},{6,7},{7,6},{8,9},{9,8},{10,11... | collective-permute-start | bytes 98312 | tf_op jit(solution)/shard_map/ppermute | solution.py:257

commit v4 on v3

--- a/solution.py
+++ b/solution.py
@@ -126,37 +126,46 @@
     )(after, *loaded, *into)
 
 
-def bin_kernel(groups, bins_ref, scale_ref, after_ref, *rest):
+def bin_kernel(stepped, bins_ref, scale_ref, after_ref, *rest):
     blocks_refs, (out_ref, acc_ref) = rest[:-2], rest[-2:]
-    parts = len(blocks_refs) // (2 * groups)
+    parts = len(blocks_refs) // 2
     step = acc_ref.shape[0]
-    low = pl.program_id(0) * step
     acc_ref[...] = jnp.zeros_like(acc_ref)
     for index, blocks_ref in enumerate(blocks_refs):
         line, part = index // parts, index % parts
-        group, source = line // 2, line % 2
         start = sum(ref.shape[0] for ref in blocks_refs[:part])
         for n in range(blocks_ref.shape[0]):
-            slot = bins_ref[line, start + n] - low
-
-            @pl.when((slot >= 0) & (slot < step))
-            def _(blocks_ref=blocks_ref, n=n, slot=slot, row=source * (group + 1), place=start + n):
-                acc_ref[slot] += scale_ref[row, place] * blocks_ref[n].astype(jnp.float32)
+            slot = bins_ref[line, start + n]
+            if stepped:
+                slot = slot - pl.program_id(0) * step
+
+            @pl.when((slot >= 0) & (slot < step) if stepped else slot >= 0)
+            def _(blocks_ref=blocks_ref, n=n, slot=slot, line=line, place=start + n):
+                acc_ref[slot] += scale_ref[line, place] * blocks_ref[n].astype(jnp.float32)
 
     out_ref[...] = acc_ref[...].astype(out_ref.dtype)
 
 
-def bin_blocks(bins, scale, blocks, groups, size, name, after):
+def bin_blocks(bins, scale, blocks, size, name, after):
     shape = blocks[0].shape[1:]
-    step = min(groups * size, 64)
-    moved = 2 * sum(part.size for part in blocks) + 2 * groups * size * shape[0] * shape[1]
-    return pl.pallas_call(
-        functools.partial(bin_kernel, groups),
-        grid=(groups * size // step,),
-        out_shape=jax.ShapeDtypeStruct((groups * size,) + shape, jnp.bfloat16),
+    step = min(size, 64)
+    stepped = step < size
+    moved = 2 * sum(part.size for part in blocks) + 2 * size * shape[0] * shape[1]
+    if stepped:
+        grid = (size // step,)
+        block_specs = [pl.BlockSpec(part.shape, lambda g: (0, 0, 0)) for part in blocks]
+        out_spec = pl.BlockSpec((step,) + shape, lambda g: (g, 0, 0))
+    else:
+        grid = ()
+        block_specs = [pl.BlockSpec(memory_space=VMEM)] * len(blocks)
+        out_spec = pl.BlockSpec(memory_space=VMEM)
+    return pl.pallas_call(
+        functools.partial(bin_kernel, stepped),
+        grid=grid,
+        out_shape=jax.ShapeDtypeStruct((size,) + shape, jnp.bfloat16),
         in_specs=[pl.BlockSpec(memory_space=SMEM), pl.BlockSpec(memory_space=SMEM), pl.BlockSpec(memory_space=pl.ANY)]
-        + [pl.BlockSpec(part.shape, lambda g: (0, 0, 0)) for part in blocks],
-        out_specs=pl.BlockSpec((step,) + shape, lambda g: (g, 0, 0)),
+        + block_specs,
+        out_specs=out_spec,
         scratch_shapes=[VMEM((step,) + shape, jnp.float32)],
         compiler_params=pltpu.CompilerParams(vmem_limit_bytes=20 << 20),
         cost_estimate=pl.CostEstimate(flops=2 * moved, bytes_accessed=moved, transcendentals=0),
@@ -305,31 +314,35 @@
     owner_off = (near_key // (CELLS * BANDS) ^ sky_here) << band_bits | (cell // CC ^ band_here)
     size = (1 << (len(orders[0]) + len(later) - 1)) * CC
     half = size // 2
-    bins, blocks = ([], [], []), []
+    blocks, bins, scales = [], [], []
     for group, order in enumerate(orders):
-        blocks += own[group] + others[group]
-        for row in (0, group + 1):
-            off = owner_off[row]
-            place = jnp.zeros_like(off)
-            for bit in [0] + order[1:] + later:
-                place = place * 2 + (off >> bit & 1)
-            place = place * CC + cell[row] % CC
-            place = jnp.where(off >> order[0] & 1 == 0, place, -1)
-            for lines, low, count in zip(bins, (size, half, 0), (size, half, half)):
-                lines.append(jnp.where((place >= low) & (place < low + count), place - low + group * count, -1))
-    for_pair, for_next, for_rest = (jnp.stack(lines) for lines in bins)
-    got = swap(bin_blocks(for_pair, scale, blocks, len(orders), size, "bins_for_pair", scale), 0)
-    sent = bin_blocks(for_next, scale, blocks, len(orders), half, "bins_for_next", scale)
+        blocks.append(own[group] + others[group])
+        scales.append(jnp.stack([scale[0], scale[group + 1]]))
+        off = jnp.stack([owner_off[0], owner_off[group + 1]])
+        place = jnp.zeros_like(off)
+        for bit in [0] + order[1:] + later:
+            place = place * 2 + (off >> bit & 1)
+        place = place * CC + jnp.stack([cell[0], cell[group + 1]]) % CC
+        place = jnp.where(off >> order[0] & 1 == 0, place, -1)
+        bins.append(
+            [
+                jnp.where((place >= low) & (place < low + count), place - low, -1)
+                for low, count in ((size, size), (half, half), (0, half))
+            ]
+        )
+    from_pair = [
+        swap(bin_blocks(lines[0], factor, parts, size, "bins_for_pair", others[1 - group][-1]), 0)
+        for group, (lines, factor, parts) in enumerate(zip(bins, scales, blocks))
+    ]
     edge = up(radius, 16)
     taps = filter_taps.astype(jnp.bfloat16).astype(jnp.float32)[None]
     row_filter, col_filter = filters(taps, block_side, edge)
-    kept = bin_blocks(for_rest, scale, blocks, len(orders), half, "bins_kept", row_filter)
     groups = []
-    for group, order in enumerate(orders):
-        mine = got[group * size : (group + 1) * size]
-        outgoing = sent[group * half : (group + 1) * half].astype(jnp.float32) + mine[half:].astype(jnp.float32)
-        back = swap(outgoing.astype(jnp.bfloat16), order[1])
-        groups.append([kept[group * half : (group + 1) * half], mine[:half], back])
+    for lines, factor, parts, order, mine in zip(bins, scales, blocks, orders, from_pair):
+        sent = bin_blocks(lines[1], factor, parts, half, "bins_for_next", factor)
+        back = swap((sent.astype(jnp.float32) + mine[half:].astype(jnp.float32)).astype(jnp.bfloat16), order[1])
+        kept = bin_blocks(lines[2], factor, parts, half, "bins_kept", row_filter)
+        groups.append([kept, mine[:half], back])
     got = [swap(halves(parts, True).astype(jnp.bfloat16), order[2]) for parts, order in zip(groups, orders)]
     groups = [first_halves(parts) + [part] for parts, part in zip(groups, got)]
     joined = []

time: 58.4 us -> 59.6 us (1.021)
  waiting for transfers between devices: 17.9 us -> 16.2 us
  starting transfers between devices: 24.6 us -> 26.1 us
  Pallas kernels: 13.7 us -> 15.1 us
    ppermute x14 -> x15, starting transfers between devices: 15.1 us -> 20.9 us  [swap(): return lax.ppermute(array, axis, [(i, i ^ 1 << bit) for i in range(count)])]
    ppermute x1, starting transfers between devices: 6.65 us -> 2.35 us  [local(): lax.ppermute(jnp.where(even, top, bottom), 'band', inner + [(i, j) for j,...]
    ppermute x14 -> x15, waiting for transfers between devices: 15.2 us -> 12.1 us  [swap(): return lax.ppermute(array, axis, [(i, i ^ 1 << bit) for i in range(count)])]
    pallas_call x3 -> x6, Pallas kernels: 5.9 us -> 7.3 us  [bin_blocks(): pl.pallas_call(functools.partial(bin_kernel, stepped), grid=grid, out_sha...]
    ppermute x1, waiting for transfers between devices: 1.5 us -> 2.85 us  [local(): lax.ppermute(jnp.where(even, top, bottom), 'band', inner + [(i, j) for j,...]
  transfers between devices with their start and end apart: 18 -> 19, of which waited for: 11 -> 8; matrix products, arithmetic and copies ran while one was open for 2% -> 3% of each run, Pallas kernels for 15% -> 21%
where the time goes in v4:
time: 59.6 us; the launch traced here: 59.4 us
  starting transfers between devices  26.1 us (44%)
  waiting for transfers between devices  16.2 us (27%)
  Pallas kernels  15.1 us (25%)
  other arithmetic  1.58 us (3%)
    ppermute x15, starting transfers between devices, swap(): return lax.ppermute(array, axis, [(i, i ^ 1 << bit) for i in range(count)])  20.9 us
    ppermute x15, waiting for transfers between devices, swap(): return lax.ppermute(array, axis, [(i, i ^ 1 << bit) for i in range(count)])  12.1 us
    pallas_call x6, Pallas kernels, bin_blocks(): pl.pallas_call(functools.partial(bin_kernel, stepped), grid=grid, out_sha...  7.3 us
    pallas_call x3, Pallas kernels, match_blocks(): pl.pallas_call(functools.partial(match_kernel, first, count, skip, not in...  4.74 us
    ppermute x3, starting transfers between devices, local(): lax.ppermute(own_facts, 'band', [(i, i ^ off) for i in range(band_count)])  2.87 us
    ppermute x1, waiting for transfers between devices, local(): lax.ppermute(jnp.where(even, top, bottom), 'band', inner + [(i, j) for j,...  2.85 us
    ppermute x1, starting transfers between devices, local(): lax.ppermute(jnp.where(even, top, bottom), 'band', inner + [(i, j) for j,...  2.35 us
    pallas_call x1, Pallas kernels, load(): pl.pallas_call(load_kernel, out_shape=out_shape, in_specs=[pl.BlockSpec(m...  1.67 us
  transfers between devices with their start and end apart: 19, of which 8 were waited for; matrix products, arithmetic and copies ran while one was open for 3% of the time, Pallas kernels for 21%

profile of v4, /device:TPU:1, one launch (start us, length us, event | category | flops | bytes accessed | tf_op | source)
XLA Modules:
  0.0 59.4 jit_solution(345510059204965076)
XLA Ops:
  0.0 1.7 %load.1 = (f32[1,2,32]{2,1,0:T(2,128)S(1)}, f32[3,32]{1,0:T(4,128)S(1)}, bf16[384,168]{1,0:T(8,128)(2,1)S(1)}, bf16[768,128]{1,0:T(8,128)(2,1)S(1)}, bf16[168,5376]{1,0:T(8,128)(2,1)S(1)}) custom-call(s32[1,32]{1,0:T(1,128)} %bitcast.29, s32[1,32]{1,0:T(1,128)} %bitcast.30, s32[1,32]{1,0:T(1,128)} %bitcast.31, bf16[32]{0:T(256)(128)(2,1)} %refs_3_.1, ...), custom_call_target="tpu_custom_call" | custom-call | flops 1048576 | bytes 4194304 | tf_op jit(solution)/shard_map/load/pallas_call | solution.py:73
  1.7 0.1 collective-permute-start.1
  1.8 2.7 %collective-permute-start = (f32[1,2,32]{2,1,0:T(2,128)S(1)}, f32[1,2,32]{2,1,0:T(2,128)S(1)}, u32[]{:S(2)}, u32[]{:S(2)}) collective-permute-start(f32[1,2,32]{2,1,0:T(2,128)S(1)} %get-tuple-element.20.after_ref), channel_id=1, source_target_pairs={{0,2},{1,3},{2,0},{3,1},{4,6},{5,7},{6,4},{7,5},{8,10},{9,11},{10,... | collective-permute-start | bytes 776 | tf_op jit(solution)/shard_map/ppermute | solution.py:286
  4.5 0.0 collective-permute-start.2
  4.5 1.7 %match_blocks.3 = (bf16[20,64,128]{2,1,0:T(8,128)(2,1)S(1)}, bf16[20,64,128]{2,1,0:T(8,128)(2,1)S(1)}) custom-call(f32[1,2,32]{2,1,0:T(2,128)S(1)} %get-tuple-element.20.after_ref, f32[3,32]{1,0:T(4,128)S(1)} %get-tuple-element.21.coef_ref, bf16[384,168]{1,0:T(8,128)(2,1)S(1)} %get-tuple-element.22.rowk_ref, ...), custom_call_target="tpu_custom_call" | custom-call | flops 1833172992 | bytes 2097152 | tf_op jit(solution)/shard_map/match_blocks/pallas_call | solution.py:117
  6.3 0.0 collective-permute-done.1
  6.3 0.0 collective-permute-done
  6.3 1.2 %collective-permute-done.2 = f32[1,2,32]{2,1,0:T(2,128)S(1)} collective-permute-done((f32[1,2,32]{2,1,0:T(2,128)S(1)}, f32[1,2,32]{2,1,0:T(2,128)S(1)}, u32[]{:S(2)}, u32[]{:S(2)}) %collective-permute-start.2) | collective-permute-done | bytes 288 | tf_op jit(solution)/shard_map/ppermute | solution.py:286
  7.5 1.2 %collective-permute-start.3 = (f32[4,2,32]{2,1,0:T(2,128)S(1)}, f32[4,2,32]{2,1,0:T(2,128)S(1)}, u32[]{:S(2)}, u32[]{:S(2)}) collective-permute-start(f32[4,2,32]{2,1,0:T(2,128)S(1)} %get-tuple-element.68.after_ref), channel_id=1, source_target_pairs={{0,4},{4,0},{8,12},{12,8},{16,20},{20,16},{24,28},{28,24},{1,5},{5... | collective-permute-start | bytes 3080 | tf_op jit(solution)/shard_map/ppermute | solution.py:266
  8.7 1.3 %match_blocks.4 = (bf16[20,64,128]{2,1,0:T(8,128)(2,1)S(1)}, bf16[20,64,128]{2,1,0:T(8,128)(2,1)S(1)}) custom-call(f32[4,2,32]{2,1,0:T(2,128)S(1)} %get-tuple-element.68.after_ref, f32[3,32]{1,0:T(4,128)S(1)} %get-tuple-element.21.coef_ref, bf16[384,168]{1,0:T(8,128)(2,1)S(1)} %get-tuple-element.22.rowk_ref, ...), custom_call_target="tpu_custom_call", output_to_operand_aliasing={{0}: (5, {}), {1}: (6, {})} | custom-call | flops 1222115328 | bytes 2097152 | tf_op jit(solution)/shard_map/match_blocks/pallas_call | solution.py:117
  10.0 0.3 collective-permute-start.12
  10.3 0.5 collective-permute-start.6
  10.9 0.0 collective-permute-done.3
  11.0 0.0 copy-start
  11.0 1.4 %collective-permute-start.4 = (f32[8,2,32]{2,1,0:T(2,128)S(1)}, f32[8,2,32]{2,1,0:T(2,128)S(1)}, u32[]{:S(2)}, u32[]{:S(2)}) collective-permute-start(f32[8,2,32]{2,1,0:T(2,128)S(1)} %get-tuple-element.49.after_ref), channel_id=1, source_target_pairs={{0,8},{4,12},{8,0},{12,4},{16,24},{20,28},{24,16},{28,20},{1,9},{5... | collective-permute-start | bytes 6152 | tf_op jit(solution)/shard_map/ppermute | solution.py:266
  12.4 1.8 %match_blocks.5 = (bf16[12,64,128]{2,1,0:T(8,128)(2,1)S(1)}, bf16[12,64,128]{2,1,0:T(8,128)(2,1)S(1)}) custom-call(f32[8,2,32]{2,1,0:T(2,128)S(1)} %get-tuple-element.49.after_ref, f32[3,32]{1,0:T(4,128)S(1)} %get-tuple-element.21.coef_ref, bf16[384,168]{1,0:T(8,128)(2,1)S(1)} %get-tuple-element.22.rowk_ref, ...), custom_call_target="tpu_custom_call" | custom-call | flops 1833172992 | bytes 2097152 | tf_op jit(solution)/shard_map/match_blocks/pallas_call | solution.py:117
  14.1 1.3 %collective-permute-start.8 = (bf16[12,64,128]{2,1,0:T(8,128)(2,1)S(1)}, bf16[12,64,128]{2,1,0:T(8,128)(2,1)S(1)}, u32[]{:S(2)}, u32[]{:S(2)}) collective-permute-start(bf16[12,64,128]{2,1,0:T(8,128)(2,1)S(1)} %get-tuple-element.29.rest_1_), channel_id=1, source_target_pairs={{0,4},{4,0},{8,12},{12,8},{16,20},{20,16},{24,28},{28,24},{1,5},{5... | collective-permute-start | bytes 589832 | tf_op jit(solution)/shard_map/ppermute | solution.py:266
  15.4 0.9 %collective-permute-start.7 = (bf16[12,64,128]{2,1,0:T(8,128)(2,1)S(1)}, bf16[12,64,128]{2,1,0:T(8,128)(2,1)S(1)}, u32[]{:S(2)}, u32[]{:S(2)}) collective-permute-start(bf16[12,64,128]{2,1,0:T(8,128)(2,1)S(1)} %get-tuple-element.28.rest_1_), channel_id=1, source_target_pairs={{0,2},{1,3},{2,0},{3,1},{4,6},{5,7},{6,4},{7,5},{8,10},{9,11},{10,... | collective-permute-start | bytes 589832 | tf_op jit(solution)/shard_map/ppermute | solution.py:266
  16.3 0.0 collective-permute-done.4
  16.4 2.4 %collective-permute-start.5 = (f32[16,2,32]{2,1,0:T(2,128)S(1)}, f32[16,2,32]{2,1,0:T(2,128)S(1)}, u32[]{:S(2)}, u32[]{:S(2)}) collective-permute-start(f32[16,2,32]{2,1,0:T(2,128)S(1)} %get-tuple-element.45), channel_id=1, source_target_pairs={{0,16},{4,20},{8,24},{12,28},{16,0},{20,4},{24,8},{28,12},{1,17},{... | collective-permute-start | bytes 12296 | tf_op jit(solution)/shard_map/ppermute | solution.py:266
  18.7 0.0 copy-done
  18.7 0.1 select_reduce_fusion.1
  18.8 1.2 %collective-permute-done.5 = f32[16,2,32]{2,1,0:T(2,128)S(1)} collective-permute-done((f32[16,2,32]{2,1,0:T(2,128)S(1)}, f32[16,2,32]{2,1,0:T(2,128)S(1)}, u32[]{:S(2)}, u32[]{:S(2)}) %collective-permute-start.5) | collective-permute-done | bytes 4128 | tf_op jit(solution)/shard_map/ppermute | solution.py:266
  20.0 0.9 %select_reduce_fusion = f32[3,32]{1,0:T(4,128)S(1)} fusion(f32[32,32]{1,0:T(8,128)S(1)} %bitcast.26, f32[32,32]{1,0:T(8,128)S(1)} %bitcast.25, f32[3,32]{1,0:T(4,128)S(1)} %bitcast.27), kind=kLoop, calls=%fused_computation | loop fusion | flops 294816 | bytes 8960 | tf_op jit(solution)/shard_map/reduce_sum | solution.py:307
  21.0 1.9 %collective-permute-done.8.after_ref.rest_3_ = bf16[12,64,128]{2,1,0:T(8,128)(2,1)S(1)} collective-permute-done((bf16[12,64,128]{2,1,0:T(8,128)(2,1)S(1)}, bf16[12,64,128]{2,1,0:T(8,128)(2,1)S(1)}, u32[]{:S(2)}, u32[]{:S(2)}) %collective-permute-start.8) | collective-permute-done | bytes 196640 | tf_op jit(solution)/shard_map/ppermute | solution.py:266
  22.9 0.0 collective-permute-done.7.rest_3_.after_ref
  22.9 0.0 collective-permute-done.12.rest_2_
  22.9 1.3 %bins_for_pair.3 = bf16[32,64,128]{2,1,0:T(8,128)(2,1)S(1)} custom-call(s32[2,32]{1,0:T(2,128)S(1)} %get-tuple-element.63.bins_ref, f32[2,32]{1,0:T(2,128)S(1)} %pad_maximum_fusion.2.scale_ref.after_ref, bf16[12,64,128]{2,1,0:T(8,128)(2,1)S(1)} %collective-permute-done.7.rest_3_.after_ref, bf16[20,64,128]{2,1,0:T(8,128)(2,1)S(1)} %get-tuple-element.30.rest_0_, ...), custom_call_target="tpu_custom_call" | custom-call | flops 3145728 | bytes 1572864 | tf_op jit(solution)/shard_map/bins_for_pair/pallas_call | solution.py:162
  24.2 1.8 %collective-permute-start.13 = (bf16[32,64,128]{2,1,0:T(8,128)(2,1)S(1)}, bf16[32,64,128]{2,1,0:T(8,128)(2,1)S(1)}, u32[]{:S(2)}, u32[]{:S(2)}) collective-permute-start(bf16[32,64,128]{2,1,0:T(8,128)(2,1)S(1)} %bins_for_pair.3), channel_id=1, source_target_pairs={{0,1},{1,0},{2,3},{3,2},{4,5},{5,4},{6,7},{7,6},{8,9},{9,8},{10,11... | collective-permute-start | bytes 1572872 | tf_op jit(solution)/shard_map/ppermute | solution.py:266
  26.1 0.0 collective-permute-done.6.rest_2_
  26.1 1.3 %bins_for_pair.2 = bf16[32,64,128]{2,1,0:T(8,128)(2,1)S(1)} custom-call(s32[2,32]{1,0:T(2,128)S(1)} %get-tuple-element.61.bins_ref, f32[2,32]{1,0:T(2,128)S(1)} %stack.24.scale_ref.after_ref, bf16[12,64,128]{2,1,0:T(8,128)(2,1)S(1)} %collective-permute-done.8.after_ref.rest_3_, bf16[20,64,128]{2,1,0:T(8,128)(2,1)S(1)} %get-tuple-element.27.rest_0_, ...), custom_call_target="tpu_custom_call" | custom-call | flops 3145728 | bytes 1572864 | tf_op jit(solution)/shard_map/bins_for_pair/pallas_call | solution.py:162
  27.4 0.1 collective-permute-start.9
  27.4 1.2 %bins_for_next.3 = bf16[16,64,128]{2,1,0:T(8,128)(2,1)S(1)} custom-call(s32[2,32]{1,0:T(2,128)S(1)} %get-tuple-element.64.bins_ref, f32[2,32]{1,0:T(2,128)S(1)} %pad_maximum_fusion.2.scale_ref.after_ref, f32[2,32]{1,0:T(2,128)S(1)} %pad_maximum_fusion.2.scale_ref.after_ref, bf16[20,64,128]{2,1,0:T(8,128)(2,1)S(1)} %get-tuple-element.30.rest_0_, ...), custom_call_target="tpu_custom_call" | custom-call | flops 2621440 | bytes 1310720 | tf_op jit(solution)/shard_map/bins_for_next/pallas_call | solution.py:162
  28.6 0.0 copy-start.1
  28.7 1.2 %bins_for_next.2 = bf16[16,64,128]{2,1,0:T(8,128)(2,1)S(1)} custom-call(s32[2,32]{1,0:T(2,128)S(1)} %get-tuple-element.62.bins_ref, f32[2,32]{1,0:T(2,128)S(1)} %stack.24.scale_ref.after_ref, f32[2,32]{1,0:T(2,128)S(1)} %stack.24.scale_ref.after_ref, bf16[20,64,128]{2,1,0:T(8,128)(2,1)S(1)} %get-tuple-element.27.rest_0_, ...), custom_call_target="tpu_custom_call" | custom-call | flops 2621440 | bytes 1310720 | tf_op jit(solution)/shard_map/bins_for_next/pallas_call | solution.py:162
  29.8 0.0 collective-permute-done.13
  29.9 0.1 add_convert_fusion
  29.9 0.6 collective-permute-start.14
  30.5 0.0 collective-permute-done.9
  30.5 0.1 add_convert_fusion.1
  30.6 1.4 %collective-permute-start.10 = (bf16[16,64,128]{2,1,0:T(8,128)(2,1)S(1)}, bf16[16,64,128]{2,1,0:T(8,128)(2,1)S(1)}, u32[]{:S(2)}, u32[]{:S(2)}) collective-permute-start(bf16[16,64,128]{2,1,0:T(8,128)(2,1)S(1)} %add_convert_fusion.1), channel_id=1, source_target_pairs={{0,8},{4,12},{8,0},{12,4},{16,24},{20,28},{24,16},{28,20},{1,9},{5... | collective-permute-start | bytes 786440 | tf_op jit(solution)/shard_map/ppermute | solution.py:266
  32.0 0.0 copy-done.1
  32.0 0.3 filters.1
  32.3 1.2 %bins_kept.3 = bf16[16,64,128]{2,1,0:T(8,128)(2,1)S(1)} custom-call(s32[2,32]{1,0:T(2,128)S(1)} %get-tuple-element.33.bins_ref, f32[2,32]{1,0:T(2,128)S(1)} %pad_maximum_fusion.2.scale_ref.after_ref, bf16[128,192]{1,0:T(8,128)(2,1)S(1)} %get-tuple-element.18.after_ref.row_filter_ref, bf16[20,64,128]{2,1,0:T(8,128)(2,1)S(1)} %get-tuple-element.30.rest_0_, ...), custom_call_target="tpu_custom_call" | custom-call | flops 2621440 | bytes 1310720 | tf_op jit(solution)/shard_map/bins_kept/pallas_call | solution.py:162
  33.5 1.2 %bins_kept.2 = bf16[16,64,128]{2,1,0:T(8,128)(2,1)S(1)} custom-call(s32[2,32]{1,0:T(2,128)S(1)} %get-tuple-element.31.bins_ref, f32[2,32]{1,0:T(2,128)S(1)} %stack.24.scale_ref.after_ref, bf16[128,192]{1,0:T(8,128)(2,1)S(1)} %get-tuple-element.18.after_ref.row_filter_ref, bf16[20,64,128]{2,1,0:T(8,128)(2,1)S(1)} %get-tuple-element.27.rest_0_, ...), custom_call_target="tpu_custom_call" | custom-call | flops 2621440 | bytes 1310720 | tf_op jit(solution)/shard_map/bins_kept/pallas_call | solution.py:162
  34.7 2.7 %collective-permute-done.14 = bf16[16,64,128]{2,1,0:T(8,128)(2,1)S(1)} collective-permute-done((bf16[16,64,128]{2,1,0:T(8,128)(2,1)S(1)}, bf16[16,64,128]{2,1,0:T(8,128)(2,1)S(1)}, u32[]{:S(2)}, u32[]{:S(2)}) %collective-permute-start.14) | collective-permute-done | bytes 262176 | tf_op jit(solution)/shard_map/ppermute | solution.py:266
  37.4 0.1 add_convert_fusion.2
  37.5 1.4 %collective-permute-start.15 = (bf16[8,64,128]{2,1,0:T(8,128)(2,1)S(1)}, bf16[8,64,128]{2,1,0:T(8,128)(2,1)S(1)}, u32[]{:S(2)}, u32[]{:S(2)}) collective-permute-start(bf16[8,64,128]{2,1,0:T(8,128)(2,1)S(1)} %add_convert_fusion.2), channel_id=1, source_target_pairs={{0,8},{4,12},{8,0},{12,4},{16,24},{20,28},{24,16},{28,20},{1,9},{5... | collective-permute-start | bytes 393224 | tf_op jit(solution)/shard_map/ppermute | solution.py:266
  38.9 0.0 collective-permute-done.10
  38.9 0.1 add_convert_fusion.3
  38.9 1.2 %collective-permute-start.11 = (bf16[8,64,128]{2,1,0:T(8,128)(2,1)S(1)}, bf16[8,64,128]{2,1,0:T(8,128)(2,1)S(1)}, u32[]{:S(2)}, u32[]{:S(2)}) collective-permute-start(bf16[8,64,128]{2,1,0:T(8,128)(2,1)S(1)} %add_convert_fusion.3), channel_id=1, source_target_pairs={{0,4},{4,0},{8,12},{12,8},{16,20},{20,16},{24,28},{28,24},{1,5},{5... | collective-permute-start | bytes 393224 | tf_op jit(solution)/shard_map/ppermute | solution.py:266
  40.1 1.2 %collective-permute-done.15 = bf16[8,64,128]{2,1,0:T(8,128)(2,1)S(1)} collective-permute-done((bf16[8,64,128]{2,1,0:T(8,128)(2,1)S(1)}, bf16[8,64,128]{2,1,0:T(8,128)(2,1)S(1)}, u32[]{:S(2)}, u32[]{:S(2)}) %collective-permute-start.15) | collective-permute-done | bytes 131104 | tf_op jit(solution)/shard_map/ppermute | solution.py:266
  41.3 0.1 add_convert_fusion.4
  41.4 1.7 %collective-permute-done.11 = bf16[8,64,128]{2,1,0:T(8,128)(2,1)S(1)} collective-permute-done((bf16[8,64,128]{2,1,0:T(8,128)(2,1)S(1)}, bf16[8,64,128]{2,1,0:T(8,128)(2,1)S(1)}, u32[]{:S(2)}, u32[]{:S(2)}) %collective-permute-start.11) | collective-permute-done | bytes 131104 | tf_op jit(solution)/shard_map/ppermute | solution.py:266
  43.1 0.1 add_convert_fusion.5
  43.2 2.4 %collective-permute-start.16 = (bf16[4,128,128]{2,1,0:T(8,128)(2,1)S(1)}, bf16[4,128,128]{2,1,0:T(8,128)(2,1)S(1)}, u32[]{:S(2)}, u32[]{:S(2)}) collective-permute-start(bf16[4,128,128]{2,1,0:T(8,128)(2,1)S(1)} %pad_maximum_fusion), channel_id=1, source_target_pairs={{0,16},{4,20},{8,24},{12,28},{16,0},{20,4},{24,8},{28,12},{1,17},{... | collective-permute-start | bytes 393224 | tf_op jit(solution)/shard_map/ppermute | solution.py:266
  45.6 3.4 %collective-permute-done.16 = bf16[4,128,128]{2,1,0:T(8,128)(2,1)S(1)} collective-permute-done((bf16[4,128,128]{2,1,0:T(8,128)(2,1)S(1)}, bf16[4,128,128]{2,1,0:T(8,128)(2,1)S(1)}, u32[]{:S(2)}, u32[]{:S(2)}) %collective-permute-start.16) | collective-permute-done | bytes 131104 | tf_op jit(solution)/shard_map/ppermute | solution.py:266
  49.1 4.0 %collective-permute-start.18 = (bf16[4,32,128]{2,1,0:T(8,128)(2,1)S(1)}, bf16[4,32,128]{2,1,0:T(8,128)(2,1)S(1)}, u32[]{:S(2)}, u32[]{:S(2)}) collective-permute-start(bf16[4,32,128]{2,1,0:T(8,128)(2,1)S(1)} %get-tuple-element.39), channel_id=1, source_target_pairs={{0,1},{1,0},{2,3},{3,2},{4,5},{5,4},{6,7},{7,6},{8,9},{9,8},{10,11... | collective-permute-start | bytes 98312 | tf_op jit(solution)/shard_map/ppermute | solution.py:266
  53.1 2.4 %collective-permute-start.17 = (bf16[4,32,128]{2,1,0:T(8,128)(2,1)S(1)}, bf16[4,32,128]{2,1,0:T(8,128)(2,1)S(1)}, u32[]{:S(2)}, u32[]{:S(2)}) collective-permute-start(bf16[4,32,128]{2,1,0:T(8,128)(2,1)S(1)} %get-tuple-element.40), channel_id=1, source_target_pairs={{1,2},{2,1},{5,6},{6,5},{9,10},{10,9},{13,14},{14,13},{17,18},{18,... | collective-permute-start | bytes 98312 | tf_op jit(solution)/shard_map/ppermute | solution.py:368
  55.5 0.0 collective-permute-done.18
  55.5 2.9 %collective-permute-done.17 = bf16[4,32,128]{2,1,0:T(8,128)(2,1)S(1)} collective-permute-done((bf16[4,32,128]{2,1,0:T(8,128)(2,1)S(1)}, bf16[4,32,128]{2,1,0:T(8,128)(2,1)S(1)}, u32[]{:S(2)}, u32[]{:S(2)}) %collective-permute-start.17) | collective-permute-done | bytes 32800 | tf_op jit(solution)/shard_map/ppermute | solution.py:368
  58.3 1.1 %detect.1 = f32[128,512]{1,0:T(8,128)} custom-call(bf16[128,192]{1,0:T(8,128)(2,1)S(1)} %get-tuple-element.18.after_ref.row_filter_ref, bf16[384,128]{1,0:T(8,128)(2,1)S(1)} %get-tuple-element.19.col_filter_ref, bf16[4,128,128]{2,1,0:T(8,128)(2,1)S(1)} %fusion.mid_ref, bf16[4,32,128]{2,1,0:T(8,128)(2,1)S(1)} %get-tuple-element.42.low_ref, ...), custom_call_target="tpu_custom_call" | custom-call | tf_op jit(solution)/shard_map/detect/pallas_call | solution.py:218
  (27 shorter events, 0.3 us)
Async XLA Ops:
  1.7 4.6 %collective-permute-start.1 = (f32[1,2,32]{2,1,0:T(2,128)S(1)}, f32[1,2,32]{2,1,0:T(2,128)S(1)}, u32[]{:S(2)}, u32[]{:S(2)}) collective-permute-start(f32[1,2,32]{2,1,0:T(2,128)S(1)} %get-tuple-element.20.after_ref), channel_id=1, source_target_pairs={{0,1},{1,0},{2,3},{3,2},{4,5},{5,4},{6,7},{7,6},{8,9},{9,8},{10,11... | collective-permute-start | bytes 776 | tf_op jit(solution)/shard_map/ppermute | solution.py:286
  1.8 4.5 %collective-permute-start = (f32[1,2,32]{2,1,0:T(2,128)S(1)}, f32[1,2,32]{2,1,0:T(2,128)S(1)}, u32[]{:S(2)}, u32[]{:S(2)}) collective-permute-start(f32[1,2,32]{2,1,0:T(2,128)S(1)} %get-tuple-element.20.after_ref), channel_id=1, source_target_pairs={{0,2},{1,3},{2,0},{3,1},{4,6},{5,7},{6,4},{7,5},{8,10},{9,11},{10,... | collective-permute-start | bytes 776 | tf_op jit(solution)/shard_map/ppermute | solution.py:286
  4.5 3.0 %collective-permute-start.2 = (f32[1,2,32]{2,1,0:T(2,128)S(1)}, f32[1,2,32]{2,1,0:T(2,128)S(1)}, u32[]{:S(2)}, u32[]{:S(2)}) collective-permute-start(f32[1,2,32]{2,1,0:T(2,128)S(1)} %get-tuple-element.20.after_ref), channel_id=1, source_target_pairs={{0,3},{1,2},{2,1},{3,0},{4,7},{5,6},{6,5},{7,4},{8,11},{9,10},{10,... | collective-permute-start | bytes 776 | tf_op jit(solution)/shard_map/ppermute | solution.py:286
  7.5 3.4 %collective-permute-start.3 = (f32[4,2,32]{2,1,0:T(2,128)S(1)}, f32[4,2,32]{2,1,0:T(2,128)S(1)}, u32[]{:S(2)}, u32[]{:S(2)}) collective-permute-start(f32[4,2,32]{2,1,0:T(2,128)S(1)} %get-tuple-element.68.after_ref), channel_id=1, source_target_pairs={{0,4},{4,0},{8,12},{12,8},{16,20},{20,16},{24,28},{28,24},{1,5},{5... | collective-permute-start | bytes 3080 | tf_op jit(solution)/shard_map/ppermute | solution.py:266
  10.0 12.9 %collective-permute-start.12 = (bf16[20,64,128]{2,1,0:T(8,128)(2,1)S(1)}, bf16[20,64,128]{2,1,0:T(8,128)(2,1)S(1)}, u32[]{:S(2)}, u32[]{:S(2)}) collective-permute-start(bf16[20,64,128]{2,1,0:T(8,128)(2,1)S(1)} %get-tuple-element.30.rest_0_), channel_id=1, source_target_pairs={{0,4},{4,0},{8,12},{12,8},{16,20},{20,16},{24,28},{28,24},{1,5},{5... | collective-permute-start | bytes 983048 | tf_op jit(solution)/shard_map/ppermute | solution.py:266
  10.3 15.7 %collective-permute-start.6 = (bf16[20,64,128]{2,1,0:T(8,128)(2,1)S(1)}, bf16[20,64,128]{2,1,0:T(8,128)(2,1)S(1)}, u32[]{:S(2)}, u32[]{:S(2)}) collective-permute-start(bf16[20,64,128]{2,1,0:T(8,128)(2,1)S(1)} %get-tuple-element.27.rest_0_), channel_id=1, source_target_pairs={{0,2},{1,3},{2,0},{3,1},{4,6},{5,7},{6,4},{7,5},{8,10},{9,11},{10,... | collective-permute-start | bytes 983048 | tf_op jit(solution)/shard_map/ppermute | solution.py:266
  11.0 7.7 %copy-start = (f32[6]{0:T(128)S(1)}, f32[6]{0:T(128)}, u32[]{:S(2)}) copy-start(f32[6]{0:T(128)} %param.18) | copy-start | bytes 76
  11.0 5.3 %collective-permute-start.4 = (f32[8,2,32]{2,1,0:T(2,128)S(1)}, f32[8,2,32]{2,1,0:T(2,128)S(1)}, u32[]{:S(2)}, u32[]{:S(2)}) collective-permute-start(f32[8,2,32]{2,1,0:T(2,128)S(1)} %get-tuple-element.49.after_ref), channel_id=1, source_target_pairs={{0,8},{4,12},{8,0},{12,4},{16,24},{20,28},{24,16},{28,20},{1,9},{5... | collective-permute-start | bytes 6152 | tf_op jit(solution)/shard_map/ppermute | solution.py:266
  14.1 8.8 %collective-permute-start.8 = (bf16[12,64,128]{2,1,0:T(8,128)(2,1)S(1)}, bf16[12,64,128]{2,1,0:T(8,128)(2,1)S(1)}, u32[]{:S(2)}, u32[]{:S(2)}) collective-permute-start(bf16[12,64,128]{2,1,0:T(8,128)(2,1)S(1)} %get-tuple-element.29.rest_1_), channel_id=1, source_target_pairs={{0,4},{4,0},{8,12},{12,8},{16,20},{20,16},{24,28},{28,24},{1,5},{5... | collective-permute-start | bytes 589832 | tf_op jit(solution)/shard_map/ppermute | solution.py:266
  15.4 7.5 %collective-permute-start.7 = (bf16[12,64,128]{2,1,0:T(8,128)(2,1)S(1)}, bf16[12,64,128]{2,1,0:T(8,128)(2,1)S(1)}, u32[]{:S(2)}, u32[]{:S(2)}) collective-permute-start(bf16[12,64,128]{2,1,0:T(8,128)(2,1)S(1)} %get-tuple-element.28.rest_1_), channel_id=1, source_target_pairs={{0,2},{1,3},{2,0},{3,1},{4,6},{5,7},{6,4},{7,5},{8,10},{9,11},{10,... | collective-permute-start | bytes 589832 | tf_op jit(solution)/shard_map/ppermute | solution.py:266
  16.4 3.6 %collective-permute-start.5 = (f32[16,2,32]{2,1,0:T(2,128)S(1)}, f32[16,2,32]{2,1,0:T(2,128)S(1)}, u32[]{:S(2)}, u32[]{:S(2)}) collective-permute-start(f32[16,2,32]{2,1,0:T(2,128)S(1)} %get-tuple-element.45), channel_id=1, source_target_pairs={{0,16},{4,20},{8,24},{12,28},{16,0},{20,4},{24,8},{28,12},{1,17},{... | collective-permute-start | bytes 12296 | tf_op jit(solution)/shard_map/ppermute | solution.py:266
  24.2 5.6 %collective-permute-start.13 = (bf16[32,64,128]{2,1,0:T(8,128)(2,1)S(1)}, bf16[32,64,128]{2,1,0:T(8,128)(2,1)S(1)}, u32[]{:S(2)}, u32[]{:S(2)}) collective-permute-start(bf16[32,64,128]{2,1,0:T(8,128)(2,1)S(1)} %bins_for_pair.3), channel_id=1, source_target_pairs={{0,1},{1,0},{2,3},{3,2},{4,5},{5,4},{6,7},{7,6},{8,9},{9,8},{10,11... | collective-permute-start | bytes 1572872 | tf_op jit(solution)/shard_map/ppermute | solution.py:266
  27.4 3.2 %collective-permute-start.9 = (bf16[32,64,128]{2,1,0:T(8,128)(2,1)S(1)}, bf16[32,64,128]{2,1,0:T(8,128)(2,1)S(1)}, u32[]{:S(2)}, u32[]{:S(2)}) collective-permute-start(bf16[32,64,128]{2,1,0:T(8,128)(2,1)S(1)} %bins_for_pair.2), channel_id=1, source_target_pairs={{0,1},{1,0},{2,3},{3,2},{4,5},{5,4},{6,7},{7,6},{8,9},{9,8},{10,11... | collective-permute-start | bytes 1572872 | tf_op jit(solution)/shard_map/ppermute | solution.py:266
  28.6 3.4 %copy-start.1 = (f32[41]{0:T(128)S(1)}, f32[41]{0:T(128)}, u32[]{:S(2)}) copy-start(f32[41]{0:T(128)} %param.19) | copy-start | bytes 496
  29.9 7.5 %collective-permute-start.14 = (bf16[16,64,128]{2,1,0:T(8,128)(2,1)S(1)}, bf16[16,64,128]{2,1,0:T(8,128)(2,1)S(1)}, u32[]{:S(2)}, u32[]{:S(2)}) collective-permute-start(bf16[16,64,128]{2,1,0:T(8,128)(2,1)S(1)} %add_convert_fusion), channel_id=1, source_target_pairs={{0,2},{1,3},{2,0},{3,1},{4,6},{5,7},{6,4},{7,5},{8,10},{9,11},{10,... | collective-permute-start | bytes 786440 | tf_op jit(solution)/shard_map/ppermute | solution.py:266
  30.6 8.3 %collective-permute-start.10 = (bf16[16,64,128]{2,1,0:T(8,128)(2,1)S(1)}, bf16[16,64,128]{2,1,0:T(8,128)(2,1)S(1)}, u32[]{:S(2)}, u32[]{:S(2)}) collective-permute-start(bf16[16,64,128]{2,1,0:T(8,128)(2,1)S(1)} %add_convert_fusion.1), channel_id=1, source_target_pairs={{0,8},{4,12},{8,0},{12,4},{16,24},{20,28},{24,16},{28,20},{1,9},{5... | collective-permute-start | bytes 786440 | tf_op jit(solution)/shard_map/ppermute | solution.py:266
  37.5 3.9 %collective-permute-start.15 = (bf16[8,64,128]{2,1,0:T(8,128)(2,1)S(1)}, bf16[8,64,128]{2,1,0:T(8,128)(2,1)S(1)}, u32[]{:S(2)}, u32[]{:S(2)}) collective-permute-start(bf16[8,64,128]{2,1,0:T(8,128)(2,1)S(1)} %add_convert_fusion.2), channel_id=1, source_target_pairs={{0,8},{4,12},{8,0},{12,4},{16,24},{20,28},{24,16},{28,20},{1,9},{5... | collective-permute-start | bytes 393224 | tf_op jit(solution)/shard_map/ppermute | solution.py:266
  38.9 4.2 %collective-permute-start.11 = (bf16[8,64,128]{2,1,0:T(8,128)(2,1)S(1)}, bf16[8,64,128]{2,1,0:T(8,128)(2,1)S(1)}, u32[]{:S(2)}, u32[]{:S(2)}) collective-permute-start(bf16[8,64,128]{2,1,0:T(8,128)(2,1)S(1)} %add_convert_fusion.3), channel_id=1, source_target_pairs={{0,4},{4,0},{8,12},{12,8},{16,20},{20,16},{24,28},{28,24},{1,5},{5... | collective-permute-start | bytes 393224 | tf_op jit(solution)/shard_map/ppermute | solution.py:266
  43.2 5.8 %collective-permute-start.16 = (bf16[4,128,128]{2,1,0:T(8,128)(2,1)S(1)}, bf16[4,128,128]{2,1,0:T(8,128)(2,1)S(1)}, u32[]{:S(2)}, u32[]{:S(2)}) collective-permute-start(bf16[4,128,128]{2,1,0:T(8,128)(2,1)S(1)} %pad_maximum_fusion), channel_id=1, source_target_pairs={{0,16},{4,20},{8,24},{12,28},{16,0},{20,4},{24,8},{28,12},{1,17},{... | collective-permute-start | bytes 393224 | tf_op jit(solution)/shard_map/ppermute | solution.py:266
  49.1 6.4 %collective-permute-start.18 = (bf16[4,32,128]{2,1,0:T(8,128)(2,1)S(1)}, bf16[4,32,128]{2,1,0:T(8,128)(2,1)S(1)}, u32[]{:S(2)}, u32[]{:S(2)}) collective-permute-start(bf16[4,32,128]{2,1,0:T(8,128)(2,1)S(1)} %get-tuple-element.39), channel_id=1, source_target_pairs={{0,1},{1,0},{2,3},{3,2},{4,5},{5,4},{6,7},{7,6},{8,9},{9,8},{10,11... | collective-permute-start | bytes 98312 | tf_op jit(solution)/shard_map/ppermute | solution.py:266
  53.1 5.2 %collective-permute-start.17 = (bf16[4,32,128]{2,1,0:T(8,128)(2,1)S(1)}, bf16[4,32,128]{2,1,0:T(8,128)(2,1)S(1)}, u32[]{:S(2)}, u32[]{:S(2)}) collective-permute-start(bf16[4,32,128]{2,1,0:T(8,128)(2,1)S(1)} %get-tuple-element.40), channel_id=1, source_target_pairs={{1,2},{2,1},{5,6},{6,5},{9,10},{10,9},{13,14},{14,13},{17,18},{18,... | collective-permute-start | bytes 98312 | tf_op jit(solution)/shard_map/ppermute | solution.py:368

commit v5 on v4

--- a/solution.py
+++ b/solution.py
@@ -197,13 +197,38 @@
     )(taps)
 
 
-def filter_kernel(row_filter_ref, col_filter_ref, mid_ref, low_ref, high_ref, out_ref):
+def smooth_kernel(even_ref, row_filter_ref, mid_ref, beyond_ref, out_ref):
     cells, side, unused = mid_ref.shape
+    edge = beyond_ref.shape[1]
+    above, below = row_filter_ref[:, :edge], row_filter_ref[:, edge + side :]
+    outer = jnp.where(even_ref[0] != 0, above.astype(jnp.float32), below.astype(jnp.float32)).astype(jnp.bfloat16)
+    for c in range(cells):
+        out_ref[c] = jnp.dot(
+            row_filter_ref[:, edge : edge + side], mid_ref[c], preferred_element_type=jnp.float32
+        ) + jnp.dot(outer, beyond_ref[c], preferred_element_type=jnp.float32)
+
+
+def smooth(even, row_filter, mid, beyond):
+    return pl.pallas_call(
+        smooth_kernel,
+        out_shape=jax.ShapeDtypeStruct(mid.shape, jnp.float32),
+        in_specs=[pl.BlockSpec(memory_space=SMEM)] + [pl.BlockSpec(memory_space=VMEM)] * 3,
+        out_specs=pl.BlockSpec(memory_space=VMEM),
+        compiler_params=pltpu.CompilerParams(vmem_limit_bytes=12 << 20),
+        cost_estimate=pl.CostEstimate(flops=1 << 26, bytes_accessed=1 << 20, transcendentals=0),
+        name="smooth",
+    )(even, row_filter, mid, beyond)
+
+
+def detect_kernel(even_ref, row_filter_ref, col_filter_ref, partial_ref, paired_ref, out_ref):
+    cells, side, unused = partial_ref.shape
+    edge = paired_ref.shape[1]
+    above, below = row_filter_ref[:, :edge], row_filter_ref[:, edge + side :]
+    outer = jnp.where(even_ref[0] != 0, below.astype(jnp.float32), above.astype(jnp.float32)).astype(jnp.bfloat16)
     zero = jnp.zeros((side, side), jnp.bfloat16)
     smoothed = [zero]
     for c in range(cells):
-        column = jnp.concatenate([low_ref[c], mid_ref[c], high_ref[c]], axis=0)
-        rows = jnp.dot(row_filter_ref[...], column, preferred_element_type=jnp.float32)
+        rows = partial_ref[c] + jnp.dot(outer, paired_ref[c], preferred_element_type=jnp.float32)
         smoothed.append(rows.astype(jnp.bfloat16))
     smoothed.append(zero)
     for c in range(cells):
@@ -213,16 +238,16 @@
         )
 
 
-def detect(row_filter, col_filter, mid, low, high):
-    cells, side, unused = mid.shape
-    return pl.pallas_call(
-        filter_kernel,
+def detect(even, row_filter, col_filter, partial, paired):
+    cells, side, unused = partial.shape
+    return pl.pallas_call(
+        detect_kernel,
         out_shape=jax.ShapeDtypeStruct((side, cells * side), jnp.float32),
-        in_specs=[pl.BlockSpec(memory_space=VMEM)] * 5,
+        in_specs=[pl.BlockSpec(memory_space=SMEM)] + [pl.BlockSpec(memory_space=VMEM)] * 4,
         out_specs=pl.BlockSpec(memory_space=VMEM),
         compiler_params=pltpu.CompilerParams(vmem_limit_bytes=12 << 20),
         name="detect",
-    )(row_filter, col_filter, mid, low, high)
+    )(even, row_filter, col_filter, partial, paired)
 
 
 def halves(parts, send):
@@ -339,7 +364,8 @@
     row_filter, col_filter = filters(taps, block_side, edge)
     groups = []
     for lines, factor, parts, order, mine in zip(bins, scales, blocks, orders, from_pair):
-        sent = bin_blocks(lines[1], factor, parts, half, "bins_for_next", factor)
+        known = factor if mine is from_pair[1] else from_pair[1]
+        sent = bin_blocks(lines[1], factor, parts, half, "bins_for_next", known)
         back = swap((sent.astype(jnp.float32) + mine[half:].astype(jnp.float32)).astype(jnp.bfloat16), order[1])
         kept = bin_blocks(lines[2], factor, parts, half, "bins_kept", row_filter)
         groups.append([kept, mine[:half], back])
@@ -367,9 +393,9 @@
     inner = [(i, i + 1) for i in range(1, band_count - 1, 2)]
     beyond = lax.ppermute(jnp.where(even, top, bottom), "band", inner + [(i, j) for j, i in inner])
     paired = swap(jnp.where(even, bottom, top), 0)
-    return detect(
-        row_filter, col_filter, combined, jnp.where(even, beyond, paired), jnp.where(even, paired, beyond)
-    )[None]
+    side = even.astype(jnp.int32)[None]
+    partial = smooth(side, row_filter, combined, beyond)
+    return detect(side, row_filter, col_filter, partial, paired)[None]
 
 
 def solution(mesh):

time: 59.6 us -> 58.3 us (0.978)
  waiting for transfers between devices: 16.2 us -> 14.2 us
    ppermute x1, starting transfers between devices: 2.35 us -> 6.62 us  [local(): lax.ppermute(jnp.where(even, top, bottom), 'band', inner + [(i, j) for j,...]
    ppermute x15, starting transfers between devices: 20.9 us -> 16.9 us  [swap(): return lax.ppermute(array, axis, [(i, i ^ 1 << bit) for i in range(count)])]
    ppermute x1, waiting for transfers between devices: 2.85 us -> 1.5 us  [local(): lax.ppermute(jnp.where(even, top, bottom), 'band', inner + [(i, j) for j,...]
    pallas_call x1 -> x2, Pallas kernels: 1.1 us -> 1.49 us  [the longest x1 1.21 us: detect(): pl.pallas_call(detect_kernel, out_shape=jax.ShapeDtypeStruct((side, cells...]
  transfers between devices with their start and end apart: 19 -> 19, of which waited for: 8 -> 9; matrix products, arithmetic and copies ran while one was open for 3% -> 3% of each run, Pallas kernels for 21% -> 22%
where the time goes in v5:
time: 58.3 us; the launch traced here: 58.1 us
  starting transfers between devices  26.4 us (45%)
  Pallas kernels  15.5 us (27%)
  waiting for transfers between devices  14.2 us (24%)
  other arithmetic  1.58 us (3%)
    ppermute x15, starting transfers between devices, swap(): return lax.ppermute(array, axis, [(i, i ^ 1 << bit) for i in range(count)])  16.9 us
    ppermute x15, waiting for transfers between devices, swap(): return lax.ppermute(array, axis, [(i, i ^ 1 << bit) for i in range(count)])  11.5 us
    pallas_call x6, Pallas kernels, bin_blocks(): pl.pallas_call(functools.partial(bin_kernel, stepped), grid=grid, out_sha...  7.25 us
    ppermute x1, starting transfers between devices, local(): lax.ppermute(jnp.where(even, top, bottom), 'band', inner + [(i, j) for j,...  6.62 us
    pallas_call x3, Pallas kernels, match_blocks(): pl.pallas_call(functools.partial(match_kernel, first, count, skip, not in...  4.74 us
    ppermute x3, starting transfers between devices, local(): lax.ppermute(own_facts, 'band', [(i, i ^ off) for i in range(band_count)])  2.87 us
    pallas_call x1, Pallas kernels, load(): pl.pallas_call(load_kernel, out_shape=out_shape, in_specs=[pl.BlockSpec(m...  1.67 us
    ppermute x1, waiting for transfers between devices, local(): lax.ppermute(jnp.where(even, top, bottom), 'band', inner + [(i, j) for j,...  1.5 us
  transfers between devices with their start and end apart: 19, of which 9 were waited for; matrix products, arithmetic and copies ran while one was open for 3% of the time, Pallas kernels for 22%

profile of v5, /device:TPU:1, one launch (start us, length us, event | category | flops | bytes accessed | tf_op | source)
XLA Modules:
  0.0 58.1 jit_solution(4741722517343779402)
XLA Ops:
  0.0 1.7 %load.1 = (f32[1,2,32]{2,1,0:T(2,128)S(1)}, f32[3,32]{1,0:T(4,128)S(1)}, bf16[384,168]{1,0:T(8,128)(2,1)S(1)}, bf16[768,128]{1,0:T(8,128)(2,1)S(1)}, bf16[168,5376]{1,0:T(8,128)(2,1)S(1)}) custom-call(s32[1,32]{1,0:T(1,128)} %bitcast.30, s32[1,32]{1,0:T(1,128)} %bitcast.31, s32[1,32]{1,0:T(1,128)} %bitcast.32, bf16[32]{0:T(256)(128)(2,1)} %refs_3_.1, ...), custom_call_target="tpu_custom_call" | custom-call | flops 1048576 | bytes 4194304 | tf_op jit(solution)/shard_map/load/pallas_call | solution.py:73
  1.7 0.1 collective-permute-start.1
  1.8 2.7 %collective-permute-start = (f32[1,2,32]{2,1,0:T(2,128)S(1)}, f32[1,2,32]{2,1,0:T(2,128)S(1)}, u32[]{:S(2)}, u32[]{:S(2)}) collective-permute-start(f32[1,2,32]{2,1,0:T(2,128)S(1)} %get-tuple-element.20.after_ref), channel_id=1, source_target_pairs={{0,2},{1,3},{2,0},{3,1},{4,6},{5,7},{6,4},{7,5},{8,10},{9,11},{10,... | collective-permute-start | bytes 776 | tf_op jit(solution)/shard_map/ppermute | solution.py:311
  4.5 0.0 collective-permute-start.2
  4.5 1.7 %match_blocks.3 = (bf16[20,64,128]{2,1,0:T(8,128)(2,1)S(1)}, bf16[20,64,128]{2,1,0:T(8,128)(2,1)S(1)}) custom-call(f32[1,2,32]{2,1,0:T(2,128)S(1)} %get-tuple-element.20.after_ref, f32[3,32]{1,0:T(4,128)S(1)} %get-tuple-element.21.coef_ref, bf16[384,168]{1,0:T(8,128)(2,1)S(1)} %get-tuple-element.22.rowk_ref, ...), custom_call_target="tpu_custom_call" | custom-call | flops 1833172992 | bytes 2097152 | tf_op jit(solution)/shard_map/match_blocks/pallas_call | solution.py:117
  6.3 0.0 collective-permute-done.1
  6.3 0.0 collective-permute-done
  6.3 1.2 %collective-permute-done.2 = f32[1,2,32]{2,1,0:T(2,128)S(1)} collective-permute-done((f32[1,2,32]{2,1,0:T(2,128)S(1)}, f32[1,2,32]{2,1,0:T(2,128)S(1)}, u32[]{:S(2)}, u32[]{:S(2)}) %collective-permute-start.2) | collective-permute-done | bytes 288 | tf_op jit(solution)/shard_map/ppermute | solution.py:311
  7.5 1.2 %collective-permute-start.3 = (f32[4,2,32]{2,1,0:T(2,128)S(1)}, f32[4,2,32]{2,1,0:T(2,128)S(1)}, u32[]{:S(2)}, u32[]{:S(2)}) collective-permute-start(f32[4,2,32]{2,1,0:T(2,128)S(1)} %get-tuple-element.66.after_ref), channel_id=1, source_target_pairs={{0,4},{4,0},{8,12},{12,8},{16,20},{20,16},{24,28},{28,24},{1,5},{5... | collective-permute-start | bytes 3080 | tf_op jit(solution)/shard_map/ppermute | solution.py:291
  8.7 1.3 %match_blocks.4 = (bf16[20,64,128]{2,1,0:T(8,128)(2,1)S(1)}, bf16[20,64,128]{2,1,0:T(8,128)(2,1)S(1)}) custom-call(f32[4,2,32]{2,1,0:T(2,128)S(1)} %get-tuple-element.66.after_ref, f32[3,32]{1,0:T(4,128)S(1)} %get-tuple-element.21.coef_ref, bf16[384,168]{1,0:T(8,128)(2,1)S(1)} %get-tuple-element.22.rowk_ref, ...), custom_call_target="tpu_custom_call", output_to_operand_aliasing={{0}: (5, {}), {1}: (6, {})} | custom-call | flops 1222115328 | bytes 2097152 | tf_op jit(solution)/shard_map/match_blocks/pallas_call | solution.py:117
  10.0 0.3 collective-permute-start.10
  10.3 0.5 collective-permute-start.6
  10.9 0.0 collective-permute-done.3
  11.0 0.0 copy-start
  11.0 1.4 %collective-permute-start.4 = (f32[8,2,32]{2,1,0:T(2,128)S(1)}, f32[8,2,32]{2,1,0:T(2,128)S(1)}, u32[]{:S(2)}, u32[]{:S(2)}) collective-permute-start(f32[8,2,32]{2,1,0:T(2,128)S(1)} %get-tuple-element.47.after_ref), channel_id=1, source_target_pairs={{0,8},{4,12},{8,0},{12,4},{16,24},{20,28},{24,16},{28,20},{1,9},{5... | collective-permute-start | bytes 6152 | tf_op jit(solution)/shard_map/ppermute | solution.py:291
  12.4 1.8 %match_blocks.5 = (bf16[12,64,128]{2,1,0:T(8,128)(2,1)S(1)}, bf16[12,64,128]{2,1,0:T(8,128)(2,1)S(1)}) custom-call(f32[8,2,32]{2,1,0:T(2,128)S(1)} %get-tuple-element.47.after_ref, f32[3,32]{1,0:T(4,128)S(1)} %get-tuple-element.21.coef_ref, bf16[384,168]{1,0:T(8,128)(2,1)S(1)} %get-tuple-element.22.rowk_ref, ...), custom_call_target="tpu_custom_call" | custom-call | flops 1833172992 | bytes 2097152 | tf_op jit(solution)/shard_map/match_blocks/pallas_call | solution.py:117
  14.1 1.3 %collective-permute-start.8 = (bf16[12,64,128]{2,1,0:T(8,128)(2,1)S(1)}, bf16[12,64,128]{2,1,0:T(8,128)(2,1)S(1)}, u32[]{:S(2)}, u32[]{:S(2)}) collective-permute-start(bf16[12,64,128]{2,1,0:T(8,128)(2,1)S(1)} %get-tuple-element.29.rest_1_), channel_id=1, source_target_pairs={{0,4},{4,0},{8,12},{12,8},{16,20},{20,16},{24,28},{28,24},{1,5},{5... | collective-permute-start | bytes 589832 | tf_op jit(solution)/shard_map/ppermute | solution.py:291
  15.4 0.9 %collective-permute-start.7 = (bf16[12,64,128]{2,1,0:T(8,128)(2,1)S(1)}, bf16[12,64,128]{2,1,0:T(8,128)(2,1)S(1)}, u32[]{:S(2)}, u32[]{:S(2)}) collective-permute-start(bf16[12,64,128]{2,1,0:T(8,128)(2,1)S(1)} %get-tuple-element.28.rest_1_), channel_id=1, source_target_pairs={{0,2},{1,3},{2,0},{3,1},{4,6},{5,7},{6,4},{7,5},{8,10},{9,11},{10,... | collective-permute-start | bytes 589832 | tf_op jit(solution)/shard_map/ppermute | solution.py:291
  16.3 0.0 collective-permute-done.4
  16.4 2.4 %collective-permute-start.5 = (f32[16,2,32]{2,1,0:T(2,128)S(1)}, f32[16,2,32]{2,1,0:T(2,128)S(1)}, u32[]{:S(2)}, u32[]{:S(2)}) collective-permute-start(f32[16,2,32]{2,1,0:T(2,128)S(1)} %get-tuple-element.43), channel_id=1, source_target_pairs={{0,16},{4,20},{8,24},{12,28},{16,0},{20,4},{24,8},{28,12},{1,17},{... | collective-permute-start | bytes 12296 | tf_op jit(solution)/shard_map/ppermute | solution.py:291
  18.7 0.0 copy-done
  18.7 0.1 select_reduce_fusion.1
  18.8 1.2 %collective-permute-done.5 = f32[16,2,32]{2,1,0:T(2,128)S(1)} collective-permute-done((f32[16,2,32]{2,1,0:T(2,128)S(1)}, f32[16,2,32]{2,1,0:T(2,128)S(1)}, u32[]{:S(2)}, u32[]{:S(2)}) %collective-permute-start.5) | collective-permute-done | bytes 4128 | tf_op jit(solution)/shard_map/ppermute | solution.py:291
  20.0 0.9 %select_reduce_fusion = f32[3,32]{1,0:T(4,128)S(1)} fusion(f32[32,32]{1,0:T(8,128)S(1)} %bitcast.27, f32[32,32]{1,0:T(8,128)S(1)} %bitcast.26, f32[3,32]{1,0:T(4,128)S(1)} %bitcast.28), kind=kLoop, calls=%fused_computation | loop fusion | flops 294816 | bytes 8960 | tf_op jit(solution)/shard_map/reduce_sum | solution.py:332
  21.0 1.9 %collective-permute-done.8.after_ref.rest_3_ = bf16[12,64,128]{2,1,0:T(8,128)(2,1)S(1)} collective-permute-done((bf16[12,64,128]{2,1,0:T(8,128)(2,1)S(1)}, bf16[12,64,128]{2,1,0:T(8,128)(2,1)S(1)}, u32[]{:S(2)}, u32[]{:S(2)}) %collective-permute-start.8) | collective-permute-done | bytes 196640 | tf_op jit(solution)/shard_map/ppermute | solution.py:291
  22.9 0.0 collective-permute-done.7.rest_3_.after_ref
  22.9 0.0 collective-permute-done.10.rest_2_
  22.9 1.3 %bins_for_pair.3 = bf16[32,64,128]{2,1,0:T(8,128)(2,1)S(1)} custom-call(s32[2,32]{1,0:T(2,128)S(1)} %get-tuple-element.61.bins_ref, f32[2,32]{1,0:T(2,128)S(1)} %pad_maximum_fusion.2.scale_ref.after_ref, bf16[12,64,128]{2,1,0:T(8,128)(2,1)S(1)} %collective-permute-done.7.rest_3_.after_ref, bf16[20,64,128]{2,1,0:T(8,128)(2,1)S(1)} %get-tuple-element.30.rest_0_, ...), custom_call_target="tpu_custom_call" | custom-call | flops 3145728 | bytes 1572864 | tf_op jit(solution)/shard_map/bins_for_pair/pallas_call | solution.py:162
  24.2 1.8 %collective-permute-start.11 = (bf16[32,64,128]{2,1,0:T(8,128)(2,1)S(1)}, bf16[32,64,128]{2,1,0:T(8,128)(2,1)S(1)}, u32[]{:S(2)}, u32[]{:S(2)}) collective-permute-start(bf16[32,64,128]{2,1,0:T(8,128)(2,1)S(1)} %bins_for_pair.3), channel_id=1, source_target_pairs={{0,1},{1,0},{2,3},{3,2},{4,5},{5,4},{6,7},{7,6},{8,9},{9,8},{10,11... | collective-permute-start | bytes 1572872 | tf_op jit(solution)/shard_map/ppermute | solution.py:291
  26.1 0.0 collective-permute-done.6.rest_2_
  26.1 1.3 %bins_for_pair.2 = bf16[32,64,128]{2,1,0:T(8,128)(2,1)S(1)} custom-call(s32[2,32]{1,0:T(2,128)S(1)} %get-tuple-element.59.bins_ref, f32[2,32]{1,0:T(2,128)S(1)} %stack.24.scale_ref, bf16[12,64,128]{2,1,0:T(8,128)(2,1)S(1)} %collective-permute-done.8.after_ref.rest_3_, bf16[20,64,128]{2,1,0:T(8,128)(2,1)S(1)} %get-tuple-element.27.rest_0_, ...), custom_call_target="tpu_custom_call" | custom-call | flops 3145728 | bytes 1572864 | tf_op jit(solution)/shard_map/bins_for_pair/pallas_call | solution.py:162
  27.3 0.1 collective-permute-start.9
  27.4 1.2 %bins_for_next.3 = bf16[16,64,128]{2,1,0:T(8,128)(2,1)S(1)} custom-call(s32[2,32]{1,0:T(2,128)S(1)} %get-tuple-element.62.bins_ref, f32[2,32]{1,0:T(2,128)S(1)} %pad_maximum_fusion.2.scale_ref.after_ref, f32[2,32]{1,0:T(2,128)S(1)} %pad_maximum_fusion.2.scale_ref.after_ref, bf16[20,64,128]{2,1,0:T(8,128)(2,1)S(1)} %get-tuple-element.30.rest_0_, ...), custom_call_target="tpu_custom_call" | custom-call | flops 2621440 | bytes 1310720 | tf_op jit(solution)/shard_map/bins_for_next/pallas_call | solution.py:162
  28.6 0.0 copy-start.1
  28.6 0.0 collective-permute-done.11.after_ref
  28.6 0.1 add_convert_fusion
  28.7 0.6 %collective-permute-start.14 = (bf16[16,64,128]{2,1,0:T(8,128)(2,1)S(1)}, bf16[16,64,128]{2,1,0:T(8,128)(2,1)S(1)}, u32[]{:S(2)}, u32[]{:S(2)}) collective-permute-start(bf16[16,64,128]{2,1,0:T(8,128)(2,1)S(1)} %add_convert_fusion), channel_id=1, source_target_pairs={{0,2},{1,3},{2,0},{3,1},{4,6},{5,7},{6,4},{7,5},{8,10},{9,11},{10,... | collective-permute-start | bytes 786440 | tf_op jit(solution)/shard_map/ppermute | solution.py:291
  29.4 1.2 %bins_for_next.2 = bf16[16,64,128]{2,1,0:T(8,128)(2,1)S(1)} custom-call(s32[2,32]{1,0:T(2,128)S(1)} %get-tuple-element.60.bins_ref, f32[2,32]{1,0:T(2,128)S(1)} %stack.24.scale_ref, bf16[32,64,128]{2,1,0:T(8,128)(2,1)S(1)} %collective-permute-done.11.after_ref, bf16[20,64,128]{2,1,0:T(8,128)(2,1)S(1)} %get-tuple-element.27.rest_0_, ...), custom_call_target="tpu_custom_call" | custom-call | flops 2621440 | bytes 1310720 | tf_op jit(solution)/shard_map/bins_for_next/pallas_call | solution.py:162
  30.5 0.0 collective-permute-done.9
  30.6 0.1 add_convert_fusion.1
  30.6 1.3 %collective-permute-start.12 = (bf16[16,64,128]{2,1,0:T(8,128)(2,1)S(1)}, bf16[16,64,128]{2,1,0:T(8,128)(2,1)S(1)}, u32[]{:S(2)}, u32[]{:S(2)}) collective-permute-start(bf16[16,64,128]{2,1,0:T(8,128)(2,1)S(1)} %add_convert_fusion.1), channel_id=1, source_target_pairs={{0,8},{4,12},{8,0},{12,4},{16,24},{20,28},{24,16},{28,20},{1,9},{5... | collective-permute-start | bytes 786440 | tf_op jit(solution)/shard_map/ppermute | solution.py:291
  32.0 0.0 copy-done.1
  32.0 0.3 filters.1
  32.3 1.2 %bins_kept.3 = bf16[16,64,128]{2,1,0:T(8,128)(2,1)S(1)} custom-call(s32[2,32]{1,0:T(2,128)S(1)} %get-tuple-element.33.bins_ref, f32[2,32]{1,0:T(2,128)S(1)} %pad_maximum_fusion.2.scale_ref.after_ref, bf16[128,192]{1,0:T(8,128)(2,1)S(1)} %get-tuple-element.18.after_ref.row_filter_ref, bf16[20,64,128]{2,1,0:T(8,128)(2,1)S(1)} %get-tuple-element.30.rest_0_, ...), custom_call_target="tpu_custom_call" | custom-call | flops 2621440 | bytes 1310720 | tf_op jit(solution)/shard_map/bins_kept/pallas_call | solution.py:162
  33.5 1.2 %bins_kept.2 = bf16[16,64,128]{2,1,0:T(8,128)(2,1)S(1)} custom-call(s32[2,32]{1,0:T(2,128)S(1)} %get-tuple-element.31.bins_ref, f32[2,32]{1,0:T(2,128)S(1)} %stack.24.scale_ref, bf16[128,192]{1,0:T(8,128)(2,1)S(1)} %get-tuple-element.18.after_ref.row_filter_ref, bf16[20,64,128]{2,1,0:T(8,128)(2,1)S(1)} %get-tuple-element.27.rest_0_, ...), custom_call_target="tpu_custom_call" | custom-call | flops 2621440 | bytes 1310720 | tf_op jit(solution)/shard_map/bins_kept/pallas_call | solution.py:162
  34.7 1.5 %collective-permute-done.14 = bf16[16,64,128]{2,1,0:T(8,128)(2,1)S(1)} collective-permute-done((bf16[16,64,128]{2,1,0:T(8,128)(2,1)S(1)}, bf16[16,64,128]{2,1,0:T(8,128)(2,1)S(1)}, u32[]{:S(2)}, u32[]{:S(2)}) %collective-permute-start.14) | collective-permute-done | bytes 262176 | tf_op jit(solution)/shard_map/ppermute | solution.py:291
  36.2 0.1 add_convert_fusion.2
  36.3 1.4 %collective-permute-start.15 = (bf16[8,64,128]{2,1,0:T(8,128)(2,1)S(1)}, bf16[8,64,128]{2,1,0:T(8,128)(2,1)S(1)}, u32[]{:S(2)}, u32[]{:S(2)}) collective-permute-start(bf16[8,64,128]{2,1,0:T(8,128)(2,1)S(1)} %add_convert_fusion.2), channel_id=1, source_target_pairs={{0,8},{4,12},{8,0},{12,4},{16,24},{20,28},{24,16},{28,20},{1,9},{5... | collective-permute-start | bytes 393224 | tf_op jit(solution)/shard_map/ppermute | solution.py:291
  37.6 0.2 collective-permute-done.12
  37.8 0.1 add_convert_fusion.3
  37.9 1.3 %collective-permute-start.13 = (bf16[8,64,128]{2,1,0:T(8,128)(2,1)S(1)}, bf16[8,64,128]{2,1,0:T(8,128)(2,1)S(1)}, u32[]{:S(2)}, u32[]{:S(2)}) collective-permute-start(bf16[8,64,128]{2,1,0:T(8,128)(2,1)S(1)} %add_convert_fusion.3), channel_id=1, source_target_pairs={{0,4},{4,0},{8,12},{12,8},{16,20},{20,16},{24,28},{28,24},{1,5},{5... | collective-permute-start | bytes 393224 | tf_op jit(solution)/shard_map/ppermute | solution.py:291
  39.1 1.0 %collective-permute-done.15 = bf16[8,64,128]{2,1,0:T(8,128)(2,1)S(1)} collective-permute-done((bf16[8,64,128]{2,1,0:T(8,128)(2,1)S(1)}, bf16[8,64,128]{2,1,0:T(8,128)(2,1)S(1)}, u32[]{:S(2)}, u32[]{:S(2)}) %collective-permute-start.15) | collective-permute-done | bytes 131104 | tf_op jit(solution)/shard_map/ppermute | solution.py:291
  40.1 0.1 add_convert_fusion.4
  40.2 1.8 %collective-permute-done.13 = bf16[8,64,128]{2,1,0:T(8,128)(2,1)S(1)} collective-permute-done((bf16[8,64,128]{2,1,0:T(8,128)(2,1)S(1)}, bf16[8,64,128]{2,1,0:T(8,128)(2,1)S(1)}, u32[]{:S(2)}, u32[]{:S(2)}) %collective-permute-start.13) | collective-permute-done | bytes 131104 | tf_op jit(solution)/shard_map/ppermute | solution.py:291
  42.0 0.1 add_convert_fusion.5
  42.1 2.3 %collective-permute-start.16 = (bf16[4,128,128]{2,1,0:T(8,128)(2,1)S(1)}, bf16[4,128,128]{2,1,0:T(8,128)(2,1)S(1)}, u32[]{:S(2)}, u32[]{:S(2)}) collective-permute-start(bf16[4,128,128]{2,1,0:T(8,128)(2,1)S(1)} %pad_maximum_fusion), channel_id=1, source_target_pairs={{0,16},{4,20},{8,24},{12,28},{16,0},{20,4},{24,8},{28,12},{1,17},{... | collective-permute-start | bytes 393224 | tf_op jit(solution)/shard_map/ppermute | solution.py:291
  44.5 3.9 %collective-permute-done.16 = bf16[4,128,128]{2,1,0:T(8,128)(2,1)S(1)} collective-permute-done((bf16[4,128,128]{2,1,0:T(8,128)(2,1)S(1)}, bf16[4,128,128]{2,1,0:T(8,128)(2,1)S(1)}, u32[]{:S(2)}, u32[]{:S(2)}) %collective-permute-start.16) | collective-permute-done | bytes 131104 | tf_op jit(solution)/shard_map/ppermute | solution.py:291
  48.4 6.6 %collective-permute-start.17 = (bf16[4,32,128]{2,1,0:T(8,128)(2,1)S(1)}, bf16[4,32,128]{2,1,0:T(8,128)(2,1)S(1)}, u32[]{:S(2)}, u32[]{:S(2)}) collective-permute-start(bf16[4,32,128]{2,1,0:T(8,128)(2,1)S(1)} %get-tuple-element.40), channel_id=1, source_target_pairs={{1,2},{2,1},{5,6},{6,5},{9,10},{10,9},{13,14},{14,13},{17,18},{18,... | collective-permute-start | bytes 98312 | tf_op jit(solution)/shard_map/ppermute | solution.py:394
  55.0 0.1 collective-permute-start.18
  55.1 1.5 %collective-permute-done.17.beyond_ref = bf16[4,32,128]{2,1,0:T(8,128)(2,1)S(1)} collective-permute-done((bf16[4,32,128]{2,1,0:T(8,128)(2,1)S(1)}, bf16[4,32,128]{2,1,0:T(8,128)(2,1)S(1)}, u32[]{:S(2)}, u32[]{:S(2)}) %collective-permute-start.17) | collective-permute-done | bytes 32800 | tf_op jit(solution)/shard_map/ppermute | solution.py:394
  56.6 0.3 smooth.1.partial_ref
  56.9 0.0 collective-permute-done.18.paired_ref
  56.9 1.2 %detect.1 = f32[128,512]{1,0:T(8,128)} custom-call(s32[1]{0:T(128)} %bitcast.even_ref, bf16[128,192]{1,0:T(8,128)(2,1)S(1)} %get-tuple-element.18.after_ref.row_filter_ref, bf16[384,128]{1,0:T(8,128)(2,1)S(1)} %get-tuple-element.19.col_filter_ref, f32[4,128,128]{2,1,0:T(8,128)S(1)} %smooth.1.partial_ref, ...), custom_call_target="tpu_custom_call" | custom-call | tf_op jit(solution)/shard_map/detect/pallas_call | solution.py:243
  (26 shorter events, 0.3 us)
Async XLA Ops:
  1.7 4.6 %collective-permute-start.1 = (f32[1,2,32]{2,1,0:T(2,128)S(1)}, f32[1,2,32]{2,1,0:T(2,128)S(1)}, u32[]{:S(2)}, u32[]{:S(2)}) collective-permute-start(f32[1,2,32]{2,1,0:T(2,128)S(1)} %get-tuple-element.20.after_ref), channel_id=1, source_target_pairs={{0,1},{1,0},{2,3},{3,2},{4,5},{5,4},{6,7},{7,6},{8,9},{9,8},{10,11... | collective-permute-start | bytes 776 | tf_op jit(solution)/shard_map/ppermute | solution.py:311
  1.8 4.5 %collective-permute-start = (f32[1,2,32]{2,1,0:T(2,128)S(1)}, f32[1,2,32]{2,1,0:T(2,128)S(1)}, u32[]{:S(2)}, u32[]{:S(2)}) collective-permute-start(f32[1,2,32]{2,1,0:T(2,128)S(1)} %get-tuple-element.20.after_ref), channel_id=1, source_target_pairs={{0,2},{1,3},{2,0},{3,1},{4,6},{5,7},{6,4},{7,5},{8,10},{9,11},{10,... | collective-permute-start | bytes 776 | tf_op jit(solution)/shard_map/ppermute | solution.py:311
  4.5 3.0 %collective-permute-start.2 = (f32[1,2,32]{2,1,0:T(2,128)S(1)}, f32[1,2,32]{2,1,0:T(2,128)S(1)}, u32[]{:S(2)}, u32[]{:S(2)}) collective-permute-start(f32[1,2,32]{2,1,0:T(2,128)S(1)} %get-tuple-element.20.after_ref), channel_id=1, source_target_pairs={{0,3},{1,2},{2,1},{3,0},{4,7},{5,6},{6,5},{7,4},{8,11},{9,10},{10,... | collective-permute-start | bytes 776 | tf_op jit(solution)/shard_map/ppermute | solution.py:311
  7.5 3.4 %collective-permute-start.3 = (f32[4,2,32]{2,1,0:T(2,128)S(1)}, f32[4,2,32]{2,1,0:T(2,128)S(1)}, u32[]{:S(2)}, u32[]{:S(2)}) collective-permute-start(f32[4,2,32]{2,1,0:T(2,128)S(1)} %get-tuple-element.66.after_ref), channel_id=1, source_target_pairs={{0,4},{4,0},{8,12},{12,8},{16,20},{20,16},{24,28},{28,24},{1,5},{5... | collective-permute-start | bytes 3080 | tf_op jit(solution)/shard_map/ppermute | solution.py:291
  10.0 12.9 %collective-permute-start.10 = (bf16[20,64,128]{2,1,0:T(8,128)(2,1)S(1)}, bf16[20,64,128]{2,1,0:T(8,128)(2,1)S(1)}, u32[]{:S(2)}, u32[]{:S(2)}) collective-permute-start(bf16[20,64,128]{2,1,0:T(8,128)(2,1)S(1)} %get-tuple-element.30.rest_0_), channel_id=1, source_target_pairs={{0,4},{4,0},{8,12},{12,8},{16,20},{20,16},{24,28},{28,24},{1,5},{5... | collective-permute-start | bytes 983048 | tf_op jit(solution)/shard_map/ppermute | solution.py:291
  10.3 15.7 %collective-permute-start.6 = (bf16[20,64,128]{2,1,0:T(8,128)(2,1)S(1)}, bf16[20,64,128]{2,1,0:T(8,128)(2,1)S(1)}, u32[]{:S(2)}, u32[]{:S(2)}) collective-permute-start(bf16[20,64,128]{2,1,0:T(8,128)(2,1)S(1)} %get-tuple-element.27.rest_0_), channel_id=1, source_target_pairs={{0,2},{1,3},{2,0},{3,1},{4,6},{5,7},{6,4},{7,5},{8,10},{9,11},{10,... | collective-permute-start | bytes 983048 | tf_op jit(solution)/shard_map/ppermute | solution.py:291
  11.0 7.7 %copy-start = (f32[6]{0:T(128)S(1)}, f32[6]{0:T(128)}, u32[]{:S(2)}) copy-start(f32[6]{0:T(128)} %param.18) | copy-start | bytes 76
  11.0 5.3 %collective-permute-start.4 = (f32[8,2,32]{2,1,0:T(2,128)S(1)}, f32[8,2,32]{2,1,0:T(2,128)S(1)}, u32[]{:S(2)}, u32[]{:S(2)}) collective-permute-start(f32[8,2,32]{2,1,0:T(2,128)S(1)} %get-tuple-element.47.after_ref), channel_id=1, source_target_pairs={{0,8},{4,12},{8,0},{12,4},{16,24},{20,28},{24,16},{28,20},{1,9},{5... | collective-permute-start | bytes 6152 | tf_op jit(solution)/shard_map/ppermute | solution.py:291
  14.1 8.8 %collective-permute-start.8 = (bf16[12,64,128]{2,1,0:T(8,128)(2,1)S(1)}, bf16[12,64,128]{2,1,0:T(8,128)(2,1)S(1)}, u32[]{:S(2)}, u32[]{:S(2)}) collective-permute-start(bf16[12,64,128]{2,1,0:T(8,128)(2,1)S(1)} %get-tuple-element.29.rest_1_), channel_id=1, source_target_pairs={{0,4},{4,0},{8,12},{12,8},{16,20},{20,16},{24,28},{28,24},{1,5},{5... | collective-permute-start | bytes 589832 | tf_op jit(solution)/shard_map/ppermute | solution.py:291
  15.4 7.5 %collective-permute-start.7 = (bf16[12,64,128]{2,1,0:T(8,128)(2,1)S(1)}, bf16[12,64,128]{2,1,0:T(8,128)(2,1)S(1)}, u32[]{:S(2)}, u32[]{:S(2)}) collective-permute-start(bf16[12,64,128]{2,1,0:T(8,128)(2,1)S(1)} %get-tuple-element.28.rest_1_), channel_id=1, source_target_pairs={{0,2},{1,3},{2,0},{3,1},{4,6},{5,7},{6,4},{7,5},{8,10},{9,11},{10,... | collective-permute-start | bytes 589832 | tf_op jit(solution)/shard_map/ppermute | solution.py:291
  16.4 3.6 %collective-permute-start.5 = (f32[16,2,32]{2,1,0:T(2,128)S(1)}, f32[16,2,32]{2,1,0:T(2,128)S(1)}, u32[]{:S(2)}, u32[]{:S(2)}) collective-permute-start(f32[16,2,32]{2,1,0:T(2,128)S(1)} %get-tuple-element.43), channel_id=1, source_target_pairs={{0,16},{4,20},{8,24},{12,28},{16,0},{20,4},{24,8},{28,12},{1,17},{... | collective-permute-start | bytes 12296 | tf_op jit(solution)/shard_map/ppermute | solution.py:291
  24.2 4.4 %collective-permute-start.11 = (bf16[32,64,128]{2,1,0:T(8,128)(2,1)S(1)}, bf16[32,64,128]{2,1,0:T(8,128)(2,1)S(1)}, u32[]{:S(2)}, u32[]{:S(2)}) collective-permute-start(bf16[32,64,128]{2,1,0:T(8,128)(2,1)S(1)} %bins_for_pair.3), channel_id=1, source_target_pairs={{0,1},{1,0},{2,3},{3,2},{4,5},{5,4},{6,7},{7,6},{8,9},{9,8},{10,11... | collective-permute-start | bytes 1572872 | tf_op jit(solution)/shard_map/ppermute | solution.py:291
  27.3 3.2 %collective-permute-start.9 = (bf16[32,64,128]{2,1,0:T(8,128)(2,1)S(1)}, bf16[32,64,128]{2,1,0:T(8,128)(2,1)S(1)}, u32[]{:S(2)}, u32[]{:S(2)}) collective-permute-start(bf16[32,64,128]{2,1,0:T(8,128)(2,1)S(1)} %bins_for_pair.2), channel_id=1, source_target_pairs={{0,1},{1,0},{2,3},{3,2},{4,5},{5,4},{6,7},{7,6},{8,9},{9,8},{10,11... | collective-permute-start | bytes 1572872 | tf_op jit(solution)/shard_map/ppermute | solution.py:291
  28.6 3.3 %copy-start.1 = (f32[41]{0:T(128)S(1)}, f32[41]{0:T(128)}, u32[]{:S(2)}) copy-start(f32[41]{0:T(128)} %param.19) | copy-start | bytes 496
  28.7 7.5 %collective-permute-start.14 = (bf16[16,64,128]{2,1,0:T(8,128)(2,1)S(1)}, bf16[16,64,128]{2,1,0:T(8,128)(2,1)S(1)}, u32[]{:S(2)}, u32[]{:S(2)}) collective-permute-start(bf16[16,64,128]{2,1,0:T(8,128)(2,1)S(1)} %add_convert_fusion), channel_id=1, source_target_pairs={{0,2},{1,3},{2,0},{3,1},{4,6},{5,7},{6,4},{7,5},{8,10},{9,11},{10,... | collective-permute-start | bytes 786440 | tf_op jit(solution)/shard_map/ppermute | solution.py:291
  30.6 7.2 %collective-permute-start.12 = (bf16[16,64,128]{2,1,0:T(8,128)(2,1)S(1)}, bf16[16,64,128]{2,1,0:T(8,128)(2,1)S(1)}, u32[]{:S(2)}, u32[]{:S(2)}) collective-permute-start(bf16[16,64,128]{2,1,0:T(8,128)(2,1)S(1)} %add_convert_fusion.1), channel_id=1, source_target_pairs={{0,8},{4,12},{8,0},{12,4},{16,24},{20,28},{24,16},{28,20},{1,9},{5... | collective-permute-start | bytes 786440 | tf_op jit(solution)/shard_map/ppermute | solution.py:291
  36.3 3.9 %collective-permute-start.15 = (bf16[8,64,128]{2,1,0:T(8,128)(2,1)S(1)}, bf16[8,64,128]{2,1,0:T(8,128)(2,1)S(1)}, u32[]{:S(2)}, u32[]{:S(2)}) collective-permute-start(bf16[8,64,128]{2,1,0:T(8,128)(2,1)S(1)} %add_convert_fusion.2), channel_id=1, source_target_pairs={{0,8},{4,12},{8,0},{12,4},{16,24},{20,28},{24,16},{28,20},{1,9},{5... | collective-permute-start | bytes 393224 | tf_op jit(solution)/shard_map/ppermute | solution.py:291
  37.9 4.2 %collective-permute-start.13 = (bf16[8,64,128]{2,1,0:T(8,128)(2,1)S(1)}, bf16[8,64,128]{2,1,0:T(8,128)(2,1)S(1)}, u32[]{:S(2)}, u32[]{:S(2)}) collective-permute-start(bf16[8,64,128]{2,1,0:T(8,128)(2,1)S(1)} %add_convert_fusion.3), channel_id=1, source_target_pairs={{0,4},{4,0},{8,12},{12,8},{16,20},{20,16},{24,28},{28,24},{1,5},{5... | collective-permute-start | bytes 393224 | tf_op jit(solution)/shard_map/ppermute | solution.py:291
  42.1 6.2 %collective-permute-start.16 = (bf16[4,128,128]{2,1,0:T(8,128)(2,1)S(1)}, bf16[4,128,128]{2,1,0:T(8,128)(2,1)S(1)}, u32[]{:S(2)}, u32[]{:S(2)}) collective-permute-start(bf16[4,128,128]{2,1,0:T(8,128)(2,1)S(1)} %pad_maximum_fusion), channel_id=1, source_target_pairs={{0,16},{4,20},{8,24},{12,28},{16,0},{20,4},{24,8},{28,12},{1,17},{... | collective-permute-start | bytes 393224 | tf_op jit(solution)/shard_map/ppermute | solution.py:291
  48.4 8.2 %collective-permute-start.17 = (bf16[4,32,128]{2,1,0:T(8,128)(2,1)S(1)}, bf16[4,32,128]{2,1,0:T(8,128)(2,1)S(1)}, u32[]{:S(2)}, u32[]{:S(2)}) collective-permute-start(bf16[4,32,128]{2,1,0:T(8,128)(2,1)S(1)} %get-tuple-element.40), channel_id=1, source_target_pairs={{1,2},{2,1},{5,6},{6,5},{9,10},{10,9},{13,14},{14,13},{17,18},{18,... | collective-permute-start | bytes 98312 | tf_op jit(solution)/shard_map/ppermute | solution.py:394
  55.0 1.9 %collective-permute-start.18 = (bf16[4,32,128]{2,1,0:T(8,128)(2,1)S(1)}, bf16[4,32,128]{2,1,0:T(8,128)(2,1)S(1)}, u32[]{:S(2)}, u32[]{:S(2)}) collective-permute-start(bf16[4,32,128]{2,1,0:T(8,128)(2,1)S(1)} %get-tuple-element.39), channel_id=1, source_target_pairs={{0,1},{1,0},{2,3},{3,2},{4,5},{5,4},{6,7},{7,6},{8,9},{9,8},{10,11... | collective-permute-start | bytes 98312 | tf_op jit(solution)/shard_map/ppermute | solution.py:291

commit v6 on v5

--- a/solution.py
+++ b/solution.py
@@ -126,9 +126,9 @@
     )(after, *loaded, *into)
 
 
-def bin_kernel(stepped, bins_ref, scale_ref, after_ref, *rest):
-    blocks_refs, (out_ref, acc_ref) = rest[:-2], rest[-2:]
-    parts = len(blocks_refs) // 2
+def bin_kernel(stepped, sources, bins_ref, scale_ref, after_ref, *rest):
+    blocks_refs, outs, acc_ref = rest[:sources], rest[sources:-1], rest[-1]
+    parts = sources // 2
     step = acc_ref.shape[0]
     acc_ref[...] = jnp.zeros_like(acc_ref)
     for index, blocks_ref in enumerate(blocks_refs):
@@ -143,34 +143,45 @@
             def _(blocks_ref=blocks_ref, n=n, slot=slot, line=line, place=start + n):
                 acc_ref[slot] += scale_ref[line, place] * blocks_ref[n].astype(jnp.float32)
 
-    out_ref[...] = acc_ref[...].astype(out_ref.dtype)
-
-
-def bin_blocks(bins, scale, blocks, size, name, after):
+    low = 0
+    for out_ref in outs:
+        out_ref[...] = acc_ref[low : low + out_ref.shape[0]].astype(out_ref.dtype)
+        low += out_ref.shape[0]
+
+
+def bin_blocks(bins, scale, blocks, sizes, name, after):
     shape = blocks[0].shape[1:]
-    step = min(size, 64)
-    stepped = step < size
+    size = sum(sizes)
+    stepped = size > 64
+    step = sizes[-1] if stepped else size
+    while step > 64:
+        step //= 2
     moved = 2 * sum(part.size for part in blocks) + 2 * size * shape[0] * shape[1]
+    given = (size,) if stepped else sizes
     if stepped:
         grid = (size // step,)
         block_specs = [pl.BlockSpec(part.shape, lambda g: (0, 0, 0)) for part in blocks]
-        out_spec = pl.BlockSpec((step,) + shape, lambda g: (g, 0, 0))
+        out_specs = [pl.BlockSpec((step,) + shape, lambda g: (g, 0, 0))]
     else:
         grid = ()
         block_specs = [pl.BlockSpec(memory_space=VMEM)] * len(blocks)
-        out_spec = pl.BlockSpec(memory_space=VMEM)
-    return pl.pallas_call(
-        functools.partial(bin_kernel, stepped),
+        out_specs = [pl.BlockSpec(memory_space=VMEM)] * len(given)
+    found = pl.pallas_call(
+        functools.partial(bin_kernel, stepped, len(blocks)),
         grid=grid,
-        out_shape=jax.ShapeDtypeStruct((size,) + shape, jnp.bfloat16),
+        out_shape=[jax.ShapeDtypeStruct((count,) + shape, jnp.bfloat16) for count in given],
         in_specs=[pl.BlockSpec(memory_space=SMEM), pl.BlockSpec(memory_space=SMEM), pl.BlockSpec(memory_space=pl.ANY)]
         + block_specs,
-        out_specs=out_spec,
+        out_specs=out_specs,
         scratch_shapes=[VMEM((step,) + shape, jnp.float32)],
         compiler_params=pltpu.CompilerParams(vmem_limit_bytes=20 << 20),
         cost_estimate=pl.CostEstimate(flops=2 * moved, bytes_accessed=moved, transcendentals=0),
         name=name,
     )(bins, scale, after, *blocks)
+    if stepped:
+        starts = [sum(sizes[:i]) for i in range(len(sizes))]
+        found = [found[0][low : low + count] for low, count in zip(starts, sizes)]
+    return found
 
 
 def filters_kernel(edge, taps_ref, rows_ref, cols_ref):
@@ -349,25 +360,20 @@
             place = place * 2 + (off >> bit & 1)
         place = place * CC + jnp.stack([cell[0], cell[group + 1]]) % CC
         place = jnp.where(off >> order[0] & 1 == 0, place, -1)
-        bins.append(
-            [
-                jnp.where((place >= low) & (place < low + count), place - low, -1)
-                for low, count in ((size, size), (half, half), (0, half))
-            ]
-        )
-    from_pair = [
-        swap(bin_blocks(lines[0], factor, parts, size, "bins_for_pair", others[1 - group][-1]), 0)
-        for group, (lines, factor, parts) in enumerate(zip(bins, scales, blocks))
-    ]
+        leaving = jnp.where(place >= size, place - size, jnp.where(place >= half, place - half + size, -1))
+        bins.append([leaving, jnp.where(place < half, place, -1)])
+    from_pair, sent = [], []
+    for group, (lines, factor, parts) in enumerate(zip(bins, scales, blocks)):
+        for_pair, for_next = bin_blocks(lines[0], factor, parts, (size, half), "bins_sent", others[1 - group][-1])
+        from_pair.append(swap(for_pair, 0))
+        sent.append(for_next)
     edge = up(radius, 16)
     taps = filter_taps.astype(jnp.bfloat16).astype(jnp.float32)[None]
     row_filter, col_filter = filters(taps, block_side, edge)
     groups = []
-    for lines, factor, parts, order, mine in zip(bins, scales, blocks, orders, from_pair):
-        known = factor if mine is from_pair[1] else from_pair[1]
-        sent = bin_blocks(lines[1], factor, parts, half, "bins_for_next", known)
-        back = swap((sent.astype(jnp.float32) + mine[half:].astype(jnp.float32)).astype(jnp.bfloat16), order[1])
-        kept = bin_blocks(lines[2], factor, parts, half, "bins_kept", row_filter)
+    for lines, factor, parts, order, mine, going in zip(bins, scales, blocks, orders, from_pair, sent):
+        back = swap((going.astype(jnp.float32) + mine[half:].astype(jnp.float32)).astype(jnp.bfloat16), order[1])
+        (kept,) = bin_blocks(lines[1], factor, parts, (half,), "bins_kept", row_filter)
         groups.append([kept, mine[:half], back])
     got = [swap(halves(parts, True).astype(jnp.bfloat16), order[2]) for parts, order in zip(groups, orders)]
     groups = [first_halves(parts) + [part] for parts, part in zip(groups, got)]

time: 58.3 us -> 57.3 us (0.983)
  waiting for transfers between devices: 14.2 us -> 16.8 us
  Pallas kernels: 15.5 us -> 13.3 us
  starting transfers between devices: 26.4 us -> 25.1 us
    ppermute x15, waiting for transfers between devices: 11.5 us -> 14.1 us  [swap(): return lax.ppermute(array, axis, [(i, i ^ 1 << bit) for i in range(count)])]
    pallas_call x6 -> x4, Pallas kernels: 7.25 us -> 5.1 us  [bin_blocks(): pl.pallas_call(functools.partial(bin_kernel, stepped, len(blocks)), grid=...]
    ppermute x1, starting transfers between devices: 6.62 us -> 5.88 us  [local(): lax.ppermute(jnp.where(even, top, bottom), 'band', inner + [(i, j) for j,...]
  transfers between devices with their start and end apart: 19 -> 19, of which waited for: 9 -> 12; matrix products, arithmetic and copies ran while one was open for 3% -> 3% of each run, Pallas kernels for 22% -> 18%
where the time goes in v6:
time: 57.3 us; the launch traced here: 57.2 us
  starting transfers between devices  25.1 us (44%)
  waiting for transfers between devices  16.8 us (29%)
  Pallas kernels  13.3 us (23%)
  other arithmetic  1.58 us (3%)
    ppermute x15, starting transfers between devices, swap(): return lax.ppermute(array, axis, [(i, i ^ 1 << bit) for i in range(count)])  16.4 us
    ppermute x15, waiting for transfers between devices, swap(): return lax.ppermute(array, axis, [(i, i ^ 1 << bit) for i in range(count)])  14.1 us
    ppermute x1, starting transfers between devices, local(): lax.ppermute(jnp.where(even, top, bottom), 'band', inner + [(i, j) for j,...  5.88 us
    pallas_call x4, Pallas kernels, bin_blocks(): pl.pallas_call(functools.partial(bin_kernel, stepped, len(blocks)), grid=...  5.1 us
    pallas_call x3, Pallas kernels, match_blocks(): pl.pallas_call(functools.partial(match_kernel, first, count, skip, not in...  4.74 us
    ppermute x3, starting transfers between devices, local(): lax.ppermute(own_facts, 'band', [(i, i ^ off) for i in range(band_count)])  2.87 us
    pallas_call x1, Pallas kernels, load(): pl.pallas_call(load_kernel, out_shape=out_shape, in_specs=[pl.BlockSpec(m...  1.67 us
    ppermute x1, waiting for transfers between devices, local(): lax.ppermute(jnp.where(even, top, bottom), 'band', inner + [(i, j) for j,...  1.5 us
  transfers between devices with their start and end apart: 19, of which 12 were waited for; matrix products, arithmetic and copies ran while one was open for 3% of the time, Pallas kernels for 18%

profile of v6, /device:TPU:1, one launch (start us, length us, event | category | flops | bytes accessed | tf_op | source)
XLA Modules:
  0.0 57.2 jit_solution(13783899761821963243)
XLA Ops:
  0.0 1.7 %load.1 = (f32[1,2,32]{2,1,0:T(2,128)S(1)}, f32[3,32]{1,0:T(4,128)S(1)}, bf16[384,168]{1,0:T(8,128)(2,1)S(1)}, bf16[768,128]{1,0:T(8,128)(2,1)S(1)}, bf16[168,5376]{1,0:T(8,128)(2,1)S(1)}) custom-call(s32[1,32]{1,0:T(1,128)} %bitcast.30, s32[1,32]{1,0:T(1,128)} %bitcast.31, s32[1,32]{1,0:T(1,128)} %bitcast.32, bf16[32]{0:T(256)(128)(2,1)} %refs_3_.1, ...), custom_call_target="tpu_custom_call" | custom-call | flops 1048576 | bytes 4194304 | tf_op jit(solution)/shard_map/load/pallas_call | solution.py:73
  1.7 0.1 collective-permute-start.1
  1.8 2.7 %collective-permute-start = (f32[1,2,32]{2,1,0:T(2,128)S(1)}, f32[1,2,32]{2,1,0:T(2,128)S(1)}, u32[]{:S(2)}, u32[]{:S(2)}) collective-permute-start(f32[1,2,32]{2,1,0:T(2,128)S(1)} %get-tuple-element.24.after_ref), channel_id=1, source_target_pairs={{0,2},{1,3},{2,0},{3,1},{4,6},{5,7},{6,4},{7,5},{8,10},{9,11},{10,... | collective-permute-start | bytes 776 | tf_op jit(solution)/shard_map/ppermute | solution.py:322
  4.5 0.0 collective-permute-start.2
  4.5 1.7 %match_blocks.3 = (bf16[20,64,128]{2,1,0:T(8,128)(2,1)S(1)}, bf16[20,64,128]{2,1,0:T(8,128)(2,1)S(1)}) custom-call(f32[1,2,32]{2,1,0:T(2,128)S(1)} %get-tuple-element.24.after_ref, f32[3,32]{1,0:T(4,128)S(1)} %get-tuple-element.25.coef_ref, bf16[384,168]{1,0:T(8,128)(2,1)S(1)} %get-tuple-element.26.rowk_ref, ...), custom_call_target="tpu_custom_call" | custom-call | flops 1833172992 | bytes 2097152 | tf_op jit(solution)/shard_map/match_blocks/pallas_call | solution.py:117
  6.3 0.0 collective-permute-done.1
  6.3 0.0 collective-permute-done
  6.3 1.2 %collective-permute-done.2 = f32[1,2,32]{2,1,0:T(2,128)S(1)} collective-permute-done((f32[1,2,32]{2,1,0:T(2,128)S(1)}, f32[1,2,32]{2,1,0:T(2,128)S(1)}, u32[]{:S(2)}, u32[]{:S(2)}) %collective-permute-start.2) | collective-permute-done | bytes 288 | tf_op jit(solution)/shard_map/ppermute | solution.py:322
  7.5 1.2 %collective-permute-start.3 = (f32[4,2,32]{2,1,0:T(2,128)S(1)}, f32[4,2,32]{2,1,0:T(2,128)S(1)}, u32[]{:S(2)}, u32[]{:S(2)}) collective-permute-start(f32[4,2,32]{2,1,0:T(2,128)S(1)} %get-tuple-element.70.after_ref), channel_id=1, source_target_pairs={{0,4},{4,0},{8,12},{12,8},{16,20},{20,16},{24,28},{28,24},{1,5},{5... | collective-permute-start | bytes 3080 | tf_op jit(solution)/shard_map/ppermute | solution.py:302
  8.7 1.3 %match_blocks.4 = (bf16[20,64,128]{2,1,0:T(8,128)(2,1)S(1)}, bf16[20,64,128]{2,1,0:T(8,128)(2,1)S(1)}) custom-call(f32[4,2,32]{2,1,0:T(2,128)S(1)} %get-tuple-element.70.after_ref, f32[3,32]{1,0:T(4,128)S(1)} %get-tuple-element.25.coef_ref, bf16[384,168]{1,0:T(8,128)(2,1)S(1)} %get-tuple-element.26.rowk_ref, ...), custom_call_target="tpu_custom_call", output_to_operand_aliasing={{0}: (5, {}), {1}: (6, {})} | custom-call | flops 1222115328 | bytes 2097152 | tf_op jit(solution)/shard_map/match_blocks/pallas_call | solution.py:117
  10.0 0.6 %collective-permute-start.6 = (bf16[20,64,128]{2,1,0:T(8,128)(2,1)S(1)}, bf16[20,64,128]{2,1,0:T(8,128)(2,1)S(1)}, u32[]{:S(2)}, u32[]{:S(2)}) collective-permute-start(bf16[20,64,128]{2,1,0:T(8,128)(2,1)S(1)} %get-tuple-element.31.rest_0_), channel_id=1, source_target_pairs={{0,2},{1,3},{2,0},{3,1},{4,6},{5,7},{6,4},{7,5},{8,10},{9,11},{10,... | collective-permute-start | bytes 983048 | tf_op jit(solution)/shard_map/ppermute | solution.py:302
  10.6 0.3 collective-permute-start.12
  10.9 0.0 collective-permute-done.3
  10.9 0.0 copy-start
  10.9 1.8 %match_blocks.5 = (bf16[12,64,128]{2,1,0:T(8,128)(2,1)S(1)}, bf16[12,64,128]{2,1,0:T(8,128)(2,1)S(1)}) custom-call(f32[8,2,32]{2,1,0:T(2,128)S(1)} %get-tuple-element.55.after_ref, f32[3,32]{1,0:T(4,128)S(1)} %get-tuple-element.25.coef_ref, bf16[384,168]{1,0:T(8,128)(2,1)S(1)} %get-tuple-element.26.rowk_ref, ...), custom_call_target="tpu_custom_call" | custom-call | flops 1833172992 | bytes 2097152 | tf_op jit(solution)/shard_map/match_blocks/pallas_call | solution.py:117
  12.7 1.4 %collective-permute-start.4 = (f32[8,2,32]{2,1,0:T(2,128)S(1)}, f32[8,2,32]{2,1,0:T(2,128)S(1)}, u32[]{:S(2)}, u32[]{:S(2)}) collective-permute-start(f32[8,2,32]{2,1,0:T(2,128)S(1)} %get-tuple-element.55.after_ref), channel_id=1, source_target_pairs={{0,8},{4,12},{8,0},{12,4},{16,24},{20,28},{24,16},{28,20},{1,9},{5... | collective-permute-start | bytes 6152 | tf_op jit(solution)/shard_map/ppermute | solution.py:302
  14.1 1.0 %collective-permute-start.7 = (bf16[12,64,128]{2,1,0:T(8,128)(2,1)S(1)}, bf16[12,64,128]{2,1,0:T(8,128)(2,1)S(1)}, u32[]{:S(2)}, u32[]{:S(2)}) collective-permute-start(bf16[12,64,128]{2,1,0:T(8,128)(2,1)S(1)} %get-tuple-element.32.rest_1_), channel_id=1, source_target_pairs={{0,2},{1,3},{2,0},{3,1},{4,6},{5,7},{6,4},{7,5},{8,10},{9,11},{10,... | collective-permute-start | bytes 589832 | tf_op jit(solution)/shard_map/ppermute | solution.py:302
  15.1 1.2 %collective-permute-start.8 = (bf16[12,64,128]{2,1,0:T(8,128)(2,1)S(1)}, bf16[12,64,128]{2,1,0:T(8,128)(2,1)S(1)}, u32[]{:S(2)}, u32[]{:S(2)}) collective-permute-start(bf16[12,64,128]{2,1,0:T(8,128)(2,1)S(1)} %get-tuple-element.33.rest_1_), channel_id=1, source_target_pairs={{0,4},{4,0},{8,12},{12,8},{16,20},{20,16},{24,28},{28,24},{1,5},{5... | collective-permute-start | bytes 589832 | tf_op jit(solution)/shard_map/ppermute | solution.py:302
  16.3 0.0 collective-permute-done.4
  16.4 2.4 %collective-permute-start.5 = (f32[16,2,32]{2,1,0:T(2,128)S(1)}, f32[16,2,32]{2,1,0:T(2,128)S(1)}, u32[]{:S(2)}, u32[]{:S(2)}) collective-permute-start(f32[16,2,32]{2,1,0:T(2,128)S(1)} %get-tuple-element.51), channel_id=1, source_target_pairs={{0,16},{4,20},{8,24},{12,28},{16,0},{20,4},{24,8},{28,12},{1,17},{... | collective-permute-start | bytes 12296 | tf_op jit(solution)/shard_map/ppermute | solution.py:302
  18.7 0.0 copy-done
  18.7 0.1 select_reduce_fusion.1
  18.8 1.1 %collective-permute-done.5 = f32[16,2,32]{2,1,0:T(2,128)S(1)} collective-permute-done((f32[16,2,32]{2,1,0:T(2,128)S(1)}, f32[16,2,32]{2,1,0:T(2,128)S(1)}, u32[]{:S(2)}, u32[]{:S(2)}) %collective-permute-start.5) | collective-permute-done | bytes 4128 | tf_op jit(solution)/shard_map/ppermute | solution.py:302
  20.0 0.9 %select_reduce_fusion = f32[3,32]{1,0:T(4,128)S(1)} fusion(f32[32,32]{1,0:T(8,128)S(1)} %bitcast.27, f32[32,32]{1,0:T(8,128)S(1)} %bitcast.26, f32[3,32]{1,0:T(4,128)S(1)} %bitcast.28), kind=kLoop, calls=%fused_computation | loop fusion | flops 294816 | bytes 8960 | tf_op jit(solution)/shard_map/reduce_sum | solution.py:343
  20.9 2.0 %collective-permute-done.7.rest_3_.after_ref = bf16[12,64,128]{2,1,0:T(8,128)(2,1)S(1)} collective-permute-done((bf16[12,64,128]{2,1,0:T(8,128)(2,1)S(1)}, bf16[12,64,128]{2,1,0:T(8,128)(2,1)S(1)}, u32[]{:S(2)}, u32[]{:S(2)}) %collective-permute-start.7) | collective-permute-done | bytes 196640 | tf_op jit(solution)/shard_map/ppermute | solution.py:302
  22.9 0.4 collective-permute-done.8.after_ref.rest_3_
  23.3 0.0 collective-permute-done.6.rest_2_
  23.3 1.4 %bins_sent.2 = (bf16[32,64,128]{2,1,0:T(8,128)(2,1)S(1)}, bf16[16,64,128]{2,1,0:T(8,128)(2,1)S(1)}) custom-call(s32[2,32]{1,0:T(2,128)S(1)} %compare_select_fusion.10.bins_ref, f32[2,32]{1,0:T(2,128)S(1)} %stack.24.scale_ref, bf16[12,64,128]{2,1,0:T(8,128)(2,1)S(1)} %collective-permute-done.8.after_ref.rest_3_, ...), custom_call_target="tpu_custom_call" | custom-call | flops 3670016 | bytes 1835008 | tf_op jit(solution)/shard_map/bins_sent/pallas_call | solution.py:169
  24.7 0.0 copy-start.1
  24.7 1.7 %collective-permute-start.9 = (bf16[32,64,128]{2,1,0:T(8,128)(2,1)S(1)}, bf16[32,64,128]{2,1,0:T(8,128)(2,1)S(1)}, u32[]{:S(2)}, u32[]{:S(2)}) collective-permute-start(bf16[32,64,128]{2,1,0:T(8,128)(2,1)S(1)} %get-tuple-element.34), channel_id=1, source_target_pairs={{0,1},{1,0},{2,3},{3,2},{4,5},{5,4},{6,7},{7,6},{8,9},{9,8},{10,11... | collective-permute-start | bytes 1572872 | tf_op jit(solution)/shard_map/ppermute | solution.py:302
  26.4 0.0 collective-permute-done.12.rest_2_
  26.4 1.4 %bins_sent.3 = (bf16[32,64,128]{2,1,0:T(8,128)(2,1)S(1)}, bf16[16,64,128]{2,1,0:T(8,128)(2,1)S(1)}) custom-call(s32[2,32]{1,0:T(2,128)S(1)} %compare_select_fusion.7.bins_ref, f32[2,32]{1,0:T(2,128)S(1)} %pad_maximum_fusion.2.scale_ref, bf16[12,64,128]{2,1,0:T(8,128)(2,1)S(1)} %collective-permute-done.7.rest_3_.after_ref, ...), custom_call_target="tpu_custom_call" | custom-call | flops 3670016 | bytes 1835008 | tf_op jit(solution)/shard_map/bins_sent/pallas_call | solution.py:169
  27.8 0.1 collective-permute-start.13
  27.9 0.1 collective-permute-done.9
  27.9 0.1 add_convert_fusion.1
  28.0 1.4 %collective-permute-start.10 = (bf16[16,64,128]{2,1,0:T(8,128)(2,1)S(1)}, bf16[16,64,128]{2,1,0:T(8,128)(2,1)S(1)}, u32[]{:S(2)}, u32[]{:S(2)}) collective-permute-start(bf16[16,64,128]{2,1,0:T(8,128)(2,1)S(1)} %add_convert_fusion.1), channel_id=1, source_target_pairs={{0,8},{4,12},{8,0},{12,4},{16,24},{20,28},{24,16},{28,20},{1,9},{5... | collective-permute-start | bytes 786440 | tf_op jit(solution)/shard_map/ppermute | solution.py:302
  29.4 0.4 collective-permute-done.13
  29.8 0.1 add_convert_fusion
  29.9 1.0 %collective-permute-start.14 = (bf16[16,64,128]{2,1,0:T(8,128)(2,1)S(1)}, bf16[16,64,128]{2,1,0:T(8,128)(2,1)S(1)}, u32[]{:S(2)}, u32[]{:S(2)}) collective-permute-start(bf16[16,64,128]{2,1,0:T(8,128)(2,1)S(1)} %add_convert_fusion), channel_id=1, source_target_pairs={{0,2},{1,3},{2,0},{3,1},{4,6},{5,7},{6,4},{7,5},{8,10},{9,11},{10,... | collective-permute-start | bytes 786440 | tf_op jit(solution)/shard_map/ppermute | solution.py:302
  30.9 0.0 copy-done.1
  30.9 0.3 filters.1
  31.2 1.2 %bins_kept.2 = bf16[16,64,128]{2,1,0:T(8,128)(2,1)S(1)} custom-call(s32[2,32]{1,0:T(2,128)S(1)} %get-tuple-element.39.bins_ref, f32[2,32]{1,0:T(2,128)S(1)} %stack.24.scale_ref, bf16[128,192]{1,0:T(8,128)(2,1)S(1)} %get-tuple-element.22.after_ref.row_filter_ref, bf16[20,64,128]{2,1,0:T(8,128)(2,1)S(1)} %get-tuple-element.31.rest_0_, ...), custom_call_target="tpu_custom_call" | custom-call | flops 2621440 | bytes 1310720 | tf_op jit(solution)/shard_map/bins_kept/pallas_call | solution.py:169
  32.4 1.2 %bins_kept.3 = bf16[16,64,128]{2,1,0:T(8,128)(2,1)S(1)} custom-call(s32[2,32]{1,0:T(2,128)S(1)} %get-tuple-element.41.bins_ref, f32[2,32]{1,0:T(2,128)S(1)} %pad_maximum_fusion.2.scale_ref, bf16[128,192]{1,0:T(8,128)(2,1)S(1)} %get-tuple-element.22.after_ref.row_filter_ref, bf16[20,64,128]{2,1,0:T(8,128)(2,1)S(1)} %get-tuple-element.36.rest_0_, ...), custom_call_target="tpu_custom_call" | custom-call | flops 2621440 | bytes 1310720 | tf_op jit(solution)/shard_map/bins_kept/pallas_call | solution.py:169
  33.5 2.0 %collective-permute-done.10 = bf16[16,64,128]{2,1,0:T(8,128)(2,1)S(1)} collective-permute-done((bf16[16,64,128]{2,1,0:T(8,128)(2,1)S(1)}, bf16[16,64,128]{2,1,0:T(8,128)(2,1)S(1)}, u32[]{:S(2)}, u32[]{:S(2)}) %collective-permute-start.10) | collective-permute-done | bytes 262176 | tf_op jit(solution)/shard_map/ppermute | solution.py:302
  35.5 0.1 add_convert_fusion.3
  35.6 0.3 collective-permute-start.11
  35.9 1.6 %collective-permute-done.14 = bf16[16,64,128]{2,1,0:T(8,128)(2,1)S(1)} collective-permute-done((bf16[16,64,128]{2,1,0:T(8,128)(2,1)S(1)}, bf16[16,64,128]{2,1,0:T(8,128)(2,1)S(1)}, u32[]{:S(2)}, u32[]{:S(2)}) %collective-permute-start.14) | collective-permute-done | bytes 262176 | tf_op jit(solution)/shard_map/ppermute | solution.py:302
  37.5 0.1 add_convert_fusion.2
  37.6 1.5 %collective-permute-start.15 = (bf16[8,64,128]{2,1,0:T(8,128)(2,1)S(1)}, bf16[8,64,128]{2,1,0:T(8,128)(2,1)S(1)}, u32[]{:S(2)}, u32[]{:S(2)}) collective-permute-start(bf16[8,64,128]{2,1,0:T(8,128)(2,1)S(1)} %add_convert_fusion.2), channel_id=1, source_target_pairs={{0,8},{4,12},{8,0},{12,4},{16,24},{20,28},{24,16},{28,20},{1,9},{5... | collective-permute-start | bytes 393224 | tf_op jit(solution)/shard_map/ppermute | solution.py:302
  39.1 0.4 collective-permute-done.11
  39.5 0.1 add_convert_fusion.5
  39.5 2.0 %collective-permute-done.15 = bf16[8,64,128]{2,1,0:T(8,128)(2,1)S(1)} collective-permute-done((bf16[8,64,128]{2,1,0:T(8,128)(2,1)S(1)}, bf16[8,64,128]{2,1,0:T(8,128)(2,1)S(1)}, u32[]{:S(2)}, u32[]{:S(2)}) %collective-permute-start.15) | collective-permute-done | bytes 131104 | tf_op jit(solution)/shard_map/ppermute | solution.py:302
  41.5 0.1 add_convert_fusion.4
  41.6 2.4 %collective-permute-start.16 = (bf16[4,128,128]{2,1,0:T(8,128)(2,1)S(1)}, bf16[4,128,128]{2,1,0:T(8,128)(2,1)S(1)}, u32[]{:S(2)}, u32[]{:S(2)}) collective-permute-start(bf16[4,128,128]{2,1,0:T(8,128)(2,1)S(1)} %pad_maximum_fusion), channel_id=1, source_target_pairs={{0,16},{4,20},{8,24},{12,28},{16,0},{20,4},{24,8},{28,12},{1,17},{... | collective-permute-start | bytes 393224 | tf_op jit(solution)/shard_map/ppermute | solution.py:302
  44.0 4.2 %collective-permute-done.16 = bf16[4,128,128]{2,1,0:T(8,128)(2,1)S(1)} collective-permute-done((bf16[4,128,128]{2,1,0:T(8,128)(2,1)S(1)}, bf16[4,128,128]{2,1,0:T(8,128)(2,1)S(1)}, u32[]{:S(2)}, u32[]{:S(2)}) %collective-permute-start.16) | collective-permute-done | bytes 131104 | tf_op jit(solution)/shard_map/ppermute | solution.py:302
  48.2 5.9 %collective-permute-start.17 = (bf16[4,32,128]{2,1,0:T(8,128)(2,1)S(1)}, bf16[4,32,128]{2,1,0:T(8,128)(2,1)S(1)}, u32[]{:S(2)}, u32[]{:S(2)}) collective-permute-start(bf16[4,32,128]{2,1,0:T(8,128)(2,1)S(1)} %get-tuple-element.48), channel_id=1, source_target_pairs={{1,2},{2,1},{5,6},{6,5},{9,10},{10,9},{13,14},{14,13},{17,18},{18,... | collective-permute-start | bytes 98312 | tf_op jit(solution)/shard_map/ppermute | solution.py:400
  54.1 0.1 collective-permute-start.18
  54.1 1.5 %collective-permute-done.17.beyond_ref = bf16[4,32,128]{2,1,0:T(8,128)(2,1)S(1)} collective-permute-done((bf16[4,32,128]{2,1,0:T(8,128)(2,1)S(1)}, bf16[4,32,128]{2,1,0:T(8,128)(2,1)S(1)}, u32[]{:S(2)}, u32[]{:S(2)}) %collective-permute-start.17) | collective-permute-done | bytes 32800 | tf_op jit(solution)/shard_map/ppermute | solution.py:400
  55.7 0.3 smooth.1.partial_ref
  55.9 0.0 collective-permute-done.18.paired_ref
  56.0 1.2 %detect.1 = f32[128,512]{1,0:T(8,128)} custom-call(s32[1]{0:T(128)} %bitcast.even_ref, bf16[128,192]{1,0:T(8,128)(2,1)S(1)} %get-tuple-element.22.after_ref.row_filter_ref, bf16[384,128]{1,0:T(8,128)(2,1)S(1)} %get-tuple-element.23.col_filter_ref, f32[4,128,128]{2,1,0:T(8,128)S(1)} %smooth.1.partial_ref, ...), custom_call_target="tpu_custom_call" | custom-call | tf_op jit(solution)/shard_map/detect/pallas_call | solution.py:254
  (26 shorter events, 0.3 us)
Async XLA Ops:
  1.7 4.6 %collective-permute-start.1 = (f32[1,2,32]{2,1,0:T(2,128)S(1)}, f32[1,2,32]{2,1,0:T(2,128)S(1)}, u32[]{:S(2)}, u32[]{:S(2)}) collective-permute-start(f32[1,2,32]{2,1,0:T(2,128)S(1)} %get-tuple-element.24.after_ref), channel_id=1, source_target_pairs={{0,1},{1,0},{2,3},{3,2},{4,5},{5,4},{6,7},{7,6},{8,9},{9,8},{10,11... | collective-permute-start | bytes 776 | tf_op jit(solution)/shard_map/ppermute | solution.py:322
  1.8 4.5 %collective-permute-start = (f32[1,2,32]{2,1,0:T(2,128)S(1)}, f32[1,2,32]{2,1,0:T(2,128)S(1)}, u32[]{:S(2)}, u32[]{:S(2)}) collective-permute-start(f32[1,2,32]{2,1,0:T(2,128)S(1)} %get-tuple-element.24.after_ref), channel_id=1, source_target_pairs={{0,2},{1,3},{2,0},{3,1},{4,6},{5,7},{6,4},{7,5},{8,10},{9,11},{10,... | collective-permute-start | bytes 776 | tf_op jit(solution)/shard_map/ppermute | solution.py:322
  4.5 3.0 %collective-permute-start.2 = (f32[1,2,32]{2,1,0:T(2,128)S(1)}, f32[1,2,32]{2,1,0:T(2,128)S(1)}, u32[]{:S(2)}, u32[]{:S(2)}) collective-permute-start(f32[1,2,32]{2,1,0:T(2,128)S(1)} %get-tuple-element.24.after_ref), channel_id=1, source_target_pairs={{0,3},{1,2},{2,1},{3,0},{4,7},{5,6},{6,5},{7,4},{8,11},{9,10},{10,... | collective-permute-start | bytes 776 | tf_op jit(solution)/shard_map/ppermute | solution.py:322
  7.5 3.4 %collective-permute-start.3 = (f32[4,2,32]{2,1,0:T(2,128)S(1)}, f32[4,2,32]{2,1,0:T(2,128)S(1)}, u32[]{:S(2)}, u32[]{:S(2)}) collective-permute-start(f32[4,2,32]{2,1,0:T(2,128)S(1)} %get-tuple-element.70.after_ref), channel_id=1, source_target_pairs={{0,4},{4,0},{8,12},{12,8},{16,20},{20,16},{24,28},{28,24},{1,5},{5... | collective-permute-start | bytes 3080 | tf_op jit(solution)/shard_map/ppermute | solution.py:302
  10.0 13.3 %collective-permute-start.6 = (bf16[20,64,128]{2,1,0:T(8,128)(2,1)S(1)}, bf16[20,64,128]{2,1,0:T(8,128)(2,1)S(1)}, u32[]{:S(2)}, u32[]{:S(2)}) collective-permute-start(bf16[20,64,128]{2,1,0:T(8,128)(2,1)S(1)} %get-tuple-element.31.rest_0_), channel_id=1, source_target_pairs={{0,2},{1,3},{2,0},{3,1},{4,6},{5,7},{6,4},{7,5},{8,10},{9,11},{10,... | collective-permute-start | bytes 983048 | tf_op jit(solution)/shard_map/ppermute | solution.py:302
  10.6 15.8 %collective-permute-start.12 = (bf16[20,64,128]{2,1,0:T(8,128)(2,1)S(1)}, bf16[20,64,128]{2,1,0:T(8,128)(2,1)S(1)}, u32[]{:S(2)}, u32[]{:S(2)}) collective-permute-start(bf16[20,64,128]{2,1,0:T(8,128)(2,1)S(1)} %get-tuple-element.36.rest_0_), channel_id=1, source_target_pairs={{0,4},{4,0},{8,12},{12,8},{16,20},{20,16},{24,28},{28,24},{1,5},{5... | collective-permute-start | bytes 983048 | tf_op jit(solution)/shard_map/ppermute | solution.py:302
  10.9 7.9 %copy-start = (f32[6]{0:T(128)S(1)}, f32[6]{0:T(128)}, u32[]{:S(2)}) copy-start(f32[6]{0:T(128)} %param.18) | copy-start | bytes 76
  12.7 3.7 %collective-permute-start.4 = (f32[8,2,32]{2,1,0:T(2,128)S(1)}, f32[8,2,32]{2,1,0:T(2,128)S(1)}, u32[]{:S(2)}, u32[]{:S(2)}) collective-permute-start(f32[8,2,32]{2,1,0:T(2,128)S(1)} %get-tuple-element.55.after_ref), channel_id=1, source_target_pairs={{0,8},{4,12},{8,0},{12,4},{16,24},{20,28},{24,16},{28,20},{1,9},{5... | collective-permute-start | bytes 6152 | tf_op jit(solution)/shard_map/ppermute | solution.py:302
  14.1 8.8 %collective-permute-start.7 = (bf16[12,64,128]{2,1,0:T(8,128)(2,1)S(1)}, bf16[12,64,128]{2,1,0:T(8,128)(2,1)S(1)}, u32[]{:S(2)}, u32[]{:S(2)}) collective-permute-start(bf16[12,64,128]{2,1,0:T(8,128)(2,1)S(1)} %get-tuple-element.32.rest_1_), channel_id=1, source_target_pairs={{0,2},{1,3},{2,0},{3,1},{4,6},{5,7},{6,4},{7,5},{8,10},{9,11},{10,... | collective-permute-start | bytes 589832 | tf_op jit(solution)/shard_map/ppermute | solution.py:302
  15.1 8.2 %collective-permute-start.8 = (bf16[12,64,128]{2,1,0:T(8,128)(2,1)S(1)}, bf16[12,64,128]{2,1,0:T(8,128)(2,1)S(1)}, u32[]{:S(2)}, u32[]{:S(2)}) collective-permute-start(bf16[12,64,128]{2,1,0:T(8,128)(2,1)S(1)} %get-tuple-element.33.rest_1_), channel_id=1, source_target_pairs={{0,4},{4,0},{8,12},{12,8},{16,20},{20,16},{24,28},{28,24},{1,5},{5... | collective-permute-start | bytes 589832 | tf_op jit(solution)/shard_map/ppermute | solution.py:302
  16.4 3.6 %collective-permute-start.5 = (f32[16,2,32]{2,1,0:T(2,128)S(1)}, f32[16,2,32]{2,1,0:T(2,128)S(1)}, u32[]{:S(2)}, u32[]{:S(2)}) collective-permute-start(f32[16,2,32]{2,1,0:T(2,128)S(1)} %get-tuple-element.51), channel_id=1, source_target_pairs={{0,16},{4,20},{8,24},{12,28},{16,0},{20,4},{24,8},{28,12},{1,17},{... | collective-permute-start | bytes 12296 | tf_op jit(solution)/shard_map/ppermute | solution.py:302
  24.7 6.1 %copy-start.1 = (f32[41]{0:T(128)S(1)}, f32[41]{0:T(128)}, u32[]{:S(2)}) copy-start(f32[41]{0:T(128)} %param.19) | copy-start | bytes 496
  24.7 3.2 %collective-permute-start.9 = (bf16[32,64,128]{2,1,0:T(8,128)(2,1)S(1)}, bf16[32,64,128]{2,1,0:T(8,128)(2,1)S(1)}, u32[]{:S(2)}, u32[]{:S(2)}) collective-permute-start(bf16[32,64,128]{2,1,0:T(8,128)(2,1)S(1)} %get-tuple-element.34), channel_id=1, source_target_pairs={{0,1},{1,0},{2,3},{3,2},{4,5},{5,4},{6,7},{7,6},{8,9},{9,8},{10,11... | collective-permute-start | bytes 1572872 | tf_op jit(solution)/shard_map/ppermute | solution.py:302
  27.8 2.0 %collective-permute-start.13 = (bf16[32,64,128]{2,1,0:T(8,128)(2,1)S(1)}, bf16[32,64,128]{2,1,0:T(8,128)(2,1)S(1)}, u32[]{:S(2)}, u32[]{:S(2)}) collective-permute-start(bf16[32,64,128]{2,1,0:T(8,128)(2,1)S(1)} %get-tuple-element.37), channel_id=1, source_target_pairs={{0,1},{1,0},{2,3},{3,2},{4,5},{5,4},{6,7},{7,6},{8,9},{9,8},{10,11... | collective-permute-start | bytes 1572872 | tf_op jit(solution)/shard_map/ppermute | solution.py:302
  28.0 7.5 %collective-permute-start.10 = (bf16[16,64,128]{2,1,0:T(8,128)(2,1)S(1)}, bf16[16,64,128]{2,1,0:T(8,128)(2,1)S(1)}, u32[]{:S(2)}, u32[]{:S(2)}) collective-permute-start(bf16[16,64,128]{2,1,0:T(8,128)(2,1)S(1)} %add_convert_fusion.1), channel_id=1, source_target_pairs={{0,8},{4,12},{8,0},{12,4},{16,24},{20,28},{24,16},{28,20},{1,9},{5... | collective-permute-start | bytes 786440 | tf_op jit(solution)/shard_map/ppermute | solution.py:302
  29.9 7.6 %collective-permute-start.14 = (bf16[16,64,128]{2,1,0:T(8,128)(2,1)S(1)}, bf16[16,64,128]{2,1,0:T(8,128)(2,1)S(1)}, u32[]{:S(2)}, u32[]{:S(2)}) collective-permute-start(bf16[16,64,128]{2,1,0:T(8,128)(2,1)S(1)} %add_convert_fusion), channel_id=1, source_target_pairs={{0,2},{1,3},{2,0},{3,1},{4,6},{5,7},{6,4},{7,5},{8,10},{9,11},{10,... | collective-permute-start | bytes 786440 | tf_op jit(solution)/shard_map/ppermute | solution.py:302
  35.6 3.9 %collective-permute-start.11 = (bf16[8,64,128]{2,1,0:T(8,128)(2,1)S(1)}, bf16[8,64,128]{2,1,0:T(8,128)(2,1)S(1)}, u32[]{:S(2)}, u32[]{:S(2)}) collective-permute-start(bf16[8,64,128]{2,1,0:T(8,128)(2,1)S(1)} %add_convert_fusion.3), channel_id=1, source_target_pairs={{0,4},{4,0},{8,12},{12,8},{16,20},{20,16},{24,28},{28,24},{1,5},{5... | collective-permute-start | bytes 393224 | tf_op jit(solution)/shard_map/ppermute | solution.py:302
  37.6 3.9 %collective-permute-start.15 = (bf16[8,64,128]{2,1,0:T(8,128)(2,1)S(1)}, bf16[8,64,128]{2,1,0:T(8,128)(2,1)S(1)}, u32[]{:S(2)}, u32[]{:S(2)}) collective-permute-start(bf16[8,64,128]{2,1,0:T(8,128)(2,1)S(1)} %add_convert_fusion.2), channel_id=1, source_target_pairs={{0,8},{4,12},{8,0},{12,4},{16,24},{20,28},{24,16},{28,20},{1,9},{5... | collective-permute-start | bytes 393224 | tf_op jit(solution)/shard_map/ppermute | solution.py:302
  41.6 6.5 %collective-permute-start.16 = (bf16[4,128,128]{2,1,0:T(8,128)(2,1)S(1)}, bf16[4,128,128]{2,1,0:T(8,128)(2,1)S(1)}, u32[]{:S(2)}, u32[]{:S(2)}) collective-permute-start(bf16[4,128,128]{2,1,0:T(8,128)(2,1)S(1)} %pad_maximum_fusion), channel_id=1, source_target_pairs={{0,16},{4,20},{8,24},{12,28},{16,0},{20,4},{24,8},{28,12},{1,17},{... | collective-permute-start | bytes 393224 | tf_op jit(solution)/shard_map/ppermute | solution.py:302
  48.2 7.5 %collective-permute-start.17 = (bf16[4,32,128]{2,1,0:T(8,128)(2,1)S(1)}, bf16[4,32,128]{2,1,0:T(8,128)(2,1)S(1)}, u32[]{:S(2)}, u32[]{:S(2)}) collective-permute-start(bf16[4,32,128]{2,1,0:T(8,128)(2,1)S(1)} %get-tuple-element.48), channel_id=1, source_target_pairs={{1,2},{2,1},{5,6},{6,5},{9,10},{10,9},{13,14},{14,13},{17,18},{18,... | collective-permute-start | bytes 98312 | tf_op jit(solution)/shard_map/ppermute | solution.py:400
  54.1 1.9 %collective-permute-start.18 = (bf16[4,32,128]{2,1,0:T(8,128)(2,1)S(1)}, bf16[4,32,128]{2,1,0:T(8,128)(2,1)S(1)}, u32[]{:S(2)}, u32[]{:S(2)}) collective-permute-start(bf16[4,32,128]{2,1,0:T(8,128)(2,1)S(1)} %get-tuple-element.47), channel_id=1, source_target_pairs={{0,1},{1,0},{2,3},{3,2},{4,5},{5,4},{6,7},{7,6},{8,9},{9,8},{10,11... | collective-permute-start | bytes 98312 | tf_op jit(solution)/shard_map/ppermute | solution.py:302

commit v7 on v6

--- a/solution.py
+++ b/solution.py
@@ -321,7 +321,7 @@
         [own_facts]
         + [lax.ppermute(own_facts, "band", [(i, i ^ off) for i in range(band_count)]) for off in range(1, band_count)]
     )
-    cut, early = block_count * 5 // 8, block_count * 3 // 8
+    cut, early = block_count // 2, block_count * 5 // 16
     own, others = [[], []], [[], []]
     begun = match_blocks(0, early, cut, loaded, heights, block_side, own_facts)
     for part in range(max(2, sky_bits)):

time: 57.3 us -> 56.9 us (level)
  starting transfers between devices: 25.1 us -> 22.3 us
  waiting for transfers between devices: 16.8 us -> 19.1 us
    ppermute x15, waiting for transfers between devices: 14.1 us -> 16.8 us  [swap(): return lax.ppermute(array, axis, [(i, i ^ 1 << bit) for i in range(count)])]
    ppermute x1, starting transfers between devices: 5.88 us -> 3.52 us  [local(): lax.ppermute(jnp.where(even, top, bottom), 'band', inner + [(i, j) for j,...]
  transfers between devices with their start and end apart: 19 -> 19, of which waited for: 12 -> 10; matrix products, arithmetic and copies ran while one was open for 3% -> 3% of each run, Pallas kernels for 18% -> 18%
where the time goes in v7:
time: 56.9 us; the launch traced here: 56.7 us
  starting transfers between devices  22.3 us (39%)
  waiting for transfers between devices  19.1 us (34%)
  Pallas kernels  13.3 us (23%)
  other arithmetic  1.57 us (3%)
    ppermute x15, waiting for transfers between devices, swap(): return lax.ppermute(array, axis, [(i, i ^ 1 << bit) for i in range(count)])  16.8 us
    ppermute x15, starting transfers between devices, swap(): return lax.ppermute(array, axis, [(i, i ^ 1 << bit) for i in range(count)])  15.9 us
    pallas_call x4, Pallas kernels, bin_blocks(): pl.pallas_call(functools.partial(bin_kernel, stepped, len(blocks)), grid=...  5.08 us
    pallas_call x3, Pallas kernels, match_blocks(): pl.pallas_call(functools.partial(match_kernel, first, count, skip, not in...  4.71 us
    ppermute x1, starting transfers between devices, local(): lax.ppermute(jnp.where(even, top, bottom), 'band', inner + [(i, j) for j,...  3.52 us
    ppermute x3, starting transfers between devices, local(): lax.ppermute(own_facts, 'band', [(i, i ^ off) for i in range(band_count)])  2.9 us
    pallas_call x1, Pallas kernels, load(): pl.pallas_call(load_kernel, out_shape=out_shape, in_specs=[pl.BlockSpec(m...  1.67 us
    ppermute x1, waiting for transfers between devices, local(): lax.ppermute(jnp.where(even, top, bottom), 'band', inner + [(i, j) for j,...  1.63 us
  transfers between devices with their start and end apart: 19, of which 10 were waited for; matrix products, arithmetic and copies ran while one was open for 3% of the time, Pallas kernels for 18%

profile of v7, /device:TPU:1, one launch (start us, length us, event | category | flops | bytes accessed | tf_op | source)
XLA Modules:
  0.0 56.7 jit_solution(16430068900034984483)
XLA Ops:
  0.0 1.7 %load.1 = (f32[1,2,32]{2,1,0:T(2,128)S(1)}, f32[3,32]{1,0:T(4,128)S(1)}, bf16[384,168]{1,0:T(8,128)(2,1)S(1)}, bf16[768,128]{1,0:T(8,128)(2,1)S(1)}, bf16[168,5376]{1,0:T(8,128)(2,1)S(1)}) custom-call(s32[1,32]{1,0:T(1,128)} %bitcast.30, s32[1,32]{1,0:T(1,128)} %bitcast.31, s32[1,32]{1,0:T(1,128)} %bitcast.32, bf16[32]{0:T(256)(128)(2,1)} %refs_3_.1, ...), custom_call_target="tpu_custom_call" | custom-call | flops 1048576 | bytes 4194304 | tf_op jit(solution)/shard_map/load/pallas_call | solution.py:73
  1.7 2.7 %collective-permute-start.2 = (f32[1,2,32]{2,1,0:T(2,128)S(1)}, f32[1,2,32]{2,1,0:T(2,128)S(1)}, u32[]{:S(2)}, u32[]{:S(2)}) collective-permute-start(f32[1,2,32]{2,1,0:T(2,128)S(1)} %get-tuple-element.24.after_ref), channel_id=1, source_target_pairs={{0,3},{1,2},{2,1},{3,0},{4,7},{5,6},{6,5},{7,4},{8,11},{9,10},{10,... | collective-permute-start | bytes 776 | tf_op jit(solution)/shard_map/ppermute | solution.py:322
  4.4 0.0 collective-permute-start.1
  4.4 0.2 collective-permute-start
  4.6 1.5 %match_blocks.3 = (bf16[16,64,128]{2,1,0:T(8,128)(2,1)S(1)}, bf16[16,64,128]{2,1,0:T(8,128)(2,1)S(1)}) custom-call(f32[1,2,32]{2,1,0:T(2,128)S(1)} %get-tuple-element.24.after_ref, f32[3,32]{1,0:T(4,128)S(1)} %get-tuple-element.25.coef_ref, bf16[384,168]{1,0:T(8,128)(2,1)S(1)} %get-tuple-element.26.rowk_ref, ...), custom_call_target="tpu_custom_call" | custom-call | flops 1527644160 | bytes 2097152 | tf_op jit(solution)/shard_map/match_blocks/pallas_call | solution.py:117
  6.1 0.0 collective-permute-done.1
  6.1 0.7 %collective-permute-done = f32[1,2,32]{2,1,0:T(2,128)S(1)} collective-permute-done((f32[1,2,32]{2,1,0:T(2,128)S(1)}, f32[1,2,32]{2,1,0:T(2,128)S(1)}, u32[]{:S(2)}, u32[]{:S(2)}) %collective-permute-start) | collective-permute-done | bytes 288 | tf_op jit(solution)/shard_map/ppermute | solution.py:322
  6.8 0.0 collective-permute-done.2
  6.8 1.3 %collective-permute-start.3 = (f32[4,2,32]{2,1,0:T(2,128)S(1)}, f32[4,2,32]{2,1,0:T(2,128)S(1)}, u32[]{:S(2)}, u32[]{:S(2)}) collective-permute-start(f32[4,2,32]{2,1,0:T(2,128)S(1)} %get-tuple-element.70.after_ref), channel_id=1, source_target_pairs={{0,4},{4,0},{8,12},{12,8},{16,20},{20,16},{24,28},{28,24},{1,5},{5... | collective-permute-start | bytes 3080 | tf_op jit(solution)/shard_map/ppermute | solution.py:302
  8.1 1.1 %match_blocks.4 = (bf16[16,64,128]{2,1,0:T(8,128)(2,1)S(1)}, bf16[16,64,128]{2,1,0:T(8,128)(2,1)S(1)}) custom-call(f32[4,2,32]{2,1,0:T(2,128)S(1)} %get-tuple-element.70.after_ref, f32[3,32]{1,0:T(4,128)S(1)} %get-tuple-element.25.coef_ref, bf16[384,168]{1,0:T(8,128)(2,1)S(1)} %get-tuple-element.26.rowk_ref, ...), custom_call_target="tpu_custom_call", output_to_operand_aliasing={{0}: (5, {}), {1}: (6, {})} | custom-call | flops 916586496 | bytes 2097152 | tf_op jit(solution)/shard_map/match_blocks/pallas_call | solution.py:117
  9.2 0.6 %collective-permute-start.6 = (bf16[16,64,128]{2,1,0:T(8,128)(2,1)S(1)}, bf16[16,64,128]{2,1,0:T(8,128)(2,1)S(1)}, u32[]{:S(2)}, u32[]{:S(2)}) collective-permute-start(bf16[16,64,128]{2,1,0:T(8,128)(2,1)S(1)} %get-tuple-element.31.rest_0_), channel_id=1, source_target_pairs={{0,2},{1,3},{2,0},{3,1},{4,6},{5,7},{6,4},{7,5},{8,10},{9,11},{10,... | collective-permute-start | bytes 786440 | tf_op jit(solution)/shard_map/ppermute | solution.py:302
  9.8 0.3 collective-permute-start.12
  10.1 0.0 collective-permute-done.3
  10.1 0.0 copy-start
  10.1 1.4 %collective-permute-start.4 = (f32[8,2,32]{2,1,0:T(2,128)S(1)}, f32[8,2,32]{2,1,0:T(2,128)S(1)}, u32[]{:S(2)}, u32[]{:S(2)}) collective-permute-start(f32[8,2,32]{2,1,0:T(2,128)S(1)} %get-tuple-element.55.after_ref), channel_id=1, source_target_pairs={{0,8},{4,12},{8,0},{12,4},{16,24},{20,28},{24,16},{28,20},{1,9},{5... | collective-permute-start | bytes 6152 | tf_op jit(solution)/shard_map/ppermute | solution.py:302
  11.5 2.2 %match_blocks.5 = (bf16[16,64,128]{2,1,0:T(8,128)(2,1)S(1)}, bf16[16,64,128]{2,1,0:T(8,128)(2,1)S(1)}) custom-call(f32[8,2,32]{2,1,0:T(2,128)S(1)} %get-tuple-element.55.after_ref, f32[3,32]{1,0:T(4,128)S(1)} %get-tuple-element.25.coef_ref, bf16[384,168]{1,0:T(8,128)(2,1)S(1)} %get-tuple-element.26.rowk_ref, ...), custom_call_target="tpu_custom_call" | custom-call | flops 2444230656 | bytes 2097152 | tf_op jit(solution)/shard_map/match_blocks/pallas_call | solution.py:117
  13.8 0.9 %collective-permute-start.7 = (bf16[16,64,128]{2,1,0:T(8,128)(2,1)S(1)}, bf16[16,64,128]{2,1,0:T(8,128)(2,1)S(1)}, u32[]{:S(2)}, u32[]{:S(2)}) collective-permute-start(bf16[16,64,128]{2,1,0:T(8,128)(2,1)S(1)} %get-tuple-element.32.rest_1_), channel_id=1, source_target_pairs={{0,2},{1,3},{2,0},{3,1},{4,6},{5,7},{6,4},{7,5},{8,10},{9,11},{10,... | collective-permute-start | bytes 786440 | tf_op jit(solution)/shard_map/ppermute | solution.py:302
  14.7 1.2 %collective-permute-start.8 = (bf16[16,64,128]{2,1,0:T(8,128)(2,1)S(1)}, bf16[16,64,128]{2,1,0:T(8,128)(2,1)S(1)}, u32[]{:S(2)}, u32[]{:S(2)}) collective-permute-start(bf16[16,64,128]{2,1,0:T(8,128)(2,1)S(1)} %get-tuple-element.33.rest_1_), channel_id=1, source_target_pairs={{0,4},{4,0},{8,12},{12,8},{16,20},{20,16},{24,28},{28,24},{1,5},{5... | collective-permute-start | bytes 786440 | tf_op jit(solution)/shard_map/ppermute | solution.py:302
  15.9 0.0 collective-permute-done.4
  15.9 2.4 %collective-permute-start.5 = (f32[16,2,32]{2,1,0:T(2,128)S(1)}, f32[16,2,32]{2,1,0:T(2,128)S(1)}, u32[]{:S(2)}, u32[]{:S(2)}) collective-permute-start(f32[16,2,32]{2,1,0:T(2,128)S(1)} %get-tuple-element.51), channel_id=1, source_target_pairs={{0,16},{4,20},{8,24},{12,28},{16,0},{20,4},{24,8},{28,12},{1,17},{... | collective-permute-start | bytes 12296 | tf_op jit(solution)/shard_map/ppermute | solution.py:302
  18.3 0.0 copy-done
  18.3 0.1 select_reduce_fusion.1
  18.4 1.1 %collective-permute-done.5 = f32[16,2,32]{2,1,0:T(2,128)S(1)} collective-permute-done((f32[16,2,32]{2,1,0:T(2,128)S(1)}, f32[16,2,32]{2,1,0:T(2,128)S(1)}, u32[]{:S(2)}, u32[]{:S(2)}) %collective-permute-start.5) | collective-permute-done | bytes 4128 | tf_op jit(solution)/shard_map/ppermute | solution.py:302
  19.6 0.9 %select_reduce_fusion = f32[3,32]{1,0:T(4,128)S(1)} fusion(f32[32,32]{1,0:T(8,128)S(1)} %bitcast.27, f32[32,32]{1,0:T(8,128)S(1)} %bitcast.26, f32[3,32]{1,0:T(4,128)S(1)} %bitcast.28), kind=kLoop, calls=%fused_computation | loop fusion | flops 294816 | bytes 8960 | tf_op jit(solution)/shard_map/reduce_sum | solution.py:343
  20.6 0.0 collective-permute-done.12.rest_2_
  20.6 0.7 %collective-permute-done.7.rest_3_.after_ref = bf16[16,64,128]{2,1,0:T(8,128)(2,1)S(1)} collective-permute-done((bf16[16,64,128]{2,1,0:T(8,128)(2,1)S(1)}, bf16[16,64,128]{2,1,0:T(8,128)(2,1)S(1)}, u32[]{:S(2)}, u32[]{:S(2)}) %collective-permute-start.7) | collective-permute-done | bytes 262176 | tf_op jit(solution)/shard_map/ppermute | solution.py:302
  21.3 0.0 collective-permute-done.8.after_ref.rest_3_
  21.3 1.4 %bins_sent.3 = (bf16[32,64,128]{2,1,0:T(8,128)(2,1)S(1)}, bf16[16,64,128]{2,1,0:T(8,128)(2,1)S(1)}) custom-call(s32[2,32]{1,0:T(2,128)S(1)} %compare_select_fusion.7.bins_ref, f32[2,32]{1,0:T(2,128)S(1)} %pad_maximum_fusion.2.scale_ref, bf16[16,64,128]{2,1,0:T(8,128)(2,1)S(1)} %collective-permute-done.7.rest_3_.after_ref, ...), custom_call_target="tpu_custom_call" | custom-call | flops 3670016 | bytes 1835008 | tf_op jit(solution)/shard_map/bins_sent/pallas_call | solution.py:169
  22.6 0.0 copy-start.1
  22.7 3.9 %collective-permute-start.13 = (bf16[32,64,128]{2,1,0:T(8,128)(2,1)S(1)}, bf16[32,64,128]{2,1,0:T(8,128)(2,1)S(1)}, u32[]{:S(2)}, u32[]{:S(2)}) collective-permute-start(bf16[32,64,128]{2,1,0:T(8,128)(2,1)S(1)} %get-tuple-element.37), channel_id=1, source_target_pairs={{0,1},{1,0},{2,3},{3,2},{4,5},{5,4},{6,7},{7,6},{8,9},{9,8},{10,11... | collective-permute-start | bytes 1572872 | tf_op jit(solution)/shard_map/ppermute | solution.py:302
  26.6 0.0 collective-permute-done.6.rest_2_
  26.6 1.4 %bins_sent.2 = (bf16[32,64,128]{2,1,0:T(8,128)(2,1)S(1)}, bf16[16,64,128]{2,1,0:T(8,128)(2,1)S(1)}) custom-call(s32[2,32]{1,0:T(2,128)S(1)} %compare_select_fusion.10.bins_ref, f32[2,32]{1,0:T(2,128)S(1)} %stack.24.scale_ref, bf16[16,64,128]{2,1,0:T(8,128)(2,1)S(1)} %collective-permute-done.8.after_ref.rest_3_, ...), custom_call_target="tpu_custom_call" | custom-call | flops 3670016 | bytes 1835008 | tf_op jit(solution)/shard_map/bins_sent/pallas_call | solution.py:169
  27.9 0.1 collective-permute-start.9
  28.0 0.0 collective-permute-done.13
  28.1 0.1 add_convert_fusion
  28.1 0.3 collective-permute-start.14
  28.4 1.5 %collective-permute-done.9 = bf16[32,64,128]{2,1,0:T(8,128)(2,1)S(1)} collective-permute-done((bf16[32,64,128]{2,1,0:T(8,128)(2,1)S(1)}, bf16[32,64,128]{2,1,0:T(8,128)(2,1)S(1)}, u32[]{:S(2)}, u32[]{:S(2)}) %collective-permute-start.9) | collective-permute-done | bytes 524320 | tf_op jit(solution)/shard_map/ppermute | solution.py:302
  29.9 0.1 add_convert_fusion.1
  30.0 0.4 collective-permute-start.10
  30.4 0.0 copy-done.1
  30.4 0.3 filters.1
  30.8 1.2 %bins_kept.2 = bf16[16,64,128]{2,1,0:T(8,128)(2,1)S(1)} custom-call(s32[2,32]{1,0:T(2,128)S(1)} %get-tuple-element.39.bins_ref, f32[2,32]{1,0:T(2,128)S(1)} %stack.24.scale_ref, bf16[128,192]{1,0:T(8,128)(2,1)S(1)} %get-tuple-element.22.after_ref.row_filter_ref, bf16[16,64,128]{2,1,0:T(8,128)(2,1)S(1)} %get-tuple-element.31.rest_0_, ...), custom_call_target="tpu_custom_call" | custom-call | flops 2621440 | bytes 1310720 | tf_op jit(solution)/shard_map/bins_kept/pallas_call | solution.py:169
  32.0 1.2 %bins_kept.3 = bf16[16,64,128]{2,1,0:T(8,128)(2,1)S(1)} custom-call(s32[2,32]{1,0:T(2,128)S(1)} %get-tuple-element.41.bins_ref, f32[2,32]{1,0:T(2,128)S(1)} %pad_maximum_fusion.2.scale_ref, bf16[128,192]{1,0:T(8,128)(2,1)S(1)} %get-tuple-element.22.after_ref.row_filter_ref, bf16[16,64,128]{2,1,0:T(8,128)(2,1)S(1)} %get-tuple-element.36.rest_0_, ...), custom_call_target="tpu_custom_call" | custom-call | flops 2621440 | bytes 1310720 | tf_op jit(solution)/shard_map/bins_kept/pallas_call | solution.py:169
  33.1 2.5 %collective-permute-done.14 = bf16[16,64,128]{2,1,0:T(8,128)(2,1)S(1)} collective-permute-done((bf16[16,64,128]{2,1,0:T(8,128)(2,1)S(1)}, bf16[16,64,128]{2,1,0:T(8,128)(2,1)S(1)}, u32[]{:S(2)}, u32[]{:S(2)}) %collective-permute-start.14) | collective-permute-done | bytes 262176 | tf_op jit(solution)/shard_map/ppermute | solution.py:302
  35.6 0.1 add_convert_fusion.2
  35.7 0.5 collective-permute-start.15
  36.2 1.7 %collective-permute-done.10 = bf16[16,64,128]{2,1,0:T(8,128)(2,1)S(1)} collective-permute-done((bf16[16,64,128]{2,1,0:T(8,128)(2,1)S(1)}, bf16[16,64,128]{2,1,0:T(8,128)(2,1)S(1)}, u32[]{:S(2)}, u32[]{:S(2)}) %collective-permute-start.10) | collective-permute-done | bytes 262176 | tf_op jit(solution)/shard_map/ppermute | solution.py:302
  37.8 0.1 add_convert_fusion.3
  37.9 0.3 collective-permute-start.11
  38.2 1.4 %collective-permute-done.15 = bf16[8,64,128]{2,1,0:T(8,128)(2,1)S(1)} collective-permute-done((bf16[8,64,128]{2,1,0:T(8,128)(2,1)S(1)}, bf16[8,64,128]{2,1,0:T(8,128)(2,1)S(1)}, u32[]{:S(2)}, u32[]{:S(2)}) %collective-permute-start.15) | collective-permute-done | bytes 131104 | tf_op jit(solution)/shard_map/ppermute | solution.py:302
  39.6 0.1 add_convert_fusion.4
  39.7 2.1 %collective-permute-done.11 = bf16[8,64,128]{2,1,0:T(8,128)(2,1)S(1)} collective-permute-done((bf16[8,64,128]{2,1,0:T(8,128)(2,1)S(1)}, bf16[8,64,128]{2,1,0:T(8,128)(2,1)S(1)}, u32[]{:S(2)}, u32[]{:S(2)}) %collective-permute-start.11) | collective-permute-done | bytes 131104 | tf_op jit(solution)/shard_map/ppermute | solution.py:302
  41.8 0.1 add_convert_fusion.5
  41.9 2.3 %collective-permute-start.16 = (bf16[4,128,128]{2,1,0:T(8,128)(2,1)S(1)}, bf16[4,128,128]{2,1,0:T(8,128)(2,1)S(1)}, u32[]{:S(2)}, u32[]{:S(2)}) collective-permute-start(bf16[4,128,128]{2,1,0:T(8,128)(2,1)S(1)} %pad_maximum_fusion), channel_id=1, source_target_pairs={{0,16},{4,20},{8,24},{12,28},{16,0},{20,4},{24,8},{28,12},{1,17},{... | collective-permute-start | bytes 393224 | tf_op jit(solution)/shard_map/ppermute | solution.py:302
  44.2 5.8 %collective-permute-done.16 = bf16[4,128,128]{2,1,0:T(8,128)(2,1)S(1)} collective-permute-done((bf16[4,128,128]{2,1,0:T(8,128)(2,1)S(1)}, bf16[4,128,128]{2,1,0:T(8,128)(2,1)S(1)}, u32[]{:S(2)}, u32[]{:S(2)}) %collective-permute-start.16) | collective-permute-done | bytes 131104 | tf_op jit(solution)/shard_map/ppermute | solution.py:302
  50.0 3.5 %collective-permute-start.17 = (bf16[4,32,128]{2,1,0:T(8,128)(2,1)S(1)}, bf16[4,32,128]{2,1,0:T(8,128)(2,1)S(1)}, u32[]{:S(2)}, u32[]{:S(2)}) collective-permute-start(bf16[4,32,128]{2,1,0:T(8,128)(2,1)S(1)} %get-tuple-element.48), channel_id=1, source_target_pairs={{1,2},{2,1},{5,6},{6,5},{9,10},{10,9},{13,14},{14,13},{17,18},{18,... | collective-permute-start | bytes 98312 | tf_op jit(solution)/shard_map/ppermute | solution.py:400
  53.5 0.1 collective-permute-start.18
  53.6 1.6 %collective-permute-done.17.beyond_ref = bf16[4,32,128]{2,1,0:T(8,128)(2,1)S(1)} collective-permute-done((bf16[4,32,128]{2,1,0:T(8,128)(2,1)S(1)}, bf16[4,32,128]{2,1,0:T(8,128)(2,1)S(1)}, u32[]{:S(2)}, u32[]{:S(2)}) %collective-permute-start.17) | collective-permute-done | bytes 32800 | tf_op jit(solution)/shard_map/ppermute | solution.py:400
  55.2 0.3 smooth.1.partial_ref
  55.5 0.0 collective-permute-done.18.paired_ref
  55.5 1.2 %detect.1 = f32[128,512]{1,0:T(8,128)} custom-call(s32[1]{0:T(128)} %bitcast.even_ref, bf16[128,192]{1,0:T(8,128)(2,1)S(1)} %get-tuple-element.22.after_ref.row_filter_ref, bf16[384,128]{1,0:T(8,128)(2,1)S(1)} %get-tuple-element.23.col_filter_ref, f32[4,128,128]{2,1,0:T(8,128)S(1)} %smooth.1.partial_ref, ...), custom_call_target="tpu_custom_call" | custom-call | tf_op jit(solution)/shard_map/detect/pallas_call | solution.py:254
  (26 shorter events, 0.3 us)
Async XLA Ops:
  1.7 5.1 %collective-permute-start.2 = (f32[1,2,32]{2,1,0:T(2,128)S(1)}, f32[1,2,32]{2,1,0:T(2,128)S(1)}, u32[]{:S(2)}, u32[]{:S(2)}) collective-permute-start(f32[1,2,32]{2,1,0:T(2,128)S(1)} %get-tuple-element.24.after_ref), channel_id=1, source_target_pairs={{0,3},{1,2},{2,1},{3,0},{4,7},{5,6},{6,5},{7,4},{8,11},{9,10},{10,... | collective-permute-start | bytes 776 | tf_op jit(solution)/shard_map/ppermute | solution.py:322
  4.4 1.7 %collective-permute-start.1 = (f32[1,2,32]{2,1,0:T(2,128)S(1)}, f32[1,2,32]{2,1,0:T(2,128)S(1)}, u32[]{:S(2)}, u32[]{:S(2)}) collective-permute-start(f32[1,2,32]{2,1,0:T(2,128)S(1)} %get-tuple-element.24.after_ref), channel_id=1, source_target_pairs={{0,1},{1,0},{2,3},{3,2},{4,5},{5,4},{6,7},{7,6},{8,9},{9,8},{10,11... | collective-permute-start | bytes 776 | tf_op jit(solution)/shard_map/ppermute | solution.py:322
  4.4 2.4 %collective-permute-start = (f32[1,2,32]{2,1,0:T(2,128)S(1)}, f32[1,2,32]{2,1,0:T(2,128)S(1)}, u32[]{:S(2)}, u32[]{:S(2)}) collective-permute-start(f32[1,2,32]{2,1,0:T(2,128)S(1)} %get-tuple-element.24.after_ref), channel_id=1, source_target_pairs={{0,2},{1,3},{2,0},{3,1},{4,6},{5,7},{6,4},{7,5},{8,10},{9,11},{10,... | collective-permute-start | bytes 776 | tf_op jit(solution)/shard_map/ppermute | solution.py:322
  6.8 3.3 %collective-permute-start.3 = (f32[4,2,32]{2,1,0:T(2,128)S(1)}, f32[4,2,32]{2,1,0:T(2,128)S(1)}, u32[]{:S(2)}, u32[]{:S(2)}) collective-permute-start(f32[4,2,32]{2,1,0:T(2,128)S(1)} %get-tuple-element.70.after_ref), channel_id=1, source_target_pairs={{0,4},{4,0},{8,12},{12,8},{16,20},{20,16},{24,28},{28,24},{1,5},{5... | collective-permute-start | bytes 3080 | tf_op jit(solution)/shard_map/ppermute | solution.py:302
  9.2 17.4 %collective-permute-start.6 = (bf16[16,64,128]{2,1,0:T(8,128)(2,1)S(1)}, bf16[16,64,128]{2,1,0:T(8,128)(2,1)S(1)}, u32[]{:S(2)}, u32[]{:S(2)}) collective-permute-start(bf16[16,64,128]{2,1,0:T(8,128)(2,1)S(1)} %get-tuple-element.31.rest_0_), channel_id=1, source_target_pairs={{0,2},{1,3},{2,0},{3,1},{4,6},{5,7},{6,4},{7,5},{8,10},{9,11},{10,... | collective-permute-start | bytes 786440 | tf_op jit(solution)/shard_map/ppermute | solution.py:302
  9.8 10.7 %collective-permute-start.12 = (bf16[16,64,128]{2,1,0:T(8,128)(2,1)S(1)}, bf16[16,64,128]{2,1,0:T(8,128)(2,1)S(1)}, u32[]{:S(2)}, u32[]{:S(2)}) collective-permute-start(bf16[16,64,128]{2,1,0:T(8,128)(2,1)S(1)} %get-tuple-element.36.rest_0_), channel_id=1, source_target_pairs={{0,4},{4,0},{8,12},{12,8},{16,20},{20,16},{24,28},{28,24},{1,5},{5... | collective-permute-start | bytes 786440 | tf_op jit(solution)/shard_map/ppermute | solution.py:302
  10.1 8.2 %copy-start = (f32[6]{0:T(128)S(1)}, f32[6]{0:T(128)}, u32[]{:S(2)}) copy-start(f32[6]{0:T(128)} %param.18) | copy-start | bytes 76
  10.1 5.8 %collective-permute-start.4 = (f32[8,2,32]{2,1,0:T(2,128)S(1)}, f32[8,2,32]{2,1,0:T(2,128)S(1)}, u32[]{:S(2)}, u32[]{:S(2)}) collective-permute-start(f32[8,2,32]{2,1,0:T(2,128)S(1)} %get-tuple-element.55.after_ref), channel_id=1, source_target_pairs={{0,8},{4,12},{8,0},{12,4},{16,24},{20,28},{24,16},{28,20},{1,9},{5... | collective-permute-start | bytes 6152 | tf_op jit(solution)/shard_map/ppermute | solution.py:302
  13.8 7.5 %collective-permute-start.7 = (bf16[16,64,128]{2,1,0:T(8,128)(2,1)S(1)}, bf16[16,64,128]{2,1,0:T(8,128)(2,1)S(1)}, u32[]{:S(2)}, u32[]{:S(2)}) collective-permute-start(bf16[16,64,128]{2,1,0:T(8,128)(2,1)S(1)} %get-tuple-element.32.rest_1_), channel_id=1, source_target_pairs={{0,2},{1,3},{2,0},{3,1},{4,6},{5,7},{6,4},{7,5},{8,10},{9,11},{10,... | collective-permute-start | bytes 786440 | tf_op jit(solution)/shard_map/ppermute | solution.py:302
  14.7 6.6 %collective-permute-start.8 = (bf16[16,64,128]{2,1,0:T(8,128)(2,1)S(1)}, bf16[16,64,128]{2,1,0:T(8,128)(2,1)S(1)}, u32[]{:S(2)}, u32[]{:S(2)}) collective-permute-start(bf16[16,64,128]{2,1,0:T(8,128)(2,1)S(1)} %get-tuple-element.33.rest_1_), channel_id=1, source_target_pairs={{0,4},{4,0},{8,12},{12,8},{16,20},{20,16},{24,28},{28,24},{1,5},{5... | collective-permute-start | bytes 786440 | tf_op jit(solution)/shard_map/ppermute | solution.py:302
  15.9 3.6 %collective-permute-start.5 = (f32[16,2,32]{2,1,0:T(2,128)S(1)}, f32[16,2,32]{2,1,0:T(2,128)S(1)}, u32[]{:S(2)}, u32[]{:S(2)}) collective-permute-start(f32[16,2,32]{2,1,0:T(2,128)S(1)} %get-tuple-element.51), channel_id=1, source_target_pairs={{0,16},{4,20},{8,24},{12,28},{16,0},{20,4},{24,8},{28,12},{1,17},{... | collective-permute-start | bytes 12296 | tf_op jit(solution)/shard_map/ppermute | solution.py:302
  22.6 7.8 %copy-start.1 = (f32[41]{0:T(128)S(1)}, f32[41]{0:T(128)}, u32[]{:S(2)}) copy-start(f32[41]{0:T(128)} %param.19) | copy-start | bytes 496
  22.7 5.4 %collective-permute-start.13 = (bf16[32,64,128]{2,1,0:T(8,128)(2,1)S(1)}, bf16[32,64,128]{2,1,0:T(8,128)(2,1)S(1)}, u32[]{:S(2)}, u32[]{:S(2)}) collective-permute-start(bf16[32,64,128]{2,1,0:T(8,128)(2,1)S(1)} %get-tuple-element.37), channel_id=1, source_target_pairs={{0,1},{1,0},{2,3},{3,2},{4,5},{5,4},{6,7},{7,6},{8,9},{9,8},{10,11... | collective-permute-start | bytes 1572872 | tf_op jit(solution)/shard_map/ppermute | solution.py:302
  27.9 2.0 %collective-permute-start.9 = (bf16[32,64,128]{2,1,0:T(8,128)(2,1)S(1)}, bf16[32,64,128]{2,1,0:T(8,128)(2,1)S(1)}, u32[]{:S(2)}, u32[]{:S(2)}) collective-permute-start(bf16[32,64,128]{2,1,0:T(8,128)(2,1)S(1)} %get-tuple-element.34), channel_id=1, source_target_pairs={{0,1},{1,0},{2,3},{3,2},{4,5},{5,4},{6,7},{7,6},{8,9},{9,8},{10,11... | collective-permute-start | bytes 1572872 | tf_op jit(solution)/shard_map/ppermute | solution.py:302
  28.1 7.5 %collective-permute-start.14 = (bf16[16,64,128]{2,1,0:T(8,128)(2,1)S(1)}, bf16[16,64,128]{2,1,0:T(8,128)(2,1)S(1)}, u32[]{:S(2)}, u32[]{:S(2)}) collective-permute-start(bf16[16,64,128]{2,1,0:T(8,128)(2,1)S(1)} %add_convert_fusion), channel_id=1, source_target_pairs={{0,2},{1,3},{2,0},{3,1},{4,6},{5,7},{6,4},{7,5},{8,10},{9,11},{10,... | collective-permute-start | bytes 786440 | tf_op jit(solution)/shard_map/ppermute | solution.py:302
  30.0 7.8 %collective-permute-start.10 = (bf16[16,64,128]{2,1,0:T(8,128)(2,1)S(1)}, bf16[16,64,128]{2,1,0:T(8,128)(2,1)S(1)}, u32[]{:S(2)}, u32[]{:S(2)}) collective-permute-start(bf16[16,64,128]{2,1,0:T(8,128)(2,1)S(1)} %add_convert_fusion.1), channel_id=1, source_target_pairs={{0,8},{4,12},{8,0},{12,4},{16,24},{20,28},{24,16},{28,20},{1,9},{5... | collective-permute-start | bytes 786440 | tf_op jit(solution)/shard_map/ppermute | solution.py:302
  35.7 3.9 %collective-permute-start.15 = (bf16[8,64,128]{2,1,0:T(8,128)(2,1)S(1)}, bf16[8,64,128]{2,1,0:T(8,128)(2,1)S(1)}, u32[]{:S(2)}, u32[]{:S(2)}) collective-permute-start(bf16[8,64,128]{2,1,0:T(8,128)(2,1)S(1)} %add_convert_fusion.2), channel_id=1, source_target_pairs={{0,8},{4,12},{8,0},{12,4},{16,24},{20,28},{24,16},{28,20},{1,9},{5... | collective-permute-start | bytes 393224 | tf_op jit(solution)/shard_map/ppermute | solution.py:302
  37.9 3.9 %collective-permute-start.11 = (bf16[8,64,128]{2,1,0:T(8,128)(2,1)S(1)}, bf16[8,64,128]{2,1,0:T(8,128)(2,1)S(1)}, u32[]{:S(2)}, u32[]{:S(2)}) collective-permute-start(bf16[8,64,128]{2,1,0:T(8,128)(2,1)S(1)} %add_convert_fusion.3), channel_id=1, source_target_pairs={{0,4},{4,0},{8,12},{12,8},{16,20},{20,16},{24,28},{28,24},{1,5},{5... | collective-permute-start | bytes 393224 | tf_op jit(solution)/shard_map/ppermute | solution.py:302
  41.9 8.1 %collective-permute-start.16 = (bf16[4,128,128]{2,1,0:T(8,128)(2,1)S(1)}, bf16[4,128,128]{2,1,0:T(8,128)(2,1)S(1)}, u32[]{:S(2)}, u32[]{:S(2)}) collective-permute-start(bf16[4,128,128]{2,1,0:T(8,128)(2,1)S(1)} %pad_maximum_fusion), channel_id=1, source_target_pairs={{0,16},{4,20},{8,24},{12,28},{16,0},{20,4},{24,8},{28,12},{1,17},{... | collective-permute-start | bytes 393224 | tf_op jit(solution)/shard_map/ppermute | solution.py:302
  50.0 5.2 %collective-permute-start.17 = (bf16[4,32,128]{2,1,0:T(8,128)(2,1)S(1)}, bf16[4,32,128]{2,1,0:T(8,128)(2,1)S(1)}, u32[]{:S(2)}, u32[]{:S(2)}) collective-permute-start(bf16[4,32,128]{2,1,0:T(8,128)(2,1)S(1)} %get-tuple-element.48), channel_id=1, source_target_pairs={{1,2},{2,1},{5,6},{6,5},{9,10},{10,9},{13,14},{14,13},{17,18},{18,... | collective-permute-start | bytes 98312 | tf_op jit(solution)/shard_map/ppermute | solution.py:400
  53.5 2.0 %collective-permute-start.18 = (bf16[4,32,128]{2,1,0:T(8,128)(2,1)S(1)}, bf16[4,32,128]{2,1,0:T(8,128)(2,1)S(1)}, u32[]{:S(2)}, u32[]{:S(2)}) collective-permute-start(bf16[4,32,128]{2,1,0:T(8,128)(2,1)S(1)} %get-tuple-element.47), channel_id=1, source_target_pairs={{0,1},{1,0},{2,3},{3,2},{4,5},{5,4},{6,7},{7,6},{8,9},{9,8},{10,11... | collective-permute-start | bytes 98312 | tf_op jit(solution)/shard_map/ppermute | solution.py:302

commit v8 on v7

--- a/solution.py
+++ b/solution.py
@@ -334,13 +334,18 @@
             for group, order in enumerate(orders):
                 own[group].append(found[group])
                 others[group].append(swap(found[group], order[0]))
-        if got is not None:
+        if got is not None and part < sky_bits - 1:
             facts = jnp.concatenate([facts, got])
+        elif got is not None:
+            last_facts = got
 
     near = jnp.stack([facts[0]] + [facts[1 << order[0]] for order in orders])
     near_key, near_weight = near[:, 0], near[:, 1]
-    same = near_key[:, :, None, None] == facts[None, None, :, 0]
-    weight_sum = jnp.sum(jnp.where(same, facts[None, None, :, 1], 0.0), axis=(2, 3))
+    weight_sum, wanted = 0.0, near_key
+    for part in (facts, last_facts):
+        same = wanted[:, :, None, None] == part[None, None, :, 0]
+        weight_sum = weight_sum + jnp.sum(jnp.where(same, part[None, None, :, 1], 0.0), axis=(2, 3))
+        weight_sum, wanted = lax.optimization_barrier((weight_sum, wanted))
     near_key = near_key.astype(jnp.int32)
     cell = near_key % CELLS
     band = near_key // CELLS % BANDS

time: 56.9 us -> 57.1 us (level)
  waiting for transfers between devices: 19.1 us -> 14.5 us
  starting transfers between devices: 22.3 us -> 26.2 us
  other arithmetic: 1.57 us -> 2.48 us
    ppermute x15, waiting for transfers between devices: 16.8 us -> 11.6 us  [swap(): return lax.ppermute(array, axis, [(i, i ^ 1 << bit) for i in range(count)])]
    ppermute x1, starting transfers between devices: 3.52 us -> 6.09 us  [local(): lax.ppermute(jnp.where(even, top, bottom), 'band', inner + [(i, j) for j,...]
    ppermute x15, starting transfers between devices: 15.9 us -> 17.2 us  [swap(): return lax.ppermute(array, axis, [(i, i ^ 1 << bit) for i in range(count)])]
    reduce_sum x1 -> x2, other arithmetic: 0.93 us -> 1.83 us  [local(): jnp.sum(jnp.where(same, part[None, None, :, 1], 0.0), axis=(2, 3))]
    ppermute x3, waiting for transfers between devices: 0.71 us -> 1.42 us  [local(): lax.ppermute(own_facts, 'band', [(i, i ^ off) for i in range(band_count)])]
  transfers between devices with their start and end apart: 19 -> 19, of which waited for: 10 -> 10; matrix products, arithmetic and copies ran while one was open for 3% -> 4% of each run, Pallas kernels for 18% -> 18%
where the time goes in v8:
time: 57.1 us; the launch traced here: 56.9 us
  starting transfers between devices  26.2 us (46%)
  waiting for transfers between devices  14.5 us (25%)
  Pallas kernels  13.3 us (23%)
  other arithmetic  2.48 us (4%)
    ppermute x15, starting transfers between devices, swap(): return lax.ppermute(array, axis, [(i, i ^ 1 << bit) for i in range(count)])  17.2 us
    ppermute x15, waiting for transfers between devices, swap(): return lax.ppermute(array, axis, [(i, i ^ 1 << bit) for i in range(count)])  11.6 us
    ppermute x1, starting transfers between devices, local(): lax.ppermute(jnp.where(even, top, bottom), 'band', inner + [(i, j) for j,...  6.09 us
    pallas_call x4, Pallas kernels, bin_blocks(): pl.pallas_call(functools.partial(bin_kernel, stepped, len(blocks)), grid=...  5.13 us
    pallas_call x3, Pallas kernels, match_blocks(): pl.pallas_call(functools.partial(match_kernel, first, count, skip, not in...  4.71 us
    ppermute x3, starting transfers between devices, local(): lax.ppermute(own_facts, 'band', [(i, i ^ off) for i in range(band_count)])  2.87 us
    reduce_sum x2, other arithmetic, local(): jnp.sum(jnp.where(same, part[None, None, :, 1], 0.0), axis=(2, 3))  1.83 us
    pallas_call x1, Pallas kernels, load(): pl.pallas_call(load_kernel, out_shape=out_shape, in_specs=[pl.BlockSpec(m...  1.67 us
  transfers between devices with their start and end apart: 19, of which 10 were waited for; matrix products, arithmetic and copies ran while one was open for 4% of the time, Pallas kernels for 18%

profile of v8, /device:TPU:1, one launch (start us, length us, event | category | flops | bytes accessed | tf_op | source)
XLA Modules:
  0.0 56.9 jit_solution(17082574037329336072)
XLA Ops:
  0.0 1.7 %load.1 = (f32[1,2,32]{2,1,0:T(2,128)S(1)}, f32[3,32]{1,0:T(4,128)S(1)}, bf16[384,168]{1,0:T(8,128)(2,1)S(1)}, bf16[768,128]{1,0:T(8,128)(2,1)S(1)}, bf16[168,5376]{1,0:T(8,128)(2,1)S(1)}) custom-call(s32[1,32]{1,0:T(1,128)} %bitcast.35, s32[1,32]{1,0:T(1,128)} %bitcast.36, s32[1,32]{1,0:T(1,128)} %bitcast.37, bf16[32]{0:T(256)(128)(2,1)} %refs_3_.1, ...), custom_call_target="tpu_custom_call" | custom-call | flops 1048576 | bytes 4194304 | tf_op jit(solution)/shard_map/load/pallas_call | solution.py:73
  1.7 0.1 collective-permute-start.1
  1.8 2.7 %collective-permute-start = (f32[1,2,32]{2,1,0:T(2,128)S(1)}, f32[1,2,32]{2,1,0:T(2,128)S(1)}, u32[]{:S(2)}, u32[]{:S(2)}) collective-permute-start(f32[1,2,32]{2,1,0:T(2,128)S(1)} %get-tuple-element.27.after_ref), channel_id=1, source_target_pairs={{0,2},{1,3},{2,0},{3,1},{4,6},{5,7},{6,4},{7,5},{8,10},{9,11},{10,... | collective-permute-start | bytes 776 | tf_op jit(solution)/shard_map/ppermute | solution.py:322
  4.5 0.0 collective-permute-start.2
  4.5 1.5 %match_blocks.3 = (bf16[16,64,128]{2,1,0:T(8,128)(2,1)S(1)}, bf16[16,64,128]{2,1,0:T(8,128)(2,1)S(1)}) custom-call(f32[1,2,32]{2,1,0:T(2,128)S(1)} %get-tuple-element.27.after_ref, f32[3,32]{1,0:T(4,128)S(1)} %get-tuple-element.31.coef_ref, bf16[384,168]{1,0:T(8,128)(2,1)S(1)} %get-tuple-element.32.rowk_ref, ...), custom_call_target="tpu_custom_call" | custom-call | flops 1527644160 | bytes 2097152 | tf_op jit(solution)/shard_map/match_blocks/pallas_call | solution.py:117
  6.0 0.0 collective-permute-done.1
  6.1 0.0 collective-permute-done
  6.1 1.4 %collective-permute-done.2 = f32[1,2,32]{2,1,0:T(2,128)S(1)} collective-permute-done((f32[1,2,32]{2,1,0:T(2,128)S(1)}, f32[1,2,32]{2,1,0:T(2,128)S(1)}, u32[]{:S(2)}, u32[]{:S(2)}) %collective-permute-start.2) | collective-permute-done | bytes 288 | tf_op jit(solution)/shard_map/ppermute | solution.py:322
  7.5 1.2 %collective-permute-start.3 = (f32[4,2,32]{2,1,0:T(2,128)S(1)}, f32[4,2,32]{2,1,0:T(2,128)S(1)}, u32[]{:S(2)}, u32[]{:S(2)}) collective-permute-start(f32[4,2,32]{2,1,0:T(2,128)S(1)} %get-tuple-element.74.after_ref), channel_id=1, source_target_pairs={{0,4},{4,0},{8,12},{12,8},{16,20},{20,16},{24,28},{28,24},{1,5},{5... | collective-permute-start | bytes 3080 | tf_op jit(solution)/shard_map/ppermute | solution.py:302
  8.7 1.1 %match_blocks.4 = (bf16[16,64,128]{2,1,0:T(8,128)(2,1)S(1)}, bf16[16,64,128]{2,1,0:T(8,128)(2,1)S(1)}) custom-call(f32[4,2,32]{2,1,0:T(2,128)S(1)} %get-tuple-element.74.after_ref, f32[3,32]{1,0:T(4,128)S(1)} %get-tuple-element.31.coef_ref, bf16[384,168]{1,0:T(8,128)(2,1)S(1)} %get-tuple-element.32.rowk_ref, ...), custom_call_target="tpu_custom_call", output_to_operand_aliasing={{0}: (5, {}), {1}: (6, {})} | custom-call | flops 916586496 | bytes 2097152 | tf_op jit(solution)/shard_map/match_blocks/pallas_call | solution.py:117
  9.8 0.4 collective-permute-start.6
  10.2 0.3 collective-permute-start.12
  10.4 0.0 collective-permute-done.3
  10.4 0.0 copy-start
  10.4 2.2 %match_blocks.5 = (bf16[16,64,128]{2,1,0:T(8,128)(2,1)S(1)}, bf16[16,64,128]{2,1,0:T(8,128)(2,1)S(1)}) custom-call(f32[8,2,32]{2,1,0:T(2,128)S(1)} %get-tuple-element.59.after_ref, f32[3,32]{1,0:T(4,128)S(1)} %get-tuple-element.31.coef_ref, bf16[384,168]{1,0:T(8,128)(2,1)S(1)} %get-tuple-element.32.rowk_ref, ...), custom_call_target="tpu_custom_call" | custom-call | flops 2444230656 | bytes 2097152 | tf_op jit(solution)/shard_map/match_blocks/pallas_call | solution.py:117
  12.6 1.4 %collective-permute-start.4 = (f32[8,2,32]{2,1,0:T(2,128)S(1)}, f32[8,2,32]{2,1,0:T(2,128)S(1)}, u32[]{:S(2)}, u32[]{:S(2)}) collective-permute-start(f32[8,2,32]{2,1,0:T(2,128)S(1)} %get-tuple-element.59.after_ref), channel_id=1, source_target_pairs={{0,8},{4,12},{8,0},{12,4},{16,24},{20,28},{24,16},{28,20},{1,9},{5... | collective-permute-start | bytes 6152 | tf_op jit(solution)/shard_map/ppermute | solution.py:302
  14.1 1.2 %collective-permute-start.7 = (bf16[16,64,128]{2,1,0:T(8,128)(2,1)S(1)}, bf16[16,64,128]{2,1,0:T(8,128)(2,1)S(1)}, u32[]{:S(2)}, u32[]{:S(2)}) collective-permute-start(bf16[16,64,128]{2,1,0:T(8,128)(2,1)S(1)} %get-tuple-element.38.rest_1_), channel_id=1, source_target_pairs={{0,2},{1,3},{2,0},{3,1},{4,6},{5,7},{6,4},{7,5},{8,10},{9,11},{10,... | collective-permute-start | bytes 786440 | tf_op jit(solution)/shard_map/ppermute | solution.py:302
  15.3 1.2 %collective-permute-start.8 = (bf16[16,64,128]{2,1,0:T(8,128)(2,1)S(1)}, bf16[16,64,128]{2,1,0:T(8,128)(2,1)S(1)}, u32[]{:S(2)}, u32[]{:S(2)}) collective-permute-start(bf16[16,64,128]{2,1,0:T(8,128)(2,1)S(1)} %get-tuple-element.39.rest_1_), channel_id=1, source_target_pairs={{0,4},{4,0},{8,12},{12,8},{16,20},{20,16},{24,28},{28,24},{1,5},{5... | collective-permute-start | bytes 786440 | tf_op jit(solution)/shard_map/ppermute | solution.py:302
  16.5 0.0 copy-done
  16.5 0.1 select_reduce_fusion.2
  16.6 0.0 collective-permute-done.4
  16.6 2.4 %collective-permute-start.5 = (f32[16,2,32]{2,1,0:T(2,128)S(1)}, f32[16,2,32]{2,1,0:T(2,128)S(1)}, u32[]{:S(2)}, u32[]{:S(2)}) collective-permute-start(f32[16,2,32]{2,1,0:T(2,128)S(1)} %constant_dynamic-update-slice_fusion.9), channel_id=1, source_target_pairs={{0,16},{4,20},{8,24},{12,28},{16,0},{20,4},{24,8},{28,12},{1,17},{... | collective-permute-start | bytes 12296 | tf_op jit(solution)/shard_map/ppermute | solution.py:302
  19.0 0.9 %select_reduce_fusion.1 = f32[3,32]{1,0:T(4,128)S(1)} fusion(f32[16,32]{1,0:T(8,128)S(1)} %bitcast.31, f32[16,32]{1,0:T(8,128)S(1)} %bitcast.30, f32[3,32]{1,0:T(4,128)S(1)} %bitcast.32), kind=kLoop, calls=%fused_computation.1 | loop fusion | flops 147360 | bytes 4864 | tf_op jit(solution)/shard_map/reduce_sum | solution.py:347
  20.0 0.3 collective-permute-done.5
  20.3 0.9 %select_reduce_fusion = f32[3,32]{1,0:T(4,128)S(1)} fusion(f32[16,32]{1,0:T(8,128)S(1)} %bitcast.29, f32[16,32]{1,0:T(8,128)S(1)} %bitcast.28, f32[3,32]{1,0:T(4,128)S(1)} %bitcast.33), kind=kLoop, calls=%fused_computation | loop fusion | flops 147360 | bytes 4864 | tf_op jit(solution)/shard_map/reduce_sum | solution.py:347
  21.2 0.0 copy-start.1
  21.2 0.0 collective-permute-done.6.rest_2_
  21.2 1.5 %collective-permute-done.7.rest_3_.after_ref = bf16[16,64,128]{2,1,0:T(8,128)(2,1)S(1)} collective-permute-done((bf16[16,64,128]{2,1,0:T(8,128)(2,1)S(1)}, bf16[16,64,128]{2,1,0:T(8,128)(2,1)S(1)}, u32[]{:S(2)}, u32[]{:S(2)}) %collective-permute-start.7) | collective-permute-done | bytes 262176 | tf_op jit(solution)/shard_map/ppermute | solution.py:302
  22.7 0.0 collective-permute-done.8.after_ref.rest_3_
  22.7 1.4 %bins_sent.2 = (bf16[32,64,128]{2,1,0:T(8,128)(2,1)S(1)}, bf16[16,64,128]{2,1,0:T(8,128)(2,1)S(1)}) custom-call(s32[2,32]{1,0:T(2,128)S(1)} %compare_select_fusion.10.bins_ref, f32[2,32]{1,0:T(2,128)S(1)} %stack.24.scale_ref, bf16[16,64,128]{2,1,0:T(8,128)(2,1)S(1)} %collective-permute-done.8.after_ref.rest_3_, ...), custom_call_target="tpu_custom_call" | custom-call | flops 3670016 | bytes 1835008 | tf_op jit(solution)/shard_map/bins_sent/pallas_call | solution.py:169
  24.1 1.8 %collective-permute-start.9 = (bf16[32,64,128]{2,1,0:T(8,128)(2,1)S(1)}, bf16[32,64,128]{2,1,0:T(8,128)(2,1)S(1)}, u32[]{:S(2)}, u32[]{:S(2)}) collective-permute-start(bf16[32,64,128]{2,1,0:T(8,128)(2,1)S(1)} %get-tuple-element.40), channel_id=1, source_target_pairs={{0,1},{1,0},{2,3},{3,2},{4,5},{5,4},{6,7},{7,6},{8,9},{9,8},{10,11... | collective-permute-start | bytes 1572872 | tf_op jit(solution)/shard_map/ppermute | solution.py:302
  26.0 0.0 collective-permute-done.12.rest_2_
  26.0 1.4 %bins_sent.3 = (bf16[32,64,128]{2,1,0:T(8,128)(2,1)S(1)}, bf16[16,64,128]{2,1,0:T(8,128)(2,1)S(1)}) custom-call(s32[2,32]{1,0:T(2,128)S(1)} %compare_select_fusion.7.bins_ref, f32[2,32]{1,0:T(2,128)S(1)} %pad_maximum_fusion.2.scale_ref, bf16[16,64,128]{2,1,0:T(8,128)(2,1)S(1)} %collective-permute-done.7.rest_3_.after_ref, ...), custom_call_target="tpu_custom_call" | custom-call | flops 3670016 | bytes 1835008 | tf_op jit(solution)/shard_map/bins_sent/pallas_call | solution.py:169
  27.4 0.1 collective-permute-start.13
  27.4 0.0 collective-permute-done.9
  27.5 0.1 add_convert_fusion.1
  27.6 1.3 %collective-permute-start.10 = (bf16[16,64,128]{2,1,0:T(8,128)(2,1)S(1)}, bf16[16,64,128]{2,1,0:T(8,128)(2,1)S(1)}, u32[]{:S(2)}, u32[]{:S(2)}) collective-permute-start(bf16[16,64,128]{2,1,0:T(8,128)(2,1)S(1)} %add_convert_fusion.1), channel_id=1, source_target_pairs={{0,8},{4,12},{8,0},{12,4},{16,24},{20,28},{24,16},{28,20},{1,9},{5... | collective-permute-start | bytes 786440 | tf_op jit(solution)/shard_map/ppermute | solution.py:302
  28.9 0.4 collective-permute-done.13
  29.3 0.1 add_convert_fusion
  29.4 1.2 %collective-permute-start.14 = (bf16[16,64,128]{2,1,0:T(8,128)(2,1)S(1)}, bf16[16,64,128]{2,1,0:T(8,128)(2,1)S(1)}, u32[]{:S(2)}, u32[]{:S(2)}) collective-permute-start(bf16[16,64,128]{2,1,0:T(8,128)(2,1)S(1)} %add_convert_fusion), channel_id=1, source_target_pairs={{0,2},{1,3},{2,0},{3,1},{4,6},{5,7},{6,4},{7,5},{8,10},{9,11},{10,... | collective-permute-start | bytes 786440 | tf_op jit(solution)/shard_map/ppermute | solution.py:302
  30.6 0.0 copy-done.1
  30.6 0.3 filters.1
  30.9 1.2 %bins_kept.2 = bf16[16,64,128]{2,1,0:T(8,128)(2,1)S(1)} custom-call(s32[2,32]{1,0:T(2,128)S(1)} %get-tuple-element.45.bins_ref, f32[2,32]{1,0:T(2,128)S(1)} %stack.24.scale_ref, bf16[128,192]{1,0:T(8,128)(2,1)S(1)} %get-tuple-element.25.after_ref.row_filter_ref, bf16[16,64,128]{2,1,0:T(8,128)(2,1)S(1)} %get-tuple-element.37.rest_0_, ...), custom_call_target="tpu_custom_call" | custom-call | flops 2621440 | bytes 1310720 | tf_op jit(solution)/shard_map/bins_kept/pallas_call | solution.py:169
  32.1 1.2 %bins_kept.3 = bf16[16,64,128]{2,1,0:T(8,128)(2,1)S(1)} custom-call(s32[2,32]{1,0:T(2,128)S(1)} %get-tuple-element.47.bins_ref, f32[2,32]{1,0:T(2,128)S(1)} %pad_maximum_fusion.2.scale_ref, bf16[128,192]{1,0:T(8,128)(2,1)S(1)} %get-tuple-element.25.after_ref.row_filter_ref, bf16[16,64,128]{2,1,0:T(8,128)(2,1)S(1)} %get-tuple-element.42.rest_0_, ...), custom_call_target="tpu_custom_call" | custom-call | flops 2621440 | bytes 1310720 | tf_op jit(solution)/shard_map/bins_kept/pallas_call | solution.py:169
  33.3 1.7 %collective-permute-done.10 = bf16[16,64,128]{2,1,0:T(8,128)(2,1)S(1)} collective-permute-done((bf16[16,64,128]{2,1,0:T(8,128)(2,1)S(1)}, bf16[16,64,128]{2,1,0:T(8,128)(2,1)S(1)}, u32[]{:S(2)}, u32[]{:S(2)}) %collective-permute-start.10) | collective-permute-done | bytes 262176 | tf_op jit(solution)/shard_map/ppermute | solution.py:302
  35.1 0.1 add_convert_fusion.3
  35.1 0.8 %collective-permute-start.11 = (bf16[8,64,128]{2,1,0:T(8,128)(2,1)S(1)}, bf16[8,64,128]{2,1,0:T(8,128)(2,1)S(1)}, u32[]{:S(2)}, u32[]{:S(2)}) collective-permute-start(bf16[8,64,128]{2,1,0:T(8,128)(2,1)S(1)} %add_convert_fusion.3), channel_id=1, source_target_pairs={{0,4},{4,0},{8,12},{12,8},{16,20},{20,16},{24,28},{28,24},{1,5},{5... | collective-permute-start | bytes 393224 | tf_op jit(solution)/shard_map/ppermute | solution.py:302
  35.9 1.1 %collective-permute-done.14 = bf16[16,64,128]{2,1,0:T(8,128)(2,1)S(1)} collective-permute-done((bf16[16,64,128]{2,1,0:T(8,128)(2,1)S(1)}, bf16[16,64,128]{2,1,0:T(8,128)(2,1)S(1)}, u32[]{:S(2)}, u32[]{:S(2)}) %collective-permute-start.14) | collective-permute-done | bytes 262176 | tf_op jit(solution)/shard_map/ppermute | solution.py:302
  37.1 0.1 add_convert_fusion.2
  37.1 1.5 %collective-permute-start.15 = (bf16[8,64,128]{2,1,0:T(8,128)(2,1)S(1)}, bf16[8,64,128]{2,1,0:T(8,128)(2,1)S(1)}, u32[]{:S(2)}, u32[]{:S(2)}) collective-permute-start(bf16[8,64,128]{2,1,0:T(8,128)(2,1)S(1)} %add_convert_fusion.2), channel_id=1, source_target_pairs={{0,8},{4,12},{8,0},{12,4},{16,24},{20,28},{24,16},{28,20},{1,9},{5... | collective-permute-start | bytes 393224 | tf_op jit(solution)/shard_map/ppermute | solution.py:302
  38.6 0.4 collective-permute-done.11
  39.0 0.1 add_convert_fusion.5
  39.1 2.0 %collective-permute-done.15 = bf16[8,64,128]{2,1,0:T(8,128)(2,1)S(1)} collective-permute-done((bf16[8,64,128]{2,1,0:T(8,128)(2,1)S(1)}, bf16[8,64,128]{2,1,0:T(8,128)(2,1)S(1)}, u32[]{:S(2)}, u32[]{:S(2)}) %collective-permute-start.15) | collective-permute-done | bytes 131104 | tf_op jit(solution)/shard_map/ppermute | solution.py:302
  41.1 0.1 add_convert_fusion.4
  41.1 2.4 %collective-permute-start.16 = (bf16[4,128,128]{2,1,0:T(8,128)(2,1)S(1)}, bf16[4,128,128]{2,1,0:T(8,128)(2,1)S(1)}, u32[]{:S(2)}, u32[]{:S(2)}) collective-permute-start(bf16[4,128,128]{2,1,0:T(8,128)(2,1)S(1)} %pad_maximum_fusion), channel_id=1, source_target_pairs={{0,16},{4,20},{8,24},{12,28},{16,0},{20,4},{24,8},{28,12},{1,17},{... | collective-permute-start | bytes 393224 | tf_op jit(solution)/shard_map/ppermute | solution.py:302
  43.5 4.1 %collective-permute-done.16 = bf16[4,128,128]{2,1,0:T(8,128)(2,1)S(1)} collective-permute-done((bf16[4,128,128]{2,1,0:T(8,128)(2,1)S(1)}, bf16[4,128,128]{2,1,0:T(8,128)(2,1)S(1)}, u32[]{:S(2)}, u32[]{:S(2)}) %collective-permute-start.16) | collective-permute-done | bytes 131104 | tf_op jit(solution)/shard_map/ppermute | solution.py:302
  47.7 6.1 %collective-permute-start.17 = (bf16[4,32,128]{2,1,0:T(8,128)(2,1)S(1)}, bf16[4,32,128]{2,1,0:T(8,128)(2,1)S(1)}, u32[]{:S(2)}, u32[]{:S(2)}) collective-permute-start(bf16[4,32,128]{2,1,0:T(8,128)(2,1)S(1)} %get-tuple-element.54), channel_id=1, source_target_pairs={{1,2},{2,1},{5,6},{6,5},{9,10},{10,9},{13,14},{14,13},{17,18},{18,... | collective-permute-start | bytes 98312 | tf_op jit(solution)/shard_map/ppermute | solution.py:405
  53.8 0.1 collective-permute-start.18
  53.9 1.5 %collective-permute-done.17.beyond_ref = bf16[4,32,128]{2,1,0:T(8,128)(2,1)S(1)} collective-permute-done((bf16[4,32,128]{2,1,0:T(8,128)(2,1)S(1)}, bf16[4,32,128]{2,1,0:T(8,128)(2,1)S(1)}, u32[]{:S(2)}, u32[]{:S(2)}) %collective-permute-start.17) | collective-permute-done | bytes 32800 | tf_op jit(solution)/shard_map/ppermute | solution.py:405
  55.4 0.3 smooth.1.partial_ref
  55.7 0.0 collective-permute-done.18.paired_ref
  55.7 1.2 %detect.1 = f32[128,512]{1,0:T(8,128)} custom-call(s32[1]{0:T(128)} %bitcast.even_ref, bf16[128,192]{1,0:T(8,128)(2,1)S(1)} %get-tuple-element.25.after_ref.row_filter_ref, bf16[384,128]{1,0:T(8,128)(2,1)S(1)} %get-tuple-element.26.col_filter_ref, f32[4,128,128]{2,1,0:T(8,128)S(1)} %smooth.1.partial_ref, ...), custom_call_target="tpu_custom_call" | custom-call | tf_op jit(solution)/shard_map/detect/pallas_call | solution.py:254
  (27 shorter events, 0.3 us)
Async XLA Ops:
  1.7 4.4 %collective-permute-start.1 = (f32[1,2,32]{2,1,0:T(2,128)S(1)}, f32[1,2,32]{2,1,0:T(2,128)S(1)}, u32[]{:S(2)}, u32[]{:S(2)}) collective-permute-start(f32[1,2,32]{2,1,0:T(2,128)S(1)} %get-tuple-element.27.after_ref), channel_id=1, source_target_pairs={{0,1},{1,0},{2,3},{3,2},{4,5},{5,4},{6,7},{7,6},{8,9},{9,8},{10,11... | collective-permute-start | bytes 776 | tf_op jit(solution)/shard_map/ppermute | solution.py:322
  1.8 4.3 %collective-permute-start = (f32[1,2,32]{2,1,0:T(2,128)S(1)}, f32[1,2,32]{2,1,0:T(2,128)S(1)}, u32[]{:S(2)}, u32[]{:S(2)}) collective-permute-start(f32[1,2,32]{2,1,0:T(2,128)S(1)} %get-tuple-element.27.after_ref), channel_id=1, source_target_pairs={{0,2},{1,3},{2,0},{3,1},{4,6},{5,7},{6,4},{7,5},{8,10},{9,11},{10,... | collective-permute-start | bytes 776 | tf_op jit(solution)/shard_map/ppermute | solution.py:322
  4.5 3.0 %collective-permute-start.2 = (f32[1,2,32]{2,1,0:T(2,128)S(1)}, f32[1,2,32]{2,1,0:T(2,128)S(1)}, u32[]{:S(2)}, u32[]{:S(2)}) collective-permute-start(f32[1,2,32]{2,1,0:T(2,128)S(1)} %get-tuple-element.27.after_ref), channel_id=1, source_target_pairs={{0,3},{1,2},{2,1},{3,0},{4,7},{5,6},{6,5},{7,4},{8,11},{9,10},{10,... | collective-permute-start | bytes 776 | tf_op jit(solution)/shard_map/ppermute | solution.py:322
  7.5 2.9 %collective-permute-start.3 = (f32[4,2,32]{2,1,0:T(2,128)S(1)}, f32[4,2,32]{2,1,0:T(2,128)S(1)}, u32[]{:S(2)}, u32[]{:S(2)}) collective-permute-start(f32[4,2,32]{2,1,0:T(2,128)S(1)} %get-tuple-element.74.after_ref), channel_id=1, source_target_pairs={{0,4},{4,0},{8,12},{12,8},{16,20},{20,16},{24,28},{28,24},{1,5},{5... | collective-permute-start | bytes 3080 | tf_op jit(solution)/shard_map/ppermute | solution.py:302
  9.8 11.4 %collective-permute-start.6 = (bf16[16,64,128]{2,1,0:T(8,128)(2,1)S(1)}, bf16[16,64,128]{2,1,0:T(8,128)(2,1)S(1)}, u32[]{:S(2)}, u32[]{:S(2)}) collective-permute-start(bf16[16,64,128]{2,1,0:T(8,128)(2,1)S(1)} %get-tuple-element.37.rest_0_), channel_id=1, source_target_pairs={{0,2},{1,3},{2,0},{3,1},{4,6},{5,7},{6,4},{7,5},{8,10},{9,11},{10,... | collective-permute-start | bytes 786440 | tf_op jit(solution)/shard_map/ppermute | solution.py:302
  10.2 15.8 %collective-permute-start.12 = (bf16[16,64,128]{2,1,0:T(8,128)(2,1)S(1)}, bf16[16,64,128]{2,1,0:T(8,128)(2,1)S(1)}, u32[]{:S(2)}, u32[]{:S(2)}) collective-permute-start(bf16[16,64,128]{2,1,0:T(8,128)(2,1)S(1)} %get-tuple-element.42.rest_0_), channel_id=1, source_target_pairs={{0,4},{4,0},{8,12},{12,8},{16,20},{20,16},{24,28},{28,24},{1,5},{5... | collective-permute-start | bytes 786440 | tf_op jit(solution)/shard_map/ppermute | solution.py:302
  10.4 6.1 %copy-start = (f32[6]{0:T(128)S(1)}, f32[6]{0:T(128)}, u32[]{:S(2)}) copy-start(f32[6]{0:T(128)} %param.18) | copy-start | bytes 76
  12.6 4.0 %collective-permute-start.4 = (f32[8,2,32]{2,1,0:T(2,128)S(1)}, f32[8,2,32]{2,1,0:T(2,128)S(1)}, u32[]{:S(2)}, u32[]{:S(2)}) collective-permute-start(f32[8,2,32]{2,1,0:T(2,128)S(1)} %get-tuple-element.59.after_ref), channel_id=1, source_target_pairs={{0,8},{4,12},{8,0},{12,4},{16,24},{20,28},{24,16},{28,20},{1,9},{5... | collective-permute-start | bytes 6152 | tf_op jit(solution)/shard_map/ppermute | solution.py:302
  14.1 8.6 %collective-permute-start.7 = (bf16[16,64,128]{2,1,0:T(8,128)(2,1)S(1)}, bf16[16,64,128]{2,1,0:T(8,128)(2,1)S(1)}, u32[]{:S(2)}, u32[]{:S(2)}) collective-permute-start(bf16[16,64,128]{2,1,0:T(8,128)(2,1)S(1)} %get-tuple-element.38.rest_1_), channel_id=1, source_target_pairs={{0,2},{1,3},{2,0},{3,1},{4,6},{5,7},{6,4},{7,5},{8,10},{9,11},{10,... | collective-permute-start | bytes 786440 | tf_op jit(solution)/shard_map/ppermute | solution.py:302
  15.3 7.4 %collective-permute-start.8 = (bf16[16,64,128]{2,1,0:T(8,128)(2,1)S(1)}, bf16[16,64,128]{2,1,0:T(8,128)(2,1)S(1)}, u32[]{:S(2)}, u32[]{:S(2)}) collective-permute-start(bf16[16,64,128]{2,1,0:T(8,128)(2,1)S(1)} %get-tuple-element.39.rest_1_), channel_id=1, source_target_pairs={{0,4},{4,0},{8,12},{12,8},{16,20},{20,16},{24,28},{28,24},{1,5},{5... | collective-permute-start | bytes 786440 | tf_op jit(solution)/shard_map/ppermute | solution.py:302
  16.6 3.6 %collective-permute-start.5 = (f32[16,2,32]{2,1,0:T(2,128)S(1)}, f32[16,2,32]{2,1,0:T(2,128)S(1)}, u32[]{:S(2)}, u32[]{:S(2)}) collective-permute-start(f32[16,2,32]{2,1,0:T(2,128)S(1)} %constant_dynamic-update-slice_fusion.9), channel_id=1, source_target_pairs={{0,16},{4,20},{8,24},{12,28},{16,0},{20,4},{24,8},{28,12},{1,17},{... | collective-permute-start | bytes 12296 | tf_op jit(solution)/shard_map/ppermute | solution.py:302
  21.2 9.4 %copy-start.1 = (f32[41]{0:T(128)S(1)}, f32[41]{0:T(128)}, u32[]{:S(2)}) copy-start(f32[41]{0:T(128)} %param.19) | copy-start | bytes 496
  24.1 3.4 %collective-permute-start.9 = (bf16[32,64,128]{2,1,0:T(8,128)(2,1)S(1)}, bf16[32,64,128]{2,1,0:T(8,128)(2,1)S(1)}, u32[]{:S(2)}, u32[]{:S(2)}) collective-permute-start(bf16[32,64,128]{2,1,0:T(8,128)(2,1)S(1)} %get-tuple-element.40), channel_id=1, source_target_pairs={{0,1},{1,0},{2,3},{3,2},{4,5},{5,4},{6,7},{7,6},{8,9},{9,8},{10,11... | collective-permute-start | bytes 1572872 | tf_op jit(solution)/shard_map/ppermute | solution.py:302
  27.4 2.0 %collective-permute-start.13 = (bf16[32,64,128]{2,1,0:T(8,128)(2,1)S(1)}, bf16[32,64,128]{2,1,0:T(8,128)(2,1)S(1)}, u32[]{:S(2)}, u32[]{:S(2)}) collective-permute-start(bf16[32,64,128]{2,1,0:T(8,128)(2,1)S(1)} %get-tuple-element.43), channel_id=1, source_target_pairs={{0,1},{1,0},{2,3},{3,2},{4,5},{5,4},{6,7},{7,6},{8,9},{9,8},{10,11... | collective-permute-start | bytes 1572872 | tf_op jit(solution)/shard_map/ppermute | solution.py:302
  27.6 7.5 %collective-permute-start.10 = (bf16[16,64,128]{2,1,0:T(8,128)(2,1)S(1)}, bf16[16,64,128]{2,1,0:T(8,128)(2,1)S(1)}, u32[]{:S(2)}, u32[]{:S(2)}) collective-permute-start(bf16[16,64,128]{2,1,0:T(8,128)(2,1)S(1)} %add_convert_fusion.1), channel_id=1, source_target_pairs={{0,8},{4,12},{8,0},{12,4},{16,24},{20,28},{24,16},{28,20},{1,9},{5... | collective-permute-start | bytes 786440 | tf_op jit(solution)/shard_map/ppermute | solution.py:302
  29.4 7.7 %collective-permute-start.14 = (bf16[16,64,128]{2,1,0:T(8,128)(2,1)S(1)}, bf16[16,64,128]{2,1,0:T(8,128)(2,1)S(1)}, u32[]{:S(2)}, u32[]{:S(2)}) collective-permute-start(bf16[16,64,128]{2,1,0:T(8,128)(2,1)S(1)} %add_convert_fusion), channel_id=1, source_target_pairs={{0,2},{1,3},{2,0},{3,1},{4,6},{5,7},{6,4},{7,5},{8,10},{9,11},{10,... | collective-permute-start | bytes 786440 | tf_op jit(solution)/shard_map/ppermute | solution.py:302
  35.1 3.9 %collective-permute-start.11 = (bf16[8,64,128]{2,1,0:T(8,128)(2,1)S(1)}, bf16[8,64,128]{2,1,0:T(8,128)(2,1)S(1)}, u32[]{:S(2)}, u32[]{:S(2)}) collective-permute-start(bf16[8,64,128]{2,1,0:T(8,128)(2,1)S(1)} %add_convert_fusion.3), channel_id=1, source_target_pairs={{0,4},{4,0},{8,12},{12,8},{16,20},{20,16},{24,28},{28,24},{1,5},{5... | collective-permute-start | bytes 393224 | tf_op jit(solution)/shard_map/ppermute | solution.py:302
  37.1 3.9 %collective-permute-start.15 = (bf16[8,64,128]{2,1,0:T(8,128)(2,1)S(1)}, bf16[8,64,128]{2,1,0:T(8,128)(2,1)S(1)}, u32[]{:S(2)}, u32[]{:S(2)}) collective-permute-start(bf16[8,64,128]{2,1,0:T(8,128)(2,1)S(1)} %add_convert_fusion.2), channel_id=1, source_target_pairs={{0,8},{4,12},{8,0},{12,4},{16,24},{20,28},{24,16},{28,20},{1,9},{5... | collective-permute-start | bytes 393224 | tf_op jit(solution)/shard_map/ppermute | solution.py:302
  41.1 6.5 %collective-permute-start.16 = (bf16[4,128,128]{2,1,0:T(8,128)(2,1)S(1)}, bf16[4,128,128]{2,1,0:T(8,128)(2,1)S(1)}, u32[]{:S(2)}, u32[]{:S(2)}) collective-permute-start(bf16[4,128,128]{2,1,0:T(8,128)(2,1)S(1)} %pad_maximum_fusion), channel_id=1, source_target_pairs={{0,16},{4,20},{8,24},{12,28},{16,0},{20,4},{24,8},{28,12},{1,17},{... | collective-permute-start | bytes 393224 | tf_op jit(solution)/shard_map/ppermute | solution.py:302
  47.7 7.7 %collective-permute-start.17 = (bf16[4,32,128]{2,1,0:T(8,128)(2,1)S(1)}, bf16[4,32,128]{2,1,0:T(8,128)(2,1)S(1)}, u32[]{:S(2)}, u32[]{:S(2)}) collective-permute-start(bf16[4,32,128]{2,1,0:T(8,128)(2,1)S(1)} %get-tuple-element.54), channel_id=1, source_target_pairs={{1,2},{2,1},{5,6},{6,5},{9,10},{10,9},{13,14},{14,13},{17,18},{18,... | collective-permute-start | bytes 98312 | tf_op jit(solution)/shard_map/ppermute | solution.py:405
  53.8 1.9 %collective-permute-start.18 = (bf16[4,32,128]{2,1,0:T(8,128)(2,1)S(1)}, bf16[4,32,128]{2,1,0:T(8,128)(2,1)S(1)}, u32[]{:S(2)}, u32[]{:S(2)}) collective-permute-start(bf16[4,32,128]{2,1,0:T(8,128)(2,1)S(1)} %get-tuple-element.53), channel_id=1, source_target_pairs={{0,1},{1,0},{2,3},{3,2},{4,5},{5,4},{6,7},{7,6},{8,9},{9,8},{10,11... | collective-permute-start | bytes 98312 | tf_op jit(solution)/shard_map/ppermute | solution.py:302

commit v9 on v7

--- a/solution.py
+++ b/solution.py
@@ -112,7 +112,7 @@
 def match_blocks(first, count, size, loaded, rows, block_side, after, into=()):
     raw = loaded[-1]
     basis_count = loaded[0].shape[0]
-    skip = size - count if into else 0
+    skip = first if into else 0
     flops = 2 * count * basis_count * block_side * raw.shape[0] * (raw.shape[0] + block_side)
     return pl.pallas_call(
         functools.partial(match_kernel, first, count, skip, not into),
@@ -317,17 +317,19 @@
         raw_blocks,
         block_side,
     )
-    facts = jnp.concatenate(
-        [own_facts]
-        + [lax.ppermute(own_facts, "band", [(i, i ^ off) for i in range(band_count)]) for off in range(1, band_count)]
-    )
-    cut, early = block_count // 2, block_count * 5 // 16
+    cut = block_count // 2
+    marks = [cut * i // (band_bits + 1) for i in range(band_bits + 2)]
     own, others = [[], []], [[], []]
-    begun = match_blocks(0, early, cut, loaded, heights, block_side, own_facts)
+    facts, found = own_facts, ()
+    for bit in range(band_bits):
+        got = swap(facts, bit)
+        found = match_blocks(marks[bit], marks[bit + 1] - marks[bit], cut, loaded, heights, block_side, facts, found)
+        facts = jnp.concatenate([facts, got])
     for part in range(max(2, sky_bits)):
         got = swap(facts, band_bits + part) if part < sky_bits else None
         if part == 0:
-            found = match_blocks(early, cut - early, cut, loaded, heights, block_side, facts, begun)
+            first, last = marks[-2:]
+            found = match_blocks(first, last - first, cut, loaded, heights, block_side, facts, found)
         elif part == 1:
             found = match_blocks(cut, block_count - cut, block_count - cut, loaded, heights, block_side, facts)
         if part < 2:

time: 56.9 us -> 57.4 us (level)
  starting transfers between devices: 22.3 us -> 26.4 us
  waiting for transfers between devices: 19.1 us -> 15.2 us
    ppermute x15 -> x17, starting transfers between devices: 15.9 us -> 20.4 us  [swap(): return lax.ppermute(array, axis, [(i, i ^ 1 << bit) for i in range(count)])]
    ppermute x15 -> x17, waiting for transfers between devices: 16.8 us -> 13.7 us  [swap(): return lax.ppermute(array, axis, [(i, i ^ 1 << bit) for i in range(count)])]
    ppermute x3 -> x0, starting transfers between devices: 2.9 us -> none  [local(): lax.ppermute(own_facts, 'band', [(i, i ^ off) for i in range(band_count)])]
    ppermute x1, starting transfers between devices: 3.52 us -> 5.95 us  [local(): lax.ppermute(jnp.where(even, top, bottom), 'band', inner + [(i, j) for j,...]
    ppermute x3 -> x0, waiting for transfers between devices: 0.71 us -> none  [local(): lax.ppermute(own_facts, 'band', [(i, i ^ off) for i in range(band_count)])]
    pallas_call x3 -> x4, Pallas kernels: 4.71 us -> 5.04 us  [match_blocks(): pl.pallas_call(functools.partial(match_kernel, first, count, skip, not in...]
  transfers between devices with their start and end apart: 19 -> 18, of which waited for: 10 -> 10; matrix products, arithmetic and copies ran while one was open for 3% -> 3% of each run, Pallas kernels for 18% -> 19%
where the time goes in v9:
time: 57.4 us; the launch traced here: 57.1 us
  starting transfers between devices  26.4 us (46%)
  waiting for transfers between devices  15.2 us (26%)
  Pallas kernels  13.6 us (24%)
  other arithmetic  1.57 us (3%)
    ppermute x17, starting transfers between devices, swap(): return lax.ppermute(array, axis, [(i, i ^ 1 << bit) for i in range(count)])  20.4 us
    ppermute x17, waiting for transfers between devices, swap(): return lax.ppermute(array, axis, [(i, i ^ 1 << bit) for i in range(count)])  13.7 us
    ppermute x1, starting transfers between devices, local(): lax.ppermute(jnp.where(even, top, bottom), 'band', inner + [(i, j) for j,...  5.95 us
    pallas_call x4, Pallas kernels, bin_blocks(): pl.pallas_call(functools.partial(bin_kernel, stepped, len(blocks)), grid=...  5.07 us
    pallas_call x4, Pallas kernels, match_blocks(): pl.pallas_call(functools.partial(match_kernel, first, count, skip, not in...  5.04 us
    pallas_call x1, Pallas kernels, load(): pl.pallas_call(load_kernel, out_shape=out_shape, in_specs=[pl.BlockSpec(m...  1.67 us
    ppermute x1, waiting for transfers between devices, local(): lax.ppermute(jnp.where(even, top, bottom), 'band', inner + [(i, j) for j,...  1.5 us
    pallas_call x1, Pallas kernels, detect(): pl.pallas_call(detect_kernel, out_shape=jax.ShapeDtypeStruct((side, cells...  1.21 us
  transfers between devices with their start and end apart: 18, of which 10 were waited for; matrix products, arithmetic and copies ran while one was open for 3% of the time, Pallas kernels for 19%

profile of v9, /device:TPU:1, one launch (start us, length us, event | category | flops | bytes accessed | tf_op | source)
XLA Modules:
  0.0 57.1 jit_solution(1886514711905544704)
XLA Ops:
  0.0 1.7 %load.1 = (f32[1,2,32]{2,1,0:T(2,128)S(1)}, f32[3,32]{1,0:T(4,128)S(1)}, bf16[384,168]{1,0:T(8,128)(2,1)S(1)}, bf16[768,128]{1,0:T(8,128)(2,1)S(1)}, bf16[168,5376]{1,0:T(8,128)(2,1)S(1)}) custom-call(s32[1,32]{1,0:T(1,128)} %bitcast.30, s32[1,32]{1,0:T(1,128)} %bitcast.31, s32[1,32]{1,0:T(1,128)} %bitcast.32, bf16[32]{0:T(256)(128)(2,1)} %refs_3_.1, ...), custom_call_target="tpu_custom_call" | custom-call | flops 1048576 | bytes 4194304 | tf_op jit(solution)/shard_map/load/pallas_call | solution.py:73
  1.7 0.1 collective-permute-start
  1.8 0.9 %match_blocks.4 = (bf16[16,64,128]{2,1,0:T(8,128)(2,1)S(1)}, bf16[16,64,128]{2,1,0:T(8,128)(2,1)S(1)}) custom-call(f32[1,2,32]{2,1,0:T(2,128)S(1)} %get-tuple-element.26.after_ref, f32[3,32]{1,0:T(4,128)S(1)} %get-tuple-element.27.coef_ref, bf16[384,168]{1,0:T(8,128)(2,1)S(1)} %get-tuple-element.28.rowk_ref, ...), custom_call_target="tpu_custom_call" | custom-call | flops 763822080 | bytes 2097152 | tf_op jit(solution)/shard_map/match_blocks/pallas_call | solution.py:117
  2.7 0.2 collective-permute-done
  2.9 2.6 %collective-permute-start.1 = (f32[2,2,32]{2,1,0:T(2,128)S(1)}, f32[2,2,32]{2,1,0:T(2,128)S(1)}, u32[]{:S(2)}, u32[]{:S(2)}) collective-permute-start(f32[2,2,32]{2,1,0:T(2,128)S(1)} %get-tuple-element.79.after_ref), channel_id=1, source_target_pairs={{0,2},{1,3},{2,0},{3,1},{4,6},{5,7},{6,4},{7,5},{8,10},{9,11},{10,... | collective-permute-start | bytes 1544 | tf_op jit(solution)/shard_map/ppermute | solution.py:302
  5.5 0.9 %match_blocks.5 = (bf16[16,64,128]{2,1,0:T(8,128)(2,1)S(1)}, bf16[16,64,128]{2,1,0:T(8,128)(2,1)S(1)}) custom-call(f32[2,2,32]{2,1,0:T(2,128)S(1)} %get-tuple-element.79.after_ref, f32[3,32]{1,0:T(4,128)S(1)} %get-tuple-element.27.coef_ref, bf16[384,168]{1,0:T(8,128)(2,1)S(1)} %get-tuple-element.28.rowk_ref, ...), custom_call_target="tpu_custom_call", output_to_operand_aliasing={{0}: (5, {}), {1}: (6, {})} | custom-call | flops 763822080 | bytes 2097152 | tf_op jit(solution)/shard_map/match_blocks/pallas_call | solution.py:117
  6.4 0.0 collective-permute-done.1
  6.4 0.0 copy-start
  6.4 1.5 %collective-permute-start.2 = (f32[4,2,32]{2,1,0:T(2,128)S(1)}, f32[4,2,32]{2,1,0:T(2,128)S(1)}, u32[]{:S(2)}, u32[]{:S(2)}) collective-permute-start(f32[4,2,32]{2,1,0:T(2,128)S(1)} %get-tuple-element.67.after_ref), channel_id=1, source_target_pairs={{0,4},{4,0},{8,12},{12,8},{16,20},{20,16},{24,28},{28,24},{1,5},{5... | collective-permute-start | bytes 3080 | tf_op jit(solution)/shard_map/ppermute | solution.py:302
  7.9 1.1 %match_blocks.6 = (bf16[16,64,128]{2,1,0:T(8,128)(2,1)S(1)}, bf16[16,64,128]{2,1,0:T(8,128)(2,1)S(1)}) custom-call(f32[4,2,32]{2,1,0:T(2,128)S(1)} %get-tuple-element.67.after_ref, f32[3,32]{1,0:T(4,128)S(1)} %get-tuple-element.27.coef_ref, bf16[384,168]{1,0:T(8,128)(2,1)S(1)} %get-tuple-element.28.rowk_ref, ...), custom_call_target="tpu_custom_call", output_to_operand_aliasing={{0}: (5, {}), {1}: (6, {})} | custom-call | flops 916586496 | bytes 2097152 | tf_op jit(solution)/shard_map/match_blocks/pallas_call | solution.py:117
  9.0 1.3 %collective-permute-start.5 = (bf16[16,64,128]{2,1,0:T(8,128)(2,1)S(1)}, bf16[16,64,128]{2,1,0:T(8,128)(2,1)S(1)}, u32[]{:S(2)}, u32[]{:S(2)}) collective-permute-start(bf16[16,64,128]{2,1,0:T(8,128)(2,1)S(1)} %get-tuple-element.35.rest_0_), channel_id=1, source_target_pairs={{0,2},{1,3},{2,0},{3,1},{4,6},{5,7},{6,4},{7,5},{8,10},{9,11},{10,... | collective-permute-start | bytes 786440 | tf_op jit(solution)/shard_map/ppermute | solution.py:302
  10.3 0.3 collective-permute-start.11
  10.6 0.0 copy-done
  10.6 0.0 collective-permute-done.2
  10.6 0.0 slice-start
  10.6 0.0 copy-start.1
  10.6 1.4 %collective-permute-start.3 = (f32[8,2,32]{2,1,0:T(2,128)S(1)}, f32[8,2,32]{2,1,0:T(2,128)S(1)}, u32[]{:S(2)}, u32[]{:S(2)}) collective-permute-start(f32[8,2,32]{2,1,0:T(2,128)S(1)} %get-tuple-element.59.after_ref), channel_id=1, source_target_pairs={{0,8},{4,12},{8,0},{12,4},{16,24},{20,28},{24,16},{28,20},{1,9},{5... | collective-permute-start | bytes 6152 | tf_op jit(solution)/shard_map/ppermute | solution.py:302
  12.0 2.2 %match_blocks.7 = (bf16[16,64,128]{2,1,0:T(8,128)(2,1)S(1)}, bf16[16,64,128]{2,1,0:T(8,128)(2,1)S(1)}) custom-call(f32[8,2,32]{2,1,0:T(2,128)S(1)} %get-tuple-element.59.after_ref, f32[3,32]{1,0:T(4,128)S(1)} %get-tuple-element.27.coef_ref, bf16[384,168]{1,0:T(8,128)(2,1)S(1)} %get-tuple-element.28.rowk_ref, ...), custom_call_target="tpu_custom_call" | custom-call | flops 2444230656 | bytes 2097152 | tf_op jit(solution)/shard_map/match_blocks/pallas_call | solution.py:117
  14.1 0.0 slice-done
  14.3 0.3 collective-permute-start.6
  14.6 1.2 %collective-permute-start.7 = (bf16[16,64,128]{2,1,0:T(8,128)(2,1)S(1)}, bf16[16,64,128]{2,1,0:T(8,128)(2,1)S(1)}, u32[]{:S(2)}, u32[]{:S(2)}) collective-permute-start(bf16[16,64,128]{2,1,0:T(8,128)(2,1)S(1)} %get-tuple-element.37.rest_1_), channel_id=1, source_target_pairs={{0,4},{4,0},{8,12},{12,8},{16,20},{20,16},{24,28},{28,24},{1,5},{5... | collective-permute-start | bytes 786440 | tf_op jit(solution)/shard_map/ppermute | solution.py:302
  15.8 0.0 collective-permute-done.3
  15.8 2.4 %collective-permute-start.4 = (f32[16,2,32]{2,1,0:T(2,128)S(1)}, f32[16,2,32]{2,1,0:T(2,128)S(1)}, u32[]{:S(2)}, u32[]{:S(2)}) collective-permute-start(f32[16,2,32]{2,1,0:T(2,128)S(1)} %get-tuple-element.55), channel_id=1, source_target_pairs={{0,16},{4,20},{8,24},{12,28},{16,0},{20,4},{24,8},{28,12},{1,17},{... | collective-permute-start | bytes 12296 | tf_op jit(solution)/shard_map/ppermute | solution.py:302
  18.2 0.0 copy-done.1
  18.2 0.1 select_reduce_fusion.1
  18.3 1.2 %collective-permute-done.4 = f32[16,2,32]{2,1,0:T(2,128)S(1)} collective-permute-done((f32[16,2,32]{2,1,0:T(2,128)S(1)}, f32[16,2,32]{2,1,0:T(2,128)S(1)}, u32[]{:S(2)}, u32[]{:S(2)}) %collective-permute-start.4) | collective-permute-done | bytes 4128 | tf_op jit(solution)/shard_map/ppermute | solution.py:302
  19.5 0.9 %select_reduce_fusion = f32[3,32]{1,0:T(4,128)S(1)} fusion(f32[32,32]{1,0:T(8,128)S(1)} %bitcast.27, f32[32,32]{1,0:T(8,128)S(1)} %bitcast.26, f32[3,32]{1,0:T(4,128)S(1)} %bitcast.28), kind=kLoop, calls=%fused_computation | loop fusion | flops 294816 | bytes 8960 | tf_op jit(solution)/shard_map/reduce_sum | solution.py:345
  20.4 0.0 collective-permute-done.11.rest_2_
  20.4 0.0 collective-permute-done.6.rest_3_.after_ref
  20.4 1.9 %collective-permute-done.7.after_ref.rest_3_ = bf16[16,64,128]{2,1,0:T(8,128)(2,1)S(1)} collective-permute-done((bf16[16,64,128]{2,1,0:T(8,128)(2,1)S(1)}, bf16[16,64,128]{2,1,0:T(8,128)(2,1)S(1)}, u32[]{:S(2)}, u32[]{:S(2)}) %collective-permute-start.7) | collective-permute-done | bytes 262176 | tf_op jit(solution)/shard_map/ppermute | solution.py:302
  22.4 1.3 %bins_sent.3 = (bf16[32,64,128]{2,1,0:T(8,128)(2,1)S(1)}, bf16[16,64,128]{2,1,0:T(8,128)(2,1)S(1)}) custom-call(s32[2,32]{1,0:T(2,128)S(1)} %compare_select_fusion.7.bins_ref, f32[2,32]{1,0:T(2,128)S(1)} %pad_maximum_fusion.2.scale_ref, bf16[16,64,128]{2,1,0:T(8,128)(2,1)S(1)} %collective-permute-done.6.rest_3_.after_ref, ...), custom_call_target="tpu_custom_call" | custom-call | flops 3670016 | bytes 1835008 | tf_op jit(solution)/shard_map/bins_sent/pallas_call | solution.py:169
  23.7 0.0 copy-start.2
  23.7 2.3 %collective-permute-start.12 = (bf16[32,64,128]{2,1,0:T(8,128)(2,1)S(1)}, bf16[32,64,128]{2,1,0:T(8,128)(2,1)S(1)}, u32[]{:S(2)}, u32[]{:S(2)}) collective-permute-start(bf16[32,64,128]{2,1,0:T(8,128)(2,1)S(1)} %get-tuple-element.41), channel_id=1, source_target_pairs={{0,1},{1,0},{2,3},{3,2},{4,5},{5,4},{6,7},{7,6},{8,9},{9,8},{10,11... | collective-permute-start | bytes 1572872 | tf_op jit(solution)/shard_map/ppermute | solution.py:302
  26.1 0.0 collective-permute-done.5.rest_2_
  26.1 1.4 %bins_sent.2 = (bf16[32,64,128]{2,1,0:T(8,128)(2,1)S(1)}, bf16[16,64,128]{2,1,0:T(8,128)(2,1)S(1)}) custom-call(s32[2,32]{1,0:T(2,128)S(1)} %compare_select_fusion.10.bins_ref, f32[2,32]{1,0:T(2,128)S(1)} %stack.24.scale_ref, bf16[16,64,128]{2,1,0:T(8,128)(2,1)S(1)} %collective-permute-done.7.after_ref.rest_3_, ...), custom_call_target="tpu_custom_call" | custom-call | flops 3670016 | bytes 1835008 | tf_op jit(solution)/shard_map/bins_sent/pallas_call | solution.py:169
  27.5 0.1 collective-permute-start.8
  27.6 0.0 collective-permute-done.12
  27.6 0.1 add_convert_fusion
  27.7 1.3 %collective-permute-start.13 = (bf16[16,64,128]{2,1,0:T(8,128)(2,1)S(1)}, bf16[16,64,128]{2,1,0:T(8,128)(2,1)S(1)}, u32[]{:S(2)}, u32[]{:S(2)}) collective-permute-start(bf16[16,64,128]{2,1,0:T(8,128)(2,1)S(1)} %add_convert_fusion), channel_id=1, source_target_pairs={{0,2},{1,3},{2,0},{3,1},{4,6},{5,7},{6,4},{7,5},{8,10},{9,11},{10,... | collective-permute-start | bytes 786440 | tf_op jit(solution)/shard_map/ppermute | solution.py:302
  29.0 0.5 collective-permute-done.8
  29.5 0.1 add_convert_fusion.1
  29.6 1.4 %collective-permute-start.9 = (bf16[16,64,128]{2,1,0:T(8,128)(2,1)S(1)}, bf16[16,64,128]{2,1,0:T(8,128)(2,1)S(1)}, u32[]{:S(2)}, u32[]{:S(2)}) collective-permute-start(bf16[16,64,128]{2,1,0:T(8,128)(2,1)S(1)} %add_convert_fusion.1), channel_id=1, source_target_pairs={{0,8},{4,12},{8,0},{12,4},{16,24},{20,28},{24,16},{28,20},{1,9},{5... | collective-permute-start | bytes 786440 | tf_op jit(solution)/shard_map/ppermute | solution.py:302
  30.9 0.0 copy-done.2
  30.9 0.3 filters.1
  31.3 1.2 %bins_kept.2 = bf16[16,64,128]{2,1,0:T(8,128)(2,1)S(1)} custom-call(s32[2,32]{1,0:T(2,128)S(1)} %get-tuple-element.43.bins_ref, f32[2,32]{1,0:T(2,128)S(1)} %stack.24.scale_ref, bf16[128,192]{1,0:T(8,128)(2,1)S(1)} %get-tuple-element.24.after_ref.row_filter_ref, bf16[16,64,128]{2,1,0:T(8,128)(2,1)S(1)} %get-tuple-element.35.rest_0_, ...), custom_call_target="tpu_custom_call" | custom-call | flops 2621440 | bytes 1310720 | tf_op jit(solution)/shard_map/bins_kept/pallas_call | solution.py:169
  32.4 1.2 %bins_kept.3 = bf16[16,64,128]{2,1,0:T(8,128)(2,1)S(1)} custom-call(s32[2,32]{1,0:T(2,128)S(1)} %get-tuple-element.45.bins_ref, f32[2,32]{1,0:T(2,128)S(1)} %pad_maximum_fusion.2.scale_ref, bf16[128,192]{1,0:T(8,128)(2,1)S(1)} %get-tuple-element.24.after_ref.row_filter_ref, bf16[16,64,128]{2,1,0:T(8,128)(2,1)S(1)} %get-tuple-element.40.rest_0_, ...), custom_call_target="tpu_custom_call" | custom-call | flops 2621440 | bytes 1310720 | tf_op jit(solution)/shard_map/bins_kept/pallas_call | solution.py:169
  33.6 1.5 %collective-permute-done.13 = bf16[16,64,128]{2,1,0:T(8,128)(2,1)S(1)} collective-permute-done((bf16[16,64,128]{2,1,0:T(8,128)(2,1)S(1)}, bf16[16,64,128]{2,1,0:T(8,128)(2,1)S(1)}, u32[]{:S(2)}, u32[]{:S(2)}) %collective-permute-start.13) | collective-permute-done | bytes 262176 | tf_op jit(solution)/shard_map/ppermute | solution.py:302
  35.2 0.1 add_convert_fusion.2
  35.2 1.4 %collective-permute-start.14 = (bf16[8,64,128]{2,1,0:T(8,128)(2,1)S(1)}, bf16[8,64,128]{2,1,0:T(8,128)(2,1)S(1)}, u32[]{:S(2)}, u32[]{:S(2)}) collective-permute-start(bf16[8,64,128]{2,1,0:T(8,128)(2,1)S(1)} %add_convert_fusion.2), channel_id=1, source_target_pairs={{0,8},{4,12},{8,0},{12,4},{16,24},{20,28},{24,16},{28,20},{1,9},{5... | collective-permute-start | bytes 393224 | tf_op jit(solution)/shard_map/ppermute | solution.py:302
  36.6 0.7 %collective-permute-done.9 = bf16[16,64,128]{2,1,0:T(8,128)(2,1)S(1)} collective-permute-done((bf16[16,64,128]{2,1,0:T(8,128)(2,1)S(1)}, bf16[16,64,128]{2,1,0:T(8,128)(2,1)S(1)}, u32[]{:S(2)}, u32[]{:S(2)}) %collective-permute-start.9) | collective-permute-done | bytes 262176 | tf_op jit(solution)/shard_map/ppermute | solution.py:302
  37.3 0.1 add_convert_fusion.3
  37.4 0.4 collective-permute-start.10
  37.8 1.3 %collective-permute-done.14 = bf16[8,64,128]{2,1,0:T(8,128)(2,1)S(1)} collective-permute-done((bf16[8,64,128]{2,1,0:T(8,128)(2,1)S(1)}, bf16[8,64,128]{2,1,0:T(8,128)(2,1)S(1)}, u32[]{:S(2)}, u32[]{:S(2)}) %collective-permute-start.14) | collective-permute-done | bytes 131104 | tf_op jit(solution)/shard_map/ppermute | solution.py:302
  39.1 0.1 add_convert_fusion.4
  39.2 2.1 %collective-permute-done.10 = bf16[8,64,128]{2,1,0:T(8,128)(2,1)S(1)} collective-permute-done((bf16[8,64,128]{2,1,0:T(8,128)(2,1)S(1)}, bf16[8,64,128]{2,1,0:T(8,128)(2,1)S(1)}, u32[]{:S(2)}, u32[]{:S(2)}) %collective-permute-start.10) | collective-permute-done | bytes 131104 | tf_op jit(solution)/shard_map/ppermute | solution.py:302
  41.3 0.1 add_convert_fusion.5
  41.3 2.5 %collective-permute-start.15 = (bf16[4,128,128]{2,1,0:T(8,128)(2,1)S(1)}, bf16[4,128,128]{2,1,0:T(8,128)(2,1)S(1)}, u32[]{:S(2)}, u32[]{:S(2)}) collective-permute-start(bf16[4,128,128]{2,1,0:T(8,128)(2,1)S(1)} %pad_maximum_fusion), channel_id=1, source_target_pairs={{0,16},{4,20},{8,24},{12,28},{16,0},{20,4},{24,8},{28,12},{1,17},{... | collective-permute-start | bytes 393224 | tf_op jit(solution)/shard_map/ppermute | solution.py:302
  43.8 4.2 %collective-permute-done.15 = bf16[4,128,128]{2,1,0:T(8,128)(2,1)S(1)} collective-permute-done((bf16[4,128,128]{2,1,0:T(8,128)(2,1)S(1)}, bf16[4,128,128]{2,1,0:T(8,128)(2,1)S(1)}, u32[]{:S(2)}, u32[]{:S(2)}) %collective-permute-start.15) | collective-permute-done | bytes 131104 | tf_op jit(solution)/shard_map/ppermute | solution.py:302
  48.1 5.9 %collective-permute-start.16 = (bf16[4,32,128]{2,1,0:T(8,128)(2,1)S(1)}, bf16[4,32,128]{2,1,0:T(8,128)(2,1)S(1)}, u32[]{:S(2)}, u32[]{:S(2)}) collective-permute-start(bf16[4,32,128]{2,1,0:T(8,128)(2,1)S(1)} %get-tuple-element.52), channel_id=1, source_target_pairs={{1,2},{2,1},{5,6},{6,5},{9,10},{10,9},{13,14},{14,13},{17,18},{18,... | collective-permute-start | bytes 98312 | tf_op jit(solution)/shard_map/ppermute | solution.py:402
  54.0 0.1 collective-permute-start.17
  54.1 1.5 %collective-permute-done.16.beyond_ref = bf16[4,32,128]{2,1,0:T(8,128)(2,1)S(1)} collective-permute-done((bf16[4,32,128]{2,1,0:T(8,128)(2,1)S(1)}, bf16[4,32,128]{2,1,0:T(8,128)(2,1)S(1)}, u32[]{:S(2)}, u32[]{:S(2)}) %collective-permute-start.16) | collective-permute-done | bytes 32800 | tf_op jit(solution)/shard_map/ppermute | solution.py:402
  55.6 0.3 smooth.1.partial_ref
  55.9 0.0 collective-permute-done.17.paired_ref
  55.9 1.2 %detect.1 = f32[128,512]{1,0:T(8,128)} custom-call(s32[1]{0:T(128)} %bitcast.even_ref, bf16[128,192]{1,0:T(8,128)(2,1)S(1)} %get-tuple-element.24.after_ref.row_filter_ref, bf16[384,128]{1,0:T(8,128)(2,1)S(1)} %get-tuple-element.25.col_filter_ref, f32[4,128,128]{2,1,0:T(8,128)S(1)} %smooth.1.partial_ref, ...), custom_call_target="tpu_custom_call" | custom-call | tf_op jit(solution)/shard_map/detect/pallas_call | solution.py:254
  (25 shorter events, 0.2 us)
Async XLA Ops:
  1.7 1.2 %collective-permute-start = (f32[1,2,32]{2,1,0:T(2,128)S(1)}, f32[1,2,32]{2,1,0:T(2,128)S(1)}, u32[]{:S(2)}, u32[]{:S(2)}) collective-permute-start(f32[1,2,32]{2,1,0:T(2,128)S(1)} %get-tuple-element.26.after_ref), channel_id=1, source_target_pairs={{0,1},{1,0},{2,3},{3,2},{4,5},{5,4},{6,7},{7,6},{8,9},{9,8},{10,11... | collective-permute-start | bytes 776 | tf_op jit(solution)/shard_map/ppermute | solution.py:302
  2.9 3.5 %collective-permute-start.1 = (f32[2,2,32]{2,1,0:T(2,128)S(1)}, f32[2,2,32]{2,1,0:T(2,128)S(1)}, u32[]{:S(2)}, u32[]{:S(2)}) collective-permute-start(f32[2,2,32]{2,1,0:T(2,128)S(1)} %get-tuple-element.79.after_ref), channel_id=1, source_target_pairs={{0,2},{1,3},{2,0},{3,1},{4,6},{5,7},{6,4},{7,5},{8,10},{9,11},{10,... | collective-permute-start | bytes 1544 | tf_op jit(solution)/shard_map/ppermute | solution.py:302
  6.4 4.1 %copy-start = (f32[2,2,32]{2,1,0:T(2,128)}, f32[2,2,32]{2,1,0:T(2,128)S(1)}, u32[]{:S(2)}) copy-start(f32[2,2,32]{2,1,0:T(2,128)S(1)} %collective-permute-done.1) | copy-start | bytes 1540
  6.4 4.1 %collective-permute-start.2 = (f32[4,2,32]{2,1,0:T(2,128)S(1)}, f32[4,2,32]{2,1,0:T(2,128)S(1)}, u32[]{:S(2)}, u32[]{:S(2)}) collective-permute-start(f32[4,2,32]{2,1,0:T(2,128)S(1)} %get-tuple-element.67.after_ref), channel_id=1, source_target_pairs={{0,4},{4,0},{8,12},{12,8},{16,20},{20,16},{24,28},{28,24},{1,5},{5... | collective-permute-start | bytes 3080 | tf_op jit(solution)/shard_map/ppermute | solution.py:302
  9.0 17.1 %collective-permute-start.5 = (bf16[16,64,128]{2,1,0:T(8,128)(2,1)S(1)}, bf16[16,64,128]{2,1,0:T(8,128)(2,1)S(1)}, u32[]{:S(2)}, u32[]{:S(2)}) collective-permute-start(bf16[16,64,128]{2,1,0:T(8,128)(2,1)S(1)} %get-tuple-element.35.rest_0_), channel_id=1, source_target_pairs={{0,2},{1,3},{2,0},{3,1},{4,6},{5,7},{6,4},{7,5},{8,10},{9,11},{10,... | collective-permute-start | bytes 786440 | tf_op jit(solution)/shard_map/ppermute | solution.py:302
  10.3 10.1 %collective-permute-start.11 = (bf16[16,64,128]{2,1,0:T(8,128)(2,1)S(1)}, bf16[16,64,128]{2,1,0:T(8,128)(2,1)S(1)}, u32[]{:S(2)}, u32[]{:S(2)}) collective-permute-start(bf16[16,64,128]{2,1,0:T(8,128)(2,1)S(1)} %get-tuple-element.40.rest_0_), channel_id=1, source_target_pairs={{0,4},{4,0},{8,12},{12,8},{16,20},{20,16},{24,28},{28,24},{1,5},{5... | collective-permute-start | bytes 786440 | tf_op jit(solution)/shard_map/ppermute | solution.py:302
  10.6 3.6 %slice-start = ((f32[2,2,32]{2,1,0:T(2,128)}), f32[1,2,32]{2,1,0:T(2,128)S(1)}, s32[]{:S(2)}) async-start(f32[2,2,32]{2,1,0:T(2,128)} %copy-done), calls=%async_computation | async-start | bytes 2048 | tf_op jit(solution)/shard_map/slice | solution.py:342
  10.6 7.6 %copy-start.1 = (f32[6]{0:T(128)S(1)}, f32[6]{0:T(128)}, u32[]{:S(2)}) copy-start(f32[6]{0:T(128)} %param.18) | copy-start | bytes 76
  10.6 5.2 %collective-permute-start.3 = (f32[8,2,32]{2,1,0:T(2,128)S(1)}, f32[8,2,32]{2,1,0:T(2,128)S(1)}, u32[]{:S(2)}, u32[]{:S(2)}) collective-permute-start(f32[8,2,32]{2,1,0:T(2,128)S(1)} %get-tuple-element.59.after_ref), channel_id=1, source_target_pairs={{0,8},{4,12},{8,0},{12,4},{16,24},{20,28},{24,16},{28,20},{1,9},{5... | collective-permute-start | bytes 6152 | tf_op jit(solution)/shard_map/ppermute | solution.py:302
  14.3 6.2 %collective-permute-start.6 = (bf16[16,64,128]{2,1,0:T(8,128)(2,1)S(1)}, bf16[16,64,128]{2,1,0:T(8,128)(2,1)S(1)}, u32[]{:S(2)}, u32[]{:S(2)}) collective-permute-start(bf16[16,64,128]{2,1,0:T(8,128)(2,1)S(1)} %get-tuple-element.36.rest_1_), channel_id=1, source_target_pairs={{0,2},{1,3},{2,0},{3,1},{4,6},{5,7},{6,4},{7,5},{8,10},{9,11},{10,... | collective-permute-start | bytes 786440 | tf_op jit(solution)/shard_map/ppermute | solution.py:302
  14.6 7.8 %collective-permute-start.7 = (bf16[16,64,128]{2,1,0:T(8,128)(2,1)S(1)}, bf16[16,64,128]{2,1,0:T(8,128)(2,1)S(1)}, u32[]{:S(2)}, u32[]{:S(2)}) collective-permute-start(bf16[16,64,128]{2,1,0:T(8,128)(2,1)S(1)} %get-tuple-element.37.rest_1_), channel_id=1, source_target_pairs={{0,4},{4,0},{8,12},{12,8},{16,20},{20,16},{24,28},{28,24},{1,5},{5... | collective-permute-start | bytes 786440 | tf_op jit(solution)/shard_map/ppermute | solution.py:302
  15.8 3.6 %collective-permute-start.4 = (f32[16,2,32]{2,1,0:T(2,128)S(1)}, f32[16,2,32]{2,1,0:T(2,128)S(1)}, u32[]{:S(2)}, u32[]{:S(2)}) collective-permute-start(f32[16,2,32]{2,1,0:T(2,128)S(1)} %get-tuple-element.55), channel_id=1, source_target_pairs={{0,16},{4,20},{8,24},{12,28},{16,0},{20,4},{24,8},{28,12},{1,17},{... | collective-permute-start | bytes 12296 | tf_op jit(solution)/shard_map/ppermute | solution.py:302
  23.7 7.2 %copy-start.2 = (f32[41]{0:T(128)S(1)}, f32[41]{0:T(128)}, u32[]{:S(2)}) copy-start(f32[41]{0:T(128)} %param.19) | copy-start | bytes 496
  23.7 3.9 %collective-permute-start.12 = (bf16[32,64,128]{2,1,0:T(8,128)(2,1)S(1)}, bf16[32,64,128]{2,1,0:T(8,128)(2,1)S(1)}, u32[]{:S(2)}, u32[]{:S(2)}) collective-permute-start(bf16[32,64,128]{2,1,0:T(8,128)(2,1)S(1)} %get-tuple-element.41), channel_id=1, source_target_pairs={{0,1},{1,0},{2,3},{3,2},{4,5},{5,4},{6,7},{7,6},{8,9},{9,8},{10,11... | collective-permute-start | bytes 1572872 | tf_op jit(solution)/shard_map/ppermute | solution.py:302
  27.5 2.0 %collective-permute-start.8 = (bf16[32,64,128]{2,1,0:T(8,128)(2,1)S(1)}, bf16[32,64,128]{2,1,0:T(8,128)(2,1)S(1)}, u32[]{:S(2)}, u32[]{:S(2)}) collective-permute-start(bf16[32,64,128]{2,1,0:T(8,128)(2,1)S(1)} %get-tuple-element.38), channel_id=1, source_target_pairs={{0,1},{1,0},{2,3},{3,2},{4,5},{5,4},{6,7},{7,6},{8,9},{9,8},{10,11... | collective-permute-start | bytes 1572872 | tf_op jit(solution)/shard_map/ppermute | solution.py:302
  27.7 7.5 %collective-permute-start.13 = (bf16[16,64,128]{2,1,0:T(8,128)(2,1)S(1)}, bf16[16,64,128]{2,1,0:T(8,128)(2,1)S(1)}, u32[]{:S(2)}, u32[]{:S(2)}) collective-permute-start(bf16[16,64,128]{2,1,0:T(8,128)(2,1)S(1)} %add_convert_fusion), channel_id=1, source_target_pairs={{0,2},{1,3},{2,0},{3,1},{4,6},{5,7},{6,4},{7,5},{8,10},{9,11},{10,... | collective-permute-start | bytes 786440 | tf_op jit(solution)/shard_map/ppermute | solution.py:302
  29.6 7.7 %collective-permute-start.9 = (bf16[16,64,128]{2,1,0:T(8,128)(2,1)S(1)}, bf16[16,64,128]{2,1,0:T(8,128)(2,1)S(1)}, u32[]{:S(2)}, u32[]{:S(2)}) collective-permute-start(bf16[16,64,128]{2,1,0:T(8,128)(2,1)S(1)} %add_convert_fusion.1), channel_id=1, source_target_pairs={{0,8},{4,12},{8,0},{12,4},{16,24},{20,28},{24,16},{28,20},{1,9},{5... | collective-permute-start | bytes 786440 | tf_op jit(solution)/shard_map/ppermute | solution.py:302
  35.2 3.9 %collective-permute-start.14 = (bf16[8,64,128]{2,1,0:T(8,128)(2,1)S(1)}, bf16[8,64,128]{2,1,0:T(8,128)(2,1)S(1)}, u32[]{:S(2)}, u32[]{:S(2)}) collective-permute-start(bf16[8,64,128]{2,1,0:T(8,128)(2,1)S(1)} %add_convert_fusion.2), channel_id=1, source_target_pairs={{0,8},{4,12},{8,0},{12,4},{16,24},{20,28},{24,16},{28,20},{1,9},{5... | collective-permute-start | bytes 393224 | tf_op jit(solution)/shard_map/ppermute | solution.py:302
  37.4 3.9 %collective-permute-start.10 = (bf16[8,64,128]{2,1,0:T(8,128)(2,1)S(1)}, bf16[8,64,128]{2,1,0:T(8,128)(2,1)S(1)}, u32[]{:S(2)}, u32[]{:S(2)}) collective-permute-start(bf16[8,64,128]{2,1,0:T(8,128)(2,1)S(1)} %add_convert_fusion.3), channel_id=1, source_target_pairs={{0,4},{4,0},{8,12},{12,8},{16,20},{20,16},{24,28},{28,24},{1,5},{5... | collective-permute-start | bytes 393224 | tf_op jit(solution)/shard_map/ppermute | solution.py:302
  41.3 6.7 %collective-permute-start.15 = (bf16[4,128,128]{2,1,0:T(8,128)(2,1)S(1)}, bf16[4,128,128]{2,1,0:T(8,128)(2,1)S(1)}, u32[]{:S(2)}, u32[]{:S(2)}) collective-permute-start(bf16[4,128,128]{2,1,0:T(8,128)(2,1)S(1)} %pad_maximum_fusion), channel_id=1, source_target_pairs={{0,16},{4,20},{8,24},{12,28},{16,0},{20,4},{24,8},{28,12},{1,17},{... | collective-permute-start | bytes 393224 | tf_op jit(solution)/shard_map/ppermute | solution.py:302
  48.1 7.5 %collective-permute-start.16 = (bf16[4,32,128]{2,1,0:T(8,128)(2,1)S(1)}, bf16[4,32,128]{2,1,0:T(8,128)(2,1)S(1)}, u32[]{:S(2)}, u32[]{:S(2)}) collective-permute-start(bf16[4,32,128]{2,1,0:T(8,128)(2,1)S(1)} %get-tuple-element.52), channel_id=1, source_target_pairs={{1,2},{2,1},{5,6},{6,5},{9,10},{10,9},{13,14},{14,13},{17,18},{18,... | collective-permute-start | bytes 98312 | tf_op jit(solution)/shard_map/ppermute | solution.py:402
  54.0 1.9 %collective-permute-start.17 = (bf16[4,32,128]{2,1,0:T(8,128)(2,1)S(1)}, bf16[4,32,128]{2,1,0:T(8,128)(2,1)S(1)}, u32[]{:S(2)}, u32[]{:S(2)}) collective-permute-start(bf16[4,32,128]{2,1,0:T(8,128)(2,1)S(1)} %get-tuple-element.51), channel_id=1, source_target_pairs={{0,1},{1,0},{2,3},{3,2},{4,5},{5,4},{6,7},{7,6},{8,9},{9,8},{10,11... | collective-permute-start | bytes 98312 | tf_op jit(solution)/shard_map/ppermute | solution.py:302

commit v10 on v7

--- a/solution.py
+++ b/solution.py
@@ -321,7 +321,7 @@
         [own_facts]
         + [lax.ppermute(own_facts, "band", [(i, i ^ off) for i in range(band_count)]) for off in range(1, band_count)]
     )
-    cut, early = block_count // 2, block_count * 5 // 16
+    cut, early = block_count // 2, block_count // 4
     own, others = [[], []], [[], []]
     begun = match_blocks(0, early, cut, loaded, heights, block_side, own_facts)
     for part in range(max(2, sky_bits)):

time: 56.9 us -> 57 us (level)
  no operation moved by 1% of the time
where the time goes in v10:
time: 57 us; the launch traced here: 56.8 us
  starting transfers between devices  22 us (39%)
  waiting for transfers between devices  19.6 us (34%)
  Pallas kernels  13.2 us (23%)
  other arithmetic  1.57 us (3%)
    ppermute x15, waiting for transfers between devices, swap(): return lax.ppermute(array, axis, [(i, i ^ 1 << bit) for i in range(count)])  17.1 us
    ppermute x15, starting transfers between devices, swap(): return lax.ppermute(array, axis, [(i, i ^ 1 << bit) for i in range(count)])  15.4 us
    pallas_call x4, Pallas kernels, bin_blocks(): pl.pallas_call(functools.partial(bin_kernel, stepped, len(blocks)), grid=...  5.09 us
    pallas_call x3, Pallas kernels, match_blocks(): pl.pallas_call(functools.partial(match_kernel, first, count, skip, not in...  4.67 us
    ppermute x1, starting transfers between devices, local(): lax.ppermute(jnp.where(even, top, bottom), 'band', inner + [(i, j) for j,...  3.71 us
    ppermute x3, starting transfers between devices, local(): lax.ppermute(own_facts, 'band', [(i, i ^ off) for i in range(band_count)])  2.9 us
    pallas_call x1, Pallas kernels, load(): pl.pallas_call(load_kernel, out_shape=out_shape, in_specs=[pl.BlockSpec(m...  1.67 us
    ppermute x1, waiting for transfers between devices, local(): lax.ppermute(jnp.where(even, top, bottom), 'band', inner + [(i, j) for j,...  1.5 us
  transfers between devices with their start and end apart: 19, of which 10 were waited for; matrix products, arithmetic and copies ran while one was open for 3% of the time, Pallas kernels for 18%

profile of v10, /device:TPU:1, one launch (start us, length us, event | category | flops | bytes accessed | tf_op | source)
XLA Modules:
  0.0 56.8 jit_solution(16143118924733239474)
XLA Ops:
  0.0 1.7 %load.1 = (f32[1,2,32]{2,1,0:T(2,128)S(1)}, f32[3,32]{1,0:T(4,128)S(1)}, bf16[384,168]{1,0:T(8,128)(2,1)S(1)}, bf16[768,128]{1,0:T(8,128)(2,1)S(1)}, bf16[168,5376]{1,0:T(8,128)(2,1)S(1)}) custom-call(s32[1,32]{1,0:T(1,128)} %bitcast.30, s32[1,32]{1,0:T(1,128)} %bitcast.31, s32[1,32]{1,0:T(1,128)} %bitcast.32, bf16[32]{0:T(256)(128)(2,1)} %refs_3_.1, ...), custom_call_target="tpu_custom_call" | custom-call | flops 1048576 | bytes 4194304 | tf_op jit(solution)/shard_map/load/pallas_call | solution.py:73
  1.7 2.7 %collective-permute-start.2 = (f32[1,2,32]{2,1,0:T(2,128)S(1)}, f32[1,2,32]{2,1,0:T(2,128)S(1)}, u32[]{:S(2)}, u32[]{:S(2)}) collective-permute-start(f32[1,2,32]{2,1,0:T(2,128)S(1)} %get-tuple-element.24.after_ref), channel_id=1, source_target_pairs={{0,3},{1,2},{2,1},{3,0},{4,7},{5,6},{6,5},{7,4},{8,11},{9,10},{10,... | collective-permute-start | bytes 776 | tf_op jit(solution)/shard_map/ppermute | solution.py:322
  4.4 0.0 collective-permute-start.1
  4.4 0.2 collective-permute-start
  4.6 1.2 %match_blocks.3 = (bf16[16,64,128]{2,1,0:T(8,128)(2,1)S(1)}, bf16[16,64,128]{2,1,0:T(8,128)(2,1)S(1)}) custom-call(f32[1,2,32]{2,1,0:T(2,128)S(1)} %get-tuple-element.24.after_ref, f32[3,32]{1,0:T(4,128)S(1)} %get-tuple-element.25.coef_ref, bf16[384,168]{1,0:T(8,128)(2,1)S(1)} %get-tuple-element.26.rowk_ref, ...), custom_call_target="tpu_custom_call" | custom-call | flops 1222115328 | bytes 2097152 | tf_op jit(solution)/shard_map/match_blocks/pallas_call | solution.py:117
  5.8 0.0 collective-permute-done.1
  5.8 1.0 %collective-permute-done = f32[1,2,32]{2,1,0:T(2,128)S(1)} collective-permute-done((f32[1,2,32]{2,1,0:T(2,128)S(1)}, f32[1,2,32]{2,1,0:T(2,128)S(1)}, u32[]{:S(2)}, u32[]{:S(2)}) %collective-permute-start) | collective-permute-done | bytes 288 | tf_op jit(solution)/shard_map/ppermute | solution.py:322
  6.8 0.0 collective-permute-done.2
  6.8 1.3 %collective-permute-start.3 = (f32[4,2,32]{2,1,0:T(2,128)S(1)}, f32[4,2,32]{2,1,0:T(2,128)S(1)}, u32[]{:S(2)}, u32[]{:S(2)}) collective-permute-start(f32[4,2,32]{2,1,0:T(2,128)S(1)} %get-tuple-element.70.after_ref), channel_id=1, source_target_pairs={{0,4},{4,0},{8,12},{12,8},{16,20},{20,16},{24,28},{28,24},{1,5},{5... | collective-permute-start | bytes 3080 | tf_op jit(solution)/shard_map/ppermute | solution.py:302
  8.1 1.3 %match_blocks.4 = (bf16[16,64,128]{2,1,0:T(8,128)(2,1)S(1)}, bf16[16,64,128]{2,1,0:T(8,128)(2,1)S(1)}) custom-call(f32[4,2,32]{2,1,0:T(2,128)S(1)} %get-tuple-element.70.after_ref, f32[3,32]{1,0:T(4,128)S(1)} %get-tuple-element.25.coef_ref, bf16[384,168]{1,0:T(8,128)(2,1)S(1)} %get-tuple-element.26.rowk_ref, ...), custom_call_target="tpu_custom_call", output_to_operand_aliasing={{0}: (5, {}), {1}: (6, {})} | custom-call | flops 1222115328 | bytes 2097152 | tf_op jit(solution)/shard_map/match_blocks/pallas_call | solution.py:117
  9.4 0.4 collective-permute-start.6
  9.8 0.3 collective-permute-start.12
  10.0 0.0 collective-permute-done.3
  10.1 0.0 copy-start
  10.1 1.4 %collective-permute-start.4 = (f32[8,2,32]{2,1,0:T(2,128)S(1)}, f32[8,2,32]{2,1,0:T(2,128)S(1)}, u32[]{:S(2)}, u32[]{:S(2)}) collective-permute-start(f32[8,2,32]{2,1,0:T(2,128)S(1)} %get-tuple-element.55.after_ref), channel_id=1, source_target_pairs={{0,8},{4,12},{8,0},{12,4},{16,24},{20,28},{24,16},{28,20},{1,9},{5... | collective-permute-start | bytes 6152 | tf_op jit(solution)/shard_map/ppermute | solution.py:302
  11.4 2.2 %match_blocks.5 = (bf16[16,64,128]{2,1,0:T(8,128)(2,1)S(1)}, bf16[16,64,128]{2,1,0:T(8,128)(2,1)S(1)}) custom-call(f32[8,2,32]{2,1,0:T(2,128)S(1)} %get-tuple-element.55.after_ref, f32[3,32]{1,0:T(4,128)S(1)} %get-tuple-element.25.coef_ref, bf16[384,168]{1,0:T(8,128)(2,1)S(1)} %get-tuple-element.26.rowk_ref, ...), custom_call_target="tpu_custom_call" | custom-call | flops 2444230656 | bytes 2097152 | tf_op jit(solution)/shard_map/match_blocks/pallas_call | solution.py:117
  13.7 1.2 %collective-permute-start.7 = (bf16[16,64,128]{2,1,0:T(8,128)(2,1)S(1)}, bf16[16,64,128]{2,1,0:T(8,128)(2,1)S(1)}, u32[]{:S(2)}, u32[]{:S(2)}) collective-permute-start(bf16[16,64,128]{2,1,0:T(8,128)(2,1)S(1)} %get-tuple-element.32.rest_1_), channel_id=1, source_target_pairs={{0,2},{1,3},{2,0},{3,1},{4,6},{5,7},{6,4},{7,5},{8,10},{9,11},{10,... | collective-permute-start | bytes 786440 | tf_op jit(solution)/shard_map/ppermute | solution.py:302
  14.9 1.2 %collective-permute-start.8 = (bf16[16,64,128]{2,1,0:T(8,128)(2,1)S(1)}, bf16[16,64,128]{2,1,0:T(8,128)(2,1)S(1)}, u32[]{:S(2)}, u32[]{:S(2)}) collective-permute-start(bf16[16,64,128]{2,1,0:T(8,128)(2,1)S(1)} %get-tuple-element.33.rest_1_), channel_id=1, source_target_pairs={{0,4},{4,0},{8,12},{12,8},{16,20},{20,16},{24,28},{28,24},{1,5},{5... | collective-permute-start | bytes 786440 | tf_op jit(solution)/shard_map/ppermute | solution.py:302
  16.1 0.0 collective-permute-done.4
  16.2 2.4 %collective-permute-start.5 = (f32[16,2,32]{2,1,0:T(2,128)S(1)}, f32[16,2,32]{2,1,0:T(2,128)S(1)}, u32[]{:S(2)}, u32[]{:S(2)}) collective-permute-start(f32[16,2,32]{2,1,0:T(2,128)S(1)} %get-tuple-element.51), channel_id=1, source_target_pairs={{0,16},{4,20},{8,24},{12,28},{16,0},{20,4},{24,8},{28,12},{1,17},{... | collective-permute-start | bytes 12296 | tf_op jit(solution)/shard_map/ppermute | solution.py:302
  18.5 0.0 copy-done
  18.5 0.1 select_reduce_fusion.1
  18.6 1.1 %collective-permute-done.5 = f32[16,2,32]{2,1,0:T(2,128)S(1)} collective-permute-done((f32[16,2,32]{2,1,0:T(2,128)S(1)}, f32[16,2,32]{2,1,0:T(2,128)S(1)}, u32[]{:S(2)}, u32[]{:S(2)}) %collective-permute-start.5) | collective-permute-done | bytes 4128 | tf_op jit(solution)/shard_map/ppermute | solution.py:302
  19.8 0.9 %select_reduce_fusion = f32[3,32]{1,0:T(4,128)S(1)} fusion(f32[32,32]{1,0:T(8,128)S(1)} %bitcast.27, f32[32,32]{1,0:T(8,128)S(1)} %bitcast.26, f32[3,32]{1,0:T(4,128)S(1)} %bitcast.28), kind=kLoop, calls=%fused_computation | loop fusion | flops 294816 | bytes 8960 | tf_op jit(solution)/shard_map/reduce_sum | solution.py:343
  20.8 0.0 collective-permute-done.12.rest_2_
  20.8 0.7 %collective-permute-done.7.rest_3_.after_ref = bf16[16,64,128]{2,1,0:T(8,128)(2,1)S(1)} collective-permute-done((bf16[16,64,128]{2,1,0:T(8,128)(2,1)S(1)}, bf16[16,64,128]{2,1,0:T(8,128)(2,1)S(1)}, u32[]{:S(2)}, u32[]{:S(2)}) %collective-permute-start.7) | collective-permute-done | bytes 262176 | tf_op jit(solution)/shard_map/ppermute | solution.py:302
  21.5 0.0 collective-permute-done.8.after_ref.rest_3_
  21.5 1.4 %bins_sent.3 = (bf16[32,64,128]{2,1,0:T(8,128)(2,1)S(1)}, bf16[16,64,128]{2,1,0:T(8,128)(2,1)S(1)}) custom-call(s32[2,32]{1,0:T(2,128)S(1)} %compare_select_fusion.7.bins_ref, f32[2,32]{1,0:T(2,128)S(1)} %pad_maximum_fusion.2.scale_ref, bf16[16,64,128]{2,1,0:T(8,128)(2,1)S(1)} %collective-permute-done.7.rest_3_.after_ref, ...), custom_call_target="tpu_custom_call" | custom-call | flops 3670016 | bytes 1835008 | tf_op jit(solution)/shard_map/bins_sent/pallas_call | solution.py:169
  22.9 0.0 copy-start.1
  22.9 3.9 %collective-permute-start.13 = (bf16[32,64,128]{2,1,0:T(8,128)(2,1)S(1)}, bf16[32,64,128]{2,1,0:T(8,128)(2,1)S(1)}, u32[]{:S(2)}, u32[]{:S(2)}) collective-permute-start(bf16[32,64,128]{2,1,0:T(8,128)(2,1)S(1)} %get-tuple-element.37), channel_id=1, source_target_pairs={{0,1},{1,0},{2,3},{3,2},{4,5},{5,4},{6,7},{7,6},{8,9},{9,8},{10,11... | collective-permute-start | bytes 1572872 | tf_op jit(solution)/shard_map/ppermute | solution.py:302
  26.8 0.0 collective-permute-done.6.rest_2_
  26.8 1.4 %bins_sent.2 = (bf16[32,64,128]{2,1,0:T(8,128)(2,1)S(1)}, bf16[16,64,128]{2,1,0:T(8,128)(2,1)S(1)}) custom-call(s32[2,32]{1,0:T(2,128)S(1)} %compare_select_fusion.10.bins_ref, f32[2,32]{1,0:T(2,128)S(1)} %stack.24.scale_ref, bf16[16,64,128]{2,1,0:T(8,128)(2,1)S(1)} %collective-permute-done.8.after_ref.rest_3_, ...), custom_call_target="tpu_custom_call" | custom-call | flops 3670016 | bytes 1835008 | tf_op jit(solution)/shard_map/bins_sent/pallas_call | solution.py:169
  28.2 0.1 collective-permute-start.9
  28.3 0.0 collective-permute-done.13
  28.3 0.1 add_convert_fusion
  28.4 0.3 collective-permute-start.14
  28.7 1.5 %collective-permute-done.9 = bf16[32,64,128]{2,1,0:T(8,128)(2,1)S(1)} collective-permute-done((bf16[32,64,128]{2,1,0:T(8,128)(2,1)S(1)}, bf16[32,64,128]{2,1,0:T(8,128)(2,1)S(1)}, u32[]{:S(2)}, u32[]{:S(2)}) %collective-permute-start.9) | collective-permute-done | bytes 524320 | tf_op jit(solution)/shard_map/ppermute | solution.py:302
  30.2 0.1 add_convert_fusion.1
  30.2 0.2 collective-permute-start.10
  30.5 0.0 copy-done.1
  30.5 0.3 filters.1
  30.8 1.2 %bins_kept.2 = bf16[16,64,128]{2,1,0:T(8,128)(2,1)S(1)} custom-call(s32[2,32]{1,0:T(2,128)S(1)} %get-tuple-element.39.bins_ref, f32[2,32]{1,0:T(2,128)S(1)} %stack.24.scale_ref, bf16[128,192]{1,0:T(8,128)(2,1)S(1)} %get-tuple-element.22.after_ref.row_filter_ref, bf16[16,64,128]{2,1,0:T(8,128)(2,1)S(1)} %get-tuple-element.31.rest_0_, ...), custom_call_target="tpu_custom_call" | custom-call | flops 2621440 | bytes 1310720 | tf_op jit(solution)/shard_map/bins_kept/pallas_call | solution.py:169
  32.0 1.2 %bins_kept.3 = bf16[16,64,128]{2,1,0:T(8,128)(2,1)S(1)} custom-call(s32[2,32]{1,0:T(2,128)S(1)} %get-tuple-element.41.bins_ref, f32[2,32]{1,0:T(2,128)S(1)} %pad_maximum_fusion.2.scale_ref, bf16[128,192]{1,0:T(8,128)(2,1)S(1)} %get-tuple-element.22.after_ref.row_filter_ref, bf16[16,64,128]{2,1,0:T(8,128)(2,1)S(1)} %get-tuple-element.36.rest_0_, ...), custom_call_target="tpu_custom_call" | custom-call | flops 2621440 | bytes 1310720 | tf_op jit(solution)/shard_map/bins_kept/pallas_call | solution.py:169
  33.2 2.7 %collective-permute-done.14 = bf16[16,64,128]{2,1,0:T(8,128)(2,1)S(1)} collective-permute-done((bf16[16,64,128]{2,1,0:T(8,128)(2,1)S(1)}, bf16[16,64,128]{2,1,0:T(8,128)(2,1)S(1)}, u32[]{:S(2)}, u32[]{:S(2)}) %collective-permute-start.14) | collective-permute-done | bytes 262176 | tf_op jit(solution)/shard_map/ppermute | solution.py:302
  35.8 0.1 add_convert_fusion.2
  35.9 0.2 collective-permute-start.15
  36.1 2.0 %collective-permute-done.10 = bf16[16,64,128]{2,1,0:T(8,128)(2,1)S(1)} collective-permute-done((bf16[16,64,128]{2,1,0:T(8,128)(2,1)S(1)}, bf16[16,64,128]{2,1,0:T(8,128)(2,1)S(1)}, u32[]{:S(2)}, u32[]{:S(2)}) %collective-permute-start.10) | collective-permute-done | bytes 262176 | tf_op jit(solution)/shard_map/ppermute | solution.py:302
  38.1 0.1 add_convert_fusion.3
  38.1 0.3 collective-permute-start.11
  38.4 1.4 %collective-permute-done.15 = bf16[8,64,128]{2,1,0:T(8,128)(2,1)S(1)} collective-permute-done((bf16[8,64,128]{2,1,0:T(8,128)(2,1)S(1)}, bf16[8,64,128]{2,1,0:T(8,128)(2,1)S(1)}, u32[]{:S(2)}, u32[]{:S(2)}) %collective-permute-start.15) | collective-permute-done | bytes 131104 | tf_op jit(solution)/shard_map/ppermute | solution.py:302
  39.8 0.1 add_convert_fusion.4
  39.9 2.1 %collective-permute-done.11 = bf16[8,64,128]{2,1,0:T(8,128)(2,1)S(1)} collective-permute-done((bf16[8,64,128]{2,1,0:T(8,128)(2,1)S(1)}, bf16[8,64,128]{2,1,0:T(8,128)(2,1)S(1)}, u32[]{:S(2)}, u32[]{:S(2)}) %collective-permute-start.11) | collective-permute-done | bytes 131104 | tf_op jit(solution)/shard_map/ppermute | solution.py:302
  42.0 0.1 add_convert_fusion.5
  42.1 2.3 %collective-permute-start.16 = (bf16[4,128,128]{2,1,0:T(8,128)(2,1)S(1)}, bf16[4,128,128]{2,1,0:T(8,128)(2,1)S(1)}, u32[]{:S(2)}, u32[]{:S(2)}) collective-permute-start(bf16[4,128,128]{2,1,0:T(8,128)(2,1)S(1)} %pad_maximum_fusion), channel_id=1, source_target_pairs={{0,16},{4,20},{8,24},{12,28},{16,0},{20,4},{24,8},{28,12},{1,17},{... | collective-permute-start | bytes 393224 | tf_op jit(solution)/shard_map/ppermute | solution.py:302
  44.4 5.6 %collective-permute-done.16 = bf16[4,128,128]{2,1,0:T(8,128)(2,1)S(1)} collective-permute-done((bf16[4,128,128]{2,1,0:T(8,128)(2,1)S(1)}, bf16[4,128,128]{2,1,0:T(8,128)(2,1)S(1)}, u32[]{:S(2)}, u32[]{:S(2)}) %collective-permute-start.16) | collective-permute-done | bytes 131104 | tf_op jit(solution)/shard_map/ppermute | solution.py:302
  50.0 3.7 %collective-permute-start.17 = (bf16[4,32,128]{2,1,0:T(8,128)(2,1)S(1)}, bf16[4,32,128]{2,1,0:T(8,128)(2,1)S(1)}, u32[]{:S(2)}, u32[]{:S(2)}) collective-permute-start(bf16[4,32,128]{2,1,0:T(8,128)(2,1)S(1)} %get-tuple-element.48), channel_id=1, source_target_pairs={{1,2},{2,1},{5,6},{6,5},{9,10},{10,9},{13,14},{14,13},{17,18},{18,... | collective-permute-start | bytes 98312 | tf_op jit(solution)/shard_map/ppermute | solution.py:400
  53.7 0.1 collective-permute-start.18
  53.8 1.5 %collective-permute-done.17.beyond_ref = bf16[4,32,128]{2,1,0:T(8,128)(2,1)S(1)} collective-permute-done((bf16[4,32,128]{2,1,0:T(8,128)(2,1)S(1)}, bf16[4,32,128]{2,1,0:T(8,128)(2,1)S(1)}, u32[]{:S(2)}, u32[]{:S(2)}) %collective-permute-start.17) | collective-permute-done | bytes 32800 | tf_op jit(solution)/shard_map/ppermute | solution.py:400
  55.3 0.3 smooth.1.partial_ref
  55.6 0.0 collective-permute-done.18.paired_ref
  55.6 1.2 %detect.1 = f32[128,512]{1,0:T(8,128)} custom-call(s32[1]{0:T(128)} %bitcast.even_ref, bf16[128,192]{1,0:T(8,128)(2,1)S(1)} %get-tuple-element.22.after_ref.row_filter_ref, bf16[384,128]{1,0:T(8,128)(2,1)S(1)} %get-tuple-element.23.col_filter_ref, f32[4,128,128]{2,1,0:T(8,128)S(1)} %smooth.1.partial_ref, ...), custom_call_target="tpu_custom_call" | custom-call | tf_op jit(solution)/shard_map/detect/pallas_call | solution.py:254
  (26 shorter events, 0.3 us)
Async XLA Ops:
  1.7 5.1 %collective-permute-start.2 = (f32[1,2,32]{2,1,0:T(2,128)S(1)}, f32[1,2,32]{2,1,0:T(2,128)S(1)}, u32[]{:S(2)}, u32[]{:S(2)}) collective-permute-start(f32[1,2,32]{2,1,0:T(2,128)S(1)} %get-tuple-element.24.after_ref), channel_id=1, source_target_pairs={{0,3},{1,2},{2,1},{3,0},{4,7},{5,6},{6,5},{7,4},{8,11},{9,10},{10,... | collective-permute-start | bytes 776 | tf_op jit(solution)/shard_map/ppermute | solution.py:322
  4.4 1.4 %collective-permute-start.1 = (f32[1,2,32]{2,1,0:T(2,128)S(1)}, f32[1,2,32]{2,1,0:T(2,128)S(1)}, u32[]{:S(2)}, u32[]{:S(2)}) collective-permute-start(f32[1,2,32]{2,1,0:T(2,128)S(1)} %get-tuple-element.24.after_ref), channel_id=1, source_target_pairs={{0,1},{1,0},{2,3},{3,2},{4,5},{5,4},{6,7},{7,6},{8,9},{9,8},{10,11... | collective-permute-start | bytes 776 | tf_op jit(solution)/shard_map/ppermute | solution.py:322
  4.4 2.4 %collective-permute-start = (f32[1,2,32]{2,1,0:T(2,128)S(1)}, f32[1,2,32]{2,1,0:T(2,128)S(1)}, u32[]{:S(2)}, u32[]{:S(2)}) collective-permute-start(f32[1,2,32]{2,1,0:T(2,128)S(1)} %get-tuple-element.24.after_ref), channel_id=1, source_target_pairs={{0,2},{1,3},{2,0},{3,1},{4,6},{5,7},{6,4},{7,5},{8,10},{9,11},{10,... | collective-permute-start | bytes 776 | tf_op jit(solution)/shard_map/ppermute | solution.py:322
  6.8 3.2 %collective-permute-start.3 = (f32[4,2,32]{2,1,0:T(2,128)S(1)}, f32[4,2,32]{2,1,0:T(2,128)S(1)}, u32[]{:S(2)}, u32[]{:S(2)}) collective-permute-start(f32[4,2,32]{2,1,0:T(2,128)S(1)} %get-tuple-element.70.after_ref), channel_id=1, source_target_pairs={{0,4},{4,0},{8,12},{12,8},{16,20},{20,16},{24,28},{28,24},{1,5},{5... | collective-permute-start | bytes 3080 | tf_op jit(solution)/shard_map/ppermute | solution.py:302
  9.4 17.4 %collective-permute-start.6 = (bf16[16,64,128]{2,1,0:T(8,128)(2,1)S(1)}, bf16[16,64,128]{2,1,0:T(8,128)(2,1)S(1)}, u32[]{:S(2)}, u32[]{:S(2)}) collective-permute-start(bf16[16,64,128]{2,1,0:T(8,128)(2,1)S(1)} %get-tuple-element.31.rest_0_), channel_id=1, source_target_pairs={{0,2},{1,3},{2,0},{3,1},{4,6},{5,7},{6,4},{7,5},{8,10},{9,11},{10,... | collective-permute-start | bytes 786440 | tf_op jit(solution)/shard_map/ppermute | solution.py:302
  9.8 11.0 %collective-permute-start.12 = (bf16[16,64,128]{2,1,0:T(8,128)(2,1)S(1)}, bf16[16,64,128]{2,1,0:T(8,128)(2,1)S(1)}, u32[]{:S(2)}, u32[]{:S(2)}) collective-permute-start(bf16[16,64,128]{2,1,0:T(8,128)(2,1)S(1)} %get-tuple-element.36.rest_0_), channel_id=1, source_target_pairs={{0,4},{4,0},{8,12},{12,8},{16,20},{20,16},{24,28},{28,24},{1,5},{5... | collective-permute-start | bytes 786440 | tf_op jit(solution)/shard_map/ppermute | solution.py:302
  10.1 8.5 %copy-start = (f32[6]{0:T(128)S(1)}, f32[6]{0:T(128)}, u32[]{:S(2)}) copy-start(f32[6]{0:T(128)} %param.18) | copy-start | bytes 76
  10.1 6.1 %collective-permute-start.4 = (f32[8,2,32]{2,1,0:T(2,128)S(1)}, f32[8,2,32]{2,1,0:T(2,128)S(1)}, u32[]{:S(2)}, u32[]{:S(2)}) collective-permute-start(f32[8,2,32]{2,1,0:T(2,128)S(1)} %get-tuple-element.55.after_ref), channel_id=1, source_target_pairs={{0,8},{4,12},{8,0},{12,4},{16,24},{20,28},{24,16},{28,20},{1,9},{5... | collective-permute-start | bytes 6152 | tf_op jit(solution)/shard_map/ppermute | solution.py:302
  13.7 7.8 %collective-permute-start.7 = (bf16[16,64,128]{2,1,0:T(8,128)(2,1)S(1)}, bf16[16,64,128]{2,1,0:T(8,128)(2,1)S(1)}, u32[]{:S(2)}, u32[]{:S(2)}) collective-permute-start(bf16[16,64,128]{2,1,0:T(8,128)(2,1)S(1)} %get-tuple-element.32.rest_1_), channel_id=1, source_target_pairs={{0,2},{1,3},{2,0},{3,1},{4,6},{5,7},{6,4},{7,5},{8,10},{9,11},{10,... | collective-permute-start | bytes 786440 | tf_op jit(solution)/shard_map/ppermute | solution.py:302
  14.9 6.6 %collective-permute-start.8 = (bf16[16,64,128]{2,1,0:T(8,128)(2,1)S(1)}, bf16[16,64,128]{2,1,0:T(8,128)(2,1)S(1)}, u32[]{:S(2)}, u32[]{:S(2)}) collective-permute-start(bf16[16,64,128]{2,1,0:T(8,128)(2,1)S(1)} %get-tuple-element.33.rest_1_), channel_id=1, source_target_pairs={{0,4},{4,0},{8,12},{12,8},{16,20},{20,16},{24,28},{28,24},{1,5},{5... | collective-permute-start | bytes 786440 | tf_op jit(solution)/shard_map/ppermute | solution.py:302
  16.2 3.6 %collective-permute-start.5 = (f32[16,2,32]{2,1,0:T(2,128)S(1)}, f32[16,2,32]{2,1,0:T(2,128)S(1)}, u32[]{:S(2)}, u32[]{:S(2)}) collective-permute-start(f32[16,2,32]{2,1,0:T(2,128)S(1)} %get-tuple-element.51), channel_id=1, source_target_pairs={{0,16},{4,20},{8,24},{12,28},{16,0},{20,4},{24,8},{28,12},{1,17},{... | collective-permute-start | bytes 12296 | tf_op jit(solution)/shard_map/ppermute | solution.py:302
  22.9 7.6 %copy-start.1 = (f32[41]{0:T(128)S(1)}, f32[41]{0:T(128)}, u32[]{:S(2)}) copy-start(f32[41]{0:T(128)} %param.19) | copy-start | bytes 496
  22.9 5.4 %collective-permute-start.13 = (bf16[32,64,128]{2,1,0:T(8,128)(2,1)S(1)}, bf16[32,64,128]{2,1,0:T(8,128)(2,1)S(1)}, u32[]{:S(2)}, u32[]{:S(2)}) collective-permute-start(bf16[32,64,128]{2,1,0:T(8,128)(2,1)S(1)} %get-tuple-element.37), channel_id=1, source_target_pairs={{0,1},{1,0},{2,3},{3,2},{4,5},{5,4},{6,7},{7,6},{8,9},{9,8},{10,11... | collective-permute-start | bytes 1572872 | tf_op jit(solution)/shard_map/ppermute | solution.py:302
  28.2 2.0 %collective-permute-start.9 = (bf16[32,64,128]{2,1,0:T(8,128)(2,1)S(1)}, bf16[32,64,128]{2,1,0:T(8,128)(2,1)S(1)}, u32[]{:S(2)}, u32[]{:S(2)}) collective-permute-start(bf16[32,64,128]{2,1,0:T(8,128)(2,1)S(1)} %get-tuple-element.34), channel_id=1, source_target_pairs={{0,1},{1,0},{2,3},{3,2},{4,5},{5,4},{6,7},{7,6},{8,9},{9,8},{10,11... | collective-permute-start | bytes 1572872 | tf_op jit(solution)/shard_map/ppermute | solution.py:302
  28.4 7.5 %collective-permute-start.14 = (bf16[16,64,128]{2,1,0:T(8,128)(2,1)S(1)}, bf16[16,64,128]{2,1,0:T(8,128)(2,1)S(1)}, u32[]{:S(2)}, u32[]{:S(2)}) collective-permute-start(bf16[16,64,128]{2,1,0:T(8,128)(2,1)S(1)} %add_convert_fusion), channel_id=1, source_target_pairs={{0,2},{1,3},{2,0},{3,1},{4,6},{5,7},{6,4},{7,5},{8,10},{9,11},{10,... | collective-permute-start | bytes 786440 | tf_op jit(solution)/shard_map/ppermute | solution.py:302
  30.2 7.8 %collective-permute-start.10 = (bf16[16,64,128]{2,1,0:T(8,128)(2,1)S(1)}, bf16[16,64,128]{2,1,0:T(8,128)(2,1)S(1)}, u32[]{:S(2)}, u32[]{:S(2)}) collective-permute-start(bf16[16,64,128]{2,1,0:T(8,128)(2,1)S(1)} %add_convert_fusion.1), channel_id=1, source_target_pairs={{0,8},{4,12},{8,0},{12,4},{16,24},{20,28},{24,16},{28,20},{1,9},{5... | collective-permute-start | bytes 786440 | tf_op jit(solution)/shard_map/ppermute | solution.py:302
  35.9 3.9 %collective-permute-start.15 = (bf16[8,64,128]{2,1,0:T(8,128)(2,1)S(1)}, bf16[8,64,128]{2,1,0:T(8,128)(2,1)S(1)}, u32[]{:S(2)}, u32[]{:S(2)}) collective-permute-start(bf16[8,64,128]{2,1,0:T(8,128)(2,1)S(1)} %add_convert_fusion.2), channel_id=1, source_target_pairs={{0,8},{4,12},{8,0},{12,4},{16,24},{20,28},{24,16},{28,20},{1,9},{5... | collective-permute-start | bytes 393224 | tf_op jit(solution)/shard_map/ppermute | solution.py:302
  38.1 3.9 %collective-permute-start.11 = (bf16[8,64,128]{2,1,0:T(8,128)(2,1)S(1)}, bf16[8,64,128]{2,1,0:T(8,128)(2,1)S(1)}, u32[]{:S(2)}, u32[]{:S(2)}) collective-permute-start(bf16[8,64,128]{2,1,0:T(8,128)(2,1)S(1)} %add_convert_fusion.3), channel_id=1, source_target_pairs={{0,4},{4,0},{8,12},{12,8},{16,20},{20,16},{24,28},{28,24},{1,5},{5... | collective-permute-start | bytes 393224 | tf_op jit(solution)/shard_map/ppermute | solution.py:302
  42.1 7.8 %collective-permute-start.16 = (bf16[4,128,128]{2,1,0:T(8,128)(2,1)S(1)}, bf16[4,128,128]{2,1,0:T(8,128)(2,1)S(1)}, u32[]{:S(2)}, u32[]{:S(2)}) collective-permute-start(bf16[4,128,128]{2,1,0:T(8,128)(2,1)S(1)} %pad_maximum_fusion), channel_id=1, source_target_pairs={{0,16},{4,20},{8,24},{12,28},{16,0},{20,4},{24,8},{28,12},{1,17},{... | collective-permute-start | bytes 393224 | tf_op jit(solution)/shard_map/ppermute | solution.py:302
  50.0 5.3 %collective-permute-start.17 = (bf16[4,32,128]{2,1,0:T(8,128)(2,1)S(1)}, bf16[4,32,128]{2,1,0:T(8,128)(2,1)S(1)}, u32[]{:S(2)}, u32[]{:S(2)}) collective-permute-start(bf16[4,32,128]{2,1,0:T(8,128)(2,1)S(1)} %get-tuple-element.48), channel_id=1, source_target_pairs={{1,2},{2,1},{5,6},{6,5},{9,10},{10,9},{13,14},{14,13},{17,18},{18,... | collective-permute-start | bytes 98312 | tf_op jit(solution)/shard_map/ppermute | solution.py:400
  53.7 1.9 %collective-permute-start.18 = (bf16[4,32,128]{2,1,0:T(8,128)(2,1)S(1)}, bf16[4,32,128]{2,1,0:T(8,128)(2,1)S(1)}, u32[]{:S(2)}, u32[]{:S(2)}) collective-permute-start(bf16[4,32,128]{2,1,0:T(8,128)(2,1)S(1)} %get-tuple-element.47), channel_id=1, source_target_pairs={{0,1},{1,0},{2,3},{3,2},{4,5},{5,4},{6,7},{7,6},{8,9},{9,8},{10,11... | collective-permute-start | bytes 98312 | tf_op jit(solution)/shard_map/ppermute | solution.py:302
